TPU v7x, 128 devices: a whole 4x4x4 slice. The times are simulated.
128 devices in a mesh: dp: 32 (over y, z, core), mp: 4 (over x).
Axes of the slice: x: 4, y: 4, z: 4, core: 2. Of those that a mesh axis runs over, the one named last changes fastest.
Arguments:
- layer_input: bfloat16 [32768, 1024], P(('dp', 'mp')), may hold values from -6 to 6
- lengths: int32 [32], P('dp'), may hold values from 769 to 1024, as said below
- routes: int32 [32768, 8], P(('dp', 'mp')), may hold values from 0 to 31, all different within a row; in each aligned block of 256 rows (0 to 255, 256 to 511, ...) at most 96 rows name the same one
- attn_gain: float32 [1024], replicated, may hold values from 0.5 to 1.5
- query_gain: float32 [64], replicated, may hold values from 0.5 to 1.5
- key_gain: float32 [64], replicated, may hold values from 0.5 to 1.5
- query_weight: bfloat16 [1024, 1024], P('dp', 'mp'), may hold values from -0.1875 to 0.1875
- key_value_weight: bfloat16 [1024, 2, 512], P('dp', None, 'mp'), may hold values from -0.1875 to 0.1875
- out_weight: bfloat16 [1024, 1024], P('dp', 'mp'), may hold values from -1.5 to 1.5
- ffn_gain: float32 [1024], replicated, may hold values from 0.5 to 1.5
- router_weight: bfloat16 [1024, 32], replicated, may hold values from -0.09375 to 0.09375
- gate_weight: bfloat16 [32, 1024, 512], P('dp'), may hold values from -0.1875 to 0.1875
- up_weight: bfloat16 [32, 1024, 512], P('dp'), may hold values from -0.1875 to 0.1875
- down_weight: bfloat16 [32, 512, 1024], P('dp'), may hold values from -0.75 to 0.75
- cotangent: bfloat16 [32768, 1024], P(('dp', 'mp')), may hold values from -6 to 6
Outputs:
- layer_output: bfloat16 [32768, 1024], P(('dp', 'mp'))
- input_grad: float32 [32768, 1024], P(('dp', 'mp'))
- attn_gain_grad: float32 [1024], replicated
- query_gain_grad: float32 [64], replicated
- key_gain_grad: float32 [64], replicated
- query_weight_grad: float32 [1024, 1024], P('dp', 'mp')
- key_value_weight_grad: float32 [1024, 2, 512], P('dp', None, 'mp')
- out_weight_grad: float32 [1024, 1024], P('dp', 'mp')
- ffn_gain_grad: float32 [1024], replicated
- router_weight_grad: float32 [1024, 32], replicated
- gate_weight_grad: float32 [32, 1024, 512], P('dp', 'mp')
- up_weight_grad: float32 [32, 1024, 512], P('dp', 'mp')
- down_weight_grad: float32 [32, 512, 1024], P('dp', 'mp')
Inputs may be any that keep to these rules, and one draw needn't show every extreme that they name: `lengths`: places at or past a sequence's length are padding; some sequence has exactly 1024 tokens. `routes`: A row names 8 different experts. In each aligned block of 256 rows (the rows of one device) no expert is named by more than 96 rows, a bound that some block reaches.
All inputs are finite; a program needn't handle non-finite values.
Results may differ from a plain program's by a relative error of at most 0.024.
Values may be sent and summed in bfloat16 or wider, within the bound.
No kernel may reach another device: no remote copies, remote signals or barrier semaphores. Data moves between devices by JAX's collectives and lax.ppermute only.
A program may use at most 192 MiB of HBM per device.

v0:
```python
from functools import partial

import jax
import jax.numpy as jnp
from jax import lax
from jax.sharding import PartitionSpec as P

HDIM = 64
EXP_DEV = 1
LEN = 1024


EPS = 1e-06


def norm_rows(tensor, gain_vec):
    return tensor * lax.rsqrt(jnp.mean(tensor * tensor, axis=-1, keepdims=True) + EPS) * gain_vec


def norm_back(tensor, gain_vec, upstream):
    scale = lax.rsqrt(jnp.mean(tensor * tensor, axis=-1, keepdims=True) + EPS)
    normed = tensor * scale
    grad_normed = upstream * gain_vec
    gain_grad = jnp.sum(upstream * normed, axis=0)
    tensor_grad = scale * (
        grad_normed - normed * jnp.mean(grad_normed * normed, axis=-1, keepdims=True)
    )
    return (tensor_grad, gain_grad)


def rope_tables():
    places = jnp.arange(LEN, dtype=jnp.float32)
    inverse = jnp.power(10000.0, -2.0 * jnp.arange(HDIM // 2, dtype=jnp.float32) / HDIM)
    angles = places[:, None] * inverse[None, :]
    return (jnp.cos(angles), jnp.sin(angles))


def rotate(tensor, cos_tab, sin_tab):
    first_half = tensor[..., : HDIM // 2]
    second_half = tensor[..., HDIM // 2 :]
    cos_b = cos_tab[:, None, :]
    sin_b = sin_tab[:, None, :]
    return jnp.concatenate(
        [first_half * cos_b - second_half * sin_b, second_half * cos_b + first_half * sin_b],
        axis=-1,
    )


def contract(left, right, left_dim, right_dim):
    return lax.dot_general(
        left, right, (((left_dim,), (right_dim,)), ((), ())), preferred_element_type=jnp.float32
    )


def prepare(cos_tab, sin_tab, query_raw, pair_raw, query_gain, key_gain):
    seq_count = query_raw.shape[0] // LEN
    head_count = query_raw.shape[1] // HDIM
    kv_count = pair_raw.shape[2] // HDIM
    query_ready = rotate(
        norm_rows(query_raw.reshape(seq_count, LEN, head_count, HDIM), query_gain), cos_tab, sin_tab
    )
    key_ready = rotate(
        norm_rows(pair_raw[:, 0].reshape(seq_count, LEN, kv_count, HDIM), key_gain),
        cos_tab,
        sin_tab,
    )
    value_ready = pair_raw[:, 1].reshape(seq_count, LEN, kv_count, HDIM)
    return (
        query_ready.reshape(seq_count, LEN, kv_count, head_count // kv_count, HDIM),
        key_ready,
        value_ready,
    )


def masked_scores(queries, keys, length):
    scores = jnp.einsum(
        "qkgd,pkd->kgqp", queries, keys, preferred_element_type=jnp.float32
    ) * HDIM ** (-0.5)
    valid_keys = jnp.arange(LEN, dtype=jnp.int32) < length
    return jnp.where(valid_keys, scores, -1e30)


def attend_forward(packed):
    queries, keys, values, length = packed
    scores = masked_scores(queries, keys, length)
    top_val = jnp.max(scores, axis=-1, keepdims=True)
    weights = jnp.exp(scores - top_val)
    total = jnp.sum(weights, axis=-1, keepdims=True)
    probs = (weights / total).astype(jnp.bfloat16)
    mixed = jnp.einsum("kgqp,pkd->qkgd", probs, values, preferred_element_type=jnp.float32)
    return (mixed, top_val + jnp.log(total))


def attend_backward(packed):
    queries, keys, values, grad_mixed, log_total, length = packed
    scores = masked_scores(queries, keys, length)
    probs = jnp.exp(scores - log_total)
    grad_probs = jnp.einsum(
        "qkgd,pkd->kgqp", grad_mixed, values, preferred_element_type=jnp.float32
    )
    grad_values = jnp.einsum(
        "kgqp,qkgd->pkd", probs.astype(jnp.bfloat16), grad_mixed, preferred_element_type=jnp.float32
    )
    row_dot = jnp.sum(probs * grad_probs, axis=-1, keepdims=True)
    grad_scores = (probs * (grad_probs - row_dot)).astype(jnp.bfloat16)
    grad_queries = jnp.einsum(
        "kgqp,pkd->qkgd", grad_scores, keys, preferred_element_type=jnp.float32
    ) * HDIM ** (-0.5)
    grad_keys = jnp.einsum(
        "kgqp,qkgd->pkd", grad_scores, queries, preferred_element_type=jnp.float32
    ) * HDIM ** (-0.5)
    return (grad_queries, grad_keys, grad_values)


def slot_plan(routes, experts, capacity):
    tok_dev, top_k = routes.shape
    flat_routes = routes.reshape(-1)
    matches = (flat_routes[:, None] == jnp.arange(experts, dtype=jnp.int32)[None, :]).astype(
        jnp.int32
    )
    rank_in = jnp.sum((jnp.cumsum(matches, axis=0) - 1) * matches, axis=1)
    slot_index = flat_routes * capacity + rank_in
    owner_row = jnp.arange(tok_dev * top_k, dtype=jnp.int32) // top_k
    source = jnp.zeros((experts * capacity,), jnp.int32).at[slot_index].set(owner_row)
    live_slot = jnp.zeros((experts * capacity,), jnp.bfloat16).at[slot_index].set(1)
    return (slot_index, source, live_slot)


def expert_forward(received, gate_weight, up_weight, down_weight):
    local_experts = gate_weight.shape[0]
    senders = received.shape[0] // local_experts
    items = received.shape[1]
    shaped = received.reshape(senders, local_experts, items, received.shape[2])
    gate_act = jnp.einsum("secd,edf->secf", shaped, gate_weight, preferred_element_type=jnp.float32)
    up_act = jnp.einsum("secd,edf->secf", shaped, up_weight, preferred_element_type=jnp.float32)
    hidden = (jax.nn.silu(gate_act) * up_act).astype(jnp.bfloat16)
    result = jnp.einsum(
        "secf,efd->secd", hidden, down_weight, preferred_element_type=jnp.float32
    ).astype(jnp.bfloat16)
    flat_shape = (senders * local_experts, items, gate_act.shape[3])
    return (
        result.reshape(received.shape),
        gate_act.reshape(flat_shape),
        up_act.reshape(flat_shape),
        hidden.reshape(flat_shape),
    )


def shards(
    layer_input,
    lengths,
    routes,
    attn_gain,
    query_gain,
    key_gain,
    query_weight,
    key_value_weight,
    out_weight,
    ffn_gain,
    router_weight,
    gate_weight,
    up_weight,
    down_weight,
    cotangent,
):
    tok_dev, width = layer_input.shape
    mp_size = lax.axis_size("mp")
    dp_size = lax.axis_size("dp")
    tok_grp = tok_dev * mp_size
    seq_count = tok_grp // LEN
    experts = EXP_DEV * dp_size
    top_k = routes.shape[1]
    capacity = max(2, min(tok_dev, 3 * tok_dev * top_k // (2 * experts)))
    x_float = layer_input.astype(jnp.float32)
    normed_one = norm_rows(x_float, attn_gain).astype(jnp.bfloat16)
    query_full, pair_full, out_full = (
        lax.all_gather(query_weight, "dp", axis=0, tiled=True),
        lax.all_gather(key_value_weight, "dp", axis=0, tiled=True),
        lax.all_gather(out_weight, "dp", axis=0, tiled=True),
    )
    group_rows = lax.all_gather(normed_one, "mp", axis=0, tiled=True)
    query_raw = jnp.dot(group_rows, query_full, preferred_element_type=jnp.float32)
    pair_raw = jnp.einsum("td,dch->tch", group_rows, pair_full, preferred_element_type=jnp.float32)
    cos_tab, sin_tab = rope_tables()
    prepared, prep_back = jax.vjp(
        partial(prepare, cos_tab, sin_tab), query_raw, pair_raw, query_gain, key_gain
    )
    query_low = prepared[0].astype(jnp.bfloat16)
    key_low = prepared[1].astype(jnp.bfloat16)
    value_low = prepared[2].astype(jnp.bfloat16)
    mixed, log_total = lax.map(attend_forward, (query_low, key_low, value_low, lengths))
    mixed_low = mixed.reshape(tok_grp, -1).astype(jnp.bfloat16)
    attn_branch = lax.psum_scatter(
        contract(mixed_low, out_full, 1, 1).astype(jnp.bfloat16),
        "mp",
        scatter_dimension=0,
        tiled=True,
    ).astype(jnp.float32)
    x_mid = x_float + attn_branch
    normed_two = norm_rows(x_mid, ffn_gain).astype(jnp.bfloat16)
    logits = jnp.dot(normed_two, router_weight, preferred_element_type=jnp.float32)
    matches_tok = routes[:, :, None] == jnp.arange(experts, dtype=jnp.int32)[None, None, :]
    chosen = jnp.sum(jnp.where(matches_tok, logits[:, None, :], 0.0), axis=2)
    top_val = jnp.max(chosen, axis=1, keepdims=True)
    gate_exp = jnp.exp(chosen - top_val)
    gates = gate_exp / jnp.sum(gate_exp, axis=1, keepdims=True)
    slot_index, source, live_slot = slot_plan(routes, experts, capacity)
    send_buf = (normed_two[source] * live_slot[:, None]).reshape(experts, capacity, width)
    received = lax.all_to_all(send_buf, "dp", split_axis=0, concat_axis=0, tiled=True)
    result, gate_act, up_act, hidden = expert_forward(received, gate_weight, up_weight, down_weight)
    returned = lax.all_to_all(result, "dp", split_axis=0, concat_axis=0, tiled=True)
    picked = returned.reshape(experts * capacity, width)[slot_index].reshape(tok_dev, top_k, width)
    picked_float = picked.astype(jnp.float32)
    expert_branch = jnp.sum(gates[:, :, None] * picked_float, axis=1)
    layer_output = (x_mid + expert_branch).astype(jnp.bfloat16)
    group_place = lax.axis_index("mp") * tok_dev + jnp.arange(tok_dev, dtype=jnp.int32)
    seq_of = group_place // LEN
    length_of = jnp.sum(
        jnp.where(
            seq_of[:, None] == jnp.arange(seq_count, dtype=jnp.int32)[None, :], lengths[None, :], 0
        ),
        axis=1,
    )
    valid_rows = (group_place % LEN < length_of).astype(jnp.float32)
    grad_out = cotangent.astype(jnp.float32) * valid_rows[:, None]
    grad_gates = jnp.sum(grad_out[:, None, :] * picked_float, axis=2)
    grad_slots = (
        (gates[:, :, None] * grad_out[:, None, :])
        .astype(jnp.bfloat16)
        .reshape(tok_dev * top_k, width)
    )
    grad_buf = (
        jnp.zeros((experts * capacity, width), jnp.bfloat16)
        .at[slot_index]
        .set(grad_slots)
        .reshape(experts, capacity, width)
    )
    grad_recv = lax.all_to_all(grad_buf, "dp", split_axis=0, concat_axis=0, tiled=True)
    grad_shaped = grad_recv.reshape(dp_size, EXP_DEV, capacity, width)
    recv_shaped = received.reshape(dp_size, EXP_DEV, capacity, width)
    gate_shaped = gate_act.reshape(dp_size, EXP_DEV, capacity, -1)
    up_shaped = up_act.reshape(dp_size, EXP_DEV, capacity, -1)
    hidden_shaped = hidden.reshape(dp_size, EXP_DEV, capacity, -1)
    grad_hidden = jnp.einsum(
        "secd,efd->secf", grad_shaped, down_weight, preferred_element_type=jnp.float32
    )
    grad_down = jnp.einsum(
        "secf,secd->efd", hidden_shaped, grad_shaped, preferred_element_type=jnp.float32
    )
    sigma = jax.nn.sigmoid(gate_shaped)
    grad_gate_act = (grad_hidden * up_shaped * sigma * (1.0 + gate_shaped * (1.0 - sigma))).astype(
        jnp.bfloat16
    )
    grad_up_act = (grad_hidden * gate_shaped * sigma).astype(jnp.bfloat16)
    grad_taken = (
        jnp.einsum("secf,edf->secd", grad_gate_act, gate_weight, preferred_element_type=jnp.float32)
        + jnp.einsum("secf,edf->secd", grad_up_act, up_weight, preferred_element_type=jnp.float32)
    ).astype(jnp.bfloat16)
    grad_gate_w = jnp.einsum(
        "secd,secf->edf", recv_shaped, grad_gate_act, preferred_element_type=jnp.float32
    )
    grad_up_w = jnp.einsum(
        "secd,secf->edf", recv_shaped, grad_up_act, preferred_element_type=jnp.float32
    )
    grad_back = lax.all_to_all(
        grad_taken.reshape(experts, capacity, width), "dp", split_axis=0, concat_axis=0, tiled=True
    )
    gate_weight_grad, up_weight_grad, down_weight_grad = (
        lax.psum_scatter(
            grad_gate_w.astype(jnp.bfloat16), "mp", scatter_dimension=1, tiled=True
        ).astype(jnp.float32),
        lax.psum_scatter(
            grad_up_w.astype(jnp.bfloat16), "mp", scatter_dimension=1, tiled=True
        ).astype(jnp.float32),
        lax.psum_scatter(
            grad_down.astype(jnp.bfloat16), "mp", scatter_dimension=1, tiled=True
        ).astype(jnp.float32),
    )
    grad_rows_back = grad_back.reshape(experts * capacity, width)[slot_index].reshape(
        tok_dev, top_k, width
    )
    grad_norm_two = jnp.sum(grad_rows_back.astype(jnp.float32), axis=1)
    grad_chosen = gates * (grad_gates - jnp.sum(gates * grad_gates, axis=1, keepdims=True))
    grad_logits = jnp.sum(jnp.where(matches_tok, grad_chosen[:, :, None], 0.0), axis=1).astype(
        jnp.bfloat16
    )
    router_part = contract(normed_two, grad_logits, 0, 0)
    grad_norm_two = grad_norm_two + contract(grad_logits, router_weight, 1, 1)
    grad_mid_norm, ffn_gain_part = norm_back(x_mid, ffn_gain, grad_norm_two)
    grad_mid = grad_out + grad_mid_norm
    grad_attn_rows = lax.all_gather(grad_mid.astype(jnp.bfloat16), "mp", axis=0, tiled=True)
    grad_mixed = jnp.dot(grad_attn_rows, out_full, preferred_element_type=jnp.float32).astype(
        jnp.bfloat16
    )
    out_grad_full = contract(grad_attn_rows, mixed_low, 0, 0)
    grad_mixed = grad_mixed.reshape(query_low.shape)
    grad_queries, grad_keys, grad_values = lax.map(
        attend_backward, (query_low, key_low, value_low, grad_mixed, log_total, lengths)
    )
    grad_query, grad_pair, query_gain_part, key_gain_part = prep_back(
        (grad_queries, grad_keys, grad_values)
    )
    grad_query = grad_query.astype(jnp.bfloat16)
    grad_pair = grad_pair.astype(jnp.bfloat16)
    query_grad_full = contract(group_rows, grad_query, 0, 0)
    pair_grad_full = jnp.einsum(
        "td,tch->dch", group_rows, grad_pair, preferred_element_type=jnp.float32
    )
    grad_rows_part = contract(grad_query, query_full, 1, 1) + jnp.einsum(
        "tch,dch->td", grad_pair, pair_full, preferred_element_type=jnp.float32
    )
    grad_norm_one = lax.psum_scatter(
        grad_rows_part.astype(jnp.bfloat16), "mp", scatter_dimension=0, tiled=True
    ).astype(jnp.float32)
    grad_in_norm, attn_gain_part = norm_back(x_float, attn_gain, grad_norm_one)
    input_grad = grad_mid + grad_in_norm
    query_weight_grad, key_value_weight_grad, out_weight_grad = (
        lax.psum_scatter(
            query_grad_full.astype(jnp.bfloat16), "dp", scatter_dimension=0, tiled=True
        ).astype(jnp.float32),
        lax.psum_scatter(
            pair_grad_full.astype(jnp.bfloat16), "dp", scatter_dimension=0, tiled=True
        ).astype(jnp.float32),
        lax.psum_scatter(
            out_grad_full.astype(jnp.bfloat16), "dp", scatter_dimension=0, tiled=True
        ).astype(jnp.float32),
    )
    summed = lax.psum(
        (attn_gain_part, query_gain_part, key_gain_part, ffn_gain_part, router_part), ("dp", "mp")
    )
    return (
        layer_output,
        input_grad,
        summed[0],
        summed[1],
        summed[2],
        query_weight_grad,
        key_value_weight_grad,
        out_weight_grad,
        summed[3],
        summed[4],
        gate_weight_grad,
        up_weight_grad,
        down_weight_grad,
    )


def solution(mesh):
    in_specs = (
        P(("dp", "mp"), None),
        P("dp"),
        P(("dp", "mp"), None),
        P(),
        P(),
        P(),
        P("dp", "mp"),
        P("dp", None, "mp"),
        P("dp", "mp"),
        P(),
        P(),
        P("dp", None, None),
        P("dp", None, None),
        P("dp", None, None),
        P(("dp", "mp"), None),
    )
    out_specs = (
        P(("dp", "mp"), None),
        P(("dp", "mp"), None),
        P(),
        P(),
        P(),
        P("dp", "mp"),
        P("dp", None, "mp"),
        P("dp", "mp"),
        P(),
        P(),
        P("dp", "mp", None),
        P("dp", "mp", None),
        P("dp", "mp", None),
    )
    return jax.shard_map(shards, mesh=mesh, in_specs=in_specs, out_specs=out_specs, check_vma=False)
```

profile of v0, /device:TPU:0, one launch (start us, length us, event | category | flops | bytes accessed | tf_op | source)
XLA Modules:
  0.0 1119.8 jit_solution(2531559165104971157)
XLA Ops:
  12.1 26.4 %all_gather.16 = bf16[1024,2,128]{2,0,1:T(8,128)(2,1)S(1)} all-gather(bf16[32,2,128]{2,0,1:T(8,128)(2,1)S(1)} %copy.71), channel_id=1, replica_groups=mesh['dp'=32,'mp'=4] {'dp'}, dimensions={0}, use_global_device_ids=true | all-gather | bytes 540672 | tf_op jit(solution)/shard_map/all_gather | solution.py:178
  38.5 24.2 %all_gather.17 = bf16[1024,256]{1,0:T(8,128)(2,1)S(1)} all-gather(bf16[32,256]{1,0:T(8,128)(2,1)} %param.21), channel_id=1, replica_groups=mesh['dp'=32,'mp'=4] {'dp'}, dimensions={0}, use_global_device_ids=true | all-gather | bytes 540672 | tf_op jit(solution)/shard_map/all_gather | solution.py:177
  62.7 22.6 %all_gather.18 = bf16[1024,256]{1,0:T(8,128)(2,1)S(1)} all-gather(bf16[32,256]{1,0:T(8,128)(2,1)} %param.23), channel_id=1, replica_groups=mesh['dp'=32,'mp'=4] {'dp'}, dimensions={0}, use_global_device_ids=true | all-gather | bytes 540672 | tf_op jit(solution)/shard_map/all_gather | solution.py:179
  93.3 7.4 bitcast_reduce_fusion
  100.7 8.0 fusion.5
  108.7 7.4 fusion.66
  119.7 9.1 reduce-window.6
  129.6 14.6 %scatter_custom_fusion.1 = bf16[3072]{0:T(1024)(128)(2,1)S(1)} fusion(s32[2048]{0:T(1024)S(1)} %bitcast.310, bf16[2048]{0:T(1024)(128)(2,1)S(1)} %broadcast.497, bf16[]{:T(256)} %constant.144.clone.1), kind=kCustom, calls=%fused_computation.188 | custom fusion | bytes 6146 | tf_op jit(solution)/shard_map/scatter | solution.py:125
  144.3 8.5 scatter_custom_fusion
  155.4 13.9 %gather_fusion = bf16[3072,1024]{1,0:T(8,128)(2,1)} fusion(bf16[256,1024]{1,0:T(8,128)(2,1)S(1)} %multiply_convert_fusion, s32[3072]{0:T(1024)S(1)} %fusion.95), kind=kCustom, calls=%fused_computation | custom fusion | bytes 12595200 | tf_op jit(solution)/shard_map/gather | solution.py:208
  169.3 5.9 broadcast_multiply_fusion
  175.3 5.3 all-to-all-start
  182.5 14.4 %scatter_custom_fusion.2 = bf16[3072,1024]{1,0:T(8,128)(2,1)} fusion(s32[2048]{0:T(1024)S(1)} %bitcast.312, f32[256,1024]{1,0:T(8,128)S(1)} %convert_multiply_fusion.5, f32[2048]{0:T(1024)S(1)} %div.149, bf16[]{:T(256)} %constant.144.clone.1), kind=kCustom, calls=%fused_computation.47 | custom fusion | flops 4194304 | bytes 7348226 | tf_op jit(solution)/shard_map/scatter | solution.py:235
  196.9 63.6 %all-to-all-done = bf16[32,96,1024]{2,1,0:T(8,128)(2,1)} async-done(((bf16[32,96,1024]{2,1,0:T(8,128)(2,1)}), bf16[32,96,1024]{2,1,0:T(8,128)(2,1)}, u32[]{:S(2)}, u32[]{:S(2)}) %all-to-all-start) | async-done | bytes 6291488 | tf_op jit(solution)/shard_map/all_to_all | solution.py:209
  260.4 12.9 %all-to-all-start.2 = ((bf16[32,96,1024]{2,1,0:T(8,128)(2,1)}), bf16[32,96,1024]{2,1,0:T(8,128)(2,1)}, u32[]{:S(2)}, u32[]{:S(2)}) async-start(bf16[32,96,1024]{2,1,0:T(8,128)(2,1)} %bitcast.289), calls=%async_computation.3 | async-start | bytes 12582912 | tf_op jit(solution)/shard_map/all_to_all | solution.py:238
  273.3 9.1 fusion.81
  282.5 8.2 fusion.84
  290.7 62.0 %all-to-all-done.2 = bf16[32,96,1024]{2,1,0:T(8,128)(2,1)} async-done(((bf16[32,96,1024]{2,1,0:T(8,128)(2,1)}), bf16[32,96,1024]{2,1,0:T(8,128)(2,1)}, u32[]{:S(2)}, u32[]{:S(2)}) %all-to-all-start.2) | async-done | bytes 6291488 | tf_op jit(solution)/shard_map/all_to_all | solution.py:238
  352.7 12.3 %fusion.18 = (bf16[32,1,96,512]{3,2,0,1:T(8,128)(2,1)}, bf16[32,1,96,512]{3,2,0,1:T(8,128)(2,1)}, bf16[32,1,96,512]{3,2,0,1:T(8,128)(2,1)S(1)}) fusion(f32[32,96,512]{2,1,0:T(8,128)} %fusion.84, f32[32,96,512]{2,1,0:T(8,128)} %fusion.81, bf16[32,96,1024]{2,1,0:T(8,128)(2,1)} %all-to-all-done.2, bf16[1,512,1024]{2,1,0:T(8,128)(2,1)S(1)} %copy-done), kind=kOutput, calls=%fused_computation.37 | convolution fusion | flops 3246391296 | bytes 29360128 | tf_op jit(solution)/shard_map/secd,efd->secf/dot_general | solution.py:244
  366.7 5.3 convolution_convert_fusion
  372.0 13.0 %all-to-all-start.1 = ((bf16[32,96,1024]{2,1,0:T(8,128)(2,1)}), bf16[32,96,1024]{2,1,0:T(8,128)(2,1)}, u32[]{:S(2)}, u32[]{:S(2)}) async-start(bf16[32,96,1024]{2,1,0:T(8,128)(2,1)} %convolution_convert_fusion), calls=%async_computation.2 | async-start | bytes 12582912 | tf_op jit(solution)/shard_map/all_to_all | solution.py:211
  385.0 5.7 fusion.34
  390.7 7.7 add_convert_fusion
  398.4 66.4 %all-to-all-done.1 = bf16[32,96,1024]{2,1,0:T(8,128)(2,1)} async-done(((bf16[32,96,1024]{2,1,0:T(8,128)(2,1)}), bf16[32,96,1024]{2,1,0:T(8,128)(2,1)}, u32[]{:S(2)}, u32[]{:S(2)}) %all-to-all-start.1) | async-done | bytes 6291488 | tf_op jit(solution)/shard_map/all_to_all | solution.py:211
  464.8 12.7 %all-to-all-start.3 = ((bf16[32,96,1024]{2,1,0:T(8,128)(2,1)}), bf16[32,96,1024]{2,1,0:T(8,128)(2,1)}, u32[]{:S(2)}, u32[]{:S(2)}) async-start(bf16[32,96,1024]{2,1,0:T(8,128)(2,1)} %add_convert_fusion), calls=%async_computation.4 | async-start | bytes 12582912 | tf_op jit(solution)/shard_map/all_to_all | solution.py:265
  478.0 14.6 %gather_fusion.1 = bf16[2048,1024]{1,0:T(8,128)(2,1)} fusion(bf16[3072,1024]{1,0:T(8,128)(2,1)} %bitcast.36, s32[2048]{0:T(1024)S(1)} %broadcast_clamp_fusion), kind=kCustom, calls=%fused_computation.1 | custom fusion | bytes 8396800 | tf_op jit(solution)/shard_map/gather | solution.py:212
  492.6 6.1 fusion.8
  498.8 58.6 %all-to-all-done.3 = bf16[32,96,1024]{2,1,0:T(8,128)(2,1)} async-done(((bf16[32,96,1024]{2,1,0:T(8,128)(2,1)}), bf16[32,96,1024]{2,1,0:T(8,128)(2,1)}, u32[]{:S(2)}, u32[]{:S(2)}) %all-to-all-start.3) | async-done | bytes 6291488 | tf_op jit(solution)/shard_map/all_to_all | solution.py:265
  557.4 14.6 %gather_fusion.2 = bf16[2048,1024]{1,0:T(8,128)(2,1)} fusion(bf16[3072,1024]{1,0:T(8,128)(2,1)} %bitcast.49, s32[2048]{0:T(1024)S(1)} %broadcast_clamp_fusion), kind=kCustom, calls=%fused_computation.2 | custom fusion | bytes 8396800 | tf_op jit(solution)/shard_map/gather | solution.py:279
  572.0 5.5 convert_reduce_fusion
  579.5 8.2 fusion.60
  587.9 8.1 fusion.57
  596.2 8.4 fusion.54
  604.6 12.3 %all-gather.5.cloned.1.call-done = bf16[1024,1024]{1,0:T(8,128)(2,1)} async-done(((bf16[256,1024]{1,0:T(8,128)(2,1)}), bf16[1024,1024]{1,0:T(8,128)(2,1)}) %all-gather.5.cloned.1.call-update) | async-done | bytes 2097168 | tf_op jit(solution)/shard_map/all_gather | solution.py:291
  619.4 15.0 %fusion = (f32[2,2,1024]{2,1,0:T(2,128)S(1)}, f32[2,1024,1024,2]{2,1,3,0:T(8,128)}) fusion(f32[2,1024,1024,2]{2,1,3,0:T(8,128)} %get-tuple-element.146, f32[2,2,1024]{2,1,0:T(2,128)S(1)} %log_add_fusion, bf16[1024,2,64,1]{0,2,3,1:T(8,128)(2,1)S(1)} %bitcast.303, bf16[1024,2,2,64]{0,3,2,1:T(8,128)(2,1)S(1)} %bitcast.296), kind=kOutput, calls=%fused_computation.8 | convolution fusion | flops 549449728 | bytes 34373632 | tf_op jit(solution)/shard_map/while/body/eval_jaxpr/qkgd,pkd->kgqp/dot_general | solution.py:98
  635.8 8.4 fusion.2
  652.1 3.2 convolution_convert_fusion.3
  655.3 9.4 fusion.9
  671.7 3.5 fusion.63
  676.1 3.6 fusion.26
  683.4 10.7 reduce-scatter.19.cloned.1.call-done
  696.8 77.7 %reduce-scatter.17.cloned.1.call-done = bf16[32,256]{1,0:T(8,128)(2,1)} async-done(((bf16[1024,256]{1,0:T(8,128)(2,1)}), bf16[32,256]{1,0:T(8,128)(2,1)}) %reduce-scatter.17.cloned.1.call-update) | async-done | bytes 16400 | tf_op jit(solution)/shard_map/reduce_scatter | solution.py:324
  775.8 78.5 %reduce-scatter.13.cloned.1.call-done = bf16[32,256]{1,0:T(8,128)(2,1)} async-done(((bf16[1024,256]{1,0:T(8,128)(2,1)}), bf16[32,256]{1,0:T(8,128)(2,1)}) %reduce-scatter.13.cloned.1.call-update) | async-done | bytes 16400 | tf_op jit(solution)/shard_map/reduce_scatter | solution.py:318
  855.6 78.5 %reduce-scatter.15.cloned.1.call-done = bf16[32,2,128]{2,0,1:T(8,128)(2,1)} async-done(((bf16[1024,2,128]{2,0,1:T(8,128)(2,1)}), bf16[32,2,128]{2,0,1:T(8,128)(2,1)}) %reduce-scatter.15.cloned.1.call-update) | async-done | bytes 16400 | tf_op jit(solution)/shard_map/reduce_scatter | solution.py:321
  935.5 29.8 %reduce-scatter.11.cloned.1.call-done = bf16[256,1024]{1,0:T(8,128)(2,1)} async-done(((bf16[1024,1024]{1,0:T(8,128)(2,1)}), bf16[256,1024]{1,0:T(8,128)(2,1)}) %reduce-scatter.11.cloned.1.call-update) | async-done | bytes 524304 | tf_op jit(solution)/shard_map/reduce_scatter | solution.py:312
  966.9 3.5 fusion.71
  970.4 65.4 %all-reduce.6 = (f32[1024]{0:T(1024)}, f32[64]{0:T(128)}, f32[64]{0:T(128)}, f32[1024]{0:T(1024)}) all-reduce(f32[1024]{0:T(1024)S(1)} %get-tuple-element.122, f32[64]{0:T(128)S(1)} %get-tuple-element.120, f32[64]{0:T(128)S(1)} %get-tuple-element.124, f32[1024]{0:T(1024)S(1)} %get-tuple-element.118), channel_id=1, replica_groups=mesh['dp'=32,'mp'=4] {'dp','mp'}, use_global_device_ids=true, to_apply=%region_28.29 | all-reduce | flops 2176 | bytes 17408 | tf_op jit(solution)/shard_map/psum | solution.py:328
  1035.8 75.6 %all-reduce.9.cloned.1.call-done = f32[1024,32]{0,1:T(8,128)} async-done(((f32[1024,32]{0,1:T(8,128)}), f32[1024,32]{0,1:T(8,128)}) %all-reduce.9.cloned.1.call-update) | async-done | bytes 131088 | tf_op jit(solution)/shard_map/psum | solution.py:328
  (235 shorter events, 57.9 us)
Async XLA Ops:
  7.2 345.5 %copy-start = (bf16[1,512,1024]{2,1,0:T(8,128)(2,1)S(1)}, bf16[1,512,1024]{2,1,0:T(8,128)(2,1)}, u32[]{:S(2)}) copy-start(bf16[1,512,1024]{2,1,0:T(8,128)(2,1)} %param.28) | copy-start | bytes 3145732
  7.2 78.7 %all-gather.3.cloned.1.call-start = ((), (), s32[]{:S(2)}) async-start(), calls=%async_computation.12 | async-start | bytes 2621440 | tf_op jit(solution)/shard_map/all_gather | solution.py:181
  10.6 81.2 %copy-start.49 = (f32[64]{0:T(128)S(1)}, f32[64]{0:T(128)}, u32[]{:S(2)}) copy-start(f32[64]{0:T(128)} %param.20) | copy-start | bytes 772
  10.6 142.2 %reduce-scatter.9.cloned.1.call-start = ((), (), s32[]{:S(2)}) async-start(), calls=%async_computation.13 | async-start | bytes 2621440 | tf_op jit(solution)/shard_map/reduce_scatter | solution.py:193
  38.5 53.5 %copy-start.19 = (bf16[1024,2,128]{2,0,1:T(8,128)(2,1)}, bf16[1024,2,128]{2,0,1:T(8,128)(2,1)S(1)}, u32[]{:S(2)}) copy-start(bf16[1024,2,128]{2,0,1:T(8,128)(2,1)S(1)} %all_gather.16) | copy-start | bytes 1572868
  62.7 30.2 %copy-start.11 = (bf16[1024,256]{1,0:T(8,128)(2,1)}, bf16[1024,256]{1,0:T(8,128)(2,1)S(1)}, u32[]{:S(2)}) copy-start(bf16[1024,256]{1,0:T(8,128)(2,1)S(1)} %all_gather.17) | copy-start | bytes 1572868
  62.7 29.9 %copy-start.51 = (f32[64]{0:T(128)S(1)}, f32[64]{0:T(128)}, u32[]{:S(2)}) copy-start(f32[64]{0:T(128)} %param.19) | copy-start | bytes 772
  85.3 30.8 %copy-start.26 = (bf16[1024,256]{1,0:T(8,128)(2,1)}, bf16[1024,256]{1,0:T(8,128)(2,1)S(1)}, u32[]{:S(2)}) copy-start(bf16[1024,256]{1,0:T(8,128)(2,1)S(1)} %all_gather.18) | copy-start | bytes 1572868
  108.7 10.4 copy-start.42
  116.1 36.7 %copy-start.4 = (bf16[256,1024]{1,0:T(8,128)(2,1)S(1)}, bf16[256,1024]{1,0:T(8,128)(2,1)}, u32[]{:S(2)}) copy-start(bf16[256,1024]{1,0:T(8,128)(2,1)} %param.15) | copy-start | bytes 1572868
  116.1 38.0 %copy-start.45 = (f32[1024]{0:T(1024)S(1)}, f32[1024]{0:T(1024)}, u32[]{:S(2)}) copy-start(f32[1024]{0:T(1024)} %param.24) | copy-start | bytes 12292
  155.4 26.4 %copy-start.2 = (bf16[256,1024]{1,0:T(8,128)(2,1)}, bf16[256,1024]{1,0:T(8,128)(2,1)S(1)}, u32[]{:S(2)}) copy-start(bf16[256,1024]{1,0:T(8,128)(2,1)S(1)} %multiply_convert_fusion) | copy-start | bytes 1572868
  175.3 85.2 %all-to-all-start = ((bf16[32,96,1024]{2,1,0:T(8,128)(2,1)}), bf16[32,96,1024]{2,1,0:T(8,128)(2,1)}, u32[]{:S(2)}, u32[]{:S(2)}) async-start(bf16[32,96,1024]{2,1,0:T(8,128)(2,1)} %broadcast_multiply_fusion), calls=%async_computation.1 | async-start | bytes 12582912 | tf_op jit(solution)/shard_map/all_to_all | solution.py:209
  260.4 92.3 %all-to-all-start.2 = ((bf16[32,96,1024]{2,1,0:T(8,128)(2,1)}), bf16[32,96,1024]{2,1,0:T(8,128)(2,1)}, u32[]{:S(2)}, u32[]{:S(2)}) async-start(bf16[32,96,1024]{2,1,0:T(8,128)(2,1)} %bitcast.289), calls=%async_computation.3 | async-start | bytes 12582912 | tf_op jit(solution)/shard_map/all_to_all | solution.py:238
  273.3 9.1 copy-start.54
  372.0 13.0 %copy-start.55 = (bf16[1,1024,512]{2,1,0:T(8,128)(2,1)S(1)}, bf16[1,1024,512]{2,1,0:T(8,128)(2,1)}, u32[]{:S(2)}) copy-start(bf16[1,1024,512]{2,1,0:T(8,128)(2,1)} %param.26) | copy-start | bytes 3145732
  372.0 92.8 %all-to-all-start.1 = ((bf16[32,96,1024]{2,1,0:T(8,128)(2,1)}), bf16[32,96,1024]{2,1,0:T(8,128)(2,1)}, u32[]{:S(2)}, u32[]{:S(2)}) async-start(bf16[32,96,1024]{2,1,0:T(8,128)(2,1)} %convolution_convert_fusion), calls=%async_computation.2 | async-start | bytes 12582912 | tf_op jit(solution)/shard_map/all_to_all | solution.py:211
  464.8 92.6 %all-to-all-start.3 = ((bf16[32,96,1024]{2,1,0:T(8,128)(2,1)}), bf16[32,96,1024]{2,1,0:T(8,128)(2,1)}, u32[]{:S(2)}, u32[]{:S(2)}) async-start(bf16[32,96,1024]{2,1,0:T(8,128)(2,1)} %add_convert_fusion), calls=%async_computation.4 | async-start | bytes 12582912 | tf_op jit(solution)/shard_map/all_to_all | solution.py:265
  477.6 139.4 %all-gather.5.cloned.1.call-start = ((), (), s32[]{:S(2)}) async-start(), calls=%async_computation.14 | async-start | bytes 2621440 | tf_op jit(solution)/shard_map/all_gather | solution.py:291
  557.4 20.1 %copy-start.7 = (bf16[256,1024]{1,0:T(8,128)(2,1)S(1)}, bf16[256,1024]{1,0:T(8,128)(2,1)}, u32[]{:S(2)}) copy-start(bf16[256,1024]{1,0:T(8,128)(2,1)} %reduce-scatter.9.cloned.1.call-done) | copy-start | bytes 1572868
  578.1 9.6 copy-start.8
  579.4 100.4 %reduce-scatter.23.cloned.1.call-start = ((), (), s32[]{:S(2)}) async-start(), calls=%async_computation.22 | async-start | bytes 1310720 | tf_op jit(solution)/shard_map/reduce_scatter | solution.py:275
  587.7 93.9 %reduce-scatter.21.cloned.1.call-start = ((), (), s32[]{:S(2)}) async-start(), calls=%async_computation.21 | async-start | bytes 1310720 | tf_op jit(solution)/shard_map/reduce_scatter | solution.py:272
  596.1 98.0 %reduce-scatter.19.cloned.1.call-start = ((), (), s32[]{:S(2)}) async-start(), calls=%async_computation.20 | async-start | bytes 1310720 | tf_op jit(solution)/shard_map/reduce_scatter | solution.py:269
  596.2 20.8 %copy-start.27 = (bf16[1024,256]{1,0:T(8,128)(2,1)S(1)}, bf16[1024,256]{1,0:T(8,128)(2,1)}, u32[]{:S(2)}) copy-start(bf16[1024,256]{1,0:T(8,128)(2,1)} %copy-done.26) | copy-start | bytes 1572868
  604.6 169.8 %reduce-scatter.17.cloned.1.call-start = ((), (), s32[]{:S(2)}) async-start(), calls=%async_computation.18 | async-start | bytes 540672 | tf_op jit(solution)/shard_map/reduce_scatter | solution.py:324
  619.3 15.1 %slice-start = ((s8[16777216]{0:T(1024)(128)(4,1)}), s8[4194304]{0:T(1024)(128)(4,1)S(1)}, s32[]{:S(2)}) async-start(s8[16777216]{0:T(1024)(128)(4,1)} %bitcast.285), calls=%async_computation.23 | async-start | bytes 8388608
  619.3 15.1 %slice-start.1 = ((s8[16777216]{0:T(1024)(128)(4,1)}), s8[4194304]{0:T(1024)(128)(4,1)S(1)}, s32[]{:S(2)}) async-start(s8[16777216]{0:T(1024)(128)(4,1)} %bitcast.285), calls=%async_computation.24 | async-start | bytes 8388608
  619.3 15.1 %slice-start.2 = ((s8[16777216]{0:T(1024)(128)(4,1)}), s8[4194304]{0:T(1024)(128)(4,1)S(1)}, s32[]{:S(2)}) async-start(s8[16777216]{0:T(1024)(128)(4,1)} %bitcast.285), calls=%async_computation.25 | async-start | bytes 8388608
  619.4 16.5 %slice-start.3 = ((s8[16777216]{0:T(1024)(128)(4,1)}), s8[4194304]{0:T(1024)(128)(4,1)S(1)}, s32[]{:S(2)}) async-start(s8[16777216]{0:T(1024)(128)(4,1)} %bitcast.285), calls=%async_computation.26 | async-start | bytes 8388608
  635.8 8.4 copy-start.30
  635.8 8.4 copy-start.32
  652.1 202.3 %reduce-scatter.13.cloned.1.call-start = ((), (), s32[]{:S(2)}) async-start(), calls=%async_computation.16 | async-start | bytes 540672 | tf_op jit(solution)/shard_map/reduce_scatter | solution.py:318
  655.3 9.8 copy-start.16
  655.3 9.8 copy-start.41
  655.3 9.8 copy-start.50
  655.3 13.2 %copy-start.44 = (f32[1024,2]{0,1:T(2,128)S(1)}, f32[1024,2]{0,1:T(2,128)}, u32[]{:S(2)}) copy-start(f32[1024,2]{0,1:T(2,128)} %copy-done.43) | copy-start | bytes 24580
  655.3 13.2 %copy-start.10 = (f32[1024,2,128]{0,2,1:T(8,128)S(1)}, f32[1024,2,128]{0,2,1:T(8,128)}, u32[]{:S(2)}) copy-start(f32[1024,2,128]{0,2,1:T(8,128)} %copy-done.9) | copy-start | bytes 3145732
  664.8 269.4 %reduce-scatter.15.cloned.1.call-start = ((), (), s32[]{:S(2)}) async-start(), calls=%async_computation.17 | async-start | bytes 540672 | tf_op jit(solution)/shard_map/reduce_scatter | solution.py:321
  665.1 10.1 copy-start.12
  666.4 8.9 copy-start.25
  675.2 290.2 %reduce-scatter.11.cloned.1.call-start = ((), (), s32[]{:S(2)}) async-start(), calls=%async_computation.15 | async-start | bytes 2621440 | tf_op jit(solution)/shard_map/reduce_scatter | solution.py:312
  676.0 19.9 %copy-start.3 = (bf16[256,1024]{1,0:T(8,128)(2,1)S(1)}, bf16[256,1024]{1,0:T(8,128)(2,1)}, u32[]{:S(2)}) copy-start(bf16[256,1024]{1,0:T(8,128)(2,1)} %copy-done.2) | copy-start | bytes 1572868
  676.0 289.3 %copy-start.46 = (f32[1024]{0:T(1024)S(1)}, f32[1024]{0:T(1024)}, u32[]{:S(2)}) copy-start(f32[1024]{0:T(1024)} %param.18) | copy-start | bytes 12292
  676.0 289.3 %copy-start.48 = (f32[256]{0:T(256)S(1)}, f32[256]{0:T(256)}, u32[]{:S(2)}) copy-start(f32[256]{0:T(256)} %copy-done.47) | copy-start | bytes 3076
  676.0 290.8 %copy-start.18 = (bf16[256,1024]{1,0:T(8,128)(2,1)S(1)}, bf16[256,1024]{1,0:T(8,128)(2,1)}, u32[]{:S(2)}) copy-start(bf16[256,1024]{1,0:T(8,128)(2,1)} %param.29) | copy-start | bytes 1572868
  676.0 437.0 %copy-start.1 = (bf16[1,512,1024]{2,1,0:T(8,128)(2,1)S(1)}, bf16[1,512,1024]{2,1,0:T(8,128)(2,1)}, u32[]{:S(2)}) copy-start(bf16[1,512,1024]{2,1,0:T(8,128)(2,1)} %param.28) | copy-start | bytes 3145732
  679.7 431.7 %all-reduce.9.cloned.1.call-start = ((), (), s32[]{:S(2)}) async-start(), calls=%async_computation.19 | async-start | bytes 262144 | tf_op jit(solution)/shard_map/psum | solution.py:328
  (29 other events, 104.4 us)
Sparse Core Ops, SparseCore 0:
  10.7 33.2 all-gather.2
  119.2 28.8 reduce-scatter.8
  579.5 37.3 all-gather.4
  619.4 23.5 reduce-scatter.22
  645.2 23.2 reduce-scatter.20
  670.8 23.2 reduce-scatter.18
  697.5 76.8 reduce-scatter.16
  777.9 76.3 reduce-scatter.12
  857.8 76.3 reduce-scatter.14
  936.4 28.8 reduce-scatter.10
  971.4 140.0 all-reduce.8
where the time goes:
time: 1130 us; the launch traced here: 1120 us
  waiting for transfers between devices  614 us (54%)
  matrix products  140 us (12%)
  blocking collectives  139 us (12%)
  other arithmetic  85.8 us (8%)
  local copies, waits for them, and re-layouts  80.1 us (7%)
  starting transfers between devices  45.1 us (4%)
  between operations  15.9 us (1%)
    reduce_scatter x1, waiting for transfers between devices, shards(): lax.psum_scatter(pair_grad_full.astype(jnp.bfloat16), 'dp', scatter_dimen...  78.5 us
    reduce_scatter x1, waiting for transfers between devices, shards(): lax.psum_scatter(query_grad_full.astype(jnp.bfloat16), 'dp', scatter_dime...  78.5 us
    reduce_scatter x1, waiting for transfers between devices, shards(): lax.psum_scatter(out_grad_full.astype(jnp.bfloat16), 'dp', scatter_dimens...  77.7 us
    psum x1, waiting for transfers between devices, shards(): lax.psum((attn_gain_part, query_gain_part, key_gain_part, ffn_gain_part,...  75.6 us
    all_to_all x1, waiting for transfers between devices, shards(): lax.all_to_all(result, 'dp', split_axis=0, concat_axis=0, tiled=True)  66.4 us
    psum x1, blocking collectives, shards(): lax.psum((attn_gain_part, query_gain_part, key_gain_part, ffn_gain_part,...  65.4 us
    all_to_all x1, waiting for transfers between devices, shards(): lax.all_to_all(send_buf, 'dp', split_axis=0, concat_axis=0, tiled=True)  63.6 us
    all_to_all x1, waiting for transfers between devices, shards(): lax.all_to_all(grad_buf, 'dp', split_axis=0, concat_axis=0, tiled=True)  62 us
  transfers between devices with their start and end apart: 15, of which 11 were waited for; matrix products, arithmetic and copies ran while one was open for 18% of the time, Pallas kernels for 0%

commit v1 on v0

v1 whole, which is shorter than its diff:
```python
from functools import partial

import jax
import jax.numpy as jnp
import numpy as np
from jax import lax
from jax.experimental import pallas as pl
from jax.experimental.pallas import tpu as pltpu
from jax.sharding import PartitionSpec as P

WIDTH = 1024
HDIM = 64
PITCH = 128
LEN = 1024
TOK = 256
CAP = 96
EXPERTS = 32
FF = 512
SIDE = 16
ROWS = TOK + SIDE
EPS = 1e-06
LOG2E = 1.4426950408889634
F32 = jnp.float32
BF16 = jnp.bfloat16
VMEM_BYTES = 60 * 1024 * 1024


def nn(left, right):
    return lax.dot_general(left, right, (((1,), (0,)), ((), ())), preferred_element_type=F32)


def nt(left, right):
    return lax.dot_general(left, right, (((1,), (1,)), ((), ())), preferred_element_type=F32)


def tn(left, right):
    return lax.dot_general(left, right, (((0,), (0,)), ((), ())), preferred_element_type=F32)


def spread(heads):
    table = np.zeros((heads * HDIM, heads * PITCH), np.float32)
    for head in range(heads):
        for lane in range(HDIM):
            table[head * HDIM + lane, head * PITCH + lane] = 1.0
    return table


def rope_tables():
    places = np.arange(LEN, dtype=np.float64)
    inverse = 10000.0 ** (-2.0 * np.arange(HDIM // 2, dtype=np.float64) / HDIM)
    angles = places[:, None] * inverse[None, :]
    cos_tab = np.zeros((LEN, PITCH), np.float32)
    sin_tab = np.zeros((LEN, PITCH), np.float32)
    cos_tab[:, : HDIM // 2] = np.cos(angles)
    cos_tab[:, HDIM // 2 : HDIM] = np.cos(angles)
    sin_tab[:, : HDIM // 2] = -np.sin(angles)
    sin_tab[:, HDIM // 2 : HDIM] = np.sin(angles)
    return cos_tab.reshape(LEN // TOK, TOK, PITCH), sin_tab.reshape(LEN // TOK, TOK, PITCH)


def lanes(shape):
    return lax.broadcasted_iota(jnp.int32, shape, 1)


def swap_halves(tensor):
    half = HDIM // 2
    ahead = pltpu.roll(tensor, PITCH - half, 1)
    behind = pltpu.roll(tensor, half, 1)
    return jnp.where(lanes(tensor.shape) < half, ahead, behind)


def head_scale(tensor):
    return lax.rsqrt(jnp.sum(tensor * tensor, axis=1, keepdims=True) * (1.0 / HDIM) + EPS)


def row_scale(tensor):
    return lax.rsqrt(jnp.mean(tensor * tensor, axis=1, keepdims=True) + EPS)


def call(body, out_shape, args, scalars=None, any_in=(), any_out=(), scratch=(), aliases=None):
    offset = 0 if scalars is None else 1
    in_specs = [pl.BlockSpec(memory_space=pl.ANY if i in any_in else pltpu.VMEM) for i in range(len(args))]
    out_specs = [pl.BlockSpec(memory_space=pl.ANY if i in any_out else pltpu.VMEM) for i in range(len(out_shape))]
    params = pltpu.CompilerParams(vmem_limit_bytes=VMEM_BYTES)
    shapes = [jax.ShapeDtypeStruct(s, d) for s, d in out_shape]
    if scalars is not None:
        in_specs = [pl.BlockSpec(memory_space=pltpu.SMEM)] + in_specs
        args = (scalars,) + tuple(args)
    return pl.pallas_call(
        body,
        out_shape=shapes,
        in_specs=in_specs,
        out_specs=out_specs,
        scratch_shapes=list(scratch),
        input_output_aliases={i + offset: o for i, o in (aliases or {}).items()},
        compiler_params=params,
    )(*args)


def start_body(sc, cot, routes, packed, ranks_out):
    base = sc[0] * TOK
    length = sc[1]
    place = base + lax.broadcasted_iota(jnp.int32, (TOK, 1), 0)
    keep = jnp.where(place < length, 1.0, 0.0)
    packed[0:TOK, :] = (cot[...].astype(F32) * keep).astype(BF16)
    names = lax.broadcasted_iota(jnp.int32, (TOK, EXPERTS), 1)
    member = jnp.zeros((TOK, EXPERTS), F32)
    for k in range(routes.shape[1]):
        member = member + jnp.where(routes[:, k : k + 1] == names, 1.0, 0.0)
    member = member.astype(BF16)
    earlier = lax.broadcasted_iota(jnp.int32, (TOK, TOK), 0)
    later = lax.broadcasted_iota(jnp.int32, (TOK, TOK), 1)
    before = jnp.where(earlier < later, 1.0, 0.0).astype(BF16)
    same = jnp.where(earlier == later, 1.0, 0.0).astype(BF16)
    counts = tn(member, before)
    chosen = tn(member, same)
    ranks = jnp.where(chosen > 0.5, counts, -1.0)
    ranks_out[...] = ranks
    quarter = EXPERTS // 4
    rows = jnp.concatenate([ranks[q * quarter : (q + 1) * quarter] for q in range(4)], axis=1)
    packed[TOK:ROWS, :] = jnp.concatenate([rows, jnp.zeros_like(rows)], axis=0).astype(BF16)


def assemble_body(sc, own, other, spread4, spread2, proj, out_w, held):
    y_at, z_at, core = sc[0], sc[1], sc[2]
    for block in range(16):
        rel = ((block // 4 - y_at + 4) % 4) * 4 + (block % 4 - z_at + 4) % 4
        mine = own[rel].astype(F32)
        theirs = other[rel].astype(F32)
        for side in range(2):
            part = jnp.where(core == side, mine, theirs).astype(BF16)
            at = (2 * block + side) * 32
            for piece in range(3):
                held[at : at + 32, piece * 256 : (piece + 1) * 256] = part[piece * 32 : (piece + 1) * 32]
    proj[:, 0:512] = nn(held[:, 0:256], spread4[...]).astype(BF16)
    proj[:, 512:768] = nn(held[:, 256:384], spread2[...]).astype(BF16)
    proj[:, 768:1024] = nn(held[:, 384:512], spread2[...]).astype(BF16)
    out_w[...] = nn(held[:, 512:768], spread4[...]).astype(BF16)


def project_body(sc, x, gain, proj, head_gain, cos, sin, h1, qa, ka, va, raw_out):
    at = sc[0]
    length = sc[1]
    xf = x[...].astype(F32)
    normed = (xf * row_scale(xf) * gain[...]).astype(BF16)
    h1[...] = normed
    raw = nn(normed, proj[...])
    raw_out[...] = raw[:, 0:768]
    cos_t = cos[at]
    sin_t = sin[at]
    lane = lanes((TOK, PITCH))
    place = at * TOK + lax.broadcasted_iota(jnp.int32, (TOK, PITCH), 0)
    bias = jnp.where(place < length, 0.0, -1e30)
    q_aug = jnp.where(lane == HDIM, 1.0, 0.0)
    k_aug = jnp.where(lane == HDIM, bias, jnp.where(lane < HDIM + 4, 1.0, 0.0))
    v_aug = jnp.where(lane < HDIM + 2, 1.0, 0.0)
    for head in range(6):
        cols = slice(head * PITCH, (head + 1) * PITCH)
        one = raw[:, cols]
        ready = one * head_scale(one) * head_gain[:, cols]
        turned = ready * cos_t + swap_halves(ready) * sin_t
        if head < 4:
            qa[:, cols] = jnp.where(lane < HDIM, turned, q_aug).astype(BF16)
        else:
            here = slice((head - 4) * PITCH, (head - 3) * PITCH)
            ka[:, here] = jnp.where(lane < HDIM, turned, k_aug).astype(BF16)
    for head in range(2):
        va[:, head * PITCH : (head + 1) * PITCH] = jnp.where(
            lane < HDIM, raw[:, 768 + head * PITCH : 768 + (head + 1) * PITCH], v_aug
        ).astype(BF16)


def attend_body(qa, k0, k1, k2, k3, v0, v1, v2, v3, out_w, branch, mixed, qb):
    lane = lanes((TOK, PITCH))
    for head in range(4):
        cols = slice(head * PITCH, (head + 1) * PITCH)
        kv = slice((head // 2) * PITCH, (head // 2 + 1) * PITCH)
        query = qa[:, cols]
        total = jnp.zeros((TOK, PITCH), F32)
        for keys, values in ((k0, v0), (k1, v1), (k2, v2), (k3, v3)):
            weight = jnp.exp2(nt(query, keys[:, kv]) * (LOG2E / 8.0)).astype(BF16)
            total = total + nn(weight, values[:, kv])
        denom = total[:, HDIM : HDIM + 1]
        mixed[:, cols] = jnp.where(lane < HDIM, total / denom, 0.0).astype(BF16)
        level = jnp.log(denom) * -8.0
        high = level.astype(BF16).astype(F32)
        middle = (level - high).astype(BF16).astype(F32)
        low = level - high - middle
        stats = jnp.where(lane == HDIM + 1, high, jnp.where(lane == HDIM + 2, middle, low))
        qb[:, cols] = jnp.where(
            (lane > HDIM) & (lane < HDIM + 4), stats, query.astype(F32)
        ).astype(BF16)
    branch[...] = nt(mixed[...], out_w[...]).astype(BF16)


def middle_body(x, p0, p1, p2, p3, gain, x_mid, h2):
    total = (
        x[...].astype(F32)
        + ((p0[...].astype(F32) + p1[...].astype(F32)) + (p2[...].astype(F32) + p3[...].astype(F32)))
    )
    x_mid[...] = total
    h2[...] = (total * row_scale(total) * gain[...]).astype(BF16)


def gates_of(logits, ranks):
    routed = ranks >= 0.0
    masked = jnp.where(routed, logits, -1e30)
    weight = jnp.where(routed, jnp.exp(masked - jnp.max(masked, axis=0, keepdims=True)), 0.0)
    return weight / jnp.sum(weight, axis=0, keepdims=True)


def gates_body(h2, router, ranks, gates):
    gates[...] = gates_of(nt(router[...], h2[...]), ranks[...])


def unfold(rows):
    return jnp.concatenate([rows[:, q * TOK : (q + 1) * TOK] for q in range(4)], axis=0)


def experts_body(pieces, unit, *refs):
    sc = refs[0]
    tokens = refs[1 : 1 + len(pieces)]
    at = 1 + len(pieces)
    cot_all, router = refs[at], refs[at + 1]
    weights = refs[at + 2 : at + 8]
    at = at + 8
    if unit > 0:
        at = at + 6
    y_out, y_back, taken_all, push_all, hidden_all, gate_all, up_all = refs[at : at + 7]
    cot, y_hold, t_hold, e_hold, h_hold, g_hold, u_hold, sems = refs[at + 7 :]
    copies_in = [pltpu.make_async_copy(cot_all.at[sc[i]], cot.at[i], sems.at[i]) for i in range(4)]
    for one in copies_in:
        one.start()
    where = []
    for index, count in enumerate(pieces):
        where += [(tokens[index], j) for j in range(count)]
    own_names = (sc[4], sc[5])
    names = lax.broadcasted_iota(jnp.int32, (EXPERTS, TOK), 0)
    slots = lax.broadcasted_iota(jnp.int32, (CAP, TOK), 0).astype(F32)
    for one in copies_in:
        one.wait()
    picks = [[], []]
    gate_rows = [[], []]
    for i in range(4):
        ref, j = where[i]
        block = ref[j]
        ranks = unfold(cot[i, TOK : TOK + EXPERTS // 4, :].astype(F32))
        gates = gates_of(nt(router[...], block), ranks)
        for e in range(2):
            hit = names == own_names[e]
            rank = jnp.sum(jnp.where(hit, ranks, 0.0), axis=0, keepdims=True)
            gate = jnp.sum(jnp.where(hit, gates, 0.0), axis=0, keepdims=True)
            pick = jnp.where(slots == rank, 1.0, 0.0)
            picks[e].append(pick.astype(BF16))
            gate_rows[e].append(jnp.sum(pick * gate, axis=1, keepdims=True))
    marks = [[], []]
    back_parts = []
    out_parts = []
    copies_out = []
    for e in range(2):
        gate_w, up_w, down_w = weights[3 * e], weights[3 * e + 1], weights[3 * e + 2]
        for i in range(4):
            ref, j = where[i]
            t_hold[e, i * CAP : (i + 1) * CAP, :] = nn(picks[e][i], ref[j]).astype(BF16)
        taken = t_hold[e]
        gate_act = nn(taken, gate_w[0])
        up_act = nn(taken, up_w[0])
        sigma = jax.nn.sigmoid(gate_act)
        silu = gate_act * sigma
        hidden = (silu * up_act).astype(BF16)
        h_hold[e] = hidden
        result = nn(hidden, down_w[0]).astype(BF16).astype(F32)
        gate_col = jnp.concatenate(gate_rows[e], axis=0)
        grad_rows = jnp.concatenate([nn(picks[e][i], cot[i, 0:TOK, :]) for i in range(4)], axis=0)
        mark = jnp.sum(grad_rows * result, axis=1, keepdims=True)
        for i in range(4):
            marks[e].append(
                jnp.sum(picks[e][i].astype(F32) * mark[i * CAP : (i + 1) * CAP], axis=0, keepdims=True)
            )
        out_parts.append((result * gate_col).astype(BF16))
        push = (grad_rows * gate_col).astype(BF16)
        e_hold[e] = push
        grad_hidden = nt(push, down_w[0])
        grad_gate = (grad_hidden * up_act * (sigma * (1.0 + gate_act * (1.0 - sigma)))).astype(BF16)
        grad_up = (grad_hidden * silu).astype(BF16)
        g_hold[e] = grad_gate
        u_hold[e] = grad_up
        back_parts.append((nt(grad_gate, gate_w[0]) + nt(grad_up, up_w[0])).astype(BF16))
    stores = (
        (t_hold, taken_all, CAP * 4),
        (e_hold, push_all, CAP * 4),
        (h_hold, hidden_all, CAP * 4),
        (g_hold, gate_all, CAP * 4),
        (u_hold, up_all, CAP * 4),
    )
    for index, (hold, target, rows) in enumerate(stores):
        for e in range(2):
            one = pltpu.make_async_copy(
                hold.at[e], target.at[e, pl.ds(unit * rows, rows)], sems.at[4 + 2 * index + e]
            )
            one.start()
            copies_out.append(one)
    for i in range(4):
        pick = jnp.concatenate([picks[0][i], picks[1][i]], axis=0)
        rows = slice(i * CAP, (i + 1) * CAP)
        y_hold[i] = tn(pick, jnp.concatenate([out_parts[0][rows], out_parts[1][rows]], axis=0)).astype(BF16)
        one = pltpu.make_async_copy(y_hold.at[i], y_out.at[sc[i]], sems.at[14 + i])
        one.start()
        copies_out.append(one)
        y_back[i, 0:TOK, :] = tn(
            pick, jnp.concatenate([back_parts[0][rows], back_parts[1][rows]], axis=0)
        ).astype(BF16)
        mark = jnp.where(names == own_names[0], marks[0][i], 0.0) + jnp.where(
            names == own_names[1], marks[1][i], 0.0
        )
        high = mark.astype(BF16).astype(F32)
        low = mark - high
        quarter = EXPERTS // 4
        fold = [
            jnp.concatenate([part[q * quarter : (q + 1) * quarter] for q in range(4)], axis=1)
            for part in (high, low)
        ]
        y_back[i, TOK:ROWS, :] = jnp.concatenate(fold, axis=0).astype(BF16)
    for one in copies_out:
        one.wait()


def token_back_body(r0, r1, r2, h2, x_mid, ranks, gates, router, gain, packed, grad_mid, branch, small):
    total = r0[...].astype(F32) + (r1[...].astype(F32) + r2[...].astype(F32))
    marks = unfold(total[TOK : TOK + 8]) + unfold(total[TOK + 8 : TOK + 16])
    gate = gates[...]
    centre = jnp.sum(gate * marks, axis=0, keepdims=True)
    grad_logits = jnp.where(ranks[...] >= 0.0, gate * (marks - centre), 0.0).astype(BF16)
    small[0:EXPERTS, :] = nn(grad_logits, h2[...])
    grad_h2 = total[0:TOK] + tn(grad_logits, router[...])
    x = x_mid[...]
    scale = row_scale(x)
    normed = x * scale
    grad_normed = grad_h2 * gain[...]
    small[EXPERTS : EXPERTS + 8, :] = jnp.broadcast_to(
        jnp.sum(grad_h2 * normed, axis=0, keepdims=True), (8, WIDTH)
    )
    out = packed[0:TOK, :].astype(F32) + scale * (
        grad_normed - normed * jnp.mean(grad_normed * normed, axis=1, keepdims=True)
    )
    grad_mid[...] = out
    branch[...] = out.astype(BF16)


def head_back(grad, raw, gain, cos_t, sin_t):
    upstream = grad * cos_t - swap_halves(grad) * sin_t
    scale = head_scale(raw)
    normed = raw * scale
    grad_normed = upstream * gain
    gain_grad = jnp.sum(upstream * normed, axis=0, keepdims=True)
    inner = jnp.sum(grad_normed * normed, axis=1, keepdims=True) * (1.0 / HDIM)
    return scale * (grad_normed - normed * inner), gain_grad


def attend_back_body(first, *refs):
    sc, rows, out_w, qb, mixed, k0, k1, k2, k3, v0, v1, v2, v3, raw, head_gain, cos, sin = refs[:17]
    rest = refs[17:] if first else refs[18:]
    before = None if first else refs[17]
    grad_query, gain_out, both = rest
    at = sc[0]
    cos_t = cos[at]
    sin_t = sin[at]
    lane = lanes((TOK, PITCH))
    pushed = nn(rows[...], out_w[...]).astype(BF16)
    gain_total = jnp.zeros((1, PITCH), F32)
    for head in range(4):
        cols = slice(head * PITCH, (head + 1) * PITCH)
        group = head // 2
        kv = slice(group * PITCH, (group + 1) * PITCH)
        grad = pushed[:, cols]
        grad_f = grad.astype(F32)
        delta = -jnp.sum(grad_f * mixed[:, cols].astype(F32), axis=1, keepdims=True)
        high = delta.astype(BF16).astype(F32)
        grad_aug = jnp.where(
            lane == HDIM, high, jnp.where(lane == HDIM + 1, delta - high, grad_f)
        ).astype(BF16)
        query = qb[:, cols]
        grad_q = jnp.zeros((TOK, PITCH), F32)
        for c, (keys, values) in enumerate(((k0, v0), (k1, v1), (k2, v2), (k3, v3))):
            probs = jnp.exp2(nt(keys[:, kv], query) * (LOG2E / 8.0))
            inner = nt(values[:, kv], grad_aug)
            grad_scores = (probs * inner).astype(BF16)
            add_k = nn(grad_scores, query)
            add_v = nn(probs.astype(BF16), grad)
            kcols = kv
            vcols = slice(256 + group * PITCH, 256 + (group + 1) * PITCH)
            if head % 2 == 0:
                if first:
                    both[c, :, kcols] = add_k
                    both[c, :, vcols] = add_v
                else:
                    both[c, :, kcols] = before[c, :, kcols] + add_k
                    both[c, :, vcols] = before[c, :, vcols] + add_v
            else:
                both[c, :, kcols] += add_k
                both[c, :, vcols] += add_v
            grad_q = grad_q + tn(grad_scores, keys[:, kv])
        grad_q = jnp.where(lane < HDIM, grad_q * 0.125, 0.0)
        back, gain_grad = head_back(grad_q, raw[:, cols], head_gain[:, cols], cos_t, sin_t)
        grad_query[:, cols] = back.astype(BF16)
        gain_total = gain_total + gain_grad
    gain_out[...] = jnp.broadcast_to(gain_total, (8, PITCH))


def finish_body(chunk, sc, both, raw, head_gain, cos, sin, grad_query, x, proj, spread4, spread2, part_out, packed, gains):
    at = sc[0]
    cos_t = cos[at]
    sin_t = sin[at]
    lane = lanes((TOK, PITCH))
    pieces = [grad_query[...]]
    key_gain = jnp.zeros((1, PITCH), F32)
    for head in range(2):
        cols = slice(head * PITCH, (head + 1) * PITCH)
        grad = jnp.where(lane < HDIM, both[chunk, :, cols] * 0.125, 0.0)
        back, gain_grad = head_back(
            grad,
            raw[:, 512 + head * PITCH : 512 + (head + 1) * PITCH],
            head_gain[:, 512 + head * PITCH : 512 + (head + 1) * PITCH],
            cos_t,
            sin_t,
        )
        pieces.append(back.astype(BF16))
        key_gain = key_gain + gain_grad
    for head in range(2):
        cols = slice(256 + head * PITCH, 256 + (head + 1) * PITCH)
        pieces.append(jnp.where(lane < HDIM, both[chunk, :, cols], 0.0).astype(BF16))
    packed[:, 0:256] = nt(pieces[0], spread4[...]).astype(BF16)
    packed[:, 256:384] = nt(jnp.concatenate(pieces[1:3], axis=1), spread2[...]).astype(BF16)
    packed[:, 384:512] = nt(jnp.concatenate(pieces[3:5], axis=1), spread2[...]).astype(BF16)
    part = nt(jnp.concatenate(pieces, axis=1), proj[...])
    part_out[...] = part.astype(BF16)
    xf = x[...].astype(F32)
    gains[0:1, :] = jnp.sum(part * (xf * row_scale(xf)), axis=0, keepdims=True)
    gains[1:8, :] = jnp.zeros((7, WIDTH), F32)
    gains[1:2, 0:PITCH] = key_gain


def weight_body(*refs):
    h1, packed, rows, mixed = refs[0:4], refs[4:8], refs[8:12], refs[12:16]
    spread4, out = refs[16], refs[17]
    total = jnp.zeros((WIDTH, 512), F32)
    other = jnp.zeros((WIDTH, 256), F32)
    for i in range(4):
        total = total + tn(h1[i][...], packed[i][...])
        other = other + tn(rows[i][...], nt(mixed[i][...], spread4[...]).astype(BF16))
    out[:, 0:512] = total.astype(BF16)
    out[:, 512:768] = other.astype(BF16)


def input_body(p0, p1, p2, p3, x, gain, grad_mid, out):
    upstream = (p0[...].astype(F32) + p1[...].astype(F32)) + (p2[...].astype(F32) + p3[...].astype(F32))
    xf = x[...].astype(F32)
    scale = row_scale(xf)
    normed = xf * scale
    grad_normed = upstream * gain[...]
    out[...] = grad_mid[...] + scale * (
        grad_normed - normed * jnp.mean(grad_normed * normed, axis=1, keepdims=True)
    )


def place_of(index):
    return index // 8, (index // 2) % 4, index % 2


def index_of(y, z, core):
    return (y % 4) * 8 + (z % 4) * 2 + core


def shift_yz(tensor, dy, dz, flip=0):
    pairs = []
    for d in range(32):
        y, z, core = place_of(d)
        pairs.append((d, index_of(y + dy, z + dz, core ^ flip)))
    return lax.ppermute(tensor, "dp", pairs)


def shift_axis(tensor, axis, step):
    pairs = []
    for d in range(32):
        y, z, core = place_of(d)
        if (core == 0) == (axis == 0):
            pairs.append((d, index_of(y + step, z, core)))
        else:
            pairs.append((d, index_of(y, z + step, core)))
    return lax.ppermute(tensor, "dp", pairs)


def shift_mp(tensor, step):
    return lax.ppermute(tensor, "mp", [(i, (i + step) % 4) for i in range(4)])


def gather_weights(shard, sc):
    along_y = [shard] + [shift_yz(shard, -s, 0) for s in (1, 2, 3)]
    rows = jnp.stack(along_y)
    along_z = [rows] + [shift_yz(rows, 0, -s) for s in (1, 2, 3)]
    own = jnp.stack(along_z, axis=1).reshape(16, *shard.shape)
    other = shift_yz(own, 0, 0, 1)
    return call(
        assemble_body,
        [((WIDTH, 1024), BF16), ((WIDTH, 512), BF16)],
        (own, other, jnp.asarray(spread(4), BF16), jnp.asarray(spread(2), BF16)),
        scalars=sc,
        scratch=[pltpu.VMEM((WIDTH, 768), BF16)],
    )


def all_sum(tensor):
    tensor = tensor + (shift_mp(tensor, 1) + shift_mp(tensor, 2) + shift_mp(tensor, 3))
    tensor = tensor + (shift_yz(tensor, 1, 0) + shift_yz(tensor, 2, 0) + shift_yz(tensor, 3, 0))
    tensor = tensor + (shift_yz(tensor, 0, 1) + shift_yz(tensor, 0, 2) + shift_yz(tensor, 0, 3))
    return tensor + shift_yz(tensor, 0, 0, 1)


def add_low(left, *others):
    total = left.astype(F32)
    for one in others:
        total = total + one.astype(F32)
    return total.astype(BF16)


PLANES = [[core + 2 * k for k in range(16)] for core in range(2)]
STEPS = (0, 1, -1, 2)


def shards(
    layer_input,
    lengths,
    routes,
    attn_gain,
    query_gain,
    key_gain,
    query_weight,
    key_value_weight,
    out_weight,
    ffn_gain,
    router_weight,
    gate_weight,
    up_weight,
    down_weight,
    cotangent,
):
    dp_at = lax.axis_index("dp").astype(jnp.int32)
    mp_at = lax.axis_index("mp").astype(jnp.int32)
    y_at, z_at, core = dp_at // 8, (dp_at // 2) % 4, dp_at % 2
    length = lengths[0].astype(jnp.int32)
    cos_np, sin_np = rope_tables()
    cos_tab, sin_tab = jnp.asarray(cos_np), jnp.asarray(sin_np)
    spread4, spread2 = jnp.asarray(spread(4), BF16), jnp.asarray(spread(2), BF16)
    attn_row = attn_gain.reshape(1, WIDTH)
    ffn_row = ffn_gain.reshape(1, WIDTH)
    pad = jnp.zeros((PITCH - HDIM,), F32)
    head_gain = jnp.concatenate([query_gain, pad] * 4 + [key_gain, pad] * 2).reshape(1, 768)
    router = router_weight.T

    chunks = [layer_input] + [shift_mp(layer_input, -s) for s in (1, 2, 3)]
    chunk_at = [(mp_at + r) % 4 for r in range(4)]
    shard = jnp.concatenate([query_weight, key_value_weight.reshape(32, 256), out_weight], axis=0)
    proj, out_w = gather_weights(shard, jnp.stack([y_at, z_at, core]))

    packed, ranks = call(
        start_body,
        [((ROWS, WIDTH), BF16), ((EXPERTS, TOK), F32)],
        (cotangent, routes),
        scalars=jnp.stack([mp_at, length]),
    )
    cot_all = lax.all_gather(packed, "dp", axis=0, tiled=False, axis_index_groups=PLANES)
    weights_own = (gate_weight, up_weight, down_weight)
    weights_other = tuple(shift_yz(w, 0, 0, 1) for w in weights_own)

    h1, qa, ka, va, raw = [], [], [], [], []
    for r in range(4):
        made = call(
            project_body,
            [
                ((TOK, WIDTH), BF16),
                ((TOK, 512), BF16),
                ((TOK, 256), BF16),
                ((TOK, 256), BF16),
                ((TOK, 768), F32),
            ],
            (chunks[r], attn_row, proj, head_gain, cos_tab, sin_tab),
            scalars=jnp.stack([chunk_at[r], length]),
        )
        for store, one in zip((h1, qa, ka, va, raw), made):
            store.append(one)

    branch, mixed, qb = [None] * 4, [None] * 4, [None] * 4
    for r in (2, 1, 3, 0):
        branch[r], mixed[r], qb[r] = call(
            attend_body,
            [((TOK, WIDTH), BF16), ((TOK, 512), BF16), ((TOK, 512), BF16)],
            (qa[r], *ka, *va, out_w),
        )
    arrived = [branch[0]] + [shift_mp(branch[r], r) for r in (1, 2, 3)]
    x_mid, h2 = call(
        middle_body,
        [((TOK, WIDTH), F32), ((TOK, WIDTH), BF16)],
        (layer_input, *arrived, ffn_row),
    )
    (gates,) = call(gates_body, [((EXPERTS, TOK), F32)], (h2, router, ranks))

    plus, minus = shift_axis(h2, 0, -1), shift_axis(h2, 0, 1)
    far_a, far_b = shift_axis(plus[: TOK // 2], 0, -1), shift_axis(minus[TOK // 2 :], 0, 1)
    near = jnp.stack([h2, plus, minus, jnp.concatenate([far_a, far_b], axis=0)])
    unit_plus, unit_minus = shift_axis(near, 1, -1), shift_axis(near, 1, 1)
    unit_far_a, unit_far_b = shift_axis(unit_plus[:2], 1, -1), shift_axis(unit_minus[2:], 1, 1)
    units = [(near,), (unit_plus,), (unit_minus,), (unit_far_a, unit_far_b)]

    first_at = jnp.where(core == 0, y_at, z_at)
    second_at = jnp.where(core == 0, z_at, y_at)
    saved = None
    backs = []
    for u, step in enumerate(STEPS):
        second = (second_at + step + 4) % 4
        order = []
        for s in STEPS:
            first = (first_at + s + 4) % 4
            order.append(jnp.where(core == 0, first * 4 + second, second * 4 + first))
        sc = jnp.stack(order + [dp_at, dp_at + 1 - 2 * core]).astype(jnp.int32)
        pieces = tuple(one.shape[0] for one in units[u])
        args = (*units[u], cot_all, router, *weights_own, *weights_other)
        any_in = [len(pieces)]
        aliases = None
        if saved is not None:
            base = len(args)
            aliases = {base + i: (0 if i == 0 else i + 1) for i in range(6)}
            any_in += list(range(base, base + 6))
            args = args + tuple(saved)
        made = call(
            partial(experts_body, pieces, u),
            [
                ((16, TOK, WIDTH), BF16),
                ((4, ROWS, WIDTH), BF16),
                ((2, 16 * CAP, WIDTH), BF16),
                ((2, 16 * CAP, WIDTH), BF16),
                ((2, 16 * CAP, FF), BF16),
                ((2, 16 * CAP, FF), BF16),
                ((2, 16 * CAP, FF), BF16),
            ],
            args,
            scalars=sc,
            any_in=any_in,
            any_out=(0, 2, 3, 4, 5, 6),
            scratch=[
                pltpu.VMEM((4, ROWS, WIDTH), BF16),
                pltpu.VMEM((4, TOK, WIDTH), BF16),
                pltpu.VMEM((2, 4 * CAP, WIDTH), BF16),
                pltpu.VMEM((2, 4 * CAP, WIDTH), BF16),
                pltpu.VMEM((2, 4 * CAP, FF), BF16),
                pltpu.VMEM((2, 4 * CAP, FF), BF16),
                pltpu.VMEM((2, 4 * CAP, FF), BF16),
                pltpu.SemaphoreType.DMA((18,)),
            ],
            aliases=aliases,
        )
        backs.append(made[1])
        saved = [made[0]] + list(made[2:])
    y_out, taken, push, hidden, grad_gate, grad_up = saved

    b0, bp, bm, bf = backs
    half_a, half_b = shift_axis(bf[:2], 1, 1), shift_axis(bf[2:], 1, -1)
    plus_late, minus_late = add_low(bp[:2], half_a), add_low(bm[2:], half_b)
    plus_a, plus_b = shift_axis(plus_late, 1, 1), shift_axis(bp[2:], 1, 1)
    minus_a, minus_b = shift_axis(bm[:2], 1, -1), shift_axis(minus_late, 1, -1)
    line_a = add_low(b0[:2], plus_a, minus_a)
    line_b = add_low(b0[2:], plus_b, minus_b)
    cut = ROWS // 2 + 8
    far_up, far_down = shift_axis(line_b[1, :cut], 0, 1), shift_axis(line_b[1, cut:], 0, -1)
    send_up = jnp.concatenate([add_low(line_a[1, :cut], far_up), line_a[1, cut:]], axis=0)
    send_down = jnp.concatenate([line_b[0, :cut], add_low(line_b[0, cut:], far_down)], axis=0)
    got_up, got_down = shift_axis(send_up, 0, 1), shift_axis(send_down, 0, -1)
    grad_mid, grad_rows, small = call(
        token_back_body,
        [((TOK, WIDTH), F32), ((TOK, WIDTH), BF16), ((EXPERTS + 8, WIDTH), F32)],
        (line_a[0], got_up, got_down, h2, x_mid, ranks, gates, router, ffn_row, packed),
    )

    def both_experts(left, right):
        def one(e, dtype):
            return lax.dot_general(
                left[e], right[e], (((0,), (0,)), ((), ())), preferred_element_type=F32
            ).astype(dtype)

        return (one(0, F32) + shift_yz(one(1, BF16), 0, 0, 1).astype(F32)).astype(BF16)

    grad_gate_w = both_experts(taken, grad_gate)
    grad_up_w = both_experts(taken, grad_up)
    grad_down_w = both_experts(hidden, push)
    stacked = jnp.concatenate(
        [grad_gate_w.reshape(4, 256, FF), grad_up_w.reshape(4, 256, FF), grad_down_w.reshape(4, 256, FF)],
        axis=1,
    ).reshape(4 * 768, FF)
    expert_grads = lax.psum_scatter(stacked, "mp", scatter_dimension=0, tiled=True).astype(F32)

    rows = [grad_rows] + [shift_mp(grad_rows, -s) for s in (1, 2, 3)]
    both = None
    grad_query, query_gains = [None] * 4, [None] * 4
    for r in (0, 1, 3, 2):
        args = (rows[r], out_w, qb[r], mixed[r], *ka, *va, raw[r], head_gain, cos_tab, sin_tab)
        first = both is None
        grad_query[r], query_gains[r], both = call(
            partial(attend_back_body, first),
            [((TOK, 512), BF16), ((8, PITCH), F32), ((4, TOK, 512), F32)],
            args if first else args + (both,),
            scalars=chunk_at[r].reshape(1),
            aliases=None if first else {len(args): 2},
        )
    parts, slim, gains = [None] * 4, [None] * 4, [None] * 4
    for r in (2, 1, 3, 0):
        parts[r], slim[r], gains[r] = call(
            partial(finish_body, r),
            [((TOK, WIDTH), BF16), ((TOK, 512), BF16), ((8, WIDTH), F32)],
            (both, raw[r], head_gain, cos_tab, sin_tab, grad_query[r], chunks[r], proj, spread4, spread2),
            scalars=chunk_at[r].reshape(1),
        )
    arrived = [parts[0]] + [shift_mp(parts[r], r) for r in (1, 2, 3)]
    (input_grad,) = call(
        input_body, [((TOK, WIDTH), F32)], (*arrived, layer_input, attn_row, grad_mid)
    )
    (weight_part,) = call(
        weight_body, [((WIDTH, 768), BF16)], (*h1, *slim, *rows, *mixed, spread4)
    )
    shared = lax.all_to_all(
        weight_part.reshape(32, 32, 768), "dp", split_axis=0, concat_axis=0, tiled=True
    )
    weight_sum = jnp.sum(shared.astype(F32), axis=0)

    router_sum = all_sum(small)
    gain_part = sum(gains)
    query_gain_part = sum(query_gains)
    gain_sum = all_sum(jnp.concatenate([gain_part[0:2], jnp.pad(query_gain_part[0:1], ((0, 0), (0, WIDTH - PITCH)))]))

    returned = lax.psum_scatter(
        y_out.reshape(16 * TOK, WIDTH), "dp", scatter_dimension=0, tiled=True, axis_index_groups=PLANES
    )
    layer_output = (x_mid + returned.astype(F32)).astype(BF16)

    return (
        layer_output,
        input_grad,
        gain_sum[0],
        gain_sum[2, :HDIM],
        gain_sum[1, :HDIM],
        weight_sum[:, 0:256],
        weight_sum[:, 256:512].reshape(32, 2, 128),
        weight_sum[:, 512:768],
        router_sum[EXPERTS],
        router_sum[:EXPERTS].T,
        expert_grads[0:256].reshape(1, 256, FF),
        expert_grads[256:512].reshape(1, 256, FF),
        expert_grads[512:768].reshape(1, 128, WIDTH),
    )


def solution(mesh):
    tokens = P(("dp", "mp"), None)
    in_specs = (
        tokens,
        P("dp"),
        tokens,
        P(),
        P(),
        P(),
        P("dp", "mp"),
        P("dp", None, "mp"),
        P("dp", "mp"),
        P(),
        P(),
        P("dp", None, None),
        P("dp", None, None),
        P("dp", None, None),
        tokens,
    )
    out_specs = (
        tokens,
        tokens,
        P(),
        P(),
        P(),
        P("dp", "mp"),
        P("dp", None, "mp"),
        P("dp", "mp"),
        P(),
        P(),
        P("dp", "mp", None),
        P("dp", "mp", None),
        P("dp", "mp", None),
    )
    return jax.shard_map(shards, mesh=mesh, in_specs=in_specs, out_specs=out_specs, check_vma=False)
```

time: 1130 us -> 539 us (0.48)
  waiting for transfers between devices: 614 us -> 167 us
  Pallas kernels: 0 us -> 190 us
  blocking collectives: 139 us -> 0 us
  matrix products: 140 us -> 22 us
  other arithmetic: 85.8 us -> 12.6 us
  starting transfers between devices: 45.1 us -> 98.8 us
  local copies, waits for them, and re-layouts: 80.1 us -> 28.4 us
    reduce_scatter x8 -> x2, waiting for transfers between devices: 275 us -> 0.01 us  [the longest x1 0.01 us: shards(): lax.psum_scatter(stacked, 'mp', scatter_dimension=0, tiled=True).astype(F32)]
    all_to_all x4 -> x1, waiting for transfers between devices: 251 us -> 0.01 us  [shards(): lax.all_to_all(weight_part.reshape(32, 32, 768), 'dp', split_axis=0, conc...]
    pallas_call x0 -> x27, Pallas kernels: none -> 190 us  [call(): pl.pallas_call(body, out_shape=shapes, in_specs=in_specs, out_specs=out_s...]
    ppermute x0 -> x63, waiting for transfers between devices: none -> 166 us  [the longest x18 92.5 us: shift_axis(): return lax.ppermute(tensor, 'dp', pairs)]
    dot_general x27 -> x6, matrix products: 140 us -> 22 us  [one(): lax.dot_general(left[e], right[e], (((0,), (0,)), ((), ())), preferred_el...]
    ppermute x0 -> x63, starting transfers between devices: none -> 94.6 us  [the longest x27 35.8 us: shift_yz(): return lax.ppermute(tensor, 'dp', pairs)]
    psum x1 -> x0, waiting for transfers between devices: 75.6 us -> none  [shards(): lax.psum((attn_gain_part, query_gain_part, key_gain_part, ffn_gain_part,...]
    all_gather x3 -> x0, blocking collectives: 73.2 us -> none  [the longest x1 26.4 us: shards(): lax.all_gather(key_value_weight, 'dp', axis=0, tiled=True)]
  transfers between devices with their start and end apart: 15 -> 67, of which waited for: 11 -> 28; matrix products, arithmetic and copies ran while one was open for 18% -> 7% of each run, Pallas kernels for 0% -> 32%
where the time goes in v1:
time: 539 us; the launch traced here: 534 us
  Pallas kernels  190 us (35%)
  waiting for transfers between devices  167 us (31%)
  starting transfers between devices  98.8 us (18%)
  local copies, waits for them, and re-layouts  28.4 us (5%)
  matrix products  22 us (4%)
  between operations  15.3 us (3%)
  other arithmetic  12.6 us (2%)
    pallas_call x27, Pallas kernels, call(): pl.pallas_call(body, out_shape=shapes, in_specs=in_specs, out_specs=out_s...  190 us
    ppermute x18, waiting for transfers between devices, shift_axis(): return lax.ppermute(tensor, 'dp', pairs)  92.5 us
    ppermute x18, waiting for transfers between devices, shift_mp(): return lax.ppermute(tensor, 'mp', [(i, (i + step) % 4) for i in range(4)])  43.7 us
    ppermute x27, starting transfers between devices, shift_yz(): return lax.ppermute(tensor, 'dp', pairs)  35.8 us
    ppermute x18, starting transfers between devices, shift_mp(): return lax.ppermute(tensor, 'mp', [(i, (i + step) % 4) for i in range(4)])  30.8 us
    ppermute x27, waiting for transfers between devices, shift_yz(): return lax.ppermute(tensor, 'dp', pairs)  30.1 us
    ppermute x18, starting transfers between devices, shift_axis(): return lax.ppermute(tensor, 'dp', pairs)  28 us
    dot_general x6, matrix products, one(): lax.dot_general(left[e], right[e], (((0,), (0,)), ((), ())), preferred_el...  22 us
  transfers between devices with their start and end apart: 67, of which 28 were waited for; matrix products, arithmetic and copies ran while one was open for 7% of the time, Pallas kernels for 32%

profile of v1, /device:TPU:0, one launch (start us, length us, event | category | flops | bytes accessed | tf_op | source)
XLA Modules:
  0.0 534.0 jit_solution(11111569264156176834)
XLA Ops:
  30.0 5.6 %collective-permute-done.5 = bf16[4,96,256]{2,1,0:T(8,128)(2,1)S(1)} collective-permute-done((bf16[4,96,256]{2,1,0:T(8,128)(2,1)S(1)}, bf16[4,96,256]{2,1,0:T(8,128)(2,1)S(1)}, u32[]{:S(2)}, u32[]{:S(2)}) %collective-permute-start.5) | collective-permute-done | bytes 196640 | tf_op jit(solution)/shard_map/ppermute | solution.py:479
  35.6 9.2 %collective-permute-done.4 = bf16[4,96,256]{2,1,0:T(8,128)(2,1)S(1)} collective-permute-done((bf16[4,96,256]{2,1,0:T(8,128)(2,1)S(1)}, bf16[4,96,256]{2,1,0:T(8,128)(2,1)S(1)}, u32[]{:S(2)}, u32[]{:S(2)}) %collective-permute-start.4) | collective-permute-done | bytes 196640 | tf_op jit(solution)/shard_map/ppermute | solution.py:479
  53.4 4.4 shard_map.300
  57.8 3.9 shard_map.301
  61.7 9.4 %collective-permute-done.7.x = bf16[256,1024]{1,0:T(8,128)(2,1)S(1)} collective-permute-done((bf16[256,1024]{1,0:T(8,128)(2,1)S(1)}, bf16[256,1024]{1,0:T(8,128)(2,1)S(1)}, u32[]{:S(2)}, u32[]{:S(2)}) %collective-permute-start.7) | collective-permute-done | bytes 524320 | tf_op jit(solution)/shard_map/ppermute | solution.py:494
  71.8 3.9 shard_map.302
  76.5 4.1 shard_map.303
  81.4 4.0 shard_map.304
  85.4 4.9 shard_map.306
  90.4 4.9 shard_map.307
  95.3 5.4 %collective-permute-start.11 = (bf16[256,1024]{1,0:T(8,128)(2,1)}, bf16[256,1024]{1,0:T(8,128)(2,1)S(1)}, u32[]{:S(2)}, u32[]{:S(2)}) collective-permute-start(bf16[256,1024]{1,0:T(8,128)(2,1)} %get-tuple-element.121), channel_id=1, source_target_pairs={{0,2},{1,3},{2,0},{3,1},{4,6},{5,7},{6,4},{7,5},{8,10},{9,11},{10,... | collective-permute-start | bytes 1572872 | tf_op jit(solution)/shard_map/ppermute | solution.py:494
  100.7 4.9 shard_map.308
  105.7 5.0 shard_map.305
  110.7 7.9 %collective-permute-done.11.p2 = bf16[256,1024]{1,0:T(8,128)(2,1)S(1)} collective-permute-done((bf16[256,1024]{1,0:T(8,128)(2,1)}, bf16[256,1024]{1,0:T(8,128)(2,1)S(1)}, u32[]{:S(2)}, u32[]{:S(2)}) %collective-permute-start.11) | collective-permute-done | bytes 524320 | tf_op jit(solution)/shard_map/ppermute | solution.py:494
  118.6 4.6 collective-permute-done.12.p3
  130.5 7.4 %collective-permute-done.14 = bf16[256,1024]{1,0:T(8,128)(2,1)S(1)} collective-permute-done((bf16[256,1024]{1,0:T(8,128)(2,1)}, bf16[256,1024]{1,0:T(8,128)(2,1)S(1)}, u32[]{:S(2)}, u32[]{:S(2)}) %collective-permute-start.14) | collective-permute-done | bytes 524320 | tf_op jit(solution)/shard_map/ppermute | solution.py:490
  141.3 4.3 collective-permute-done.16
  148.6 23.4 %collective-permute-done.17.refs_1_ = bf16[4,256,1024]{2,1,0:T(8,128)(2,1)S(1)} collective-permute-done((bf16[4,256,1024]{2,1,0:T(8,128)(2,1)S(1)}, bf16[4,256,1024]{2,1,0:T(8,128)(2,1)S(1)}, u32[]{:S(2)}, u32[]{:S(2)}) %collective-permute-start.17) | collective-permute-done | bytes 2097184 | tf_op jit(solution)/shard_map/ppermute | solution.py:490
  180.5 16.2 %shard_map.311 = (bf16[16,256,1024]{2,1,0:T(8,128)(2,1)}, bf16[4,272,1024]{2,1,0:T(8,128)(2,1)}, bf16[2,1536,1024]{2,1,0:T(8,128)(2,1)}, bf16[2,1536,1024]{2,1,0...) custom-call(s32[6]{0:T(128)} %stack.209.refs_0_, ...), custom_call_target="tpu_custom_call" | custom-call | tf_op jit(solution)/shard_map/pallas_call | solution.py:89
  196.7 16.3 %shard_map.312 = (bf16[16,256,1024]{2,1,0:T(8,128)(2,1)}, bf16[4,272,1024]{2,1,0:T(8,128)(2,1)}, bf16[2,1536,1024]{2,1,0:T(8,128)(2,1)}, bf16[2,1536,1024]{2,1,0...) custom-call(s32[6]{0:T(128)} %stack.204.refs_0_, ...), custom_call_target="tpu_custom_call", output_to_operand_aliasing={{0}: (10, {}), {2}: (11, {}), {3}: (12, {}), {4}: (13, {}),... | custom-call | tf_op jit(solution)/shard_map/pallas_call | solution.py:89
  213.0 16.2 %shard_map.313 = (bf16[16,256,1024]{2,1,0:T(8,128)(2,1)}, bf16[4,272,1024]{2,1,0:T(8,128)(2,1)}, bf16[2,1536,1024]{2,1,0:T(8,128)(2,1)}, bf16[2,1536,1024]{2,1,0...) custom-call(s32[6]{0:T(128)} %stack.199.refs_0_, ...), custom_call_target="tpu_custom_call", output_to_operand_aliasing={{0}: (10, {}), {2}: (11, {}), {3}: (12, {}), {4}: (13, {}),... | custom-call | tf_op jit(solution)/shard_map/pallas_call | solution.py:89
  229.3 16.6 %shard_map.314 = (bf16[16,256,1024]{2,1,0:T(8,128)(2,1)}, bf16[4,272,1024]{2,1,0:T(8,128)(2,1)}, bf16[2,1536,1024]{2,1,0:T(8,128)(2,1)}, bf16[2,1536,1024]{2,1,0...) custom-call(s32[6]{0:T(128)} %stack.187.refs_0_, ...), custom_call_target="tpu_custom_call", output_to_operand_aliasing={{0}: (11, {}), {2}: (12, {}), {3}: (13, {}), {4}: (14, {}),... | custom-call | tf_op jit(solution)/shard_map/pallas_call | solution.py:89
  245.9 4.3 fusion.40
  250.3 4.4 fusion.35
  262.7 4.6 add_convert_fusion.5
  280.4 9.5 %collective-permute-done.28 = bf16[2,272,1024]{2,1,0:T(8,128)(2,1)S(1)} collective-permute-done((bf16[2,272,1024]{2,1,0:T(8,128)(2,1)S(1)}, bf16[2,272,1024]{2,1,0:T(8,128)(2,1)S(1)}, u32[]{:S(2)}, u32[]{:S(2)}) %collective-permute-start.28) | collective-permute-done | bytes 1114144 | tf_op jit(solution)/shard_map/ppermute | solution.py:490
  290.3 3.7 collective-permute-start.29
  294.6 10.9 %collective-permute-done.27 = bf16[2,272,1024]{2,1,0:T(8,128)(2,1)S(1)} collective-permute-done((bf16[2,272,1024]{2,1,0:T(8,128)(2,1)S(1)}, bf16[2,272,1024]{2,1,0:T(8,128)(2,1)S(1)}, u32[]{:S(2)}, u32[]{:S(2)}) %collective-permute-start.27) | collective-permute-done | bytes 1114144 | tf_op jit(solution)/shard_map/ppermute | solution.py:490
  305.5 8.3 %collective-permute-done.29 = bf16[2,272,1024]{2,1,0:T(8,128)(2,1)S(1)} collective-permute-done((bf16[2,272,1024]{2,1,0:T(8,128)(2,1)S(1)}, bf16[2,272,1024]{2,1,0:T(8,128)(2,1)S(1)}, u32[]{:S(2)}, u32[]{:S(2)}) %collective-permute-start.29) | collective-permute-done | bytes 1114144 | tf_op jit(solution)/shard_map/ppermute | solution.py:490
  322.5 6.5 %collective-permute-done.32 = bf16[128,1024]{1,0:T(8,128)(2,1)S(1)} collective-permute-done((bf16[128,1024]{1,0:T(8,128)(2,1)S(1)}, bf16[128,1024]{1,0:T(8,128)(2,1)S(1)}, u32[]{:S(2)}, u32[]{:S(2)}) %collective-permute-start.32) | collective-permute-done | bytes 262176 | tf_op jit(solution)/shard_map/ppermute | solution.py:490
  329.2 3.8 collective-permute-start.33
  337.9 11.7 %collective-permute-done.33.r2 = bf16[272,1024]{1,0:T(8,128)(2,1)S(1)} collective-permute-done((bf16[272,1024]{1,0:T(8,128)(2,1)S(1)}, bf16[272,1024]{1,0:T(8,128)(2,1)S(1)}, u32[]{:S(2)}, u32[]{:S(2)}) %collective-permute-start.33) | collective-permute-done | bytes 557088 | tf_op jit(solution)/shard_map/ppermute | solution.py:490
  349.7 4.9 collective-permute-done.31.r1
  355.4 4.4 shard_map.316
  364.5 9.8 %shard_map.317 = (bf16[256,512]{1,0:T(8,128)(2,1)}, f32[8,128]{1,0:T(8,128)}, f32[4,256,512]{2,1,0:T(8,128)}) custom-call(s32[1]{0:T(128)} %bitcast.refs_0_.sc, bf16[256,1024]{1,0:T(8,128)(2,1)} %get-tuple-element.151.refs_1_.refs_8_, bf16[1024,512]{1,0:T(8,128)(2,1)} %get-tuple-element.116.out_w.refs_2_, bf16[256,512]{1,0:T(8,128)(2,1)} %get-tuple-element.161.refs_3_, ...), custom_call_target="tpu_custom_call" | custom-call | tf_op jit(solution)/shard_map/pallas_call | solution.py:89
  374.3 7.1 %collective-permute-done.36.refs_1_.refs_9_ = bf16[256,1024]{1,0:T(8,128)(2,1)S(1)} collective-permute-done((bf16[256,1024]{1,0:T(8,128)(2,1)}, bf16[256,1024]{1,0:T(8,128)(2,1)S(1)}, u32[]{:S(2)}, u32[]{:S(2)}) %collective-permute-start.36) | collective-permute-done | bytes 524320 | tf_op jit(solution)/shard_map/ppermute | solution.py:494
  382.3 10.1 %shard_map.318 = (bf16[256,512]{1,0:T(8,128)(2,1)}, f32[8,128]{1,0:T(8,128)}, f32[4,256,512]{2,1,0:T(8,128)}) custom-call(s32[1]{0:T(128)} %bitcast.14.refs_0_.sc, bf16[256,1024]{1,0:T(8,128)(2,1)} %copy-done.22, bf16[1024,512]{1,0:T(8,128)(2,1)} %get-tuple-element.116.out_w.refs_2_, ...), custom_call_target="tpu_custom_call", output_to_operand_aliasing={{2}: (17, {})} | custom-call | tf_op jit(solution)/shard_map/pallas_call | solution.py:89
  393.2 10.4 %shard_map.319 = (bf16[256,512]{1,0:T(8,128)(2,1)}, f32[8,128]{1,0:T(8,128)}, f32[4,256,512]{2,1,0:T(8,128)}) custom-call(s32[1]{0:T(128)} %bitcast.16.refs_0_.sc, bf16[256,1024]{1,0:T(8,128)(2,1)} %copy-done.23, bf16[1024,512]{1,0:T(8,128)(2,1)} %get-tuple-element.116.out_w.refs_2_, ...), custom_call_target="tpu_custom_call", output_to_operand_aliasing={{2}: (17, {})} | custom-call | tf_op jit(solution)/shard_map/pallas_call | solution.py:89
  404.3 10.1 %shard_map.320 = (bf16[256,512]{1,0:T(8,128)(2,1)}, f32[8,128]{1,0:T(8,128)}, f32[4,256,512]{2,1,0:T(8,128)}) custom-call(s32[1]{0:T(128)} %bitcast.15.refs_0_.sc, bf16[256,1024]{1,0:T(8,128)(2,1)} %copy-done.24, bf16[1024,512]{1,0:T(8,128)(2,1)} %get-tuple-element.116.out_w.refs_2_, ...), custom_call_target="tpu_custom_call", output_to_operand_aliasing={{2}: (17, {})} | custom-call | tf_op jit(solution)/shard_map/pallas_call | solution.py:89
  415.2 5.4 %shard_map.321 = (bf16[256,1024]{1,0:T(8,128)(2,1)}, bf16[256,512]{1,0:T(8,128)(2,1)}, f32[8,1024]{1,0:T(8,128)}) custom-call(s32[1]{0:T(128)} %bitcast.refs_0_.sc, f32[4,256,512]{2,1,0:T(8,128)} %get-tuple-element.167.both, f32[256,768]{1,0:T(8,128)} %get-tuple-element.163.refs_13_.raw, f32[1,768]{1,0:T(1,128)} %reshape.86.head_gain.refs_14_, ...), custom_call_target="tpu_custom_call" | custom-call | tf_op jit(solution)/shard_map/pallas_call | solution.py:89
  420.5 5.3 shard_map.322
  425.9 5.3 shard_map.323
  431.2 5.6 %shard_map.324 = (bf16[256,1024]{1,0:T(8,128)(2,1)}, bf16[256,512]{1,0:T(8,128)(2,1)}, f32[8,1024]{1,0:T(8,128)}) custom-call(s32[1]{0:T(128)} %bitcast.16.refs_0_.sc, f32[4,256,512]{2,1,0:T(8,128)} %get-tuple-element.167.both, f32[256,768]{1,0:T(8,128)} %get-tuple-element.157.refs_13_.raw, f32[1,768]{1,0:T(1,128)} %reshape.86.head_gain.refs_14_, ...), custom_call_target="tpu_custom_call" | custom-call | tf_op jit(solution)/shard_map/pallas_call | solution.py:89
  445.3 6.6 %shard_map.326 = bf16[1024,768]{1,0:T(8,128)(2,1)} custom-call(bf16[256,1024]{1,0:T(8,128)(2,1)} %get-tuple-element.185.refs_0_, bf16[256,1024]{1,0:T(8,128)(2,1)} %get-tuple-element.186.refs_1_, bf16[256,1024]{1,0:T(8,128)(2,1)} %get-tuple-element.187.refs_2_, bf16[256,1024]{1,0:T(8,128)(2,1)} %get-tuple-element.188.refs_3_, ...), custom_call_target="tpu_custom_call" | custom-call | tf_op jit(solution)/shard_map/pallas_call | solution.py:89
  451.9 4.1 all-to-all-start
  467.1 9.6 %collective-permute-done.45 = f32[3,1024]{1,0:T(4,128)S(1)} collective-permute-done((f32[3,1024]{1,0:T(4,128)S(1)}, f32[3,1024]{1,0:T(4,128)S(1)}, u32[]{:S(2)}, u32[]{:S(2)}) %collective-permute-start.45) | collective-permute-done | bytes 12320 | tf_op jit(solution)/shard_map/ppermute | solution.py:479
  501.7 3.9 collective-permute-done.37.p1
  505.6 10.2 %collective-permute-done.38.p2 = bf16[256,1024]{1,0:T(8,128)(2,1)S(1)} collective-permute-done((bf16[256,1024]{1,0:T(8,128)(2,1)}, bf16[256,1024]{1,0:T(8,128)(2,1)S(1)}, u32[]{:S(2)}, u32[]{:S(2)}) %collective-permute-start.38) | collective-permute-done | bytes 524320 | tf_op jit(solution)/shard_map/ppermute | solution.py:494
  (278 shorter events, 155.4 us)
Async XLA Ops:
  7.2 173.3 %all-gather.3.cloned.1.call-start = ((), (), s32[]{:S(2)}) async-start(), calls=%async_computation.5 | async-start | bytes 9469952 | tf_op jit(solution)/shard_map/all_gather | solution.py:571
  12.5 509.5 %reduce-scatter.5.cloned.1.call-start = ((), (), s32[]{:S(2)}) async-start(), calls=%async_computation.4 | async-start | bytes 3932160 | tf_op jit(solution)/shard_map/reduce_scatter | solution.py:698
  23.4 12.2 %collective-permute-start.5 = (bf16[4,96,256]{2,1,0:T(8,128)(2,1)S(1)}, bf16[4,96,256]{2,1,0:T(8,128)(2,1)S(1)}, u32[]{:S(2)}, u32[]{:S(2)}) collective-permute-start(bf16[4,96,256]{2,1,0:T(8,128)(2,1)S(1)} %get-tuple-element.208), channel_id=1, source_target_pairs={{0,8},{4,12},{8,16},{12,20},{16,24},{20,28},{24,0},{28,4},{32,40},... | collective-permute-start | bytes 589832 | tf_op jit(solution)/shard_map/ppermute | solution.py:479
  25.4 19.5 %collective-permute-start.4 = (bf16[4,96,256]{2,1,0:T(8,128)(2,1)S(1)}, bf16[4,96,256]{2,1,0:T(8,128)(2,1)S(1)}, u32[]{:S(2)}, u32[]{:S(2)}) collective-permute-start(bf16[4,96,256]{2,1,0:T(8,128)(2,1)S(1)} %get-tuple-element.208), channel_id=1, source_target_pairs={{0,16},{4,20},{8,24},{12,28},{16,0},{20,4},{24,8},{28,12},{32,48},... | collective-permute-start | bytes 589832 | tf_op jit(solution)/shard_map/ppermute | solution.py:479
  29.0 15.9 %collective-permute-start.3 = (bf16[4,96,256]{2,1,0:T(8,128)(2,1)S(1)}, bf16[4,96,256]{2,1,0:T(8,128)(2,1)S(1)}, u32[]{:S(2)}, u32[]{:S(2)}) collective-permute-start(bf16[4,96,256]{2,1,0:T(8,128)(2,1)S(1)} %get-tuple-element.208), channel_id=1, source_target_pairs={{0,24},{4,28},{8,0},{12,4},{16,8},{20,12},{24,16},{28,20},{32,56},... | collective-permute-start | bytes 589832 | tf_op jit(solution)/shard_map/ppermute | solution.py:479
  45.1 25.9 %collective-permute-start.7 = (bf16[256,1024]{1,0:T(8,128)(2,1)S(1)}, bf16[256,1024]{1,0:T(8,128)(2,1)S(1)}, u32[]{:S(2)}, u32[]{:S(2)}) collective-permute-start(bf16[256,1024]{1,0:T(8,128)(2,1)S(1)} %copy-done.8), channel_id=1, source_target_pairs={{0,3},{1,0},{2,1},{3,2},{4,7},{5,4},{6,5},{7,6},{8,11},{9,8},{10,9... | collective-permute-start | bytes 1572872 | tf_op jit(solution)/shard_map/ppermute | solution.py:494
  48.0 27.7 %collective-permute-start.8 = (bf16[256,1024]{1,0:T(8,128)(2,1)S(1)}, bf16[256,1024]{1,0:T(8,128)(2,1)S(1)}, u32[]{:S(2)}, u32[]{:S(2)}) collective-permute-start(bf16[256,1024]{1,0:T(8,128)(2,1)S(1)} %copy-done.8), channel_id=1, source_target_pairs={{0,2},{1,3},{2,0},{3,1},{4,6},{5,7},{6,4},{7,5},{8,10},{9,11},{10,... | collective-permute-start | bytes 1572872 | tf_op jit(solution)/shard_map/ppermute | solution.py:494
  48.8 31.8 %collective-permute-start.9 = (bf16[256,1024]{1,0:T(8,128)(2,1)S(1)}, bf16[256,1024]{1,0:T(8,128)(2,1)S(1)}, u32[]{:S(2)}, u32[]{:S(2)}) collective-permute-start(bf16[256,1024]{1,0:T(8,128)(2,1)S(1)} %copy-done.8), channel_id=1, source_target_pairs={{0,1},{1,2},{2,3},{3,0},{4,5},{5,6},{6,7},{7,4},{8,9},{9,10},{10,1... | collective-permute-start | bytes 1572872 | tf_op jit(solution)/shard_map/ppermute | solution.py:494
  90.4 20.3 %collective-permute-start.10 = (bf16[256,1024]{1,0:T(8,128)(2,1)}, bf16[256,1024]{1,0:T(8,128)(2,1)S(1)}, u32[]{:S(2)}, u32[]{:S(2)}) collective-permute-start(bf16[256,1024]{1,0:T(8,128)(2,1)} %get-tuple-element.119), channel_id=1, source_target_pairs={{0,1},{1,2},{2,3},{3,0},{4,5},{5,6},{6,7},{7,4},{8,9},{9,10},{10,1... | collective-permute-start | bytes 1572872 | tf_op jit(solution)/shard_map/ppermute | solution.py:494
  95.3 23.3 %collective-permute-start.11 = (bf16[256,1024]{1,0:T(8,128)(2,1)}, bf16[256,1024]{1,0:T(8,128)(2,1)S(1)}, u32[]{:S(2)}, u32[]{:S(2)}) collective-permute-start(bf16[256,1024]{1,0:T(8,128)(2,1)} %get-tuple-element.121), channel_id=1, source_target_pairs={{0,2},{1,3},{2,0},{3,1},{4,6},{5,7},{6,4},{7,5},{8,10},{9,11},{10,... | collective-permute-start | bytes 1572872 | tf_op jit(solution)/shard_map/ppermute | solution.py:494
  105.7 17.5 %collective-permute-start.12 = (bf16[256,1024]{1,0:T(8,128)(2,1)}, bf16[256,1024]{1,0:T(8,128)(2,1)S(1)}, u32[]{:S(2)}, u32[]{:S(2)}) collective-permute-start(bf16[256,1024]{1,0:T(8,128)(2,1)} %get-tuple-element.123), channel_id=1, source_target_pairs={{0,3},{1,0},{2,1},{3,2},{4,7},{5,4},{6,5},{7,6},{8,11},{9,8},{10,9... | collective-permute-start | bytes 1572872 | tf_op jit(solution)/shard_map/ppermute | solution.py:494
  127.3 10.6 %collective-permute-start.14 = (bf16[256,1024]{1,0:T(8,128)(2,1)}, bf16[256,1024]{1,0:T(8,128)(2,1)S(1)}, u32[]{:S(2)}, u32[]{:S(2)}) collective-permute-start(bf16[256,1024]{1,0:T(8,128)(2,1)} %get-tuple-element.125.h2), channel_id=1, source_target_pairs={{0,32},{4,12},{8,40},{12,20},{16,48},{20,28},{24,56},{28,4},{32,64... | collective-permute-start | bytes 1572872 | tf_op jit(solution)/shard_map/ppermute | solution.py:490
  127.3 10.7 %collective-permute-start.13 = (bf16[256,1024]{1,0:T(8,128)(2,1)}, bf16[256,1024]{1,0:T(8,128)(2,1)S(1)}, u32[]{:S(2)}, u32[]{:S(2)}) collective-permute-start(bf16[256,1024]{1,0:T(8,128)(2,1)} %get-tuple-element.125.h2), channel_id=1, source_target_pairs={{0,96},{4,28},{8,104},{12,4},{16,112},{20,12},{24,120},{28,20},{32... | collective-permute-start | bytes 1572872 | tf_op jit(solution)/shard_map/ppermute | solution.py:490
  145.9 26.1 %collective-permute-start.17 = (bf16[4,256,1024]{2,1,0:T(8,128)(2,1)S(1)}, bf16[4,256,1024]{2,1,0:T(8,128)(2,1)S(1)}, u32[]{:S(2)}, u32[]{:S(2)}) collective-permute-start(bf16[4,256,1024]{2,1,0:T(8,128)(2,1)S(1)} %pad_maximum_fusion.1.refs_1_), channel_id=1, source_target_pairs={{0,24},{4,100},{8,0},{12,108},{16,8},{20,116},{24,16},{28,124},{32... | collective-permute-start | bytes 6291464 | tf_op jit(solution)/shard_map/ppermute | solution.py:490
  146.0 28.3 %collective-permute-start.19 = (bf16[4,256,1024]{2,1,0:T(8,128)(2,1)S(1)}, bf16[4,256,1024]{2,1,0:T(8,128)(2,1)S(1)}, u32[]{:S(2)}, u32[]{:S(2)}) collective-permute-start(bf16[4,256,1024]{2,1,0:T(8,128)(2,1)S(1)} %pad_maximum_fusion.1.refs_1_), channel_id=1, source_target_pairs={{0,8},{4,36},{8,16},{12,44},{16,24},{20,52},{24,0},{28,60},{32,40}... | collective-permute-start | bytes 6291464 | tf_op jit(solution)/shard_map/ppermute | solution.py:490
  148.0 32.4 %collective-permute-start.21 = (bf16[1,1024,512]{2,1,0:T(8,128)(2,1)S(1)}, bf16[1,1024,512]{2,1,0:T(8,128)(2,1)}, u32[]{:S(2)}, u32[]{:S(2)}) collective-permute-start(bf16[1,1024,512]{2,1,0:T(8,128)(2,1)S(1)} %copy-done.4), channel_id=1, source_target_pairs={{0,4},{4,0},{8,12},{12,8},{16,20},{20,16},{24,28},{28,24},{32,36},... | collective-permute-start | bytes 3145736 | tf_op jit(solution)/shard_map/ppermute | solution.py:479
  148.0 32.4 %collective-permute-start.22 = (bf16[1,1024,512]{2,1,0:T(8,128)(2,1)S(1)}, bf16[1,1024,512]{2,1,0:T(8,128)(2,1)}, u32[]{:S(2)}, u32[]{:S(2)}) collective-permute-start(bf16[1,1024,512]{2,1,0:T(8,128)(2,1)S(1)} %copy-done.5), channel_id=1, source_target_pairs={{0,4},{4,0},{8,12},{12,8},{16,20},{20,16},{24,28},{28,24},{32,36},... | collective-permute-start | bytes 3145736 | tf_op jit(solution)/shard_map/ppermute | solution.py:479
  148.5 31.9 %collective-permute-start.23 = (bf16[1,512,1024]{2,1,0:T(8,128)(2,1)S(1)}, bf16[1,512,1024]{2,1,0:T(8,128)(2,1)}, u32[]{:S(2)}, u32[]{:S(2)}) collective-permute-start(bf16[1,512,1024]{2,1,0:T(8,128)(2,1)S(1)} %copy-done.6), channel_id=1, source_target_pairs={{0,4},{4,0},{8,12},{12,8},{16,20},{20,16},{24,28},{28,24},{32,36},... | collective-permute-start | bytes 3145736 | tf_op jit(solution)/shard_map/ppermute | solution.py:479
  173.1 56.1 %collective-permute-start.18 = (bf16[2,256,1024]{2,1,0:T(8,128)(2,1)}, bf16[2,256,1024]{2,1,0:T(8,128)(2,1)}, u32[]{:S(2)}, u32[]{:S(2)}) collective-permute-start(bf16[2,256,1024]{2,1,0:T(8,128)(2,1)} %slice.172), channel_id=1, source_target_pairs={{0,24},{4,100},{8,0},{12,108},{16,8},{20,116},{24,16},{28,124},{32... | collective-permute-start | bytes 3145736 | tf_op jit(solution)/shard_map/ppermute | solution.py:490
  176.8 52.5 %collective-permute-start.20 = (bf16[2,256,1024]{2,1,0:T(8,128)(2,1)}, bf16[2,256,1024]{2,1,0:T(8,128)(2,1)}, u32[]{:S(2)}, u32[]{:S(2)}) collective-permute-start(bf16[2,256,1024]{2,1,0:T(8,128)(2,1)} %slice.173), channel_id=1, source_target_pairs={{0,8},{4,36},{8,16},{12,44},{16,24},{20,52},{24,0},{28,60},{32,40}... | collective-permute-start | bytes 3145736 | tf_op jit(solution)/shard_map/ppermute | solution.py:490
  272.4 252.9 %reduce-scatter.3.cloned.1.call-start = ((), (), s32[]{:S(2)}) async-start(), calls=%async_computation.3 | async-start | bytes 8912896 | tf_op jit(solution)/shard_map/reduce_scatter | solution.py:738
  274.3 15.6 %collective-permute-start.28 = (bf16[2,272,1024]{2,1,0:T(8,128)(2,1)S(1)}, bf16[2,272,1024]{2,1,0:T(8,128)(2,1)S(1)}, u32[]{:S(2)}, u32[]{:S(2)}) collective-permute-start(bf16[2,272,1024]{2,1,0:T(8,128)(2,1)S(1)} %get-tuple-element.201), channel_id=1, source_target_pairs={{0,24},{4,100},{8,0},{12,108},{16,8},{20,116},{24,16},{28,124},{32... | collective-permute-start | bytes 3342344 | tf_op jit(solution)/shard_map/ppermute | solution.py:490
  276.8 17.2 %collective-permute-start.24 = (bf16[2,272,1024]{2,1,0:T(8,128)(2,1)S(1)}, bf16[2,272,1024]{2,1,0:T(8,128)(2,1)S(1)}, u32[]{:S(2)}, u32[]{:S(2)}) collective-permute-start(bf16[2,272,1024]{2,1,0:T(8,128)(2,1)S(1)} %get-tuple-element.202), channel_id=1, source_target_pairs={{0,8},{4,36},{8,16},{12,44},{16,24},{20,52},{24,0},{28,60},{32,40}... | collective-permute-start | bytes 3342344 | tf_op jit(solution)/shard_map/ppermute | solution.py:490
  276.9 28.6 %collective-permute-start.27 = (bf16[2,272,1024]{2,1,0:T(8,128)(2,1)S(1)}, bf16[2,272,1024]{2,1,0:T(8,128)(2,1)S(1)}, u32[]{:S(2)}, u32[]{:S(2)}) collective-permute-start(bf16[2,272,1024]{2,1,0:T(8,128)(2,1)S(1)} %slice.139), channel_id=1, source_target_pairs={{0,8},{4,36},{8,16},{12,44},{16,24},{20,52},{24,0},{28,60},{32,40}... | collective-permute-start | bytes 3342344 | tf_op jit(solution)/shard_map/ppermute | solution.py:490
  277.1 28.4 %collective-permute-start.26 = (bf16[2,272,1024]{2,1,0:T(8,128)(2,1)S(1)}, bf16[2,272,1024]{2,1,0:T(8,128)(2,1)S(1)}, u32[]{:S(2)}, u32[]{:S(2)}) collective-permute-start(bf16[2,272,1024]{2,1,0:T(8,128)(2,1)S(1)} %slice.135), channel_id=1, source_target_pairs={{0,24},{4,100},{8,0},{12,108},{16,8},{20,116},{24,16},{28,124},{32... | collective-permute-start | bytes 3342344 | tf_op jit(solution)/shard_map/ppermute | solution.py:490
  290.3 23.4 %collective-permute-start.29 = (bf16[2,272,1024]{2,1,0:T(8,128)(2,1)S(1)}, bf16[2,272,1024]{2,1,0:T(8,128)(2,1)S(1)}, u32[]{:S(2)}, u32[]{:S(2)}) collective-permute-start(bf16[2,272,1024]{2,1,0:T(8,128)(2,1)S(1)} %add_convert_fusion.1), channel_id=1, source_target_pairs={{0,24},{4,100},{8,0},{12,108},{16,8},{20,116},{24,16},{28,124},{32... | collective-permute-start | bytes 3342344 | tf_op jit(solution)/shard_map/ppermute | solution.py:490
  294.5 22.9 %collective-permute-start.25 = (bf16[2,272,1024]{2,1,0:T(8,128)(2,1)S(1)}, bf16[2,272,1024]{2,1,0:T(8,128)(2,1)S(1)}, u32[]{:S(2)}, u32[]{:S(2)}) collective-permute-start(bf16[2,272,1024]{2,1,0:T(8,128)(2,1)S(1)} %add_convert_fusion.3), channel_id=1, source_target_pairs={{0,8},{4,36},{8,16},{12,44},{16,24},{20,52},{24,0},{28,60},{32,40}... | collective-permute-start | bytes 3342344 | tf_op jit(solution)/shard_map/ppermute | solution.py:490
  322.4 12.5 %collective-permute-start.30 = (bf16[144,1024]{1,0:T(8,128)(2,1)S(1)}, bf16[144,1024]{1,0:T(8,128)(2,1)S(1)}, u32[]{:S(2)}, u32[]{:S(2)}) collective-permute-start(bf16[144,1024]{1,0:T(8,128)(2,1)S(1)} %get-tuple-element.206), channel_id=1, source_target_pairs={{0,32},{4,12},{8,40},{12,20},{16,48},{20,28},{24,56},{28,4},{32,64... | collective-permute-start | bytes 884744 | tf_op jit(solution)/shard_map/ppermute | solution.py:490
  329.2 20.5 %collective-permute-start.33 = (bf16[272,1024]{1,0:T(8,128)(2,1)S(1)}, bf16[272,1024]{1,0:T(8,128)(2,1)S(1)}, u32[]{:S(2)}, u32[]{:S(2)}) collective-permute-start(bf16[272,1024]{1,0:T(8,128)(2,1)S(1)} %pad_maximum_fusion.4), channel_id=1, source_target_pairs={{0,96},{4,28},{8,104},{12,4},{16,112},{20,12},{24,120},{28,20},{32... | collective-permute-start | bytes 1671176 | tf_op jit(solution)/shard_map/ppermute | solution.py:490
  335.0 19.6 %collective-permute-start.31 = (bf16[272,1024]{1,0:T(8,128)(2,1)S(1)}, bf16[272,1024]{1,0:T(8,128)(2,1)S(1)}, u32[]{:S(2)}, u32[]{:S(2)}) collective-permute-start(bf16[272,1024]{1,0:T(8,128)(2,1)S(1)} %pad_maximum_fusion.3), channel_id=1, source_target_pairs={{0,32},{4,12},{8,40},{12,20},{16,48},{20,28},{24,56},{28,4},{32,64... | collective-permute-start | bytes 1671176 | tf_op jit(solution)/shard_map/ppermute | solution.py:490
  359.8 21.6 %collective-permute-start.36 = (bf16[256,1024]{1,0:T(8,128)(2,1)}, bf16[256,1024]{1,0:T(8,128)(2,1)S(1)}, u32[]{:S(2)}, u32[]{:S(2)}) collective-permute-start(bf16[256,1024]{1,0:T(8,128)(2,1)} %get-tuple-element.151.refs_1_.refs_8_), channel_id=1, source_target_pairs={{0,3},{1,0},{2,1},{3,2},{4,7},{5,4},{6,5},{7,6},{8,11},{9,8},{10,9... | collective-permute-start | bytes 1572872 | tf_op jit(solution)/shard_map/ppermute | solution.py:494
  362.7 29.7 %collective-permute-start.35 = (bf16[256,1024]{1,0:T(8,128)(2,1)}, bf16[256,1024]{1,0:T(8,128)(2,1)S(1)}, u32[]{:S(2)}, u32[]{:S(2)}) collective-permute-start(bf16[256,1024]{1,0:T(8,128)(2,1)} %get-tuple-element.151.refs_1_.refs_8_), channel_id=1, source_target_pairs={{0,1},{1,2},{2,3},{3,0},{4,5},{5,6},{6,7},{7,4},{8,9},{9,10},{10,1... | collective-permute-start | bytes 1572872 | tf_op jit(solution)/shard_map/ppermute | solution.py:494
  362.7 40.8 %collective-permute-start.34 = (bf16[256,1024]{1,0:T(8,128)(2,1)}, bf16[256,1024]{1,0:T(8,128)(2,1)S(1)}, u32[]{:S(2)}, u32[]{:S(2)}) collective-permute-start(bf16[256,1024]{1,0:T(8,128)(2,1)} %get-tuple-element.151.refs_1_.refs_8_), channel_id=1, source_target_pairs={{0,2},{1,3},{2,0},{3,1},{4,6},{5,7},{6,4},{7,5},{8,10},{9,11},{10,... | collective-permute-start | bytes 1572872 | tf_op jit(solution)/shard_map/ppermute | solution.py:494
  437.7 18.4 %collective-permute-start.42 = (f32[3,1024]{1,0:T(4,128)S(1)}, f32[3,1024]{1,0:T(4,128)S(1)}, u32[]{:S(2)}, u32[]{:S(2)}) collective-permute-start(f32[3,1024]{1,0:T(4,128)S(1)} %select_maximum_fusion), channel_id=1, source_target_pairs={{0,3},{1,0},{2,1},{3,2},{4,7},{5,4},{6,5},{7,6},{8,11},{9,8},{10,9... | collective-permute-start | bytes 36872 | tf_op jit(solution)/shard_map/ppermute | solution.py:494
  441.2 17.0 %collective-permute-start.40 = (f32[3,1024]{1,0:T(4,128)S(1)}, f32[3,1024]{1,0:T(4,128)S(1)}, u32[]{:S(2)}, u32[]{:S(2)}) collective-permute-start(f32[3,1024]{1,0:T(4,128)S(1)} %select_maximum_fusion), channel_id=1, source_target_pairs={{0,1},{1,2},{2,3},{3,0},{4,5},{5,6},{6,7},{7,4},{8,9},{9,10},{10,1... | collective-permute-start | bytes 36872 | tf_op jit(solution)/shard_map/ppermute | solution.py:494
  441.2 17.0 %collective-permute-start.41 = (f32[3,1024]{1,0:T(4,128)S(1)}, f32[3,1024]{1,0:T(4,128)S(1)}, u32[]{:S(2)}, u32[]{:S(2)}) collective-permute-start(f32[3,1024]{1,0:T(4,128)S(1)} %select_maximum_fusion), channel_id=1, source_target_pairs={{0,2},{1,3},{2,0},{3,1},{4,6},{5,7},{6,4},{7,5},{8,10},{9,11},{10,... | collective-permute-start | bytes 36872 | tf_op jit(solution)/shard_map/ppermute | solution.py:494
  442.7 18.6 %collective-permute-start.52 = (f32[40,1024]{1,0:T(8,128)S(1)}, f32[40,1024]{1,0:T(8,128)S(1)}, u32[]{:S(2)}, u32[]{:S(2)}) collective-permute-start(f32[40,1024]{1,0:T(8,128)S(1)} %copy-done.33), channel_id=1, source_target_pairs={{0,3},{1,0},{2,1},{3,2},{4,7},{5,4},{6,5},{7,6},{8,11},{9,8},{10,9... | collective-permute-start | bytes 491528 | tf_op jit(solution)/shard_map/ppermute | solution.py:494
  444.4 19.2 %collective-permute-start.50 = (f32[40,1024]{1,0:T(8,128)S(1)}, f32[40,1024]{1,0:T(8,128)S(1)}, u32[]{:S(2)}, u32[]{:S(2)}) collective-permute-start(f32[40,1024]{1,0:T(8,128)S(1)} %copy-done.33), channel_id=1, source_target_pairs={{0,1},{1,2},{2,3},{3,0},{4,5},{5,6},{6,7},{7,4},{8,9},{9,10},{10,1... | collective-permute-start | bytes 491528 | tf_op jit(solution)/shard_map/ppermute | solution.py:494
  451.9 68.6 %all-to-all-start = ((bf16[32,32,768]{2,1,0:T(8,128)(2,1)}), bf16[32,32,768]{2,1,0:T(8,128)(2,1)S(1)}, u32[]{:S(2)}, u32[]{:S(2)}) async-start(bf16[32,32,768]{2,1,0:T(8,128)(2,1)} %bitcast.153), calls=%async_computation.1 | async-start | bytes 3145728 | tf_op jit(solution)/shard_map/all_to_all | solution.py:728
  458.2 18.4 %collective-permute-start.45 = (f32[3,1024]{1,0:T(4,128)S(1)}, f32[3,1024]{1,0:T(4,128)S(1)}, u32[]{:S(2)}, u32[]{:S(2)}) collective-permute-start(f32[3,1024]{1,0:T(4,128)S(1)} %add_add_fusion.5), channel_id=1, source_target_pairs={{0,96},{4,100},{8,104},{12,108},{16,112},{20,116},{24,120},{28,124... | collective-permute-start | bytes 36872 | tf_op jit(solution)/shard_map/ppermute | solution.py:479
  461.3 18.1 %collective-permute-start.43 = (f32[3,1024]{1,0:T(4,128)S(1)}, f32[3,1024]{1,0:T(4,128)S(1)}, u32[]{:S(2)}, u32[]{:S(2)}) collective-permute-start(f32[3,1024]{1,0:T(4,128)S(1)} %add_add_fusion.5), channel_id=1, source_target_pairs={{0,32},{4,36},{8,40},{12,44},{16,48},{20,52},{24,56},{28,60},{32,6... | collective-permute-start | bytes 36872 | tf_op jit(solution)/shard_map/ppermute | solution.py:479
  461.4 18.1 %collective-permute-start.44 = (f32[3,1024]{1,0:T(4,128)S(1)}, f32[3,1024]{1,0:T(4,128)S(1)}, u32[]{:S(2)}, u32[]{:S(2)}) collective-permute-start(f32[3,1024]{1,0:T(4,128)S(1)} %add_add_fusion.5), channel_id=1, source_target_pairs={{0,64},{4,68},{8,72},{12,76},{16,80},{20,84},{24,88},{28,92},{32,9... | collective-permute-start | bytes 36872 | tf_op jit(solution)/shard_map/ppermute | solution.py:479
  464.0 18.4 %collective-permute-start.55 = (f32[40,1024]{1,0:T(8,128)S(1)}, f32[40,1024]{1,0:T(8,128)S(1)}, u32[]{:S(2)}, u32[]{:S(2)}) collective-permute-start(f32[40,1024]{1,0:T(8,128)S(1)} %add_add_fusion.2), channel_id=1, source_target_pairs={{0,96},{4,100},{8,104},{12,108},{16,112},{20,116},{24,120},{28,124... | collective-permute-start | bytes 491528 | tf_op jit(solution)/shard_map/ppermute | solution.py:479
  467.1 17.5 %collective-permute-start.53 = (f32[40,1024]{1,0:T(8,128)S(1)}, f32[40,1024]{1,0:T(8,128)S(1)}, u32[]{:S(2)}, u32[]{:S(2)}) collective-permute-start(f32[40,1024]{1,0:T(8,128)S(1)} %add_add_fusion.2), channel_id=1, source_target_pairs={{0,32},{4,36},{8,40},{12,44},{16,48},{20,52},{24,56},{28,60},{32,6... | collective-permute-start | bytes 491528 | tf_op jit(solution)/shard_map/ppermute | solution.py:479
  487.9 10.2 %collective-permute-start.56 = (f32[40,1024]{1,0:T(8,128)S(1)}, f32[40,1024]{1,0:T(8,128)S(1)}, u32[]{:S(2)}, u32[]{:S(2)}) collective-permute-start(f32[40,1024]{1,0:T(8,128)S(1)} %add_add_fusion.1), channel_id=1, source_target_pairs={{0,8},{4,12},{8,16},{12,20},{16,24},{20,28},{24,0},{28,4},{32,40},... | collective-permute-start | bytes 491528 | tf_op jit(solution)/shard_map/ppermute | solution.py:479
  490.1 15.5 %collective-permute-start.37 = (bf16[256,1024]{1,0:T(8,128)(2,1)S(1)}, bf16[256,1024]{1,0:T(8,128)(2,1)S(1)}, u32[]{:S(2)}, u32[]{:S(2)}) collective-permute-start(bf16[256,1024]{1,0:T(8,128)(2,1)S(1)} %copy-done.39), channel_id=1, source_target_pairs={{0,1},{1,2},{2,3},{3,0},{4,5},{5,6},{6,7},{7,4},{8,9},{9,10},{10,1... | collective-permute-start | bytes 1572872 | tf_op jit(solution)/shard_map/ppermute | solution.py:494
  492.2 23.7 %collective-permute-start.38 = (bf16[256,1024]{1,0:T(8,128)(2,1)}, bf16[256,1024]{1,0:T(8,128)(2,1)S(1)}, u32[]{:S(2)}, u32[]{:S(2)}) collective-permute-start(bf16[256,1024]{1,0:T(8,128)(2,1)} %get-tuple-element.173), channel_id=1, source_target_pairs={{0,2},{1,3},{2,0},{3,1},{4,6},{5,7},{6,4},{7,5},{8,10},{9,11},{10,... | collective-permute-start | bytes 1572872 | tf_op jit(solution)/shard_map/ppermute | solution.py:494
  494.7 21.3 %collective-permute-start.39 = (bf16[256,1024]{1,0:T(8,128)(2,1)}, bf16[256,1024]{1,0:T(8,128)(2,1)S(1)}, u32[]{:S(2)}, u32[]{:S(2)}) collective-permute-start(bf16[256,1024]{1,0:T(8,128)(2,1)} %get-tuple-element.175), channel_id=1, source_target_pairs={{0,3},{1,0},{2,1},{3,2},{4,7},{5,4},{6,5},{7,6},{8,11},{9,8},{10,9... | collective-permute-start | bytes 1572872 | tf_op jit(solution)/shard_map/ppermute | solution.py:494
  (63 other events, 488.3 us)
Sparse Core Ops, SparseCore 0:
  12.6 81.1 all-gather.2
  272.6 38.7 reduce-scatter.4
  314.8 87.5 reduce-scatter.2

commit v2 on v1

v2 whole, which is shorter than its diff:
```python
from functools import partial

import jax
import jax.numpy as jnp
import numpy as np
from jax import lax
from jax.experimental import pallas as pl
from jax.experimental.pallas import tpu as pltpu
from jax.sharding import PartitionSpec as P

WIDTH = 1024
HDIM = 64
PITCH = 128
LEN = 1024
TOK = 256
CAP = 96
EXPERTS = 32
FF = 512
SIDE = 16
ROWS = TOK + SIDE
EPS = 1e-06
LOG2E = 1.4426950408889634
F32 = jnp.float32
BF16 = jnp.bfloat16


def nn(left, right):
    return lax.dot_general(left, right, (((1,), (0,)), ((), ())), preferred_element_type=F32)


def nt(left, right):
    return lax.dot_general(left, right, (((1,), (1,)), ((), ())), preferred_element_type=F32)


def tn(left, right):
    return lax.dot_general(left, right, (((0,), (0,)), ((), ())), preferred_element_type=F32)


def spread(heads):
    table = np.zeros((heads * HDIM, heads * PITCH), np.float32)
    for head in range(heads):
        for lane in range(HDIM):
            table[head * HDIM + lane, head * PITCH + lane] = 1.0
    return table


def rope_tables():
    places = np.arange(LEN, dtype=np.float64)
    inverse = 10000.0 ** (-2.0 * np.arange(HDIM // 2, dtype=np.float64) / HDIM)
    angles = places[:, None] * inverse[None, :]
    cos_tab = np.zeros((LEN, PITCH), np.float32)
    sin_tab = np.zeros((LEN, PITCH), np.float32)
    cos_tab[:, : HDIM // 2] = np.cos(angles)
    cos_tab[:, HDIM // 2 : HDIM] = np.cos(angles)
    sin_tab[:, : HDIM // 2] = -np.sin(angles)
    sin_tab[:, HDIM // 2 : HDIM] = np.sin(angles)
    return cos_tab.reshape(LEN // TOK, TOK, PITCH), sin_tab.reshape(LEN // TOK, TOK, PITCH)


def lanes(shape):
    return lax.broadcasted_iota(jnp.int32, shape, 1)


def swap_halves(tensor):
    half = HDIM // 2
    ahead = pltpu.roll(tensor, PITCH - half, 1)
    behind = pltpu.roll(tensor, half, 1)
    return jnp.where(lanes(tensor.shape) < half, ahead, behind)


def head_scale(tensor):
    return lax.rsqrt(jnp.sum(tensor * tensor, axis=1, keepdims=True) * (1.0 / HDIM) + EPS)


def row_scale(tensor):
    return lax.rsqrt(jnp.mean(tensor * tensor, axis=1, keepdims=True) + EPS)


def call(body, out_shape, args, scalars=None, any_in=(), any_out=(), scratch=(), aliases=None, near=(), local=(), mb=24, lazy=False):
    scratch, aliases = list(scratch), aliases or {}
    offset = 0 if scalars is None else 1
    count = offset + len(args)
    fetched = [i for i in range(len(args)) if i not in any_in and i not in local]
    stored = [i for i in range(len(out_shape)) if i not in any_out and i not in near]
    holds = [pltpu.VMEM(args[i].shape, args[i].dtype) for i in fetched]
    holds += [pltpu.VMEM(*out_shape[i]) for i in stored]
    scratch = [*scratch, *holds, pltpu.SemaphoreType.DMA((max(1, len(holds)),))]

    def kernel(*refs):
        refs = list(refs)
        own, sems = refs[len(refs) - len(holds) - 1 : -1], refs[-1]
        refs = refs[: len(refs) - len(holds) - 1]
        copies = {}
        for n, i in enumerate(fetched):
            copies[i] = pltpu.make_async_copy(refs[i + offset], own[n], sems.at[n])
            copies[i].start()
            refs[i + offset] = own[n]
        stores = []
        for n, i in enumerate(stored, len(fetched)):
            stores.append(pltpu.make_async_copy(own[n], refs[i + count], sems.at[n]))
            refs[i + count] = own[n]
        if lazy:
            body(*refs, wait=lambda *which: [copies.pop(i).wait() for i in which])
        else:
            for one in copies.values():
                one.wait()
            body(*refs)
        for one in stores:
            one.start()
        for one in stores:
            one.wait()

    def placed(i, one):
        if i in any_in and i not in aliases:
            return one
        return pltpu.with_memory_space_constraint(one, pltpu.VMEM if i in local else pltpu.HBM)

    def space(i):
        return pltpu.VMEM if i in local else pl.ANY if i in any_in and i not in aliases else pltpu.HBM

    args = [placed(i, one) for i, one in enumerate(args)]
    in_specs = [pl.BlockSpec(memory_space=space(i)) for i in range(len(args))]
    out_specs = [pl.BlockSpec(memory_space=pltpu.VMEM if i in near else pltpu.HBM) for i in range(len(out_shape))]
    shapes = [pltpu.VMEM(s, d) if i in near else pltpu.HBM(s, d) for i, (s, d) in enumerate(out_shape)]
    if scalars is not None:
        in_specs = [pl.BlockSpec(memory_space=pltpu.SMEM)] + in_specs
        args = [scalars] + args
    return pl.pallas_call(
        kernel,
        out_shape=shapes,
        in_specs=in_specs,
        out_specs=out_specs,
        scratch_shapes=scratch,
        input_output_aliases={i + offset: o for i, o in aliases.items()},
        compiler_params=pltpu.CompilerParams(vmem_limit_bytes=mb * 1024 * 1024),
        cost_estimate=pl.CostEstimate(flops=1, bytes_accessed=1, transcendentals=0),
    )(*args)


def start_body(sc, cot, routes, packed, ranks_out):
    base = sc[0] * TOK
    length = sc[1]
    place = base + lax.broadcasted_iota(jnp.int32, (TOK, 1), 0)
    keep = jnp.where(place < length, 1.0, 0.0)
    packed[0:TOK, :] = (cot[...].astype(F32) * keep).astype(BF16)
    names = lax.broadcasted_iota(jnp.int32, (TOK, EXPERTS), 1)
    member = jnp.zeros((TOK, EXPERTS), F32)
    for k in range(routes.shape[1]):
        member = member + jnp.where(routes[:, k : k + 1] == names, 1.0, 0.0)
    member = member.astype(BF16)
    earlier = lax.broadcasted_iota(jnp.int32, (TOK, TOK), 0)
    later = lax.broadcasted_iota(jnp.int32, (TOK, TOK), 1)
    before = jnp.where(earlier < later, 1.0, 0.0).astype(BF16)
    same = jnp.where(earlier == later, 1.0, 0.0).astype(BF16)
    counts = tn(member, before)
    chosen = tn(member, same)
    ranks = jnp.where(chosen > 0.5, counts, -1.0)
    ranks_out[...] = ranks
    quarter = EXPERTS // 4
    rows = jnp.concatenate([ranks[q * quarter : (q + 1) * quarter] for q in range(4)], axis=1)
    packed[TOK:ROWS, :] = jnp.concatenate([rows, jnp.zeros_like(rows)], axis=0).astype(BF16)


def project_body(sc, own, other, x0, x1, x2, x3, gain, head_gain, cos, sin, spread4, spread2, *refs, wait):
    wait(0, 1)
    outs, raws, pairs, queries, ka, va, out_w, turns = (
        refs[:2], refs[2:6], refs[6:10], refs[10:14], refs[14], refs[15], refs[16], refs[17:21]
    )
    h1, raw_hold, pair_hold, proj, held, sems = refs[21:]
    y_at, z_at, core, mp_at, length = sc[0], sc[1], sc[2], sc[3], sc[4]
    for block in range(16):
        y_rel = (block // 4 - y_at + 4) % 4
        z_rel = (block % 4 - z_at + 4) % 4
        for side in range(2):
            rel = z_rel * 4 + y_rel if side == 0 else y_rel * 4 + z_rel
            part = jnp.where(core == side, own[rel].astype(F32), other[rel].astype(F32)).astype(BF16)
            at = (2 * block + side) * 32
            for piece in range(3):
                held[at : at + 32, piece * 256 : (piece + 1) * 256] = part[piece * 32 : (piece + 1) * 32]
    wait(10, 11)
    proj[:, 0:512] = nn(held[:, 0:256], spread4[...]).astype(BF16)
    proj[:, 512:768] = nn(held[:, 256:384], spread2[...]).astype(BF16)
    proj[:, 768:1024] = nn(held[:, 384:512], spread2[...]).astype(BF16)
    out_w[...] = nn(held[:, 512:768], spread4[...]).astype(BF16)
    copies = [pltpu.make_async_copy(proj, outs[1], sems.at[12])]
    copies[0].start()
    lane = lanes((TOK, PITCH))
    below = lax.broadcasted_iota(jnp.int32, (TOK, PITCH), 0)
    q_aug = jnp.where(lane == HDIM, 1.0, 0.0)
    v_aug = jnp.where(lane < HDIM + 2, 1.0, 0.0)
    for chunk, x in enumerate((x0, x1, x2, x3)):
        rows = slice(chunk * TOK, (chunk + 1) * TOK)
        at = (mp_at + chunk) % 4
        wait(*((2, 6, 7, 8, 9) if chunk == 0 else (2 + chunk,)))
        xf = x[...].astype(F32)
        normed = (xf * row_scale(xf) * gain[...]).astype(BF16)
        h1[rows, :] = normed
        raw = nn(normed, proj[...])
        raw_hold[rows, :] = raw[:, 0:512]
        pair_hold[rows, :] = raw[:, 512:768]
        cos_t = cos[at]
        sin_t = sin[at]
        turns[chunk][...] = jnp.where(lane < HDIM, cos_t, pltpu.roll(sin_t, HDIM, 1))
        bias = jnp.where(at * TOK + below < length, 0.0, -1e30)
        k_aug = jnp.where(lane == HDIM, bias, jnp.where(lane < HDIM + 4, 1.0, 0.0))
        for head in range(6):
            cols = slice(head * PITCH, (head + 1) * PITCH)
            one = raw[:, cols]
            ready = one * head_scale(one) * head_gain[:, cols]
            turned = ready * cos_t + swap_halves(ready) * sin_t
            if head < 4:
                queries[chunk][:, cols] = jnp.where(lane < HDIM, turned, q_aug).astype(BF16)
            else:
                here = slice((head - 4) * PITCH, (head - 3) * PITCH)
                ka[rows, here] = jnp.where(lane < HDIM, turned, k_aug).astype(BF16)
        for head in range(2):
            va[rows, head * PITCH : (head + 1) * PITCH] = jnp.where(
                lane < HDIM, raw[:, 768 + head * PITCH : 768 + (head + 1) * PITCH], v_aug
            ).astype(BF16)
        here = pl.ds(chunk * TOK, TOK)
        for index, (hold, target) in enumerate(
            ((h1, outs[0].at[here]), (raw_hold, raws[chunk]), (pair_hold, pairs[chunk]))
        ):
            one = pltpu.make_async_copy(hold.at[here], target, sems.at[chunk * 3 + index])
            one.start()
            copies.append(one)
    for one in copies:
        one.wait()


def turn_tables(turn):
    lane = lanes(turn.shape)
    return jnp.where(lane < HDIM, turn, 0.0), jnp.where(lane < HDIM, pltpu.roll(turn, HDIM, 1), 0.0)


def attend_body(qa, ka, va, out_w, branch, mixed, qb):
    lane = lanes((TOK, PITCH))
    for head in range(4):
        cols = slice(head * PITCH, (head + 1) * PITCH)
        kv = slice((head // 2) * PITCH, (head // 2 + 1) * PITCH)
        query = qa[:, cols]
        weight = jnp.exp2(nt(query, ka[:, kv]) * (LOG2E / 8.0)).astype(BF16)
        total = nn(weight, va[:, kv])
        denom = total[:, HDIM : HDIM + 1]
        mixed[:, cols] = jnp.where(lane < HDIM, total / denom, 0.0).astype(BF16)
        level = jnp.log(denom) * -8.0
        high = level.astype(BF16).astype(F32)
        middle = (level - high).astype(BF16).astype(F32)
        low = level - high - middle
        stats = jnp.where(lane == HDIM + 1, high, jnp.where(lane == HDIM + 2, middle, low))
        qb[:, cols] = jnp.where(
            (lane > HDIM) & (lane < HDIM + 4), stats, query.astype(F32)
        ).astype(BF16)
    branch[...] = nt(mixed[...], out_w[...]).astype(BF16)


def middle_body(x, p0, p1, p2, p3, gain, x_mid, h2):
    total = (
        x[...].astype(F32)
        + ((p0[...].astype(F32) + p1[...].astype(F32)) + (p2[...].astype(F32) + p3[...].astype(F32)))
    )
    x_mid[...] = total
    h2[...] = (total * row_scale(total) * gain[...]).astype(BF16)


def gates_of(logits, ranks):
    routed = ranks >= 0.0
    masked = jnp.where(routed, logits, -1e30)
    weight = jnp.where(routed, jnp.exp(masked - jnp.max(masked, axis=0, keepdims=True)), 0.0)
    return weight / jnp.sum(weight, axis=0, keepdims=True)


def gates_body(h2, router, ranks, gates):
    gates[...] = gates_of(nt(router[...], h2[...]), ranks[...])


def unfold(rows):
    return jnp.concatenate([rows[:, q * TOK : (q + 1) * TOK] for q in range(4)], axis=0)


def experts_body(pieces, unit, *refs):
    sc = refs[0]
    tokens = refs[1 : 1 + len(pieces)]
    at = 1 + len(pieces)
    cot_all, router = refs[at], refs[at + 1]
    weights_in = refs[at + 2 : at + 8]
    at = at + 8
    if unit > 0:
        at = at + 6
    y_out, back_a, back_b, taken_all, push_all, hidden_all, gate_all, up_all = refs[at : at + 8]
    (tok, cot, gate_v, up_v, down_v, y_hold, y_back, t_hold, e_hold, h_hold, g_hold, u_hold, sems) = refs[at + 8 :]
    cot_in = [pltpu.make_async_copy(cot_all.at[sc[i]], cot.at[i], sems.at[i]) for i in range(4)]
    tok_in = []
    for index, count in enumerate(pieces):
        for j in range(count):
            i = len(tok_in)
            tok_in.append(pltpu.make_async_copy(tokens[index].at[j], tok.at[i], sems.at[4 + i]))
    weight_in = []
    for e in range(2):
        for j, hold in enumerate((gate_v, up_v, down_v)):
            weight_in.append(
                pltpu.make_async_copy(weights_in[3 * e + j].at[0], hold.at[e], sems.at[8 + 3 * e + j])
            )
    for one in cot_in + tok_in + weight_in:
        one.start()
    own_names = (sc[4], sc[5])
    names = lax.broadcasted_iota(jnp.int32, (EXPERTS, TOK), 0)
    slots = lax.broadcasted_iota(jnp.int32, (CAP, TOK), 0).astype(F32)
    picks = [[], []]
    gate_rows = [[], []]
    for i in range(4):
        cot_in[i].wait()
        tok_in[i].wait()
        block = tok[i]
        ranks = unfold(cot[i, TOK : TOK + EXPERTS // 4, :].astype(F32))
        gates = gates_of(nt(router[...], block), ranks)
        for e in range(2):
            hit = names == own_names[e]
            rank = jnp.sum(jnp.where(hit, ranks, 0.0), axis=0, keepdims=True)
            gate = jnp.sum(jnp.where(hit, gates, 0.0), axis=0, keepdims=True)
            pick = jnp.where(slots == rank, 1.0, 0.0)
            picks[e].append(pick.astype(BF16))
            gate_rows[e].append(jnp.sum(pick * gate, axis=1, keepdims=True))
    taken_rows = [nn(jnp.concatenate([picks[0][i], picks[1][i]], axis=0), tok[i]) for i in range(4)]
    grad_rows_all = [
        nn(jnp.concatenate([picks[0][i], picks[1][i]], axis=0), cot[i, 0:TOK, :]) for i in range(4)
    ]
    marks = [[], []]
    back_parts = []
    out_parts = []
    copies_out = []

    def put(source, target, sem):
        one = pltpu.make_async_copy(source, target, sems.at[sem])
        one.start()
        copies_out.append(one)

    for e in range(2):
        half = slice(e * CAP, (e + 1) * CAP)
        here = pl.ds(unit * 4 * CAP, 4 * CAP)
        for i in range(4):
            t_hold[e, i * CAP : (i + 1) * CAP, :] = taken_rows[i][half].astype(BF16)
        put(t_hold.at[e], taken_all.at[e, here], 14 + 5 * e)
        taken = t_hold[e]
        for one in weight_in[3 * e : 3 * e + 2]:
            one.wait()
        gate_act = nn(taken, gate_v[e])
        up_act = nn(taken, up_v[e])
        sigma = jax.nn.sigmoid(gate_act)
        silu = gate_act * sigma
        hidden = (silu * up_act).astype(BF16)
        h_hold[e] = hidden
        put(h_hold.at[e], hidden_all.at[e, here], 15 + 5 * e)
        weight_in[3 * e + 2].wait()
        result = nn(hidden, down_v[e]).astype(BF16).astype(F32)
        gate_col = jnp.concatenate(gate_rows[e], axis=0)
        grad_rows = jnp.concatenate([grad_rows_all[i][half] for i in range(4)], axis=0)
        mark = jnp.sum(grad_rows * result, axis=1, keepdims=True)
        for i in range(4):
            marks[e].append(
                jnp.sum(picks[e][i].astype(F32) * mark[i * CAP : (i + 1) * CAP], axis=0, keepdims=True)
            )
        out_parts.append((result * gate_col).astype(BF16))
        push = (grad_rows * gate_col).astype(BF16)
        e_hold[e] = push
        put(e_hold.at[e], push_all.at[e, here], 16 + 5 * e)
        grad_hidden = nt(push, down_v[e])
        grad_gate = (grad_hidden * up_act * (sigma * (1.0 + gate_act * (1.0 - sigma)))).astype(BF16)
        grad_up = (grad_hidden * silu).astype(BF16)
        g_hold[e] = grad_gate
        u_hold[e] = grad_up
        put(g_hold.at[e], gate_all.at[e, here], 17 + 5 * e)
        put(u_hold.at[e], up_all.at[e, here], 18 + 5 * e)
        back_parts.append((nt(grad_gate, gate_v[e]) + nt(grad_up, up_v[e])).astype(BF16))
    for i in range(4):
        pick = jnp.concatenate([picks[0][i], picks[1][i]], axis=0)
        rows = slice(i * CAP, (i + 1) * CAP)
        y_back[i, 0:TOK, :] = tn(
            pick, jnp.concatenate([back_parts[0][rows], back_parts[1][rows]], axis=0)
        ).astype(BF16)
        mark = jnp.where(names == own_names[0], marks[0][i], 0.0) + jnp.where(
            names == own_names[1], marks[1][i], 0.0
        )
        high = mark.astype(BF16).astype(F32)
        low = mark - high
        quarter = EXPERTS // 4
        fold = [
            jnp.concatenate([part[q * quarter : (q + 1) * quarter] for q in range(4)], axis=1)
            for part in (high, low)
        ]
        y_back[i, TOK:ROWS, :] = jnp.concatenate(fold, axis=0).astype(BF16)
        put(y_back.at[i], (back_a if i < 2 else back_b).at[i % 2], 24 + i)
    for i in range(4):
        pick = jnp.concatenate([picks[0][i], picks[1][i]], axis=0)
        rows = slice(i * CAP, (i + 1) * CAP)
        y_hold[i] = tn(pick, jnp.concatenate([out_parts[0][rows], out_parts[1][rows]], axis=0)).astype(BF16)
        put(y_hold.at[i], y_out.at[sc[i]], 28 + i)
    for one in copies_out:
        one.wait()


def expert_weights_body(joined, sc, taken, push, hidden, gate, up, *refs):
    got, refs = (refs[:3], refs[3:]) if joined else ((), refs)
    outs, (gate_sum, up_sum, down_sum) = refs[:-3], refs[-3:]
    step = pl.program_id(0)

    @pl.when(step == 0)
    def _():
        gate_sum[...] = tn(taken[0], gate[0])
        up_sum[...] = tn(taken[0], up[0])
        down_sum[...] = tn(hidden[0], push[0])

    @pl.when(step > 0)
    def _():
        gate_sum[...] += tn(taken[0], gate[0])
        up_sum[...] += tn(taken[0], up[0])
        down_sum[...] += tn(hidden[0], push[0])

    @pl.when(step == pl.num_programs(0) - 1)
    def _():
        if not joined:
            for target, total in zip(outs, (gate_sum, up_sum, down_sum)):
                target[...] = total[...].astype(BF16)
            return
        for part in range(4):
            at = (sc[0] + part) % 4
            out = outs[part]
            rows = pl.ds(pl.multiple_of(at * 256, 256), 256)
            out[0:256, :] = (gate_sum[rows, :] + got[0][rows, :].astype(F32)).astype(BF16)
            out[256:512, :] = (up_sum[rows, :] + got[1][rows, :].astype(F32)).astype(BF16)
            rows = pl.ds(pl.multiple_of(at * 128, 128), 128)
            down = (down_sum[rows, :] + got[2][rows, :].astype(F32)).astype(BF16)
            out[512:640, :] = down[:, 0:FF]
            out[640:768, :] = down[:, FF:WIDTH]


def expert_weights(saved, expert, mp_at, got=()):
    widths = [one.shape[2] for one in saved]
    saved = [pltpu.with_memory_space_constraint(one, pltpu.HBM) for one in saved]
    got = [pltpu.with_memory_space_constraint(one, pltpu.VMEM) for one in got]
    rows = 4 * CAP
    shapes = [((768, FF), BF16)] * 4 if got else [((WIDTH, FF), BF16), ((WIDTH, FF), BF16), ((FF, WIDTH), BF16)]
    return pl.pallas_call(
        partial(expert_weights_body, bool(got)),
        out_shape=[jax.ShapeDtypeStruct(s, d) for s, d in shapes],
        grid=(4,),
        in_specs=[pl.BlockSpec(memory_space=pltpu.SMEM)]
        + [pl.BlockSpec((1, rows, w), lambda step: (expert, step, 0)) for w in widths]
        + [pl.BlockSpec(memory_space=pltpu.VMEM) for _ in got],
        out_specs=[pl.BlockSpec(memory_space=pltpu.VMEM) for _ in shapes],
        scratch_shapes=[pltpu.VMEM((WIDTH, FF), F32), pltpu.VMEM((WIDTH, FF), F32), pltpu.VMEM((FF, WIDTH), F32)],
        compiler_params=pltpu.CompilerParams(vmem_limit_bytes=40 * 1024 * 1024),
        cost_estimate=pl.CostEstimate(flops=1, bytes_accessed=1, transcendentals=0),
    )(mp_at.reshape(1), *saved, *got)


def token_back_body(r0, r1, r2, h2, x_mid, ranks, gates, router, gain, packed, grad_mid, branch, small):
    total = r0[...].astype(F32) + (r1[...].astype(F32) + r2[...].astype(F32))
    marks = unfold(total[TOK : TOK + 8]) + unfold(total[TOK + 8 : TOK + 16])
    gate = gates[...]
    centre = jnp.sum(gate * marks, axis=0, keepdims=True)
    grad_logits = jnp.where(ranks[...] >= 0.0, gate * (marks - centre), 0.0).astype(BF16)
    small[0:EXPERTS, :] = nn(grad_logits, h2[...])
    grad_h2 = total[0:TOK] + tn(grad_logits, router[...])
    x = x_mid[...]
    scale = row_scale(x)
    normed = x * scale
    grad_normed = grad_h2 * gain[...]
    small[EXPERTS : EXPERTS + 8, :] = jnp.broadcast_to(
        jnp.sum(grad_h2 * normed, axis=0, keepdims=True), (8, WIDTH)
    )
    out = packed[0:TOK, :].astype(F32) + scale * (
        grad_normed - normed * jnp.mean(grad_normed * normed, axis=1, keepdims=True)
    )
    grad_mid[...] = out
    branch[...] = out.astype(BF16)


def head_back(grad, raw, gain, cos_t, sin_t):
    upstream = grad * cos_t - swap_halves(grad) * sin_t
    scale = head_scale(raw)
    normed = raw * scale
    grad_normed = upstream * gain
    gain_grad = jnp.sum(upstream * normed, axis=0, keepdims=True)
    inner = jnp.sum(grad_normed * normed, axis=1, keepdims=True) * (1.0 / HDIM)
    return scale * (grad_normed - normed * inner), gain_grad


def attend_back_body(first, *refs, wait):
    rows, out_w, qb, mixed, ka, va, raw, head_gain, turn, spread4 = refs[:10]
    rest = refs[10:] if first else refs[11:]
    grad_query, gain_out, slim, both_out, both, sems = rest
    loads = []
    if not first:
        loads = [pltpu.make_async_copy(refs[10].at[g], both.at[g], sems.at[g]) for g in range(2)]
        for one in loads:
            one.start()
    stores = [pltpu.make_async_copy(both.at[g], both_out.at[g], sems.at[2 + g]) for g in range(2)]
    lane = lanes((TOK, PITCH))
    pushed = nn(rows[...], out_w[...]).astype(BF16)
    gain_total = jnp.zeros((1, PITCH), F32)
    wait(2, 3)
    for head in range(4):
        cols = slice(head * PITCH, (head + 1) * PITCH)
        group = head // 2
        kv = slice(group * PITCH, (group + 1) * PITCH)
        grad = pushed[:, cols]
        grad_f = grad.astype(F32)
        delta = -jnp.sum(grad_f * mixed[:, cols].astype(F32), axis=1, keepdims=True)
        high = delta.astype(BF16).astype(F32)
        grad_aug = jnp.where(
            lane == HDIM, high, jnp.where(lane == HDIM + 1, delta - high, grad_f)
        ).astype(BF16)
        query = qb[:, cols]
        probs = jnp.exp2(nt(ka[:, kv], query) * (LOG2E / 8.0))
        inner = nt(va[:, kv], grad_aug)
        grad_scores = (probs * inner).astype(BF16)
        add_k = nn(grad_scores, query)
        add_v = nn(probs.astype(BF16), grad)
        if head % 2 == 0 and first:
            both[group, :, 0:PITCH] = add_k
            both[group, :, PITCH : 2 * PITCH] = add_v
        else:
            if head % 2 == 0:
                loads[group].wait()
            both[group, :, 0:PITCH] += add_k
            both[group, :, PITCH : 2 * PITCH] += add_v
        if head % 2 == 1:
            stores[group].start()
        grad_q = jnp.where(lane < HDIM, tn(grad_scores, ka[:, kv]) * 0.125, 0.0)
        if head == 0:
            wait(6, 7, 8)
            cos_t, sin_t = turn_tables(turn[...])
        back, gain_grad = head_back(grad_q, raw[:, cols], head_gain[:, cols], cos_t, sin_t)
        grad_query[:, cols] = back.astype(BF16)
        gain_total = gain_total + gain_grad
    wait(9)
    slim[...] = nt(grad_query[...], spread4[...]).astype(BF16)
    gain_out[...] = jnp.broadcast_to(gain_total, (8, PITCH))
    for one in stores:
        one.wait()


def keys_back_body(*refs, wait):
    both, raws, turns, head_gain, query, proj, x = refs[0], refs[1:5], refs[5:9], refs[9], refs[10], refs[11], refs[12]
    far_up, far_down, wide, gains = refs[13:]
    half = TOK // 2
    lane = lanes((TOK, PITCH))
    key_gain = jnp.zeros((1, PITCH), F32)
    wait(0, 9)
    for chunk in (2, 0, 1, 3):
        wait(1 + chunk, 5 + chunk)
        at = slice(chunk * TOK, (chunk + 1) * TOK)
        cos_t, sin_t = turn_tables(turns[chunk][...])
        for head in range(2):
            cols = slice(head * PITCH, (head + 1) * PITCH)
            grad = jnp.where(lane < HDIM, both[head, at, 0:PITCH] * 0.125, 0.0)
            back, gain_grad = head_back(
                grad, raws[chunk][:, cols], head_gain[:, 512 + head * PITCH : 640 + head * PITCH], cos_t, sin_t
            )
            wide[at, cols] = back.astype(BF16)
            key_gain = key_gain + gain_grad
            wide[at, 256 + head * PITCH : 384 + head * PITCH] = jnp.where(
                lane < HDIM, both[head, at, PITCH : 2 * PITCH], 0.0
            ).astype(BF16)
    wait(10, 11, 12)
    part = nt(query[...], proj[:, 0:512]) + nt(wide[2 * TOK : 3 * TOK, :], proj[:, 512:1024])
    far_up[...] = part[:half].astype(BF16)
    far_down[...] = part[half:].astype(BF16)
    xf = x[...].astype(F32)
    gains[...] = jnp.zeros((8, WIDTH), F32)
    gains[0:1, :] = jnp.sum(part * (xf * row_scale(xf)), axis=0, keepdims=True)
    gains[1:2, 0:PITCH] = key_gain


def tail_body(*refs, wait):
    sc, refs = refs[0], refs[1:]
    wide, gains_in, small, spread2, spread4 = refs[0:5]
    queries, proj, xs, rows, mixed, h1, slims, query_gains = (
        refs[5:8], refs[8], refs[9:12], refs[12:16], refs[16:20], refs[20], refs[21:25], refs[25:29]
    )
    p1, p3, p0, keep, send, extra = refs[29:35]
    (slim_pair,) = refs[35:]
    y_at, z_at, core = sc[0], sc[1], sc[2]
    total = gains_in[0:1, :]
    wait(8)
    for n, (chunk, target) in enumerate(((1, p1), (3, p3), (0, p0))):
        wait(5 + n, 9 + n)
        at = slice(chunk * TOK, (chunk + 1) * TOK)
        part = nt(queries[n][...], proj[:, 0:512]) + nt(wide[at, :], proj[:, 512:1024])
        target[...] = part.astype(BF16)
        xf = xs[n][...].astype(F32)
        total = total + jnp.sum(part * (xf * row_scale(xf)), axis=0, keepdims=True)
    wait(2, 25, 26, 27, 28)
    query_gain = (query_gains[0][0:1, :] + query_gains[1][0:1, :]) + (
        query_gains[2][0:1, :] + query_gains[3][0:1, :]
    )
    extra[...] = jnp.zeros((56, 768), F32)
    extra[0:1, :] = total[:, 0:768]
    extra[1:2, 0:256] = total[:, 768:1024]
    extra[1:2, 256:384] = query_gain
    extra[1:2, 384:512] = gains_in[1:2, 0:PITCH]
    extra[8:56, :] = small[...]
    send[16] = split3(extra[0:4, :])
    send[17] = small[0:32, :].astype(BF16)
    send[18, 0:16, :] = small[32:48, :].astype(BF16)
    send[18, 16:32, :] = jnp.zeros((16, 768), BF16)
    wait(3, 4)
    slim_pair[:, 0:128] = nt(wide[:, 0:256], spread2[...]).astype(BF16)
    slim_pair[:, 128:256] = nt(wide[:, 256:512], spread2[...]).astype(BF16)
    wait(20)
    pair_rows = tn(h1[...], slim_pair[...]).astype(BF16)
    query_total = jnp.zeros((WIDTH, 256), F32)
    out_total = jnp.zeros((WIDTH, 256), F32)
    for chunk in range(4):
        wait(12 + chunk, 16 + chunk, 21 + chunk)
        at = slice(chunk * TOK, (chunk + 1) * TOK)
        query_total = query_total + tn(h1[at, :], slims[chunk][...])
        out_total = out_total + tn(rows[chunk][...], nt(mixed[chunk][...], spread4[...]).astype(BF16))
    query_rows, out_rows = query_total.astype(BF16), out_total.astype(BF16)
    for block in range(16):
        y_rel = (block // 4 - y_at + 4) % 4
        z_rel = (block % 4 - z_at + 4) % 4
        for side in range(2):
            at = (2 * block + side) * 32
            rel = y_rel * 4 + z_rel if side == 0 else z_rel * 4 + y_rel

            def put(target):
                target[rel, :, 0:256] = query_rows[at : at + 32]
                target[rel, :, 256:512] = pair_rows[at : at + 32]
                target[rel, :, 512:768] = out_rows[at : at + 32]

            pl.when(core == side)(partial(put, keep))
            pl.when(core != side)(partial(put, send))


def near_body(p1, p3, far_up, far_down, out1, out3):
    half = TOK // 2
    out1[:half, :] = (p1[:half, :].astype(F32) + far_up[...].astype(F32)).astype(BF16)
    out1[half:, :] = p1[half:, :]
    out3[:half, :] = p3[:half, :]
    out3[half:, :] = (p3[half:, :].astype(F32) + far_down[...].astype(F32)).astype(BF16)


def split3(value):
    high = value.astype(BF16).astype(F32)
    middle = (value - high).astype(BF16).astype(F32)
    low = value - high - middle
    return jnp.concatenate([high, middle, low, jnp.zeros((20, 768), F32)], axis=0).astype(BF16)


def join3(rows):
    value = rows.astype(F32)
    return value[0:4] + value[4:8] + value[8:12]


def ride_first_body(keep, got, extra, *outs):
    gain = split3(extra[0:4, :] + join3(got[16]))
    router = jnp.concatenate(
        [extra[8:40, :] + got[17].astype(F32), extra[40:56, :] + got[18, 0:16, :].astype(F32)], axis=0
    ).astype(BF16)
    for first in range(4):
        for second in range(4):
            at = first * 4 + second
            outs[first][second * 32 : (second + 1) * 32, :] = (
                keep[at].astype(F32) + got[at].astype(F32)
            ).astype(BF16)
        outs[first][128:160, :] = gain
        outs[first][160:208, :] = router


def add4(own, g1, g2, g3, start, stop):
    return own[start:stop, :].astype(F32) + (
        g1[start:stop, :].astype(F32) + (g2[start:stop, :].astype(F32) + g3[start:stop, :].astype(F32))
    )


def add_gains(own, g1, g2, g3, start):
    stop = start + 32
    return (join3(own[start:stop, :]) + join3(g1[start:stop, :])) + (
        join3(g2[start:stop, :]) + join3(g3[start:stop, :])
    )


def ride_second_body(own, g1, g2, g3, *outs):
    rows = add4(own, g1, g2, g3, 0, 128)
    gain = split3(add_gains(own, g1, g2, g3, 128))
    router = add4(own, g1, g2, g3, 160, 208).astype(BF16)
    for second in range(4):
        outs[second][0:32, :] = rows[second * 32 : (second + 1) * 32].astype(BF16)
        outs[second][32:64, :] = gain
        outs[second][64:112, :] = router


def ride_last_body(own, g1, g2, g3, rows, gain, router):
    rows[...] = add4(own, g1, g2, g3, 0, 32)
    gain[...] = add_gains(own, g1, g2, g3, 32)
    router[...] = add4(own, g1, g2, g3, 64, 112)


def input_body(p0, p1, p2, x, gain, grad_mid, out):
    upstream = p0[...].astype(F32) + (p1[...].astype(F32) + p2[...].astype(F32))
    xf = x[...].astype(F32)
    scale = row_scale(xf)
    normed = xf * scale
    grad_normed = upstream * gain[...]
    out[...] = grad_mid[...] + scale * (
        grad_normed - normed * jnp.mean(grad_normed * normed, axis=1, keepdims=True)
    )


def place_of(index):
    return index // 8, (index // 2) % 4, index % 2


def index_of(y, z, core):
    return (y % 4) * 8 + (z % 4) * 2 + core


def shift_yz(tensor, dy, dz, flip=0):
    pairs = []
    for d in range(32):
        y, z, core = place_of(d)
        pairs.append((d, index_of(y + dy, z + dz, core ^ flip)))
    return lax.ppermute(tensor, "dp", pairs)


def shift_axis(tensor, axis, step):
    pairs = []
    for d in range(32):
        y, z, core = place_of(d)
        if (core == 0) == (axis == 0):
            pairs.append((d, index_of(y + step, z, core)))
        else:
            pairs.append((d, index_of(y, z + step, core)))
    return lax.ppermute(tensor, "dp", pairs)


def shift_mp(tensor, step):
    return lax.ppermute(tensor, "mp", [(i, (i + step) % 4) for i in range(4)])


def gather_weights(shard, chunks):
    rows = jnp.stack([shard] + [shift_axis(shard, 0, -s) for s in (1, 2, 3)])
    own = jnp.concatenate([rows] + [shift_axis(rows, 1, -s) for s in (1, 2, 3)], axis=0)
    near = own
    own = after(own, chunks)
    return near, own, shift_yz(own, 0, 0, 1)


def gather_mp(tensor):
    plus, minus = shift_mp(tensor, -1), shift_mp(tensor, 1)
    half = tensor.shape[0] // 2
    far = jnp.concatenate([shift_mp(plus[:half], -1), shift_mp(minus[half:], 1)], axis=0)
    return [tensor, plus, far, minus]


def after(value, *others):
    return lax.optimization_barrier((value, others))[0]


def add_low(left, *others):
    total = left.astype(F32)
    for one in others:
        total = total + one.astype(F32)
    return total.astype(BF16)


PLANES = [[core + 2 * k for k in range(16)] for core in range(2)]
STEPS = (0, 1, -1, 2)


def shards(
    layer_input,
    lengths,
    routes,
    attn_gain,
    query_gain,
    key_gain,
    query_weight,
    key_value_weight,
    out_weight,
    ffn_gain,
    router_weight,
    gate_weight,
    up_weight,
    down_weight,
    cotangent,
):
    dp_at = lax.axis_index("dp").astype(jnp.int32)
    mp_at = lax.axis_index("mp").astype(jnp.int32)
    y_at, z_at, core = dp_at // 8, (dp_at // 2) % 4, dp_at % 2
    length = lengths[0].astype(jnp.int32)
    cos_np, sin_np = rope_tables()
    cos_tab, sin_tab = jnp.asarray(cos_np), jnp.asarray(sin_np)
    spread4, spread2 = jnp.asarray(spread(4), BF16), jnp.asarray(spread(2), BF16)
    attn_row = attn_gain.reshape(1, WIDTH)
    ffn_row = ffn_gain.reshape(1, WIDTH)
    pad = jnp.zeros((PITCH - HDIM,), F32)
    head_gain = jnp.concatenate([query_gain, pad] * 4 + [key_gain, pad] * 2).reshape(1, 768)
    router = router_weight.T

    chunks = gather_mp(layer_input)
    chunk_at = [(mp_at + r) % 4 for r in range(4)]
    shard = jnp.concatenate([query_weight, key_value_weight.reshape(32, 256), out_weight], axis=0)
    shards_near, shards_own, shards_other = gather_weights(shard, chunks)

    packed, ranks = call(
        start_body,
        [((ROWS, WIDTH), BF16), ((EXPERTS, TOK), F32)],
        after((cotangent, routes), shards_near),
        scalars=jnp.stack([mp_at, length]),
    )
    cot_all = lax.all_gather(packed, "dp", axis=0, tiled=False, axis_index_groups=PLANES)
    weights_own = (gate_weight, up_weight, down_weight)
    weights_other = tuple(shift_yz(after(w, shards_other), 0, 0, 1) for w in weights_own)

    out = call(
        project_body,
        [((LEN, WIDTH), BF16), ((WIDTH, 1024), BF16)]
        + [((TOK, 512), F32)] * 4
        + [((TOK, 256), F32)] * 4
        + [((TOK, 512), BF16)] * 4
        + [((LEN, 256), BF16), ((LEN, 256), BF16), ((WIDTH, 512), BF16)]
        + [((TOK, PITCH), F32)] * 4,
        (shards_own, shards_other, *chunks, attn_row, head_gain, cos_tab, sin_tab, spread4, spread2),
        scalars=jnp.stack([y_at, z_at, core, mp_at, length]),
        any_out=range(10),
        near=range(10, 17),
        scratch=[
            pltpu.VMEM((LEN, WIDTH), BF16),
            pltpu.VMEM((LEN, 512), F32),
            pltpu.VMEM((LEN, 256), F32),
            pltpu.VMEM((WIDTH, 1024), BF16),
            pltpu.VMEM((WIDTH, 768), BF16),
            pltpu.SemaphoreType.DMA((13,)),
        ],
        mb=40,
        lazy=True,
    )
    h1, proj, raw, raw_pair, qa = out[0], out[1], out[2:6], out[6:10], out[10:14]
    ka, va, out_w, turn_tab = out[14], out[15], out[16], out[17:21]

    qa = list(after(tuple(qa), weights_other))
    branch, mixed, qb = [None] * 4, [None] * 4, [None] * 4
    arrived = [None] * 4
    for r in (2, 1, 3, 0):
        if r == 0:
            qa[0] = after(qa[0], arrived[2])
        branch[r], mixed[r], qb[r] = call(
            attend_body,
            [((TOK, WIDTH), BF16), ((TOK, 512), BF16), ((TOK, 512), BF16)],
            (qa[r], ka, va, out_w),
            near=(0,),
            local=(0, 1, 2, 3),
        )
        arrived[r] = shift_mp(branch[r], r) if r else branch[r]
    x_mid, h2 = call(
        middle_body,
        [((TOK, WIDTH), F32), ((TOK, WIDTH), BF16)],
        (layer_input, *arrived, ffn_row),
        local=(1, 2, 3, 4),
    )
    (gates,) = call(gates_body, [((EXPERTS, TOK), F32)], (h2, router, ranks))

    plus, minus = shift_axis(h2, 0, -1), shift_axis(h2, 0, 1)
    far_a, far_b = shift_axis(plus[: TOK // 2], 0, -1), shift_axis(minus[TOK // 2 :], 0, 1)
    near_a, near_b = jnp.stack([h2, plus]), jnp.stack([minus, jnp.concatenate([far_a, far_b], axis=0)])
    plus_a, plus_b = shift_axis(near_a, 1, -1), shift_axis(near_b, 1, -1)
    minus_a, minus_b = shift_axis(near_a, 1, 1), shift_axis(near_b, 1, 1)
    units = [(near_a, near_b), (plus_a, plus_b), (minus_a, minus_b), None]

    first_at = jnp.where(core == 0, y_at, z_at)
    second_at = jnp.where(core == 0, z_at, y_at)
    saved = None
    backs = []
    for u, step in enumerate(STEPS):
        if u == 1:
            far_plus, far_minus = after((plus_a, minus_b), backs[0])
            units[3] = (shift_axis(far_plus, 1, -1), shift_axis(far_minus, 1, 1))
        second = (second_at + step + 4) % 4
        order = []
        for s in STEPS:
            first = (first_at + s + 4) % 4
            order.append(jnp.where(core == 0, first * 4 + second, second * 4 + first))
        sc = jnp.stack(order + [dp_at, dp_at + 1 - 2 * core]).astype(jnp.int32)
        pieces = tuple(one.shape[0] for one in units[u])
        args = (*units[u], cot_all, router, *weights_own, *weights_other)
        any_in = list(range(len(pieces) + 1)) + list(range(len(pieces) + 2, len(pieces) + 8))
        aliases = None
        if saved is not None:
            base = len(args)
            aliases = {base + i: (0 if i == 0 else i + 2) for i in range(6)}
            any_in += list(range(base, base + 6))
            args = args + tuple(saved)
        made = call(
            partial(experts_body, pieces, u),
            [
                ((16, TOK, WIDTH), BF16),
                ((2, ROWS, WIDTH), BF16),
                ((2, ROWS, WIDTH), BF16),
                ((2, 16 * CAP, WIDTH), BF16),
                ((2, 16 * CAP, WIDTH), BF16),
                ((2, 16 * CAP, FF), BF16),
                ((2, 16 * CAP, FF), BF16),
                ((2, 16 * CAP, FF), BF16),
            ],
            args,
            scalars=sc,
            any_in=any_in,
            any_out=range(8),
            scratch=[
                pltpu.VMEM((4, TOK, WIDTH), BF16),
                pltpu.VMEM((4, ROWS, WIDTH), BF16),
                pltpu.VMEM((2, WIDTH, FF), BF16),
                pltpu.VMEM((2, WIDTH, FF), BF16),
                pltpu.VMEM((2, FF, WIDTH), BF16),
                pltpu.VMEM((4, TOK, WIDTH), BF16),
                pltpu.VMEM((4, ROWS, WIDTH), BF16),
                pltpu.VMEM((2, 4 * CAP, WIDTH), BF16),
                pltpu.VMEM((2, 4 * CAP, WIDTH), BF16),
                pltpu.VMEM((2, 4 * CAP, FF), BF16),
                pltpu.VMEM((2, 4 * CAP, FF), BF16),
                pltpu.VMEM((2, 4 * CAP, FF), BF16),
                pltpu.SemaphoreType.DMA((32,)),
            ],
            aliases=aliases,
            mb=40,
        )
        backs.append(made[1:3])
        saved = [made[0]] + list(made[3:])
    y_out, taken, push, hidden, grad_gate, grad_up = saved

    (b0_a, b0_b), (bp_a, bp_b), (bm_a, bm_b), (bf_a, bf_b) = backs
    half_a, half_b = shift_axis(bf_a, 1, 1), shift_axis(bf_b, 1, -1)
    saved = (taken, push, hidden, grad_gate, grad_up)
    for_other = expert_weights(saved, 1, mp_at)
    from_other = [shift_yz(one, 0, 0, 1) for one in for_other]
    half_a, half_b = after((half_a, half_b), for_other)
    plus_late, minus_late = add_low(bp_a, half_a), add_low(bm_b, half_b)
    plus_a, plus_b = shift_axis(plus_late, 1, 1), shift_axis(bp_b, 1, 1)
    minus_a, minus_b = shift_axis(bm_a, 1, -1), shift_axis(minus_late, 1, -1)
    shard_grads = expert_weights(after(saved, plus_late, minus_late), 0, mp_at, from_other)
    b0_a, b0_b = after((b0_a, b0_b), shard_grads)
    line_a = add_low(b0_a, plus_a, minus_a)
    line_b = add_low(b0_b, plus_b, minus_b)
    cut = ROWS // 2 + 8
    far_up, far_down = shift_axis(line_b[1, :cut], 0, 1), shift_axis(line_b[1, cut:], 0, -1)
    send_up = jnp.concatenate([add_low(line_a[1, :cut], far_up), line_a[1, cut:]], axis=0)
    send_down = jnp.concatenate([line_b[0, :cut], add_low(line_b[0, cut:], far_down)], axis=0)
    got_up, got_down = shift_axis(send_up, 0, 1), shift_axis(send_down, 0, -1)
    shards_got = [shift_mp(shard_grads[step], step) for step in (1, 2, 3)]
    got_up, got_down = after((got_up, got_down), shards_got[0], shards_got[2])
    grad_mid, grad_rows, small = call(
        token_back_body,
        [((TOK, WIDTH), F32), ((TOK, WIDTH), BF16), ((EXPERTS + 8, WIDTH), F32)],
        (line_a[0], got_up, got_down, h2, x_mid, ranks, gates, router, ffn_row, packed),
        local=(0, 1, 2),
    )

    returned = lax.psum_scatter(
        after(y_out, grad_rows).reshape(16 * TOK, WIDTH), "dp", scatter_dimension=0, tiled=True, axis_index_groups=PLANES
    )
    both = None
    grad_query, query_gains, slim = [None] * 4, [None] * 4, [None] * 4
    def sum_mp(t):
        return t + (shift_mp(t, 1) + shift_mp(t, 2) + shift_mp(t, 3))

    rows = [grad_rows, shift_mp(grad_rows, -1), None, shift_mp(grad_rows, 1)]
    for turn, r in enumerate((0, 1, 3, 2)):
        if turn == 1:
            near_a, near_b = after((rows[1], rows[3]), grad_query[0])
            rows[2] = jnp.concatenate(
                [shift_mp(near_a[: TOK // 2], -1), shift_mp(near_b[TOK // 2 :], 1)], axis=0
            )
        if turn == 2:
            small = sum_mp(after(small, rows[2], grad_query[1]))[:36].reshape(48, 768)
        if turn == 3:
            expert_grads = shard_grads[0].astype(F32) + (
                shards_got[0].astype(F32) + (shards_got[1].astype(F32) + shards_got[2].astype(F32))
            )
            rows[r] = after(rows[r], small, expert_grads)
        args = (rows[r], out_w, qb[r], mixed[r], ka, va, raw[r], head_gain, turn_tab[r], spread4)
        first = both is None
        grad_query[r], query_gains[r], slim[r], both = call(
            partial(attend_back_body, first),
            [((TOK, 512), BF16), ((8, PITCH), F32), ((TOK, 256), BF16), ((2, LEN, 256), F32)],
            args if first else args + (both,),
            any_in=() if first else (len(args),),
            any_out=(3,),
            scratch=[pltpu.VMEM((2, LEN, 256), F32), pltpu.SemaphoreType.DMA((4,))],
            aliases=None if first else {len(args): 3},
            local=(0, 1, 4, 5),
            mb=32,
            lazy=True,
        )
    far_up, far_down, wide, gains = call(
        keys_back_body,
        [((TOK // 2, WIDTH), BF16)] * 2 + [((LEN, 512), BF16), ((8, WIDTH), F32)],
        (both, *raw_pair, *turn_tab, head_gain, grad_query[2], proj, chunks[2]),
        near=range(4),
        mb=32,
        lazy=True,
    )
    far_up, far_down = shift_mp(far_up, 1), shift_mp(far_down, -1)
    others = (1, 3, 0)
    part_up, part_down, part_own, keep, send, extra = call(
        tail_body,
        [((TOK, WIDTH), BF16)] * 3 + [((16, 32, 768), BF16), ((19, 32, 768), BF16), ((56, 768), F32)],
        (
            wide,
            gains,
            small,
            spread2,
            spread4,
            *(grad_query[r] for r in others),
            proj,
            *(chunks[r] for r in others),
            *rows,
            *mixed,
            h1,
            *slim,
            *query_gains,
        ),
        scalars=jnp.stack([y_at, z_at, core]),
        scratch=[pltpu.VMEM((LEN, 256), BF16)],
        near=range(6),
        local=(0, 1),
        mb=40,
        lazy=True,
    )
    part_up, part_down = call(
        near_body,
        [((TOK, WIDTH), BF16)] * 2,
        (part_up, part_down, far_up, far_down),
        near=(0, 1),
        local=range(4),
    )
    part_up, part_down = shift_mp(part_up, 1), shift_mp(part_down, -1)
    layer_output = (x_mid + returned.astype(F32)).astype(BF16)
    expert_outs = (
        expert_grads[0:256].reshape(1, 256, FF),
        expert_grads[256:512].reshape(1, 256, FF),
        jnp.concatenate([expert_grads[512:640], expert_grads[640:768]], axis=1).reshape(1, 128, WIDTH),
    )
    first_msg = call(
        ride_first_body,
        [((208, 768), BF16)] * 4,
        (keep, shift_yz(send, 0, 0, 1), extra),
        near=range(4),
        local=range(3),
    )
    second_msg = call(
        ride_second_body,
        [((112, 768), BF16)] * 4,
        after((first_msg[0], *(shift_axis(first_msg[s], 0, s) for s in (1, 2, 3))), part_up, part_down, layer_output, expert_outs),
        near=range(4),
        local=range(4),
    )
    weight_sum, gain_sum, router_sum = call(
        ride_last_body,
        [((32, 768), F32), ((4, 768), F32), ((48, 768), F32)],
        (second_msg[0], *(shift_axis(second_msg[s], 1, s) for s in (1, 2, 3))),
        local=range(4),
    )
    gain_sum, router_sum = sum_mp(gain_sum), router_sum.reshape(36, WIDTH)
    attn_gain_grad = jnp.concatenate([gain_sum[0], gain_sum[1, 0:256]])
    (input_grad,) = call(
        input_body,
        [((TOK, WIDTH), F32)],
        (part_own, part_up, part_down, layer_input, attn_row, grad_mid),
        local=(0, 1, 2),
    )

    return (
        layer_output,
        input_grad,
        attn_gain_grad,
        gain_sum[1, 256 : 256 + HDIM],
        gain_sum[1, 384 : 384 + HDIM],
        weight_sum[:, 0:256],
        weight_sum[:, 256:512].reshape(32, 2, 128),
        weight_sum[:, 512:768],
        router_sum[EXPERTS],
        router_sum[:EXPERTS].T,
        *expert_outs,
    )


def solution(mesh):
    tokens = P(("dp", "mp"), None)
    in_specs = (
        tokens,
        P("dp"),
        tokens,
        P(),
        P(),
        P(),
        P("dp", "mp"),
        P("dp", None, "mp"),
        P("dp", "mp"),
        P(),
        P(),
        P("dp", None, None),
        P("dp", None, None),
        P("dp", None, None),
        tokens,
    )
    out_specs = (
        tokens,
        tokens,
        P(),
        P(),
        P(),
        P("dp", "mp"),
        P("dp", None, "mp"),
        P("dp", "mp"),
        P(),
        P(),
        P("dp", "mp", None),
        P("dp", "mp", None),
        P("dp", "mp", None),
    )
    return jax.shard_map(shards, mesh=mesh, in_specs=in_specs, out_specs=out_specs, check_vma=False)
```

time: 539 us -> 403 us (0.75)
  waiting for transfers between devices: 167 us -> 116 us
  Pallas kernels: 190 us -> 160 us
  matrix products: 22 us -> 0 us
  starting transfers between devices: 98.8 us -> 79.3 us
  local copies, waits for them, and re-layouts: 28.4 us -> 13.6 us
    ppermute x18 -> x32, waiting for transfers between devices: 92.5 us -> 49.4 us  [shift_axis(): return lax.ppermute(tensor, 'dp', pairs)]
    ppermute x27 -> x8, starting transfers between devices: 35.8 us -> 1.96 us  [shift_yz(): return lax.ppermute(tensor, 'dp', pairs)]
    pallas_call x27 -> x26, Pallas kernels: 190 us -> 160 us  [the longest x24 140 us: call(): pl.pallas_call(kernel, out_shape=shapes, in_specs=in_specs, out_specs=out...]
    ppermute x27 -> x8, waiting for transfers between devices: 30.1 us -> 1.6 us  [shift_yz(): return lax.ppermute(tensor, 'dp', pairs)]
    dot_general x6 -> x0, matrix products: 22 us -> none  [one(): lax.dot_general(left[e], right[e], (((0,), (0,)), ((), ())), preferred_el...]
    ppermute x18 -> x24, waiting for transfers between devices: 43.7 us -> 65.2 us  [shift_mp(): return lax.ppermute(tensor, 'mp', [(i, (i + step) % 4) for i in range(4)])]
    ppermute x18 -> x32, starting transfers between devices: 28 us -> 47.3 us  [shift_axis(): return lax.ppermute(tensor, 'dp', pairs)]
    unnamed x91 -> x68, local copies, waits for them, and re-layouts: 12.7 us -> 4 us
  transfers between devices with their start and end apart: 67 -> 66, of which waited for: 28 -> 30; matrix products, arithmetic and copies ran while one was open for 7% -> 5% of each run, Pallas kernels for 32% -> 35%
where the time goes in v2:
time: 403 us; the launch traced here: 397 us
  Pallas kernels  160 us (40%)
  waiting for transfers between devices  116 us (29%)
  starting transfers between devices  79.3 us (20%)
  between operations  16.2 us (4%)
  local copies, waits for them, and re-layouts  13.6 us (3%)
  other arithmetic  12 us (3%)
    pallas_call x24, Pallas kernels, call(): pl.pallas_call(kernel, out_shape=shapes, in_specs=in_specs, out_specs=out...  140 us
    ppermute x24, waiting for transfers between devices, shift_mp(): return lax.ppermute(tensor, 'mp', [(i, (i + step) % 4) for i in range(4)])  65.2 us
    ppermute x32, waiting for transfers between devices, shift_axis(): return lax.ppermute(tensor, 'dp', pairs)  49.4 us
    ppermute x32, starting transfers between devices, shift_axis(): return lax.ppermute(tensor, 'dp', pairs)  47.3 us
    ppermute x24, starting transfers between devices, shift_mp(): return lax.ppermute(tensor, 'mp', [(i, (i + step) % 4) for i in range(4)])  30 us
    pallas_call x2, Pallas kernels, expert_weights(): pl.pallas_call(partial(expert_weights_body, bool(got)), out_shape=[jax.Sh...  19.7 us
  transfers between devices with their start and end apart: 66, of which 30 were waited for; matrix products, arithmetic and copies ran while one was open for 5% of the time, Pallas kernels for 35%

profile of v2, /device:TPU:0, one launch (start us, length us, event | category | flops | bytes accessed | tf_op | source)
XLA Modules:
  0.0 397.4 jit_solution(9748935047992044025)
XLA Ops:
  9.4 3.1 collective-permute-start
  14.8 3.3 collective-permute-done.1
  18.6 4.1 %collective-permute-start.3 = (bf16[4,96,256]{2,1,0:T(8,128)(2,1)S(1)}, bf16[4,96,256]{2,1,0:T(8,128)(2,1)S(1)}, u32[]{:S(2)}, u32[]{:S(2)}) collective-permute-start(bf16[4,96,256]{2,1,0:T(8,128)(2,1)S(1)} %pad_maximum_fusion.4), channel_id=1, source_target_pairs={{0,24},{4,100},{8,0},{12,108},{16,8},{20,116},{24,16},{28,124},{32... | collective-permute-start | bytes 589832 | tf_op jit(solution)/shard_map/ppermute | solution.py:736
  24.0 4.0 %collective-permute-done.3 = bf16[4,96,256]{2,1,0:T(8,128)(2,1)S(1)} collective-permute-done((bf16[4,96,256]{2,1,0:T(8,128)(2,1)S(1)}, bf16[4,96,256]{2,1,0:T(8,128)(2,1)S(1)}, u32[]{:S(2)}, u32[]{:S(2)}) %collective-permute-start.3) | collective-permute-done | bytes 196640 | tf_op jit(solution)/shard_map/ppermute | solution.py:736
  32.7 3.0 shard_map.288
  35.8 2.8 collective-permute-start.6
  38.6 9.0 %collective-permute-done.6.refs_4_.refs_10_ = bf16[256,1024]{1,0:T(8,128)(2,1)S(1)} collective-permute-done((bf16[256,1024]{1,0:T(8,128)(2,1)S(1)}, bf16[256,1024]{1,0:T(8,128)(2,1)S(1)}, u32[]{:S(2)}, u32[]{:S(2)}) %collective-permute-start.6) | collective-permute-done | bytes 524320 | tf_op jit(solution)/shard_map/ppermute | solution.py:740
  47.6 3.4 collective-permute-start.7
  51.2 3.8 collective-permute-done.7
  55.0 3.8 collective-permute-done.9
  63.6 10.9 %shard_map.282 = (bf16[1024,1024]{1,0:T(8,128)(2,1)}, bf16[1024,1024]{1,0:T(8,128)(2,1)}, f32[256,512]{1,0:T(8,128)}, f32[256,512]{1,0:T(8,128)}, f32[256,512]{1...) custom-call(s32[5]{0:T(128)S(1)} %stack.134.refs_0_, ...), custom_call_target="tpu_custom_call" | custom-call | flops 1 | bytes 1 | tf_op jit(solution)/shard_map/pallas_call | solution.py:128
  82.4 2.7 collective-permute-start.16
  85.2 8.0 %collective-permute-done.14.refs_3_ = bf16[256,1024]{1,0:T(8,128)(2,1)S(1)} collective-permute-done((bf16[256,1024]{1,0:T(8,128)(2,1)S(1)}, bf16[256,1024]{1,0:T(8,128)(2,1)S(1)}, u32[]{:S(2)}, u32[]{:S(2)}) %collective-permute-start.14) | collective-permute-done | bytes 524320 | tf_op jit(solution)/shard_map/ppermute | solution.py:740
  95.5 8.3 %collective-permute-done.15.refs_2_ = bf16[256,1024]{1,0:T(8,128)(2,1)S(1)} collective-permute-done((bf16[256,1024]{1,0:T(8,128)(2,1)S(1)}, bf16[256,1024]{1,0:T(8,128)(2,1)S(1)}, u32[]{:S(2)}, u32[]{:S(2)}) %collective-permute-start.15) | collective-permute-done | bytes 524320 | tf_op jit(solution)/shard_map/ppermute | solution.py:740
  106.5 3.2 collective-permute-start.17
  109.8 7.4 %collective-permute-done.19 = bf16[256,1024]{1,0:T(8,128)(2,1)S(1)} collective-permute-done((bf16[256,1024]{1,0:T(8,128)(2,1)}, bf16[256,1024]{1,0:T(8,128)(2,1)S(1)}, u32[]{:S(2)}, u32[]{:S(2)}) %collective-permute-start.19) | collective-permute-done | bytes 524320 | tf_op jit(solution)/shard_map/ppermute | solution.py:736
  117.3 3.3 collective-permute-start.20
  127.7 3.2 collective-permute-start.26
  131.0 14.7 %shard_map.289 = (bf16[16,256,1024]{2,1,0:T(8,128)(2,1)}, bf16[2,272,1024]{2,1,0:T(8,128)(2,1)}, bf16[2,272,1024]{2,1,0:T(8,128)(2,1)}, bf16[2,1536,1024]{2,1,0:...) custom-call(s32[6]{0:T(128)S(1)} %stack.157.refs_0_, ...), custom_call_target="tpu_custom_call" | custom-call | flops 1 | bytes 1 | tf_op jit(solution)/shard_map/pallas_call | solution.py:128
  145.8 3.2 collective-permute-start.23
  149.7 14.6 %shard_map.290 = (bf16[16,256,1024]{2,1,0:T(8,128)(2,1)}, bf16[2,272,1024]{2,1,0:T(8,128)(2,1)}, bf16[2,272,1024]{2,1,0:T(8,128)(2,1)}, bf16[2,1536,1024]{2,1,0:...) custom-call(s32[6]{0:T(128)S(1)} %stack.168.refs_0_, ...), custom_call_target="tpu_custom_call", output_to_operand_aliasing={{0}: (11, {}), {3}: (12, {}), {4}: (13, {}), {5}: (14, {}),... | custom-call | flops 1 | bytes 1 | tf_op jit(solution)/shard_map/pallas_call | solution.py:128
  164.4 14.7 %shard_map.291 = (bf16[16,256,1024]{2,1,0:T(8,128)(2,1)}, bf16[2,272,1024]{2,1,0:T(8,128)(2,1)}, bf16[2,272,1024]{2,1,0:T(8,128)(2,1)}, bf16[2,1536,1024]{2,1,0:...) custom-call(s32[6]{0:T(128)S(1)} %stack.163.refs_0_, ...), custom_call_target="tpu_custom_call", output_to_operand_aliasing={{0}: (11, {}), {3}: (12, {}), {4}: (13, {}), {5}: (14, {}),... | custom-call | flops 1 | bytes 1 | tf_op jit(solution)/shard_map/pallas_call | solution.py:128
  179.1 14.7 %shard_map.292 = (bf16[16,256,1024]{2,1,0:T(8,128)(2,1)}, bf16[2,272,1024]{2,1,0:T(8,128)(2,1)}, bf16[2,272,1024]{2,1,0:T(8,128)(2,1)}, bf16[2,1536,1024]{2,1,0:...) custom-call(s32[6]{0:T(128)S(1)} %stack.146.refs_0_, ...), custom_call_target="tpu_custom_call", output_to_operand_aliasing={{0}: (11, {}), {3}: (12, {}), {4}: (13, {}), {5}: (14, {}),... | custom-call | flops 1 | bytes 1 | tf_op jit(solution)/shard_map/pallas_call | solution.py:128
  193.9 3.2 collective-permute-start.28
  197.1 9.6 %shard_map.293 = (bf16[1024,512]{1,0:T(8,128)(2,1)S(1)}, bf16[1024,512]{1,0:T(8,128)(2,1)S(1)}, bf16[512,1024]{1,0:T(8,128)(2,1)S(1)}) custom-call(s32[1]{0:T(128)} %bitcast.3.sc, bf16[2,1536,1024]{2,1,0:T(8,128)(2,1)} %get-tuple-element.226.taken, bf16[2,1536,1024]{2,1,0:T(8,128)(2,1)} %get-tuple-element.227.push, ...), custom_call_target="tpu_custom_call" | custom-call | flops 1 | bytes 1 | tf_op jit(solution)/shard_map/pallas_call | solution.py:443
  207.8 3.0 collective-permute-done.27
  211.3 3.3 collective-permute-start.35
  217.8 10.1 %shard_map.294 = (bf16[768,512]{1,0:T(8,128)(2,1)S(1)}, bf16[768,512]{1,0:T(8,128)(2,1)S(1)}, bf16[768,512]{1,0:T(8,128)(2,1)S(1)}, bf16[768,512]{1,0:T(8,128)(2,1)S(1)}) custom-call(s32[1]{0:T(128)} %bitcast.3.sc, bf16[2,1536,1024]{2,1,0:T(8,128)(2,1)} %get-tuple-element.226.taken, bf16[2,1536,1024]{2,1,0:T(8,128)(2,1)} %get-tuple-element.227.push, ...), custom_call_target="tpu_custom_call" | custom-call | flops 1 | bytes 1 | tf_op jit(solution)/shard_map/pallas_call | solution.py:443
  228.0 3.2 collective-permute-start.41
  232.2 7.4 %collective-permute-done.33 = bf16[2,272,1024]{2,1,0:T(8,128)(2,1)S(1)} collective-permute-done((bf16[2,272,1024]{2,1,0:T(8,128)(2,1)S(1)}, bf16[2,272,1024]{2,1,0:T(8,128)(2,1)S(1)}, u32[]{:S(2)}, u32[]{:S(2)}) %collective-permute-start.33) | collective-permute-done | bytes 1114144 | tf_op jit(solution)/shard_map/ppermute | solution.py:736
  239.5 3.7 collective-permute-start.38
  244.0 3.1 collective-permute-done.38
  247.2 3.8 collective-permute-start.39
  253.3 4.7 %collective-permute-done.39.refs_2_ = bf16[272,1024]{1,0:T(8,128)(2,1)S(1)} collective-permute-done((bf16[272,1024]{1,0:T(8,128)(2,1)S(1)}, bf16[272,1024]{1,0:T(8,128)(2,1)S(1)}, u32[]{:S(2)}, u32[]{:S(2)}) %collective-permute-start.39) | collective-permute-done | bytes 557088 | tf_op jit(solution)/shard_map/ppermute | solution.py:736
  258.0 3.9 collective-permute-done.37.refs_1_
  261.9 3.7 shard_map.296
  268.4 7.5 %shard_map.297 = (bf16[256,512]{1,0:T(8,128)(2,1)}, f32[8,128]{1,0:T(8,128)}, bf16[256,256]{1,0:T(8,128)(2,1)}, f32[2,1024,256]{2,1,0:T(8,128)}) custom-call(bf16[256,1024]{1,0:T(8,128)(2,1)} %get-tuple-element.242.refs_0_.refs_13_, bf16[1024,512]{1,0:T(8,128)(2,1)S(1)} %get-tuple-element.176.refs_3_.refs_1_, bf16[256,512]{1,0:T(8,128)(2,1)} %get-tuple-element.244.refs_2_, ...), custom_call_target="tpu_custom_call" | custom-call | flops 1 | bytes 1 | tf_op jit(solution)/shard_map/pallas_call | solution.py:128
  275.9 12.1 %collective-permute-done.42.refs_0_.refs_14_ = bf16[256,1024]{1,0:T(8,128)(2,1)S(1)} collective-permute-done((bf16[256,1024]{1,0:T(8,128)(2,1)}, bf16[256,1024]{1,0:T(8,128)(2,1)S(1)}, u32[]{:S(2)}, u32[]{:S(2)}) %collective-permute-start.42) | collective-permute-done | bytes 524320 | tf_op jit(solution)/shard_map/ppermute | solution.py:740
  288.0 7.6 %collective-permute-done.43.refs_0_.refs_16_ = bf16[256,1024]{1,0:T(8,128)(2,1)S(1)} collective-permute-done((bf16[256,1024]{1,0:T(8,128)(2,1)}, bf16[256,1024]{1,0:T(8,128)(2,1)S(1)}, u32[]{:S(2)}, u32[]{:S(2)}) %collective-permute-start.43) | collective-permute-done | bytes 524320 | tf_op jit(solution)/shard_map/ppermute | solution.py:740
  297.9 7.2 %shard_map.298 = (bf16[256,512]{1,0:T(8,128)(2,1)}, f32[8,128]{1,0:T(8,128)}, bf16[256,256]{1,0:T(8,128)(2,1)}, f32[2,1024,256]{2,1,0:T(8,128)}) custom-call(bf16[256,1024]{1,0:T(8,128)(2,1)S(1)} %collective-permute-done.42.refs_0_.refs_14_, bf16[1024,512]{1,0:T(8,128)(2,1)S(1)} %get-tuple-element.176.refs_3_.refs_1_, ...), custom_call_target="tpu_custom_call", output_to_operand_aliasing={{3}: (10, {})} | custom-call | flops 1 | bytes 1 | tf_op jit(solution)/shard_map/pallas_call | solution.py:128
  310.5 6.9 %shard_map.299 = (bf16[256,512]{1,0:T(8,128)(2,1)}, f32[8,128]{1,0:T(8,128)}, bf16[256,256]{1,0:T(8,128)(2,1)}, f32[2,1024,256]{2,1,0:T(8,128)}) custom-call(bf16[256,1024]{1,0:T(8,128)(2,1)S(1)} %collective-permute-done.43.refs_0_.refs_16_, bf16[1024,512]{1,0:T(8,128)(2,1)S(1)} %get-tuple-element.176.refs_3_.refs_1_, ...), custom_call_target="tpu_custom_call", output_to_operand_aliasing={{3}: (10, {})} | custom-call | flops 1 | bytes 1 | tf_op jit(solution)/shard_map/pallas_call | solution.py:128
  318.2 6.9 %shard_map.300 = (bf16[256,512]{1,0:T(8,128)(2,1)}, f32[8,128]{1,0:T(8,128)}, bf16[256,256]{1,0:T(8,128)(2,1)}, f32[2,1024,256]{2,1,0:T(8,128)}) custom-call(bf16[256,1024]{1,0:T(8,128)(2,1)S(1)} %constant_dynamic-update-slice_fusion.12.refs_0_.refs_15_, bf16[1024,512]{1,0:T(8,128)(2,1)S(1)} %get-tuple-element.176.refs_3_.refs_1_, ...), custom_call_target="tpu_custom_call", output_to_operand_aliasing={{3}: (10, {})} | custom-call | flops 1 | bytes 1 | tf_op jit(solution)/shard_map/pallas_call | solution.py:128
  325.0 5.0 %shard_map.301 = (bf16[128,1024]{1,0:T(8,128)(2,1)S(1)}, bf16[128,1024]{1,0:T(8,128)(2,1)S(1)}, bf16[1024,512]{1,0:T(8,128)(2,1)S(1)}, f32[8,1024]{1,0:T(8,128)S(1)}) custom-call(f32[2,1024,256]{2,1,0:T(8,128)} %get-tuple-element.270.refs_0_, f32[256,256]{1,0:T(8,128)} %get-tuple-element.271.refs_1_, f32[256,256]{1,0:T(8,128)} %get-tuple-element.272.refs_2_, ...), custom_call_target="tpu_custom_call" | custom-call | flops 1 | bytes 1 | tf_op jit(solution)/shard_map/pallas_call | solution.py:128
  330.1 11.0 %shard_map.302 = (bf16[256,1024]{1,0:T(8,128)(2,1)S(1)}, bf16[256,1024]{1,0:T(8,128)(2,1)S(1)}, bf16[256,1024]{1,0:T(8,128)(2,1)S(1)}, bf16[16,32,768]{2,1,0:T(8...) custom-call(s32[3]{0:T(128)S(1)} %pad_add_fusion.1.refs_0_, ...), custom_call_target="tpu_custom_call" | custom-call | flops 1 | bytes 1 | tf_op jit(solution)/shard_map/pallas_call | solution.py:128
  345.5 5.6 %collective-permute-done.50.refs_2_ = bf16[128,1024]{1,0:T(8,128)(2,1)S(1)} collective-permute-done((bf16[128,1024]{1,0:T(8,128)(2,1)S(1)}, bf16[128,1024]{1,0:T(8,128)(2,1)S(1)}, u32[]{:S(2)}, u32[]{:S(2)}) %collective-permute-start.50) | collective-permute-done | bytes 262176 | tf_op jit(solution)/shard_map/ppermute | solution.py:740
  357.7 2.6 collective-permute-start.56
  364.1 4.1 %collective-permute-done.52.refs_1_ = bf16[256,1024]{1,0:T(8,128)(2,1)S(1)} collective-permute-done((bf16[256,1024]{1,0:T(8,128)(2,1)}, bf16[256,1024]{1,0:T(8,128)(2,1)S(1)}, u32[]{:S(2)}, u32[]{:S(2)}) %collective-permute-start.52) | collective-permute-done | bytes 524320 | tf_op jit(solution)/shard_map/ppermute | solution.py:740
  373.9 3.0 shard_map.304
  (234 shorter events, 89.8 us)
Async XLA Ops:
  7.2 123.8 %all-gather.3.cloned.1.call-start = ((), (), s32[]{:S(2)}) async-start(), calls=%async_computation.2 | async-start | bytes 9469952 | tf_op jit(solution)/shard_map/all_gather | solution.py:814
  18.6 9.4 %collective-permute-start.3 = (bf16[4,96,256]{2,1,0:T(8,128)(2,1)S(1)}, bf16[4,96,256]{2,1,0:T(8,128)(2,1)S(1)}, u32[]{:S(2)}, u32[]{:S(2)}) collective-permute-start(bf16[4,96,256]{2,1,0:T(8,128)(2,1)S(1)} %pad_maximum_fusion.4), channel_id=1, source_target_pairs={{0,24},{4,100},{8,0},{12,108},{16,8},{20,116},{24,16},{28,124},{32... | collective-permute-start | bytes 589832 | tf_op jit(solution)/shard_map/ppermute | solution.py:736
  35.7 326.0 %reduce-scatter.2.cloned.1.call-start = ((), (), s32[]{:S(2)}) async-start(), calls=%async_computation.1 | async-start | bytes 8912896 | tf_op jit(solution)/shard_map/reduce_scatter | solution.py:961
  35.8 11.8 %collective-permute-start.6 = (bf16[256,1024]{1,0:T(8,128)(2,1)S(1)}, bf16[256,1024]{1,0:T(8,128)(2,1)S(1)}, u32[]{:S(2)}, u32[]{:S(2)}) collective-permute-start(bf16[256,1024]{1,0:T(8,128)(2,1)S(1)} %copy-done.7), channel_id=1, source_target_pairs={{0,3},{1,0},{2,1},{3,2},{4,7},{5,4},{6,5},{7,6},{8,11},{9,8},{10,9... | collective-permute-start | bytes 1572872 | tf_op jit(solution)/shard_map/ppermute | solution.py:740
  38.6 12.4 %collective-permute-start.8 = (bf16[256,1024]{1,0:T(8,128)(2,1)S(1)}, bf16[256,1024]{1,0:T(8,128)(2,1)S(1)}, u32[]{:S(2)}, u32[]{:S(2)}) collective-permute-start(bf16[256,1024]{1,0:T(8,128)(2,1)S(1)} %copy-done.7), channel_id=1, source_target_pairs={{0,1},{1,2},{2,3},{3,0},{4,5},{5,6},{6,7},{7,4},{8,9},{9,10},{10,1... | collective-permute-start | bytes 1572872 | tf_op jit(solution)/shard_map/ppermute | solution.py:740
  62.0 12.4 %collective-permute-start.11 = (bf16[1,1024,512]{2,1,0:T(8,128)(2,1)S(1)}, bf16[1,1024,512]{2,1,0:T(8,128)(2,1)}, u32[]{:S(2)}, u32[]{:S(2)}) collective-permute-start(bf16[1,1024,512]{2,1,0:T(8,128)(2,1)S(1)} %copy-done), channel_id=1, source_target_pairs={{0,4},{4,0},{8,12},{12,8},{16,20},{20,16},{24,28},{28,24},{32,36},... | collective-permute-start | bytes 3145736 | tf_op jit(solution)/shard_map/ppermute | solution.py:725
  62.2 12.3 %collective-permute-start.12 = (bf16[1,1024,512]{2,1,0:T(8,128)(2,1)}, bf16[1,1024,512]{2,1,0:T(8,128)(2,1)}, u32[]{:S(2)}, u32[]{:S(2)}) collective-permute-start(bf16[1,1024,512]{2,1,0:T(8,128)(2,1)} %refs_6_.7), channel_id=1, source_target_pairs={{0,4},{4,0},{8,12},{12,8},{16,20},{20,16},{24,28},{28,24},{32,36},... | collective-permute-start | bytes 3145736 | tf_op jit(solution)/shard_map/ppermute | solution.py:725
  62.5 12.0 %collective-permute-start.13 = (bf16[1,512,1024]{2,1,0:T(8,128)(2,1)}, bf16[1,512,1024]{2,1,0:T(8,128)(2,1)}, u32[]{:S(2)}, u32[]{:S(2)}) collective-permute-start(bf16[1,512,1024]{2,1,0:T(8,128)(2,1)} %refs_7_.7), channel_id=1, source_target_pairs={{0,4},{4,0},{8,12},{12,8},{16,20},{20,16},{24,28},{28,24},{32,36},... | collective-permute-start | bytes 3145736 | tf_op jit(solution)/shard_map/ppermute | solution.py:725
  76.8 16.4 %collective-permute-start.14 = (bf16[256,1024]{1,0:T(8,128)(2,1)S(1)}, bf16[256,1024]{1,0:T(8,128)(2,1)S(1)}, u32[]{:S(2)}, u32[]{:S(2)}) collective-permute-start(bf16[256,1024]{1,0:T(8,128)(2,1)S(1)} %get-tuple-element.177), channel_id=1, source_target_pairs={{0,2},{1,3},{2,0},{3,1},{4,6},{5,7},{6,4},{7,5},{8,10},{9,11},{10,... | collective-permute-start | bytes 1572872 | tf_op jit(solution)/shard_map/ppermute | solution.py:740
  79.2 24.6 %collective-permute-start.15 = (bf16[256,1024]{1,0:T(8,128)(2,1)S(1)}, bf16[256,1024]{1,0:T(8,128)(2,1)S(1)}, u32[]{:S(2)}, u32[]{:S(2)}) collective-permute-start(bf16[256,1024]{1,0:T(8,128)(2,1)S(1)} %get-tuple-element.181), channel_id=1, source_target_pairs={{0,1},{1,2},{2,3},{3,0},{4,5},{5,6},{6,7},{7,4},{8,9},{9,10},{10,1... | collective-permute-start | bytes 1572872 | tf_op jit(solution)/shard_map/ppermute | solution.py:740
  82.4 21.4 %collective-permute-start.16 = (bf16[256,1024]{1,0:T(8,128)(2,1)S(1)}, bf16[256,1024]{1,0:T(8,128)(2,1)S(1)}, u32[]{:S(2)}, u32[]{:S(2)}) collective-permute-start(bf16[256,1024]{1,0:T(8,128)(2,1)S(1)} %get-tuple-element.183), channel_id=1, source_target_pairs={{0,3},{1,0},{2,1},{3,2},{4,7},{5,4},{6,5},{7,6},{8,11},{9,8},{10,9... | collective-permute-start | bytes 1572872 | tf_op jit(solution)/shard_map/ppermute | solution.py:740
  106.4 10.7 %collective-permute-start.19 = (bf16[256,1024]{1,0:T(8,128)(2,1)}, bf16[256,1024]{1,0:T(8,128)(2,1)S(1)}, u32[]{:S(2)}, u32[]{:S(2)}) collective-permute-start(bf16[256,1024]{1,0:T(8,128)(2,1)} %get-tuple-element.185.refs_0_.refs_3_), channel_id=1, source_target_pairs={{0,32},{4,12},{8,40},{12,20},{16,48},{20,28},{24,56},{28,4},{32,64... | collective-permute-start | bytes 1572872 | tf_op jit(solution)/shard_map/ppermute | solution.py:736
  106.5 10.7 %collective-permute-start.17 = (bf16[256,1024]{1,0:T(8,128)(2,1)}, bf16[256,1024]{1,0:T(8,128)(2,1)S(1)}, u32[]{:S(2)}, u32[]{:S(2)}) collective-permute-start(bf16[256,1024]{1,0:T(8,128)(2,1)} %get-tuple-element.185.refs_0_.refs_3_), channel_id=1, source_target_pairs={{0,96},{4,28},{8,104},{12,4},{16,112},{20,12},{24,120},{28,20},{32... | collective-permute-start | bytes 1572872 | tf_op jit(solution)/shard_map/ppermute | solution.py:736
  117.3 9.3 %collective-permute-start.20 = (bf16[128,1024]{1,0:T(8,128)(2,1)S(1)}, bf16[128,1024]{1,0:T(8,128)(2,1)S(1)}, u32[]{:S(2)}, u32[]{:S(2)}) collective-permute-start(bf16[128,1024]{1,0:T(8,128)(2,1)S(1)} %slice.110), channel_id=1, source_target_pairs={{0,96},{4,28},{8,104},{12,4},{16,112},{20,12},{24,120},{28,20},{32... | collective-permute-start | bytes 786440 | tf_op jit(solution)/shard_map/ppermute | solution.py:736
  122.7 23.1 %collective-permute-start.18 = (bf16[2,256,1024]{2,1,0:T(8,128)(2,1)}, bf16[2,256,1024]{2,1,0:T(8,128)(2,1)}, u32[]{:S(2)}, u32[]{:S(2)}) collective-permute-start(bf16[2,256,1024]{2,1,0:T(8,128)(2,1)} %pad_maximum_fusion.refs_1_), channel_id=1, source_target_pairs={{0,24},{4,100},{8,0},{12,108},{16,8},{20,116},{24,16},{28,124},{32... | collective-permute-start | bytes 3145736 | tf_op jit(solution)/shard_map/ppermute | solution.py:736
  127.7 18.1 %collective-permute-start.22 = (bf16[2,256,1024]{2,1,0:T(8,128)(2,1)}, bf16[2,256,1024]{2,1,0:T(8,128)(2,1)}, u32[]{:S(2)}, u32[]{:S(2)}) collective-permute-start(bf16[2,256,1024]{2,1,0:T(8,128)(2,1)} %pad_maximum_fusion.1.refs_2_), channel_id=1, source_target_pairs={{0,8},{4,36},{8,16},{12,44},{16,24},{20,52},{24,0},{28,60},{32,40}... | collective-permute-start | bytes 3145736 | tf_op jit(solution)/shard_map/ppermute | solution.py:736
  127.7 22.1 %collective-permute-start.26 = (bf16[2,256,1024]{2,1,0:T(8,128)(2,1)}, bf16[2,256,1024]{2,1,0:T(8,128)(2,1)}, u32[]{:S(2)}, u32[]{:S(2)}) collective-permute-start(bf16[2,256,1024]{2,1,0:T(8,128)(2,1)} %pad_maximum_fusion.1.refs_2_), channel_id=1, source_target_pairs={{0,24},{4,100},{8,0},{12,108},{16,8},{20,116},{24,16},{28,124},{32... | collective-permute-start | bytes 3145736 | tf_op jit(solution)/shard_map/ppermute | solution.py:736
  131.0 33.4 %collective-permute-start.25 = (bf16[2,256,1024]{2,1,0:T(8,128)(2,1)}, bf16[2,256,1024]{2,1,0:T(8,128)(2,1)}, u32[]{:S(2)}, u32[]{:S(2)}) collective-permute-start(bf16[2,256,1024]{2,1,0:T(8,128)(2,1)} %pad_maximum_fusion.refs_1_), channel_id=1, source_target_pairs={{0,8},{4,36},{8,16},{12,44},{16,24},{20,52},{24,0},{28,60},{32,40}... | collective-permute-start | bytes 3145736 | tf_op jit(solution)/shard_map/ppermute | solution.py:736
  145.8 33.3 %collective-permute-start.23 = (bf16[2,256,1024]{2,1,0:T(8,128)(2,1)}, bf16[2,256,1024]{2,1,0:T(8,128)(2,1)}, u32[]{:S(2)}, u32[]{:S(2)}) collective-permute-start(bf16[2,256,1024]{2,1,0:T(8,128)(2,1)} %collective-permute-done.18.refs_1_), channel_id=1, source_target_pairs={{0,24},{4,100},{8,0},{12,108},{16,8},{20,116},{24,16},{28,124},{32... | collective-permute-start | bytes 3145736 | tf_op jit(solution)/shard_map/ppermute | solution.py:736
  149.0 30.1 %collective-permute-start.24 = (bf16[2,256,1024]{2,1,0:T(8,128)(2,1)}, bf16[2,256,1024]{2,1,0:T(8,128)(2,1)}, u32[]{:S(2)}, u32[]{:S(2)}) collective-permute-start(bf16[2,256,1024]{2,1,0:T(8,128)(2,1)} %collective-permute-done.22.refs_2_), channel_id=1, source_target_pairs={{0,8},{4,36},{8,16},{12,44},{16,24},{20,52},{24,0},{28,60},{32,40}... | collective-permute-start | bytes 3145736 | tf_op jit(solution)/shard_map/ppermute | solution.py:736
  193.8 17.0 %collective-permute-start.27 = (bf16[2,272,1024]{2,1,0:T(8,128)(2,1)}, bf16[2,272,1024]{2,1,0:T(8,128)(2,1)S(1)}, u32[]{:S(2)}, u32[]{:S(2)}) collective-permute-start(bf16[2,272,1024]{2,1,0:T(8,128)(2,1)} %get-tuple-element.218), channel_id=1, source_target_pairs={{0,8},{4,36},{8,16},{12,44},{16,24},{20,52},{24,0},{28,60},{32,40}... | collective-permute-start | bytes 3342344 | tf_op jit(solution)/shard_map/ppermute | solution.py:736
  193.9 16.9 %collective-permute-start.28 = (bf16[2,272,1024]{2,1,0:T(8,128)(2,1)}, bf16[2,272,1024]{2,1,0:T(8,128)(2,1)S(1)}, u32[]{:S(2)}, u32[]{:S(2)}) collective-permute-start(bf16[2,272,1024]{2,1,0:T(8,128)(2,1)} %get-tuple-element.219), channel_id=1, source_target_pairs={{0,24},{4,100},{8,0},{12,108},{16,8},{20,116},{24,16},{28,124},{32... | collective-permute-start | bytes 3342344 | tf_op jit(solution)/shard_map/ppermute | solution.py:736
  197.1 30.9 %collective-permute-start.34 = (bf16[2,272,1024]{2,1,0:T(8,128)(2,1)S(1)}, bf16[2,272,1024]{2,1,0:T(8,128)(2,1)S(1)}, u32[]{:S(2)}, u32[]{:S(2)}) collective-permute-start(bf16[2,272,1024]{2,1,0:T(8,128)(2,1)S(1)} %copy-done.28), channel_id=1, source_target_pairs={{0,8},{4,36},{8,16},{12,44},{16,24},{20,52},{24,0},{28,60},{32,40}... | collective-permute-start | bytes 3342344 | tf_op jit(solution)/shard_map/ppermute | solution.py:736
  207.3 9.3 %collective-permute-start.30 = (bf16[1024,512]{1,0:T(8,128)(2,1)S(1)}, bf16[1024,512]{1,0:T(8,128)(2,1)S(1)}, u32[]{:S(2)}, u32[]{:S(2)}) collective-permute-start(bf16[1024,512]{1,0:T(8,128)(2,1)S(1)} %get-tuple-element.221), channel_id=1, source_target_pairs={{0,4},{4,0},{8,12},{12,8},{16,20},{20,16},{24,28},{28,24},{32,36},... | collective-permute-start | bytes 3145736 | tf_op jit(solution)/shard_map/ppermute | solution.py:725
  211.3 20.0 %collective-permute-start.35 = (bf16[2,272,1024]{2,1,0:T(8,128)(2,1)S(1)}, bf16[2,272,1024]{2,1,0:T(8,128)(2,1)S(1)}, u32[]{:S(2)}, u32[]{:S(2)}) collective-permute-start(bf16[2,272,1024]{2,1,0:T(8,128)(2,1)S(1)} %add_convert_fusion.2), channel_id=1, source_target_pairs={{0,24},{4,100},{8,0},{12,108},{16,8},{20,116},{24,16},{28,124},{32... | collective-permute-start | bytes 3342344 | tf_op jit(solution)/shard_map/ppermute | solution.py:736
  215.8 23.7 %collective-permute-start.33 = (bf16[2,272,1024]{2,1,0:T(8,128)(2,1)S(1)}, bf16[2,272,1024]{2,1,0:T(8,128)(2,1)S(1)}, u32[]{:S(2)}, u32[]{:S(2)}) collective-permute-start(bf16[2,272,1024]{2,1,0:T(8,128)(2,1)S(1)} %copy-done.27), channel_id=1, source_target_pairs={{0,24},{4,100},{8,0},{12,108},{16,8},{20,116},{24,16},{28,124},{32... | collective-permute-start | bytes 3342344 | tf_op jit(solution)/shard_map/ppermute | solution.py:736
  216.5 26.7 %collective-permute-start.32 = (bf16[2,272,1024]{2,1,0:T(8,128)(2,1)S(1)}, bf16[2,272,1024]{2,1,0:T(8,128)(2,1)S(1)}, u32[]{:S(2)}, u32[]{:S(2)}) collective-permute-start(bf16[2,272,1024]{2,1,0:T(8,128)(2,1)S(1)} %add_convert_fusion.3), channel_id=1, source_target_pairs={{0,8},{4,36},{8,16},{12,44},{16,24},{20,52},{24,0},{28,60},{32,40}... | collective-permute-start | bytes 3342344 | tf_op jit(solution)/shard_map/ppermute | solution.py:736
  227.9 25.3 %collective-permute-start.40 = (bf16[768,512]{1,0:T(8,128)(2,1)S(1)}, bf16[768,512]{1,0:T(8,128)(2,1)S(1)}, u32[]{:S(2)}, u32[]{:S(2)}) collective-permute-start(bf16[768,512]{1,0:T(8,128)(2,1)S(1)} %get-tuple-element.232), channel_id=1, source_target_pairs={{0,1},{1,2},{2,3},{3,0},{4,5},{5,6},{6,7},{7,4},{8,9},{9,10},{10,1... | collective-permute-start | bytes 2359304 | tf_op jit(solution)/shard_map/ppermute | solution.py:740
  228.0 25.2 %collective-permute-start.41 = (bf16[768,512]{1,0:T(8,128)(2,1)S(1)}, bf16[768,512]{1,0:T(8,128)(2,1)S(1)}, u32[]{:S(2)}, u32[]{:S(2)}) collective-permute-start(bf16[768,512]{1,0:T(8,128)(2,1)S(1)} %get-tuple-element.234), channel_id=1, source_target_pairs={{0,3},{1,0},{2,1},{3,2},{4,7},{5,4},{6,5},{7,6},{8,11},{9,8},{10,9... | collective-permute-start | bytes 2359304 | tf_op jit(solution)/shard_map/ppermute | solution.py:740
  232.0 18.9 %collective-permute-start.36 = (bf16[144,1024]{1,0:T(8,128)(2,1)S(1)}, bf16[144,1024]{1,0:T(8,128)(2,1)S(1)}, u32[]{:S(2)}, u32[]{:S(2)}) collective-permute-start(bf16[144,1024]{1,0:T(8,128)(2,1)S(1)} %get-tuple-element.320), channel_id=1, source_target_pairs={{0,32},{4,12},{8,40},{12,20},{16,48},{20,28},{24,56},{28,4},{32,64... | collective-permute-start | bytes 884744 | tf_op jit(solution)/shard_map/ppermute | solution.py:736
  247.2 10.8 %collective-permute-start.39 = (bf16[272,1024]{1,0:T(8,128)(2,1)S(1)}, bf16[272,1024]{1,0:T(8,128)(2,1)S(1)}, u32[]{:S(2)}, u32[]{:S(2)}) collective-permute-start(bf16[272,1024]{1,0:T(8,128)(2,1)S(1)} %pad_maximum_fusion.3), channel_id=1, source_target_pairs={{0,96},{4,28},{8,104},{12,4},{16,112},{20,12},{24,120},{28,20},{32... | collective-permute-start | bytes 1671176 | tf_op jit(solution)/shard_map/ppermute | solution.py:736
  251.1 10.8 %collective-permute-start.37 = (bf16[272,1024]{1,0:T(8,128)(2,1)S(1)}, bf16[272,1024]{1,0:T(8,128)(2,1)S(1)}, u32[]{:S(2)}, u32[]{:S(2)}) collective-permute-start(bf16[272,1024]{1,0:T(8,128)(2,1)S(1)} %pad_maximum_fusion.2), channel_id=1, source_target_pairs={{0,32},{4,12},{8,40},{12,20},{16,48},{20,28},{24,56},{28,4},{32,64... | collective-permute-start | bytes 1671176 | tf_op jit(solution)/shard_map/ppermute | solution.py:736
  265.7 22.3 %collective-permute-start.42 = (bf16[256,1024]{1,0:T(8,128)(2,1)}, bf16[256,1024]{1,0:T(8,128)(2,1)S(1)}, u32[]{:S(2)}, u32[]{:S(2)}) collective-permute-start(bf16[256,1024]{1,0:T(8,128)(2,1)} %get-tuple-element.242.refs_0_.refs_13_), channel_id=1, source_target_pairs={{0,3},{1,0},{2,1},{3,2},{4,7},{5,4},{6,5},{7,6},{8,11},{9,8},{10,9... | collective-permute-start | bytes 1572872 | tf_op jit(solution)/shard_map/ppermute | solution.py:740
  266.7 28.8 %collective-permute-start.43 = (bf16[256,1024]{1,0:T(8,128)(2,1)}, bf16[256,1024]{1,0:T(8,128)(2,1)S(1)}, u32[]{:S(2)}, u32[]{:S(2)}) collective-permute-start(bf16[256,1024]{1,0:T(8,128)(2,1)} %get-tuple-element.242.refs_0_.refs_13_), channel_id=1, source_target_pairs={{0,1},{1,2},{2,3},{3,0},{4,5},{5,6},{6,7},{7,4},{8,9},{9,10},{10,1... | collective-permute-start | bytes 1572872 | tf_op jit(solution)/shard_map/ppermute | solution.py:740
  267.8 41.1 %collective-permute-start.49 = (bf16[768,512]{1,0:T(8,128)(2,1)}, bf16[768,512]{1,0:T(8,128)(2,1)S(1)}, u32[]{:S(2)}, u32[]{:S(2)}) collective-permute-start(bf16[768,512]{1,0:T(8,128)(2,1)} %copy-done.6), channel_id=1, source_target_pairs={{0,2},{1,3},{2,0},{3,1},{4,6},{5,7},{6,4},{7,5},{8,10},{9,11},{10,... | collective-permute-start | bytes 2359304 | tf_op jit(solution)/shard_map/ppermute | solution.py:740
  295.6 9.5 %collective-permute-start.44 = (bf16[128,1024]{1,0:T(8,128)(2,1)S(1)}, bf16[128,1024]{1,0:T(8,128)(2,1)S(1)}, u32[]{:S(2)}, u32[]{:S(2)}) collective-permute-start(bf16[128,1024]{1,0:T(8,128)(2,1)S(1)} %slice.92), channel_id=1, source_target_pairs={{0,3},{1,0},{2,1},{3,2},{4,7},{5,4},{6,5},{7,6},{8,11},{9,8},{10,9... | collective-permute-start | bytes 786440 | tf_op jit(solution)/shard_map/ppermute | solution.py:740
  295.7 10.9 %collective-permute-start.45 = (bf16[128,1024]{1,0:T(8,128)(2,1)S(1)}, bf16[128,1024]{1,0:T(8,128)(2,1)S(1)}, u32[]{:S(2)}, u32[]{:S(2)}) collective-permute-start(bf16[128,1024]{1,0:T(8,128)(2,1)S(1)} %slice.93), channel_id=1, source_target_pairs={{0,1},{1,2},{2,3},{3,0},{4,5},{5,6},{6,7},{7,4},{8,9},{9,10},{10,1... | collective-permute-start | bytes 786440 | tf_op jit(solution)/shard_map/ppermute | solution.py:740
  306.6 10.8 %collective-permute-start.48 = (f32[40,1024]{1,0:T(8,128)S(1)}, f32[40,1024]{1,0:T(8,128)S(1)}, u32[]{:S(2)}, u32[]{:S(2)}) collective-permute-start(f32[40,1024]{1,0:T(8,128)S(1)} %copy-done.23), channel_id=1, source_target_pairs={{0,3},{1,0},{2,1},{3,2},{4,7},{5,4},{6,5},{7,6},{8,11},{9,8},{10,9... | collective-permute-start | bytes 491528 | tf_op jit(solution)/shard_map/ppermute | solution.py:740
  306.7 10.7 %collective-permute-start.47 = (f32[40,1024]{1,0:T(8,128)S(1)}, f32[40,1024]{1,0:T(8,128)S(1)}, u32[]{:S(2)}, u32[]{:S(2)}) collective-permute-start(f32[40,1024]{1,0:T(8,128)S(1)} %copy-done.23), channel_id=1, source_target_pairs={{0,2},{1,3},{2,0},{3,1},{4,6},{5,7},{6,4},{7,5},{8,10},{9,11},{10,... | collective-permute-start | bytes 491528 | tf_op jit(solution)/shard_map/ppermute | solution.py:740
  307.2 10.2 %collective-permute-start.46 = (f32[40,1024]{1,0:T(8,128)S(1)}, f32[40,1024]{1,0:T(8,128)S(1)}, u32[]{:S(2)}, u32[]{:S(2)}) collective-permute-start(f32[40,1024]{1,0:T(8,128)S(1)} %copy-done.23), channel_id=1, source_target_pairs={{0,1},{1,2},{2,3},{3,0},{4,5},{5,6},{6,7},{7,4},{8,9},{9,10},{10,1... | collective-permute-start | bytes 491528 | tf_op jit(solution)/shard_map/ppermute | solution.py:740
  341.1 15.5 %collective-permute-start.54 = (bf16[19,32,768]{2,1,0:T(8,128)(2,1)S(1)}, bf16[19,32,768]{2,1,0:T(8,128)(2,1)S(1)}, u32[]{:S(2)}, u32[]{:S(2)}) collective-permute-start(bf16[19,32,768]{2,1,0:T(8,128)(2,1)S(1)} %get-tuple-element.298), channel_id=1, source_target_pairs={{0,4},{4,0},{8,12},{12,8},{16,20},{20,16},{24,28},{28,24},{32,36},... | collective-permute-start | bytes 2801672 | tf_op jit(solution)/shard_map/ppermute | solution.py:725
  341.2 9.9 %collective-permute-start.50 = (bf16[128,1024]{1,0:T(8,128)(2,1)S(1)}, bf16[128,1024]{1,0:T(8,128)(2,1)S(1)}, u32[]{:S(2)}, u32[]{:S(2)}) collective-permute-start(bf16[128,1024]{1,0:T(8,128)(2,1)S(1)} %get-tuple-element.292), channel_id=1, source_target_pairs={{0,1},{1,2},{2,3},{3,0},{4,5},{5,6},{6,7},{7,4},{8,9},{9,10},{10,1... | collective-permute-start | bytes 786440 | tf_op jit(solution)/shard_map/ppermute | solution.py:740
  342.8 9.4 %collective-permute-start.51 = (bf16[128,1024]{1,0:T(8,128)(2,1)S(1)}, bf16[128,1024]{1,0:T(8,128)(2,1)S(1)}, u32[]{:S(2)}, u32[]{:S(2)}) collective-permute-start(bf16[128,1024]{1,0:T(8,128)(2,1)S(1)} %get-tuple-element.293), channel_id=1, source_target_pairs={{0,3},{1,0},{2,1},{3,2},{4,7},{5,4},{6,5},{7,6},{8,11},{9,8},{10,9... | collective-permute-start | bytes 786440 | tf_op jit(solution)/shard_map/ppermute | solution.py:740
  353.2 15.0 %collective-permute-start.52 = (bf16[256,1024]{1,0:T(8,128)(2,1)}, bf16[256,1024]{1,0:T(8,128)(2,1)S(1)}, u32[]{:S(2)}, u32[]{:S(2)}) collective-permute-start(bf16[256,1024]{1,0:T(8,128)(2,1)} %get-tuple-element.294), channel_id=1, source_target_pairs={{0,1},{1,2},{2,3},{3,0},{4,5},{5,6},{6,7},{7,4},{8,9},{9,10},{10,1... | collective-permute-start | bytes 1572872 | tf_op jit(solution)/shard_map/ppermute | solution.py:740
  355.0 13.2 %collective-permute-start.53 = (bf16[256,1024]{1,0:T(8,128)(2,1)S(1)}, bf16[256,1024]{1,0:T(8,128)(2,1)S(1)}, u32[]{:S(2)}, u32[]{:S(2)}) collective-permute-start(bf16[256,1024]{1,0:T(8,128)(2,1)S(1)} %get-tuple-element.295), channel_id=1, source_target_pairs={{0,3},{1,0},{2,1},{3,2},{4,7},{5,4},{6,5},{7,6},{8,11},{9,8},{10,9... | collective-permute-start | bytes 1572872 | tf_op jit(solution)/shard_map/ppermute | solution.py:740
  357.6 11.9 %collective-permute-start.55 = (bf16[208,768]{1,0:T(8,128)(2,1)}, bf16[208,768]{1,0:T(8,128)(2,1)S(1)}, u32[]{:S(2)}, u32[]{:S(2)}) collective-permute-start(bf16[208,768]{1,0:T(8,128)(2,1)} %get-tuple-element.301), channel_id=1, source_target_pairs={{0,32},{4,12},{8,40},{12,20},{16,48},{20,28},{24,56},{28,4},{32,64... | collective-permute-start | bytes 958472 | tf_op jit(solution)/shard_map/ppermute | solution.py:736
  357.7 11.8 %collective-permute-start.56 = (bf16[208,768]{1,0:T(8,128)(2,1)}, bf16[208,768]{1,0:T(8,128)(2,1)S(1)}, u32[]{:S(2)}, u32[]{:S(2)}) collective-permute-start(bf16[208,768]{1,0:T(8,128)(2,1)} %get-tuple-element.302), channel_id=1, source_target_pairs={{0,64},{4,20},{8,72},{12,28},{16,80},{20,4},{24,88},{28,12},{32,96... | collective-permute-start | bytes 958472 | tf_op jit(solution)/shard_map/ppermute | solution.py:736
  360.3 10.1 %collective-permute-start.57 = (bf16[208,768]{1,0:T(8,128)(2,1)}, bf16[208,768]{1,0:T(8,128)(2,1)S(1)}, u32[]{:S(2)}, u32[]{:S(2)}) collective-permute-start(bf16[208,768]{1,0:T(8,128)(2,1)} %get-tuple-element.303), channel_id=1, source_target_pairs={{0,96},{4,28},{8,104},{12,4},{16,112},{20,12},{24,120},{28,20},{32... | collective-permute-start | bytes 958472 | tf_op jit(solution)/shard_map/ppermute | solution.py:736
  (47 other events, 509.8 us)
Sparse Core Ops, SparseCore 0:
  35.9 70.8 all-gather.2
  265.9 82.3 reduce-scatter.1

commit v3 on v2

--- a/solution.py
+++ b/solution.py
@@ -111,12 +111,10 @@
             one.wait()
 
     def placed(i, one):
-        if i in any_in and i not in aliases:
-            return one
         return pltpu.with_memory_space_constraint(one, pltpu.VMEM if i in local else pltpu.HBM)
 
     def space(i):
-        return pltpu.VMEM if i in local else pl.ANY if i in any_in and i not in aliases else pltpu.HBM
+        return pltpu.VMEM if i in local else pltpu.HBM
 
     args = [placed(i, one) for i, one in enumerate(args)]
     in_specs = [pl.BlockSpec(memory_space=space(i)) for i in range(len(args))]
@@ -137,12 +135,8 @@
     )(*args)
 
 
-def start_body(sc, cot, routes, packed, ranks_out):
-    base = sc[0] * TOK
-    length = sc[1]
-    place = base + lax.broadcasted_iota(jnp.int32, (TOK, 1), 0)
-    keep = jnp.where(place < length, 1.0, 0.0)
-    packed[0:TOK, :] = (cot[...].astype(F32) * keep).astype(BF16)
+def start_body(sc, routes, ranks_out, coded):
+    place = sc[0] * TOK + lax.broadcasted_iota(jnp.int32, (1, TOK), 1)
     names = lax.broadcasted_iota(jnp.int32, (TOK, EXPERTS), 1)
     member = jnp.zeros((TOK, EXPERTS), F32)
     for k in range(routes.shape[1]):
@@ -152,21 +146,21 @@
     later = lax.broadcasted_iota(jnp.int32, (TOK, TOK), 1)
     before = jnp.where(earlier < later, 1.0, 0.0).astype(BF16)
     same = jnp.where(earlier == later, 1.0, 0.0).astype(BF16)
-    counts = tn(member, before)
-    chosen = tn(member, same)
-    ranks = jnp.where(chosen > 0.5, counts, -1.0)
+    routed = tn(member, same) > 0.5
+    ranks = jnp.where(routed, tn(member, before), -1.0)
     ranks_out[...] = ranks
+    ranks = jnp.where(routed & (place >= sc[1]), ranks + 128.0, ranks)
     quarter = EXPERTS // 4
     rows = jnp.concatenate([ranks[q * quarter : (q + 1) * quarter] for q in range(4)], axis=1)
-    packed[TOK:ROWS, :] = jnp.concatenate([rows, jnp.zeros_like(rows)], axis=0).astype(BF16)
+    coded[...] = jnp.concatenate([rows, jnp.zeros_like(rows)], axis=0).astype(BF16)
 
 
 def project_body(sc, own, other, x0, x1, x2, x3, gain, head_gain, cos, sin, spread4, spread2, *refs, wait):
     wait(0, 1)
     outs, raws, pairs, queries, ka, va, out_w, turns = (
-        refs[:2], refs[2:6], refs[6:10], refs[10:14], refs[14], refs[15], refs[16], refs[17:21]
-    )
-    h1, raw_hold, pair_hold, proj, held, sems = refs[21:]
+        refs[:3], refs[3:7], refs[7:11], refs[11:15], refs[15], refs[16], refs[17], refs[18:22]
+    )
+    h1, raw_hold, pair_hold, proj, held, sems = refs[22:]
     y_at, z_at, core, mp_at, length = sc[0], sc[1], sc[2], sc[3], sc[4]
     for block in range(16):
         y_rel = (block // 4 - y_at + 4) % 4
@@ -182,8 +176,12 @@
     proj[:, 512:768] = nn(held[:, 256:384], spread2[...]).astype(BF16)
     proj[:, 768:1024] = nn(held[:, 384:512], spread2[...]).astype(BF16)
     out_w[...] = nn(held[:, 512:768], spread4[...]).astype(BF16)
-    copies = [pltpu.make_async_copy(proj, outs[1], sems.at[12])]
-    copies[0].start()
+    copies = [
+        pltpu.make_async_copy(proj, outs[1], sems.at[12]),
+        pltpu.make_async_copy(held, outs[2], sems.at[13]),
+    ]
+    for one in copies:
+        one.start()
     lane = lanes((TOK, PITCH))
     below = lax.broadcasted_iota(jnp.int32, (TOK, PITCH), 0)
     q_aug = jnp.where(lane == HDIM, 1.0, 0.0)
@@ -254,13 +252,14 @@
     branch[...] = nt(mixed[...], out_w[...]).astype(BF16)
 
 
-def middle_body(x, p0, p1, p2, p3, gain, x_mid, h2):
+def middle_body(x, p0, p1, p2, p3, gain, coded, x_mid, h2):
     total = (
         x[...].astype(F32)
         + ((p0[...].astype(F32) + p1[...].astype(F32)) + (p2[...].astype(F32) + p3[...].astype(F32)))
     )
     x_mid[...] = total
-    h2[...] = (total * row_scale(total) * gain[...]).astype(BF16)
+    h2[0:TOK, :] = (total * row_scale(total) * gain[...]).astype(BF16)
+    h2[TOK:ROWS, :] = coded[...]
 
 
 def gates_of(logits, ranks):
@@ -271,63 +270,34 @@
 
 
 def gates_body(h2, router, ranks, gates):
-    gates[...] = gates_of(nt(router[...], h2[...]), ranks[...])
+    gates[...] = gates_of(nt(router[...], h2[0:TOK, :]), ranks[...])
 
 
 def unfold(rows):
     return jnp.concatenate([rows[:, q * TOK : (q + 1) * TOK] for q in range(4)], axis=0)
 
 
-def experts_body(pieces, unit, *refs):
+def experts_body(pieces, unit, *refs, wait):
     sc = refs[0]
     tokens = refs[1 : 1 + len(pieces)]
     at = 1 + len(pieces)
     cot_all, router = refs[at], refs[at + 1]
-    weights_in = refs[at + 2 : at + 8]
+    weights = refs[at + 2 : at + 8]
     at = at + 8
     if unit > 0:
         at = at + 6
     y_out, back_a, back_b, taken_all, push_all, hidden_all, gate_all, up_all = refs[at : at + 8]
-    (tok, cot, gate_v, up_v, down_v, y_hold, y_back, t_hold, e_hold, h_hold, g_hold, u_hold, sems) = refs[at + 8 :]
+    cot, y_hold, y_back, t_hold, r_hold, e_hold, h_hold, g_hold, u_hold, sems = refs[at + 8 :]
     cot_in = [pltpu.make_async_copy(cot_all.at[sc[i]], cot.at[i], sems.at[i]) for i in range(4)]
-    tok_in = []
-    for index, count in enumerate(pieces):
-        for j in range(count):
-            i = len(tok_in)
-            tok_in.append(pltpu.make_async_copy(tokens[index].at[j], tok.at[i], sems.at[4 + i]))
-    weight_in = []
-    for e in range(2):
-        for j, hold in enumerate((gate_v, up_v, down_v)):
-            weight_in.append(
-                pltpu.make_async_copy(weights_in[3 * e + j].at[0], hold.at[e], sems.at[8 + 3 * e + j])
-            )
-    for one in cot_in + tok_in + weight_in:
+    for one in cot_in:
         one.start()
+    tok = [(tokens[index], j) for index, count in enumerate(pieces) for j in range(count)]
     own_names = (sc[4], sc[5])
     names = lax.broadcasted_iota(jnp.int32, (EXPERTS, TOK), 0)
     slots = lax.broadcasted_iota(jnp.int32, (CAP, TOK), 0).astype(F32)
-    picks = [[], []]
-    gate_rows = [[], []]
-    for i in range(4):
-        cot_in[i].wait()
-        tok_in[i].wait()
-        block = tok[i]
-        ranks = unfold(cot[i, TOK : TOK + EXPERTS // 4, :].astype(F32))
-        gates = gates_of(nt(router[...], block), ranks)
-        for e in range(2):
-            hit = names == own_names[e]
-            rank = jnp.sum(jnp.where(hit, ranks, 0.0), axis=0, keepdims=True)
-            gate = jnp.sum(jnp.where(hit, gates, 0.0), axis=0, keepdims=True)
-            pick = jnp.where(slots == rank, 1.0, 0.0)
-            picks[e].append(pick.astype(BF16))
-            gate_rows[e].append(jnp.sum(pick * gate, axis=1, keepdims=True))
-    taken_rows = [nn(jnp.concatenate([picks[0][i], picks[1][i]], axis=0), tok[i]) for i in range(4)]
-    grad_rows_all = [
-        nn(jnp.concatenate([picks[0][i], picks[1][i]], axis=0), cot[i, 0:TOK, :]) for i in range(4)
-    ]
-    marks = [[], []]
-    back_parts = []
-    out_parts = []
+    picks, live_picks = [[], []], [[], []]
+    gate_cols = [[], []]
+    all_ranks = []
     copies_out = []
 
     def put(source, target, sem):
@@ -335,43 +305,77 @@
         one.start()
         copies_out.append(one)
 
+    for i in range(4):
+        ref, j = tok[i]
+        rows = slice(i * CAP, (i + 1) * CAP)
+        ranks = unfold(ref[j, TOK : TOK + EXPERTS // 4, :].astype(F32))
+        all_ranks.append(ranks)
+        for e in range(2):
+            rank = jnp.sum(jnp.where(names == own_names[e], ranks, 0.0), axis=0, keepdims=True)
+            live_picks[e].append(jnp.where(slots == rank, 1.0, 0.0).astype(BF16))
+            picks[e].append(jnp.where((slots == rank) | (slots + 128.0 == rank), 1.0, 0.0).astype(BF16))
+        got = nn(jnp.concatenate([picks[0][i], picks[1][i]], axis=0), ref[j, 0:TOK, :]).astype(BF16)
+        t_hold[0, rows, :] = got[:CAP]
+        t_hold[1, rows, :] = got[CAP:]
+    wait(len(pieces) + 1)
+    for i in range(4):
+        ref, j = tok[i]
+        gates = gates_of(nt(router[...], ref[j, 0:TOK, :]), all_ranks[i])
+        for e in range(2):
+            gate = jnp.sum(jnp.where(names == own_names[e], gates, 0.0), axis=0, keepdims=True)
+            gate_cols[e].append(jnp.sum(picks[e][i].astype(F32) * gate, axis=1, keepdims=True))
+    here = pl.ds(unit * 4 * CAP, 4 * CAP)
+    kept = []
+    out_parts = []
     for e in range(2):
-        half = slice(e * CAP, (e + 1) * CAP)
-        here = pl.ds(unit * 4 * CAP, 4 * CAP)
-        for i in range(4):
-            t_hold[e, i * CAP : (i + 1) * CAP, :] = taken_rows[i][half].astype(BF16)
+        gate_w, up_w, down_w = weights[3 * e : 3 * e + 3]
         put(t_hold.at[e], taken_all.at[e, here], 14 + 5 * e)
         taken = t_hold[e]
-        for one in weight_in[3 * e : 3 * e + 2]:
-            one.wait()
-        gate_act = nn(taken, gate_v[e])
-        up_act = nn(taken, up_v[e])
+        gate_act = nn(taken, gate_w[0])
+        up_act = nn(taken, up_w[0])
         sigma = jax.nn.sigmoid(gate_act)
         silu = gate_act * sigma
+        slope = up_act * (sigma + silu * (1.0 - sigma))
         hidden = (silu * up_act).astype(BF16)
         h_hold[e] = hidden
         put(h_hold.at[e], hidden_all.at[e, here], 15 + 5 * e)
-        weight_in[3 * e + 2].wait()
-        result = nn(hidden, down_v[e]).astype(BF16).astype(F32)
-        gate_col = jnp.concatenate(gate_rows[e], axis=0)
-        grad_rows = jnp.concatenate([grad_rows_all[i][half] for i in range(4)], axis=0)
-        mark = jnp.sum(grad_rows * result, axis=1, keepdims=True)
-        for i in range(4):
-            marks[e].append(
-                jnp.sum(picks[e][i].astype(F32) * mark[i * CAP : (i + 1) * CAP], axis=0, keepdims=True)
-            )
-        out_parts.append((result * gate_col).astype(BF16))
+        result = nn(hidden, down_w[0]).astype(BF16)
+        gate_col = jnp.concatenate(gate_cols[e], axis=0)
+        kept.append((silu, slope, result, gate_col))
+        out_parts.append((result.astype(F32) * gate_col).astype(BF16))
+    for i in range(4):
+        pick = jnp.concatenate([picks[0][i], picks[1][i]], axis=0)
+        rows = slice(i * CAP, (i + 1) * CAP)
+        y_hold[i] = tn(pick, jnp.concatenate([out_parts[0][rows], out_parts[1][rows]], axis=0)).astype(BF16)
+        put(y_hold.at[i], y_out.at[sc[i]], 28 + i)
+    for i in range(4):
+        rows = slice(i * CAP, (i + 1) * CAP)
+        cot_in[i].wait()
+        got = nn(jnp.concatenate([live_picks[0][i], live_picks[1][i]], axis=0), cot[i]).astype(BF16)
+        r_hold[0, rows, :] = got[:CAP]
+        r_hold[1, rows, :] = got[CAP:]
+    marks = [[], []]
+    back_parts = []
+    for e in range(2):
+        gate_w, up_w, down_w = weights[3 * e : 3 * e + 3]
+        silu, slope, result, gate_col = kept[e]
+        grad_rows = r_hold[e].astype(F32)
         push = (grad_rows * gate_col).astype(BF16)
         e_hold[e] = push
         put(e_hold.at[e], push_all.at[e, here], 16 + 5 * e)
-        grad_hidden = nt(push, down_v[e])
-        grad_gate = (grad_hidden * up_act * (sigma * (1.0 + gate_act * (1.0 - sigma)))).astype(BF16)
+        grad_hidden = nt(push, down_w[0])
+        grad_gate = (grad_hidden * slope).astype(BF16)
         grad_up = (grad_hidden * silu).astype(BF16)
         g_hold[e] = grad_gate
         u_hold[e] = grad_up
         put(g_hold.at[e], gate_all.at[e, here], 17 + 5 * e)
         put(u_hold.at[e], up_all.at[e, here], 18 + 5 * e)
-        back_parts.append((nt(grad_gate, gate_v[e]) + nt(grad_up, up_v[e])).astype(BF16))
+        back_parts.append((nt(grad_gate, gate_w[0]) + nt(grad_up, up_w[0])).astype(BF16))
+        mark = jnp.sum(grad_rows * result.astype(F32), axis=1, keepdims=True)
+        for i in range(4):
+            marks[e].append(
+                jnp.sum(picks[e][i].astype(F32) * mark[i * CAP : (i + 1) * CAP], axis=0, keepdims=True)
+            )
     for i in range(4):
         pick = jnp.concatenate([picks[0][i], picks[1][i]], axis=0)
         rows = slice(i * CAP, (i + 1) * CAP)
@@ -390,86 +394,103 @@
         ]
         y_back[i, TOK:ROWS, :] = jnp.concatenate(fold, axis=0).astype(BF16)
         put(y_back.at[i], (back_a if i < 2 else back_b).at[i % 2], 24 + i)
-    for i in range(4):
-        pick = jnp.concatenate([picks[0][i], picks[1][i]], axis=0)
-        rows = slice(i * CAP, (i + 1) * CAP)
-        y_hold[i] = tn(pick, jnp.concatenate([out_parts[0][rows], out_parts[1][rows]], axis=0)).astype(BF16)
-        put(y_hold.at[i], y_out.at[sc[i]], 28 + i)
     for one in copies_out:
         one.wait()
 
 
-def expert_weights_body(joined, sc, taken, push, hidden, gate, up, *refs):
-    got, refs = (refs[:3], refs[3:]) if joined else ((), refs)
-    outs, (gate_sum, up_sum, down_sum) = refs[:-3], refs[-3:]
-    step = pl.program_id(0)
-
-    @pl.when(step == 0)
-    def _():
-        gate_sum[...] = tn(taken[0], gate[0])
-        up_sum[...] = tn(taken[0], up[0])
-        down_sum[...] = tn(hidden[0], push[0])
-
-    @pl.when(step > 0)
-    def _():
-        gate_sum[...] += tn(taken[0], gate[0])
-        up_sum[...] += tn(taken[0], up[0])
-        down_sum[...] += tn(hidden[0], push[0])
-
-    @pl.when(step == pl.num_programs(0) - 1)
-    def _():
-        if not joined:
-            for target, total in zip(outs, (gate_sum, up_sum, down_sum)):
-                target[...] = total[...].astype(BF16)
-            return
-        for part in range(4):
-            at = (sc[0] + part) % 4
-            out = outs[part]
-            rows = pl.ds(pl.multiple_of(at * 256, 256), 256)
-            out[0:256, :] = (gate_sum[rows, :] + got[0][rows, :].astype(F32)).astype(BF16)
-            out[256:512, :] = (up_sum[rows, :] + got[1][rows, :].astype(F32)).astype(BF16)
-            rows = pl.ds(pl.multiple_of(at * 128, 128), 128)
-            down = (down_sum[rows, :] + got[2][rows, :].astype(F32)).astype(BF16)
-            out[512:640, :] = down[:, 0:FF]
-            out[640:768, :] = down[:, FF:WIDTH]
+def expert_weights_body(expert, sc, *refs):
+    count = 5 + (1 - expert)
+    sources, outs = refs[:5], refs[count : count + (1 if expert == 1 else 5)]
+    holds, sums, sems = refs[len(refs) - 9 : len(refs) - 4], refs[len(refs) - 4 : len(refs) - 1], refs[-1]
+    copies = [pltpu.make_async_copy(one.at[expert], hold, sems.at[n]) for n, (one, hold) in enumerate(zip(sources, holds))]
+    for one in copies:
+        one.start()
+    taken, gate, up, hidden, push = holds
+    copies[0].wait()
+    copies[1].wait()
+    sums[0][...] = tn(taken[...], gate[...])
+    copies[2].wait()
+    sums[1][...] = tn(taken[...], up[...])
+    copies[3].wait()
+    copies[4].wait()
+    sums[2][...] = tn(hidden[...], push[...])
+    if expert == 1:
+        (out,) = outs
+        out[0:1024, :] = sums[0][...].astype(BF16)
+        out[1024:2048, :] = sums[1][...].astype(BF16)
+        out[2048:2560, :] = sums[2][:, 0:FF].astype(BF16)
+        out[2560:3072, :] = sums[2][:, FF:WIDTH].astype(BF16)
+        return
+    got = refs[5]
+    for part in range(4):
+        at = (sc[0] + part) % 4
+        rows = pl.ds(pl.multiple_of(at * 256, 256), 256)
+
+        def put(start, value):
+            if part == 2:
+                outs[3 + start // 384][start % 384 : start % 384 + 128, :] = value.astype(BF16)
+            else:
+                outs[min(part, 2)][start : start + 128, :] = value.astype(BF16)
+
+        def more(start, count):
+            return got[pl.ds(pl.multiple_of(start + at * count, count), count), :].astype(F32)
+
+        for n, start in enumerate((0, 1024)):
+            value = sums[n][rows, :] + more(start, 256)
+            put(256 * n, value[0:128])
+            put(256 * n + 128, value[128:256])
+        rows = pl.ds(pl.multiple_of(at * 128, 128), 128)
+        put(512, sums[2][rows, 0:FF] + more(2048, 128))
+        put(640, sums[2][rows, FF:WIDTH] + more(2560, 128))
+
+
+def shard_near_body(up, down, far_up, far_down, out_up, out_down):
+    out_up[0:384, :] = (up[0:384, :].astype(F32) + far_up[...].astype(F32)).astype(BF16)
+    out_up[384:768, :] = up[384:768, :]
+    out_down[0:384, :] = down[0:384, :]
+    out_down[384:768, :] = (down[384:768, :].astype(F32) + far_down[...].astype(F32)).astype(BF16)
 
 
 def expert_weights(saved, expert, mp_at, got=()):
-    widths = [one.shape[2] for one in saved]
-    saved = [pltpu.with_memory_space_constraint(one, pltpu.HBM) for one in saved]
-    got = [pltpu.with_memory_space_constraint(one, pltpu.VMEM) for one in got]
-    rows = 4 * CAP
-    shapes = [((768, FF), BF16)] * 4 if got else [((WIDTH, FF), BF16), ((WIDTH, FF), BF16), ((FF, WIDTH), BF16)]
-    return pl.pallas_call(
-        partial(expert_weights_body, bool(got)),
-        out_shape=[jax.ShapeDtypeStruct(s, d) for s, d in shapes],
-        grid=(4,),
-        in_specs=[pl.BlockSpec(memory_space=pltpu.SMEM)]
-        + [pl.BlockSpec((1, rows, w), lambda step: (expert, step, 0)) for w in widths]
-        + [pl.BlockSpec(memory_space=pltpu.VMEM) for _ in got],
-        out_specs=[pl.BlockSpec(memory_space=pltpu.VMEM) for _ in shapes],
-        scratch_shapes=[pltpu.VMEM((WIDTH, FF), F32), pltpu.VMEM((WIDTH, FF), F32), pltpu.VMEM((FF, WIDTH), F32)],
-        compiler_params=pltpu.CompilerParams(vmem_limit_bytes=40 * 1024 * 1024),
-        cost_estimate=pl.CostEstimate(flops=1, bytes_accessed=1, transcendentals=0),
-    )(mp_at.reshape(1), *saved, *got)
-
-
-def token_back_body(r0, r1, r2, h2, x_mid, ranks, gates, router, gain, packed, grad_mid, branch, small):
+    taken, push, hidden, gate, up = saved
+    sources = (taken, gate, up, hidden, push)
+    shapes = [((3072, FF), BF16)] if expert == 1 else [((768, FF), BF16)] * 3 + [((384, FF), BF16)] * 2
+    return call(
+        partial(expert_weights_body, expert),
+        shapes,
+        (*sources, *got),
+        scalars=mp_at.reshape(1),
+        any_in=range(5),
+        scratch=[pltpu.VMEM(one.shape[1:], one.dtype) for one in sources]
+        + [pltpu.VMEM((WIDTH, FF), F32), pltpu.VMEM((WIDTH, FF), F32), pltpu.VMEM((FF, WIDTH), F32)]
+        + [pltpu.SemaphoreType.DMA((5,))],
+        near=range(len(shapes)),
+        local=range(5, 5 + len(got)),
+        mb=36,
+    )
+
+
+def token_back_body(sc, r0, r1, r2, h2, x_mid, ranks, gates, router, gain, cot, grad_mid, branch, small):
     total = r0[...].astype(F32) + (r1[...].astype(F32) + r2[...].astype(F32))
     marks = unfold(total[TOK : TOK + 8]) + unfold(total[TOK + 8 : TOK + 16])
     gate = gates[...]
     centre = jnp.sum(gate * marks, axis=0, keepdims=True)
     grad_logits = jnp.where(ranks[...] >= 0.0, gate * (marks - centre), 0.0).astype(BF16)
-    small[0:EXPERTS, :] = nn(grad_logits, h2[...])
+    router_part = nn(grad_logits, h2[0:TOK, :])
+    small[0:32, :] = router_part[:, 0:768]
+    small[32:48, 0:256] = router_part[0:16, 768:1024]
+    small[32:48, 256:512] = router_part[16:32, 768:1024]
+    small[32:48, 512:768] = jnp.zeros((16, 256), F32)
     grad_h2 = total[0:TOK] + tn(grad_logits, router[...])
     x = x_mid[...]
     scale = row_scale(x)
     normed = x * scale
     grad_normed = grad_h2 * gain[...]
-    small[EXPERTS : EXPERTS + 8, :] = jnp.broadcast_to(
-        jnp.sum(grad_h2 * normed, axis=0, keepdims=True), (8, WIDTH)
-    )
-    out = packed[0:TOK, :].astype(F32) + scale * (
+    gain_part = jnp.sum(grad_h2 * normed, axis=0, keepdims=True)
+    for quarter in range(4):
+        small[32 + quarter : 33 + quarter, 512:768] = gain_part[:, quarter * 256 : (quarter + 1) * 256]
+    place = sc[0] * TOK + lax.broadcasted_iota(jnp.int32, (TOK, 1), 0)
+    out = cot[...].astype(F32) * jnp.where(place < sc[1], 1.0, 0.0) + scale * (
         grad_normed - normed * jnp.mean(grad_normed * normed, axis=1, keepdims=True)
     )
     grad_mid[...] = out
@@ -542,8 +563,8 @@
 
 
 def keys_back_body(*refs, wait):
-    both, raws, turns, head_gain, query, proj, x = refs[0], refs[1:5], refs[5:9], refs[9], refs[10], refs[11], refs[12]
-    far_up, far_down, wide, gains = refs[13:]
+    both, raws, turns, head_gain, query, proj = refs[0], refs[1:5], refs[5:9], refs[9], refs[10], refs[11]
+    far_up, far_down, wide, gains = refs[12:]
     half = TOK // 2
     lane = lanes((TOK, PITCH))
     key_gain = jnp.zeros((1, PITCH), F32)
@@ -563,61 +584,66 @@
             wide[at, 256 + head * PITCH : 384 + head * PITCH] = jnp.where(
                 lane < HDIM, both[head, at, PITCH : 2 * PITCH], 0.0
             ).astype(BF16)
-    wait(10, 11, 12)
+    wait(10, 11)
     part = nt(query[...], proj[:, 0:512]) + nt(wide[2 * TOK : 3 * TOK, :], proj[:, 512:1024])
     far_up[...] = part[:half].astype(BF16)
     far_down[...] = part[half:].astype(BF16)
-    xf = x[...].astype(F32)
-    gains[...] = jnp.zeros((8, WIDTH), F32)
-    gains[0:1, :] = jnp.sum(part * (xf * row_scale(xf)), axis=0, keepdims=True)
-    gains[1:2, 0:PITCH] = key_gain
+    gains[...] = jnp.broadcast_to(key_gain, (8, PITCH))
+
+
+def parts_body(*refs, wait):
+    wide, far_up, far_down, proj, queries, outs = refs[0], refs[1], refs[2], refs[3], refs[4:7], refs[7:10]
+    half = TOK // 2
+    wait(3)
+    for n, chunk in enumerate((1, 3, 0)):
+        wait(4 + n)
+        at = slice(chunk * TOK, (chunk + 1) * TOK)
+        part = nt(queries[n][...], proj[:, 0:512]) + nt(wide[at, :], proj[:, 512:1024])
+        if chunk == 1:
+            outs[n][:half, :] = (part[:half] + far_up[...].astype(F32)).astype(BF16)
+            outs[n][half:, :] = part[half:].astype(BF16)
+        elif chunk == 3:
+            outs[n][:half, :] = part[:half].astype(BF16)
+            outs[n][half:, :] = (part[half:] + far_down[...].astype(F32)).astype(BF16)
+        else:
+            outs[n][...] = part.astype(BF16)
 
 
 def tail_body(*refs, wait):
     sc, refs = refs[0], refs[1:]
-    wide, gains_in, small, spread2, spread4 = refs[0:5]
-    queries, proj, xs, rows, mixed, h1, slims, query_gains = (
-        refs[5:8], refs[8], refs[9:12], refs[12:16], refs[16:20], refs[20], refs[21:25], refs[25:29]
-    )
-    p1, p3, p0, keep, send, extra = refs[29:35]
-    (slim_pair,) = refs[35:]
+    wide, key_gain, small, spread2, spread4, weights, gain_row = refs[0:7]
+    rows, mixed, h1, slims, query_gains = refs[7:11], refs[11:15], refs[15], refs[16:20], refs[20:24]
+    keep, send, extra = refs[24:27]
+    (slim_pair,) = refs[27:]
     y_at, z_at, core = sc[0], sc[1], sc[2]
-    total = gains_in[0:1, :]
-    wait(8)
-    for n, (chunk, target) in enumerate(((1, p1), (3, p3), (0, p0))):
-        wait(5 + n, 9 + n)
+    wait(3, 4)
+    slim_pair[:, 0:128] = nt(wide[:, 0:256], spread2[...]).astype(BF16)
+    slim_pair[:, 128:256] = nt(wide[:, 256:512], spread2[...]).astype(BF16)
+    wait(15)
+    pair_total = tn(h1[...], slim_pair[...])
+    query_total = jnp.zeros((WIDTH, 256), F32)
+    out_total = jnp.zeros((WIDTH, 256), F32)
+    for chunk in range(4):
+        wait(7 + chunk, 11 + chunk, 16 + chunk)
         at = slice(chunk * TOK, (chunk + 1) * TOK)
-        part = nt(queries[n][...], proj[:, 0:512]) + nt(wide[at, :], proj[:, 512:1024])
-        target[...] = part.astype(BF16)
-        xf = xs[n][...].astype(F32)
-        total = total + jnp.sum(part * (xf * row_scale(xf)), axis=0, keepdims=True)
-    wait(2, 25, 26, 27, 28)
+        query_total = query_total + tn(h1[at, :], slims[chunk][...])
+        out_total = out_total + tn(rows[chunk][...], nt(mixed[chunk][...], spread4[...]).astype(BF16))
+    wait(2, 5, 6, 20, 21, 22, 23)
+    shares = query_total * weights[:, 0:256].astype(F32) + pair_total * weights[:, 256:512].astype(F32)
+    ones = jnp.ones((8, 256), BF16)
+    high = shares.astype(BF16)
+    low = (shares - high.astype(F32)).astype(BF16)
+    total = (nt(ones, high) + nt(ones, low))[0:1, :] / gain_row[...]
     query_gain = (query_gains[0][0:1, :] + query_gains[1][0:1, :]) + (
         query_gains[2][0:1, :] + query_gains[3][0:1, :]
     )
-    extra[...] = jnp.zeros((56, 768), F32)
+    extra[0:8, :] = jnp.zeros((8, 768), F32)
+    extra[8:56, :] = small[...]
     extra[0:1, :] = total[:, 0:768]
     extra[1:2, 0:256] = total[:, 768:1024]
     extra[1:2, 256:384] = query_gain
-    extra[1:2, 384:512] = gains_in[1:2, 0:PITCH]
-    extra[8:56, :] = small[...]
-    send[16] = split3(extra[0:4, :])
-    send[17] = small[0:32, :].astype(BF16)
-    send[18, 0:16, :] = small[32:48, :].astype(BF16)
-    send[18, 16:32, :] = jnp.zeros((16, 768), BF16)
-    wait(3, 4)
-    slim_pair[:, 0:128] = nt(wide[:, 0:256], spread2[...]).astype(BF16)
-    slim_pair[:, 128:256] = nt(wide[:, 256:512], spread2[...]).astype(BF16)
-    wait(20)
-    pair_rows = tn(h1[...], slim_pair[...]).astype(BF16)
-    query_total = jnp.zeros((WIDTH, 256), F32)
-    out_total = jnp.zeros((WIDTH, 256), F32)
-    for chunk in range(4):
-        wait(12 + chunk, 16 + chunk, 21 + chunk)
-        at = slice(chunk * TOK, (chunk + 1) * TOK)
-        query_total = query_total + tn(h1[at, :], slims[chunk][...])
-        out_total = out_total + tn(rows[chunk][...], nt(mixed[chunk][...], spread4[...]).astype(BF16))
-    query_rows, out_rows = query_total.astype(BF16), out_total.astype(BF16)
+    extra[1:2, 384:512] = key_gain[0:1, :]
+    query_rows, pair_rows, out_rows = query_total.astype(BF16), pair_total.astype(BF16), out_total.astype(BF16)
     for block in range(16):
         y_rel = (block // 4 - y_at + 4) % 4
         z_rel = (block % 4 - z_at + 4) % 4
@@ -634,14 +660,6 @@
             pl.when(core != side)(partial(put, send))
 
 
-def near_body(p1, p3, far_up, far_down, out1, out3):
-    half = TOK // 2
-    out1[:half, :] = (p1[:half, :].astype(F32) + far_up[...].astype(F32)).astype(BF16)
-    out1[half:, :] = p1[half:, :]
-    out3[:half, :] = p3[:half, :]
-    out3[half:, :] = (p3[half:, :].astype(F32) + far_down[...].astype(F32)).astype(BF16)
-
-
 def split3(value):
     high = value.astype(BF16).astype(F32)
     middle = (value - high).astype(BF16).astype(F32)
@@ -654,11 +672,9 @@
     return value[0:4] + value[4:8] + value[8:12]
 
 
-def ride_first_body(keep, got, extra, *outs):
-    gain = split3(extra[0:4, :] + join3(got[16]))
-    router = jnp.concatenate(
-        [extra[8:40, :] + got[17].astype(F32), extra[40:56, :] + got[18, 0:16, :].astype(F32)], axis=0
-    ).astype(BF16)
+def ride_first_body(keep, got, extra, extra_got, *outs):
+    gain = split3(extra[0:4, :] + extra_got[0:4, :])
+    router = (extra[8:56, :] + extra_got[8:56, :]).astype(BF16)
     for first in range(4):
         for second in range(4):
             at = first * 4 + second
@@ -692,10 +708,16 @@
         outs[second][64:112, :] = router
 
 
-def ride_last_body(own, g1, g2, g3, rows, gain, router):
+def ride_last_body(own, g1, g2, g3, rows, gain, router, ffn):
     rows[...] = add4(own, g1, g2, g3, 0, 32)
     gain[...] = add_gains(own, g1, g2, g3, 32)
-    router[...] = add4(own, g1, g2, g3, 64, 112)
+    total = add4(own, g1, g2, g3, 64, 112)
+    whole = jnp.concatenate(
+        [total[0:32], jnp.concatenate([total[32:48, 0:256], total[32:48, 256:512]], axis=0)], axis=1
+    )
+    router[...] = jnp.transpose(whole)
+    for quarter in range(4):
+        ffn[:, quarter * 256 : (quarter + 1) * 256] = total[32 + quarter : 33 + quarter, 512:768]
 
 
 def input_body(p0, p1, p2, x, gain, grad_mid, out):
@@ -742,6 +764,7 @@
 
 def gather_weights(shard, chunks):
     rows = jnp.stack([shard] + [shift_axis(shard, 0, -s) for s in (1, 2, 3)])
+    rows = after(rows, chunks[1], chunks[3])
     own = jnp.concatenate([rows] + [shift_axis(rows, 1, -s) for s in (1, 2, 3)], axis=0)
     near = own
     own = after(own, chunks)
@@ -805,19 +828,19 @@
     shard = jnp.concatenate([query_weight, key_value_weight.reshape(32, 256), out_weight], axis=0)
     shards_near, shards_own, shards_other = gather_weights(shard, chunks)
 
-    packed, ranks = call(
+    cot_all = lax.all_gather(cotangent, "dp", axis=0, tiled=False, axis_index_groups=PLANES)
+    ranks, coded = call(
         start_body,
-        [((ROWS, WIDTH), BF16), ((EXPERTS, TOK), F32)],
-        after((cotangent, routes), shards_near),
+        [((EXPERTS, TOK), F32), ((SIDE, WIDTH), BF16)],
+        after((routes,), shards_near),
         scalars=jnp.stack([mp_at, length]),
     )
-    cot_all = lax.all_gather(packed, "dp", axis=0, tiled=False, axis_index_groups=PLANES)
     weights_own = (gate_weight, up_weight, down_weight)
     weights_other = tuple(shift_yz(after(w, shards_other), 0, 0, 1) for w in weights_own)
 
     out = call(
         project_body,
-        [((LEN, WIDTH), BF16), ((WIDTH, 1024), BF16)]
+        [((LEN, WIDTH), BF16), ((WIDTH, 1024), BF16), ((WIDTH, 768), BF16)]
         + [((TOK, 512), F32)] * 4
         + [((TOK, 256), F32)] * 4
         + [((TOK, 512), BF16)] * 4
@@ -825,21 +848,21 @@
         + [((TOK, PITCH), F32)] * 4,
         (shards_own, shards_other, *chunks, attn_row, head_gain, cos_tab, sin_tab, spread4, spread2),
         scalars=jnp.stack([y_at, z_at, core, mp_at, length]),
-        any_out=range(10),
-        near=range(10, 17),
+        any_out=range(11),
+        near=range(11, 18),
         scratch=[
             pltpu.VMEM((LEN, WIDTH), BF16),
             pltpu.VMEM((LEN, 512), F32),
             pltpu.VMEM((LEN, 256), F32),
             pltpu.VMEM((WIDTH, 1024), BF16),
             pltpu.VMEM((WIDTH, 768), BF16),
-            pltpu.SemaphoreType.DMA((13,)),
+            pltpu.SemaphoreType.DMA((14,)),
         ],
         mb=40,
         lazy=True,
     )
-    h1, proj, raw, raw_pair, qa = out[0], out[1], out[2:6], out[6:10], out[10:14]
-    ka, va, out_w, turn_tab = out[14], out[15], out[16], out[17:21]
+    h1, proj, weights_in, raw, raw_pair, qa = out[0], out[1], out[2], out[3:7], out[7:11], out[11:15]
+    ka, va, out_w, turn_tab = out[15], out[16], out[17], out[18:22]
 
     qa = list(after(tuple(qa), weights_other))
     branch, mixed, qb = [None] * 4, [None] * 4, [None] * 4
@@ -857,14 +880,15 @@
         arrived[r] = shift_mp(branch[r], r) if r else branch[r]
     x_mid, h2 = call(
         middle_body,
-        [((TOK, WIDTH), F32), ((TOK, WIDTH), BF16)],
-        (layer_input, *arrived, ffn_row),
+        [((TOK, WIDTH), F32), ((ROWS, WIDTH), BF16)],
+        (layer_input, *arrived, ffn_row, coded),
+        near=(1,),
         local=(1, 2, 3, 4),
     )
     (gates,) = call(gates_body, [((EXPERTS, TOK), F32)], (h2, router, ranks))
 
     plus, minus = shift_axis(h2, 0, -1), shift_axis(h2, 0, 1)
-    far_a, far_b = shift_axis(plus[: TOK // 2], 0, -1), shift_axis(minus[TOK // 2 :], 0, 1)
+    far_a, far_b = shift_axis(plus[:144], 0, -1), shift_axis(minus[144:], 0, 1)
     near_a, near_b = jnp.stack([h2, plus]), jnp.stack([minus, jnp.concatenate([far_a, far_b], axis=0)])
     plus_a, plus_b = shift_axis(near_a, 1, -1), shift_axis(near_b, 1, -1)
     minus_a, minus_b = shift_axis(near_a, 1, 1), shift_axis(near_b, 1, 1)
@@ -878,6 +902,12 @@
         if u == 1:
             far_plus, far_minus = after((plus_a, minus_b), backs[0])
             units[3] = (shift_axis(far_plus, 1, -1), shift_axis(far_minus, 1, 1))
+            units[2] = after(units[2], units[3])
+        if u == 2:
+            plus_b = shift_axis(backs[1][1], 1, 1)
+        if u == 3:
+            minus_a = shift_axis(backs[2][0], 1, -1)
+            units[3] = after(units[3], plus_b)
         second = (second_at + step + 4) % 4
         order = []
         for s in STEPS:
@@ -886,7 +916,7 @@
         sc = jnp.stack(order + [dp_at, dp_at + 1 - 2 * core]).astype(jnp.int32)
         pieces = tuple(one.shape[0] for one in units[u])
         args = (*units[u], cot_all, router, *weights_own, *weights_other)
-        any_in = list(range(len(pieces) + 1)) + list(range(len(pieces) + 2, len(pieces) + 8))
+        any_in = [len(pieces)]
         aliases = None
         if saved is not None:
             base = len(args)
@@ -911,12 +941,9 @@
             any_out=range(8),
             scratch=[
                 pltpu.VMEM((4, TOK, WIDTH), BF16),
-                pltpu.VMEM((4, ROWS, WIDTH), BF16),
-                pltpu.VMEM((2, WIDTH, FF), BF16),
-                pltpu.VMEM((2, WIDTH, FF), BF16),
-                pltpu.VMEM((2, FF, WIDTH), BF16),
                 pltpu.VMEM((4, TOK, WIDTH), BF16),
                 pltpu.VMEM((4, ROWS, WIDTH), BF16),
+                pltpu.VMEM((2, 4 * CAP, WIDTH), BF16),
                 pltpu.VMEM((2, 4 * CAP, WIDTH), BF16),
                 pltpu.VMEM((2, 4 * CAP, WIDTH), BF16),
                 pltpu.VMEM((2, 4 * CAP, FF), BF16),
@@ -925,22 +952,24 @@
                 pltpu.SemaphoreType.DMA((32,)),
             ],
             aliases=aliases,
-            mb=40,
+            local=(*range(len(pieces)), *range(len(pieces) + 2, len(pieces) + 8)),
+            mb=36,
+            lazy=True,
         )
         backs.append(made[1:3])
         saved = [made[0]] + list(made[3:])
     y_out, taken, push, hidden, grad_gate, grad_up = saved
 
-    (b0_a, b0_b), (bp_a, bp_b), (bm_a, bm_b), (bf_a, bf_b) = backs
+    (b0_a, b0_b), (bp_a, _), (_, bm_b), (bf_a, bf_b) = backs
     half_a, half_b = shift_axis(bf_a, 1, 1), shift_axis(bf_b, 1, -1)
     saved = (taken, push, hidden, grad_gate, grad_up)
-    for_other = expert_weights(saved, 1, mp_at)
-    from_other = [shift_yz(one, 0, 0, 1) for one in for_other]
-    half_a, half_b = after((half_a, half_b), for_other)
+    for_other = expert_weights(after(saved, minus_a), 1, mp_at)
+    for_other = after(for_other, half_a, half_b)
     plus_late, minus_late = add_low(bp_a, half_a), add_low(bm_b, half_b)
-    plus_a, plus_b = shift_axis(plus_late, 1, 1), shift_axis(bp_b, 1, 1)
-    minus_a, minus_b = shift_axis(bm_a, 1, -1), shift_axis(minus_late, 1, -1)
-    shard_grads = expert_weights(after(saved, plus_late, minus_late), 0, mp_at, from_other)
+    plus_a, minus_b = shift_axis(plus_late, 1, 1), shift_axis(minus_late, 1, -1)
+    from_other = shift_yz(for_other[0], 0, 0, 1)
+    shard_grads = expert_weights(after(saved, plus_late, minus_late), 0, mp_at, (from_other,))
+    shard_far = shift_mp(shard_grads[3], 1), shift_mp(shard_grads[4], -1)
     b0_a, b0_b = after((b0_a, b0_b), shard_grads)
     line_a = add_low(b0_a, plus_a, minus_a)
     line_b = add_low(b0_b, plus_b, minus_b)
@@ -948,13 +977,20 @@
     far_up, far_down = shift_axis(line_b[1, :cut], 0, 1), shift_axis(line_b[1, cut:], 0, -1)
     send_up = jnp.concatenate([add_low(line_a[1, :cut], far_up), line_a[1, cut:]], axis=0)
     send_down = jnp.concatenate([line_b[0, :cut], add_low(line_b[0, cut:], far_down)], axis=0)
+    shard_near = call(
+        shard_near_body,
+        [((768, FF), BF16)] * 2,
+        (shard_grads[1], shard_grads[2], *shard_far),
+        near=(0, 1),
+        local=range(4),
+    )
+    send_up, send_down = after((send_up, send_down), shard_near)
     got_up, got_down = shift_axis(send_up, 0, 1), shift_axis(send_down, 0, -1)
-    shards_got = [shift_mp(shard_grads[step], step) for step in (1, 2, 3)]
-    got_up, got_down = after((got_up, got_down), shards_got[0], shards_got[2])
     grad_mid, grad_rows, small = call(
         token_back_body,
-        [((TOK, WIDTH), F32), ((TOK, WIDTH), BF16), ((EXPERTS + 8, WIDTH), F32)],
-        (line_a[0], got_up, got_down, h2, x_mid, ranks, gates, router, ffn_row, packed),
+        [((TOK, WIDTH), F32), ((TOK, WIDTH), BF16), ((48, 768), F32)],
+        (line_a[0], got_up, got_down, h2, x_mid, ranks, gates, router, ffn_row, cotangent),
+        scalars=jnp.stack([mp_at, length]),
         local=(0, 1, 2),
     )
 
@@ -968,18 +1004,15 @@
 
     rows = [grad_rows, shift_mp(grad_rows, -1), None, shift_mp(grad_rows, 1)]
     for turn, r in enumerate((0, 1, 3, 2)):
-        if turn == 1:
-            near_a, near_b = after((rows[1], rows[3]), grad_query[0])
+        if turn == 2:
+            near_a, near_b = after((rows[1], rows[3]), grad_query[1])
             rows[2] = jnp.concatenate(
                 [shift_mp(near_a[: TOK // 2], -1), shift_mp(near_b[TOK // 2 :], 1)], axis=0
             )
-        if turn == 2:
-            small = sum_mp(after(small, rows[2], grad_query[1]))[:36].reshape(48, 768)
-        if turn == 3:
-            expert_grads = shard_grads[0].astype(F32) + (
-                shards_got[0].astype(F32) + (shards_got[1].astype(F32) + shards_got[2].astype(F32))
-            )
-            rows[r] = after(rows[r], small, expert_grads)
+        if turn == 1:
+            shard_near = after(shard_near, rows[1], rows[3], grad_query[0])
+            shards_got = shift_mp(shard_near[0], 1), shift_mp(shard_near[1], -1)
+            rows[r] = after(rows[r], rows[3])
         args = (rows[r], out_w, qb[r], mixed[r], ka, va, raw[r], head_gain, turn_tab[r], spread4)
         first = both is None
         grad_query[r], query_gains[r], slim[r], both = call(
@@ -994,28 +1027,26 @@
             mb=32,
             lazy=True,
         )
-    far_up, far_down, wide, gains = call(
+    far_up, far_down, wide, key_gain_part = call(
         keys_back_body,
-        [((TOK // 2, WIDTH), BF16)] * 2 + [((LEN, 512), BF16), ((8, WIDTH), F32)],
-        (both, *raw_pair, *turn_tab, head_gain, grad_query[2], proj, chunks[2]),
+        [((TOK // 2, WIDTH), BF16)] * 2 + [((LEN, 512), BF16), ((8, PITCH), F32)],
+        (after(both, shards_got), *raw_pair, *turn_tab, head_gain, grad_query[2], proj),
         near=range(4),
         mb=32,
         lazy=True,
     )
     far_up, far_down = shift_mp(far_up, 1), shift_mp(far_down, -1)
-    others = (1, 3, 0)
-    part_up, part_down, part_own, keep, send, extra = call(
+    keep, send, extra = call(
         tail_body,
-        [((TOK, WIDTH), BF16)] * 3 + [((16, 32, 768), BF16), ((19, 32, 768), BF16), ((56, 768), F32)],
+        [((16, 32, 768), BF16), ((16, 32, 768), BF16), ((56, 768), F32)],
         (
             wide,
-            gains,
+            key_gain_part,
             small,
             spread2,
             spread4,
-            *(grad_query[r] for r in others),
-            proj,
-            *(chunks[r] for r in others),
+            weights_in,
+            attn_row,
             *rows,
             *mixed,
             h1,
@@ -1024,20 +1055,24 @@
         ),
         scalars=jnp.stack([y_at, z_at, core]),
         scratch=[pltpu.VMEM((LEN, 256), BF16)],
-        near=range(6),
+        near=range(3),
         local=(0, 1),
         mb=40,
         lazy=True,
     )
-    part_up, part_down = call(
-        near_body,
-        [((TOK, WIDTH), BF16)] * 2,
-        (part_up, part_down, far_up, far_down),
-        near=(0, 1),
-        local=range(4),
+    send = after(send, far_up, far_down)
+    extra = sum_mp(extra)
+    part_up, part_down, part_own = call(
+        parts_body,
+        [((TOK, WIDTH), BF16)] * 3,
+        (wide, far_up, far_down, proj, *(grad_query[r] for r in (1, 3, 0))),
+        near=range(3),
+        local=(0, 1, 2),
+        lazy=True,
     )
     part_up, part_down = shift_mp(part_up, 1), shift_mp(part_down, -1)
     layer_output = (x_mid + returned.astype(F32)).astype(BF16)
+    expert_grads = shard_grads[0].astype(F32) + (shards_got[0].astype(F32) + shards_got[1].astype(F32))
     expert_outs = (
         expert_grads[0:256].reshape(1, 256, FF),
         expert_grads[256:512].reshape(1, 256, FF),
@@ -1046,9 +1081,9 @@
     first_msg = call(
         ride_first_body,
         [((208, 768), BF16)] * 4,
-        (keep, shift_yz(send, 0, 0, 1), extra),
+        (keep, shift_yz(send, 0, 0, 1), extra, shift_yz(extra, 0, 0, 1)),
         near=range(4),
-        local=range(3),
+        local=range(4),
     )
     second_msg = call(
         ride_second_body,
@@ -1057,13 +1092,12 @@
         near=range(4),
         local=range(4),
     )
-    weight_sum, gain_sum, router_sum = call(
+    weight_sum, gain_sum, router_grad, ffn_grad = call(
         ride_last_body,
-        [((32, 768), F32), ((4, 768), F32), ((48, 768), F32)],
+        [((32, 768), F32), ((4, 768), F32), ((WIDTH, EXPERTS), F32), ((1, WIDTH), F32)],
         (second_msg[0], *(shift_axis(second_msg[s], 1, s) for s in (1, 2, 3))),
         local=range(4),
     )
-    gain_sum, router_sum = sum_mp(gain_sum), router_sum.reshape(36, WIDTH)
     attn_gain_grad = jnp.concatenate([gain_sum[0], gain_sum[1, 0:256]])
     (input_grad,) = call(
         input_body,
@@ -1081,8 +1115,8 @@
         weight_sum[:, 0:256],
         weight_sum[:, 256:512].reshape(32, 2, 128),
         weight_sum[:, 512:768],
-        router_sum[EXPERTS],
-        router_sum[:EXPERTS].T,
+        ffn_grad.reshape(WIDTH),
+        router_grad,
         *expert_outs,
     )
 

time: 403 us -> 374 us (0.928)
  waiting for transfers between devices: 116 us -> 87.4 us
    ppermute x24 -> x22, waiting for transfers between devices: 65.2 us -> 29.7 us  [shift_mp(): return lax.ppermute(tensor, 'mp', [(i, (i + step) % 4) for i in range(4)])]
    pallas_call x24 -> x27, Pallas kernels: 140 us -> 162 us  [call(): pl.pallas_call(kernel, out_shape=shapes, in_specs=in_specs, out_specs=out...]
    pallas_call x2 -> x0, Pallas kernels: 19.7 us -> none  [expert_weights(): pl.pallas_call(partial(expert_weights_body, bool(got)), out_shape=[jax.Sh...]
    ppermute x24 -> x22, starting transfers between devices: 30 us -> 29.2 us  [shift_mp(): return lax.ppermute(tensor, 'mp', [(i, (i + step) % 4) for i in range(4)])]
  transfers between devices with their start and end apart: 66 -> 63, of which waited for: 30 -> 32; matrix products, arithmetic and copies ran while one was open for 5% -> 4% of each run, Pallas kernels for 35% -> 42%
where the time goes in v3:
time: 374 us; the launch traced here: 369 us
  Pallas kernels  162 us (43%)
  waiting for transfers between devices  87.4 us (23%)
  starting transfers between devices  77.9 us (21%)
  local copies, waits for them, and re-layouts  16.3 us (4%)
  between operations  15.9 us (4%)
  other arithmetic  10.2 us (3%)
    pallas_call x27, Pallas kernels, call(): pl.pallas_call(kernel, out_shape=shapes, in_specs=in_specs, out_specs=out...  162 us
    ppermute x32, waiting for transfers between devices, shift_axis(): return lax.ppermute(tensor, 'dp', pairs)  53.1 us
    ppermute x32, starting transfers between devices, shift_axis(): return lax.ppermute(tensor, 'dp', pairs)  47.3 us
    ppermute x22, waiting for transfers between devices, shift_mp(): return lax.ppermute(tensor, 'mp', [(i, (i + step) % 4) for i in range(4)])  29.7 us
    ppermute x22, starting transfers between devices, shift_mp(): return lax.ppermute(tensor, 'mp', [(i, (i + step) % 4) for i in range(4)])  29.2 us
    unnamed x52, local copies, waits for them, and re-layouts  7.71 us
  transfers between devices with their start and end apart: 63, of which 32 were waited for; matrix products, arithmetic and copies ran while one was open for 4% of the time, Pallas kernels for 42%

profile of v3, /device:TPU:0, one launch (start us, length us, event | category | flops | bytes accessed | tf_op | source)
XLA Modules:
  0.0 369.4 jit_solution(10781572598672084124)
XLA Ops:
  8.0 2.9 collective-permute-start.3
  13.0 3.0 collective-permute-start
  17.8 3.9 %collective-permute-done.1 = bf16[96,256]{1,0:T(8,128)(2,1)S(1)} collective-permute-done((bf16[96,256]{1,0:T(8,128)(2,1)S(1)}, bf16[96,256]{1,0:T(8,128)(2,1)S(1)}, u32[]{:S(2)}, u32[]{:S(2)}) %collective-permute-start.1) | collective-permute-done | bytes 49184 | tf_op jit(solution)/shard_map/ppermute | solution.py:758
  22.4 3.3 collective-permute-done.4.refs_6_
  25.7 4.0 %collective-permute-start.5 = (bf16[4,96,256]{2,1,0:T(8,128)(2,1)S(1)}, bf16[4,96,256]{2,1,0:T(8,128)(2,1)S(1)}, u32[]{:S(2)}, u32[]{:S(2)}) collective-permute-start(bf16[4,96,256]{2,1,0:T(8,128)(2,1)S(1)} %pad_maximum_fusion.4), channel_id=1, source_target_pairs={{0,24},{4,100},{8,0},{12,108},{16,8},{20,116},{24,16},{28,124},{32... | collective-permute-start | bytes 589832 | tf_op jit(solution)/shard_map/ppermute | solution.py:758
  35.1 4.4 %collective-permute-done.6 = bf16[4,96,256]{2,1,0:T(8,128)(2,1)S(1)} collective-permute-done((bf16[4,96,256]{2,1,0:T(8,128)(2,1)S(1)}, bf16[4,96,256]{2,1,0:T(8,128)(2,1)S(1)}, u32[]{:S(2)}, u32[]{:S(2)}) %collective-permute-start.6) | collective-permute-done | bytes 196640 | tf_op jit(solution)/shard_map/ppermute | solution.py:758
  47.5 11.6 %shard_map.282 = (bf16[1024,1024]{1,0:T(8,128)(2,1)}, bf16[1024,1024]{1,0:T(8,128)(2,1)}, bf16[1024,768]{1,0:T(8,128)(2,1)}, f32[256,512]{1,0:T(8,128)}, f32[256...) custom-call(s32[5]{0:T(128)S(1)} %stack.136.refs_0_, ...), custom_call_target="tpu_custom_call" | custom-call | flops 1 | bytes 1 | tf_op jit(solution)/shard_map/pallas_call | solution.py:126
  59.1 3.2 shard_map.283
  62.4 3.2 shard_map.286
  67.8 3.2 shard_map.285
  74.8 4.2 %collective-permute-done.14.refs_3_ = bf16[256,1024]{1,0:T(8,128)(2,1)} collective-permute-done((bf16[256,1024]{1,0:T(8,128)(2,1)}, bf16[256,1024]{1,0:T(8,128)(2,1)}, u32[]{:S(2)}, u32[]{:S(2)}) %collective-permute-start.14) | collective-permute-done | bytes 524320 | tf_op jit(solution)/shard_map/ppermute | solution.py:762
  81.3 6.1 %collective-permute-done.16.refs_4_ = bf16[256,1024]{1,0:T(8,128)(2,1)} collective-permute-done((bf16[256,1024]{1,0:T(8,128)(2,1)}, bf16[256,1024]{1,0:T(8,128)(2,1)}, u32[]{:S(2)}, u32[]{:S(2)}) %collective-permute-start.16) | collective-permute-done | bytes 524320 | tf_op jit(solution)/shard_map/ppermute | solution.py:762
  89.4 3.8 %shard_map.288 = (f32[256,1024]{1,0:T(8,128)}, bf16[272,1024]{1,0:T(8,128)(2,1)S(1)}) custom-call(bf16[256,1024]{1,0:T(8,128)(2,1)} %refs_3_.3, bf16[256,1024]{1,0:T(8,128)(2,1)S(1)} %get-tuple-element.191.refs_1_, bf16[256,1024]{1,0:T(8,128)(2,1)} %collective-permute-done.15.refs_2_, bf16[256,1024]{1,0:T(8,128)(2,1)} %collective-permute-done.14.refs_3_, ...), custom_call_target="tpu_custom_call" | custom-call | flops 1 | bytes 1 | tf_op jit(solution)/shard_map/pallas_call | solution.py:126
  95.4 7.4 %collective-permute-done.17 = bf16[272,1024]{1,0:T(8,128)(2,1)S(1)} collective-permute-done((bf16[272,1024]{1,0:T(8,128)(2,1)S(1)}, bf16[272,1024]{1,0:T(8,128)(2,1)S(1)}, u32[]{:S(2)}, u32[]{:S(2)}) %collective-permute-start.17) | collective-permute-done | bytes 557088 | tf_op jit(solution)/shard_map/ppermute | solution.py:758
  102.8 3.4 collective-permute-start.20
  108.1 5.8 %collective-permute-done.21 = bf16[128,1024]{1,0:T(8,128)(2,1)S(1)} collective-permute-done((bf16[128,1024]{1,0:T(8,128)(2,1)S(1)}, bf16[128,1024]{1,0:T(8,128)(2,1)S(1)}, u32[]{:S(2)}, u32[]{:S(2)}) %collective-permute-start.21) | collective-permute-done | bytes 262176 | tf_op jit(solution)/shard_map/ppermute | solution.py:758
  115.0 3.2 collective-permute-start.25
  118.4 14.4 %shard_map.289 = (bf16[16,256,1024]{2,1,0:T(8,128)(2,1)}, bf16[2,272,1024]{2,1,0:T(8,128)(2,1)}, bf16[2,272,1024]{2,1,0:T(8,128)(2,1)}, bf16[2,1536,1024]{2,1,0:...) custom-call(s32[6]{0:T(128)S(1)} %stack.160.refs_0_, ...), custom_call_target="tpu_custom_call" | custom-call | flops 1 | bytes 1 | tf_op jit(solution)/shard_map/pallas_call | solution.py:126
  132.8 3.3 collective-permute-start.23
  136.4 14.4 %shard_map.290 = (bf16[16,256,1024]{2,1,0:T(8,128)(2,1)}, bf16[2,272,1024]{2,1,0:T(8,128)(2,1)}, bf16[2,272,1024]{2,1,0:T(8,128)(2,1)}, bf16[2,1536,1024]{2,1,0:...) custom-call(s32[6]{0:T(128)S(1)} %stack.165.refs_0_, ...), custom_call_target="tpu_custom_call", output_to_operand_aliasing={{0}: (11, {}), {3}: (12, {}), {4}: (13, {}), {5}: (14, {}),... | custom-call | flops 1 | bytes 1 | tf_op jit(solution)/shard_map/pallas_call | solution.py:126
  151.5 4.4 %collective-permute-done.24.refs_2_ = bf16[2,272,1024]{2,1,0:T(8,128)(2,1)} collective-permute-done((bf16[2,272,1024]{2,1,0:T(8,128)(2,1)}, bf16[2,272,1024]{2,1,0:T(8,128)(2,1)}, u32[]{:S(2)}, u32[]{:S(2)}) %collective-permute-start.24) | collective-permute-done | bytes 1114144 | tf_op jit(solution)/shard_map/ppermute | solution.py:758
  155.9 14.4 %shard_map.291 = (bf16[16,256,1024]{2,1,0:T(8,128)(2,1)}, bf16[2,272,1024]{2,1,0:T(8,128)(2,1)}, bf16[2,272,1024]{2,1,0:T(8,128)(2,1)}, bf16[2,1536,1024]{2,1,0:...) custom-call(s32[6]{0:T(128)S(1)} %stack.170.refs_0_, ...), custom_call_target="tpu_custom_call", output_to_operand_aliasing={{0}: (11, {}), {3}: (12, {}), {4}: (13, {}), {5}: (14, {}),... | custom-call | flops 1 | bytes 1 | tf_op jit(solution)/shard_map/pallas_call | solution.py:126
  170.6 14.4 %shard_map.292 = (bf16[16,256,1024]{2,1,0:T(8,128)(2,1)}, bf16[2,272,1024]{2,1,0:T(8,128)(2,1)}, bf16[2,272,1024]{2,1,0:T(8,128)(2,1)}, bf16[2,1536,1024]{2,1,0:...) custom-call(s32[6]{0:T(128)S(1)} %stack.149.refs_0_, ...), custom_call_target="tpu_custom_call", output_to_operand_aliasing={{0}: (11, {}), {3}: (12, {}), {4}: (13, {}), {5}: (14, {}),... | custom-call | flops 1 | bytes 1 | tf_op jit(solution)/shard_map/pallas_call | solution.py:126
  188.5 8.1 %shard_map.293 = bf16[3072,512]{1,0:T(8,128)(2,1)S(1)} custom-call(s32[1]{0:T(128)} %bitcast.3.refs_0_, bf16[2,1536,1024]{2,1,0:T(8,128)(2,1)} %get-tuple-element.243.refs_1_, bf16[2,1536,512]{2,1,0:T(8,128)(2,1)} %get-tuple-element.244.refs_2_, bf16[2,1536,512]{2,1,0:T(8,128)(2,1)} %get-tuple-element.245.refs_3_, ...), custom_call_target="tpu_custom_call" | custom-call | flops 1 | bytes 1 | tf_op jit(solution)/shard_map/pallas_call | solution.py:126
  196.6 5.3 %collective-permute-done.28 = bf16[2,272,1024]{2,1,0:T(8,128)(2,1)S(1)} collective-permute-done((bf16[2,272,1024]{2,1,0:T(8,128)(2,1)}, bf16[2,272,1024]{2,1,0:T(8,128)(2,1)S(1)}, u32[]{:S(2)}, u32[]{:S(2)}) %collective-permute-start.28) | collective-permute-done | bytes 1114144 | tf_op jit(solution)/shard_map/ppermute | solution.py:758
  208.6 8.7 %shard_map.294 = (bf16[768,512]{1,0:T(8,128)(2,1)S(1)}, bf16[768,512]{1,0:T(8,128)(2,1)S(1)}, bf16[768,512]{1,0:T(8,128)(2,1)S(1)}, bf16[384,512]{1,0:T(8,128)(2,1)S(1)}, bf16[384,512]{1,0:T(8,128)(2,1)S(1)}) custom-call(s32[1]{0:T(128)} %bitcast.3.refs_0_, bf16[2,1536,1024]{2,1,0:T(8,128)(2,1)} %get-tuple-element.243.refs_1_, ...), custom_call_target="tpu_custom_call" | custom-call | flops 1 | bytes 1 | tf_op jit(solution)/shard_map/pallas_call | solution.py:126
  217.4 3.7 collective-permute-start.37
  223.0 3.4 collective-permute-start.35
  227.3 3.0 collective-permute-done.35
  230.5 4.0 %collective-permute-done.34 = bf16[144,1024]{1,0:T(8,128)(2,1)S(1)} collective-permute-done((bf16[144,1024]{1,0:T(8,128)(2,1)S(1)}, bf16[144,1024]{1,0:T(8,128)(2,1)S(1)}, u32[]{:S(2)}, u32[]{:S(2)}) %collective-permute-start.34) | collective-permute-done | bytes 294944 | tf_op jit(solution)/shard_map/ppermute | solution.py:758
  236.7 3.2 collective-permute-start.39
  242.0 5.4 %collective-permute-done.38.refs_2_ = bf16[272,1024]{1,0:T(8,128)(2,1)S(1)} collective-permute-done((bf16[272,1024]{1,0:T(8,128)(2,1)S(1)}, bf16[272,1024]{1,0:T(8,128)(2,1)S(1)}, u32[]{:S(2)}, u32[]{:S(2)}) %collective-permute-start.38) | collective-permute-done | bytes 557088 | tf_op jit(solution)/shard_map/ppermute | solution.py:758
  247.4 4.3 %shard_map.297 = (f32[256,1024]{1,0:T(8,128)}, bf16[256,1024]{1,0:T(8,128)(2,1)}, f32[48,768]{1,0:T(8,128)}) custom-call(s32[2]{0:T(128)S(1)} %pad_add_fusion.refs_0_, bf16[272,1024]{1,0:T(8,128)(2,1)S(1)} %slice_bitcast_fusion.refs_1_, bf16[272,1024]{1,0:T(8,128)(2,1)S(1)} %collective-permute-done.38.refs_2_, ...), custom_call_target="tpu_custom_call" | custom-call | flops 1 | bytes 1 | tf_op jit(solution)/shard_map/pallas_call | solution.py:126
  254.8 6.6 %shard_map.298 = (bf16[256,512]{1,0:T(8,128)(2,1)}, f32[8,128]{1,0:T(8,128)}, bf16[256,256]{1,0:T(8,128)(2,1)}, f32[2,1024,256]{2,1,0:T(8,128)}) custom-call(bf16[256,1024]{1,0:T(8,128)(2,1)S(1)} %copy-done.5, bf16[1024,512]{1,0:T(8,128)(2,1)S(1)} %get-tuple-element.188.refs_3_.refs_1_, bf16[256,512]{1,0:T(8,128)(2,1)} %get-tuple-element.268.refs_2_, ...), custom_call_target="tpu_custom_call" | custom-call | flops 1 | bytes 1 | tf_op jit(solution)/shard_map/pallas_call | solution.py:126
  268.2 6.9 %shard_map.299 = (bf16[256,512]{1,0:T(8,128)(2,1)}, f32[8,128]{1,0:T(8,128)}, bf16[256,256]{1,0:T(8,128)(2,1)}, f32[2,1024,256]{2,1,0:T(8,128)}) custom-call(bf16[256,1024]{1,0:T(8,128)(2,1)S(1)} %collective-permute-done.40.refs_0_.refs_9_, bf16[1024,512]{1,0:T(8,128)(2,1)S(1)} %get-tuple-element.188.refs_3_.refs_1_, ...), custom_call_target="tpu_custom_call", output_to_operand_aliasing={{3}: (10, {})} | custom-call | flops 1 | bytes 1 | tf_op jit(solution)/shard_map/pallas_call | solution.py:126
  277.4 6.9 %shard_map.300 = (bf16[256,512]{1,0:T(8,128)(2,1)}, f32[8,128]{1,0:T(8,128)}, bf16[256,256]{1,0:T(8,128)(2,1)}, f32[2,1024,256]{2,1,0:T(8,128)}) custom-call(bf16[256,1024]{1,0:T(8,128)(2,1)S(1)} %collective-permute-done.41.refs_0_.refs_11_, bf16[1024,512]{1,0:T(8,128)(2,1)S(1)} %get-tuple-element.188.refs_3_.refs_1_, ...), custom_call_target="tpu_custom_call", output_to_operand_aliasing={{3}: (10, {})} | custom-call | flops 1 | bytes 1 | tf_op jit(solution)/shard_map/pallas_call | solution.py:126
  287.1 6.9 %shard_map.301 = (bf16[256,512]{1,0:T(8,128)(2,1)}, f32[8,128]{1,0:T(8,128)}, bf16[256,256]{1,0:T(8,128)(2,1)}, f32[2,1024,256]{2,1,0:T(8,128)}) custom-call(bf16[256,1024]{1,0:T(8,128)(2,1)S(1)} %constant_dynamic-update-slice_fusion.9.refs_0_.refs_10_, bf16[1024,512]{1,0:T(8,128)(2,1)S(1)} %get-tuple-element.188.refs_3_.refs_1_, ...), custom_call_target="tpu_custom_call", output_to_operand_aliasing={{3}: (10, {})} | custom-call | flops 1 | bytes 1 | tf_op jit(solution)/shard_map/pallas_call | solution.py:126
  294.0 5.0 %shard_map.302 = (bf16[128,1024]{1,0:T(8,128)(2,1)S(1)}, bf16[128,1024]{1,0:T(8,128)(2,1)S(1)}, bf16[1024,512]{1,0:T(8,128)(2,1)S(1)}, f32[8,128]{1,0:T(8,128)S(1)}) custom-call(f32[2,1024,256]{2,1,0:T(8,128)} %get-tuple-element.290.refs_0_, f32[256,256]{1,0:T(8,128)} %get-tuple-element.291.refs_1_, f32[256,256]{1,0:T(8,128)} %get-tuple-element.292.refs_2_, ...), custom_call_target="tpu_custom_call" | custom-call | flops 1 | bytes 1 | tf_op jit(solution)/shard_map/pallas_call | solution.py:126
  299.6 2.9 collective-permute-start.47
  302.5 9.5 %shard_map.305 = (bf16[16,32,768]{2,1,0:T(8,128)(2,1)S(1)}, bf16[16,32,768]{2,1,0:T(8,128)(2,1)S(1)}, f32[56,768]{1,0:T(8,128)S(1)}) custom-call(s32[3]{0:T(128)S(1)} %pad_add_fusion.1.refs_0_, bf16[1024,512]{1,0:T(8,128)(2,1)S(1)} %get-tuple-element.297.refs_0_.refs_1_, f32[8,128]{1,0:T(8,128)S(1)} %get-tuple-element.305.refs_2_, ...), custom_call_target="tpu_custom_call" | custom-call | flops 1 | bytes 1 | tf_op jit(solution)/shard_map/pallas_call | solution.py:126
  312.1 2.8 collective-permute-start.52
  316.9 3.7 collective-permute-done.51
  321.6 3.9 %shard_map.303 = (bf16[256,1024]{1,0:T(8,128)(2,1)}, bf16[256,1024]{1,0:T(8,128)(2,1)S(1)}, bf16[256,1024]{1,0:T(8,128)(2,1)S(1)}) custom-call(bf16[1024,512]{1,0:T(8,128)(2,1)S(1)} %get-tuple-element.297.refs_0_.refs_1_, bf16[128,1024]{1,0:T(8,128)(2,1)S(1)} %collective-permute-done.46.refs_1_, bf16[128,1024]{1,0:T(8,128)(2,1)S(1)} %collective-permute-done.47.refs_2_, ...), custom_call_target="tpu_custom_call" | custom-call | flops 1 | bytes 1 | tf_op jit(solution)/shard_map/pallas_call | solution.py:126
  325.8 3.1 collective-permute-start.49
  330.1 4.8 %collective-permute-start.56 = (bf16[208,768]{1,0:T(8,128)(2,1)}, bf16[208,768]{1,0:T(8,128)(2,1)S(1)}, u32[]{:S(2)}, u32[]{:S(2)}) collective-permute-start(bf16[208,768]{1,0:T(8,128)(2,1)} %get-tuple-element.323), channel_id=1, source_target_pairs={{0,64},{4,20},{8,72},{12,28},{16,80},{20,4},{24,88},{28,12},{32,96... | collective-permute-start | bytes 958472 | tf_op jit(solution)/shard_map/ppermute | solution.py:758
  338.2 3.1 collective-permute-done.48.refs_1_
  344.1 4.6 %collective-permute-start.59 = (bf16[112,768]{1,0:T(8,128)(2,1)S(1)}, bf16[112,768]{1,0:T(8,128)(2,1)S(1)}, u32[]{:S(2)}, u32[]{:S(2)}) collective-permute-start(bf16[112,768]{1,0:T(8,128)(2,1)S(1)} %get-tuple-element.331), channel_id=1, source_target_pairs={{0,16},{4,68},{8,24},{12,76},{16,0},{20,84},{24,8},{28,92},{32,48}... | collective-permute-start | bytes 516104 | tf_op jit(solution)/shard_map/ppermute | solution.py:758
  349.6 3.0 shard_map.304
  (208 shorter events, 88.7 us)
Async XLA Ops:
  7.2 111.2 %all-gather.3.cloned.1.call-start = ((), (), s32[]{:S(2)}) async-start(), calls=%async_computation.2 | async-start | bytes 8912896 | tf_op jit(solution)/shard_map/all_gather | solution.py:831
  7.9 328.0 %reduce-scatter.2.cloned.1.call-start = ((), (), s32[]{:S(2)}) async-start(), calls=%async_computation.1 | async-start | bytes 8912896 | tf_op jit(solution)/shard_map/reduce_scatter | solution.py:997
  8.0 14.4 %collective-permute-start.3 = (bf16[256,1024]{1,0:T(8,128)(2,1)}, bf16[256,1024]{1,0:T(8,128)(2,1)S(1)}, u32[]{:S(2)}, u32[]{:S(2)}) collective-permute-start(bf16[256,1024]{1,0:T(8,128)(2,1)} %refs_3_.3), channel_id=1, source_target_pairs={{0,3},{1,0},{2,1},{3,2},{4,7},{5,4},{6,5},{7,6},{8,11},{9,8},{10,9... | collective-permute-start | bytes 1572872 | tf_op jit(solution)/shard_map/ppermute | solution.py:762
  10.9 14.8 %collective-permute-start.4 = (bf16[256,1024]{1,0:T(8,128)(2,1)}, bf16[256,1024]{1,0:T(8,128)(2,1)S(1)}, u32[]{:S(2)}, u32[]{:S(2)}) collective-permute-start(bf16[256,1024]{1,0:T(8,128)(2,1)} %refs_3_.3), channel_id=1, source_target_pairs={{0,1},{1,2},{2,3},{3,0},{4,5},{5,6},{6,7},{7,4},{8,9},{9,10},{10,1... | collective-permute-start | bytes 1572872 | tf_op jit(solution)/shard_map/ppermute | solution.py:762
  25.7 9.4 %collective-permute-start.5 = (bf16[4,96,256]{2,1,0:T(8,128)(2,1)S(1)}, bf16[4,96,256]{2,1,0:T(8,128)(2,1)S(1)}, u32[]{:S(2)}, u32[]{:S(2)}) collective-permute-start(bf16[4,96,256]{2,1,0:T(8,128)(2,1)S(1)} %pad_maximum_fusion.4), channel_id=1, source_target_pairs={{0,24},{4,100},{8,0},{12,108},{16,8},{20,116},{24,16},{28,124},{32... | collective-permute-start | bytes 589832 | tf_op jit(solution)/shard_map/ppermute | solution.py:758
  29.7 9.8 %collective-permute-start.6 = (bf16[4,96,256]{2,1,0:T(8,128)(2,1)S(1)}, bf16[4,96,256]{2,1,0:T(8,128)(2,1)S(1)}, u32[]{:S(2)}, u32[]{:S(2)}) collective-permute-start(bf16[4,96,256]{2,1,0:T(8,128)(2,1)S(1)} %pad_maximum_fusion.4), channel_id=1, source_target_pairs={{0,16},{4,68},{8,24},{12,76},{16,0},{20,84},{24,8},{28,92},{32,48}... | collective-permute-start | bytes 589832 | tf_op jit(solution)/shard_map/ppermute | solution.py:758
  29.7 12.0 %collective-permute-start.7 = (bf16[4,96,256]{2,1,0:T(8,128)(2,1)S(1)}, bf16[4,96,256]{2,1,0:T(8,128)(2,1)S(1)}, u32[]{:S(2)}, u32[]{:S(2)}) collective-permute-start(bf16[4,96,256]{2,1,0:T(8,128)(2,1)S(1)} %pad_maximum_fusion.4), channel_id=1, source_target_pairs={{0,8},{4,36},{8,16},{12,44},{16,24},{20,52},{24,0},{28,60},{32,40}... | collective-permute-start | bytes 589832 | tf_op jit(solution)/shard_map/ppermute | solution.py:758
  31.0 10.8 %collective-permute-start.8 = (bf16[128,1024]{1,0:T(8,128)(2,1)S(1)}, bf16[128,1024]{1,0:T(8,128)(2,1)S(1)}, u32[]{:S(2)}, u32[]{:S(2)}) collective-permute-start(bf16[128,1024]{1,0:T(8,128)(2,1)S(1)} %slice.96), channel_id=1, source_target_pairs={{0,3},{1,0},{2,1},{3,2},{4,7},{5,4},{6,5},{7,6},{8,11},{9,8},{10,9... | collective-permute-start | bytes 786440 | tf_op jit(solution)/shard_map/ppermute | solution.py:762
  31.5 10.3 %collective-permute-start.9 = (bf16[128,1024]{1,0:T(8,128)(2,1)S(1)}, bf16[128,1024]{1,0:T(8,128)(2,1)S(1)}, u32[]{:S(2)}, u32[]{:S(2)}) collective-permute-start(bf16[128,1024]{1,0:T(8,128)(2,1)S(1)} %slice.97), channel_id=1, source_target_pairs={{0,1},{1,2},{2,3},{3,0},{4,5},{5,6},{6,7},{7,4},{8,9},{9,10},{10,1... | collective-permute-start | bytes 786440 | tf_op jit(solution)/shard_map/ppermute | solution.py:762
  44.2 14.9 %collective-permute-start.11 = (bf16[1,1024,512]{2,1,0:T(8,128)(2,1)S(1)}, bf16[1,1024,512]{2,1,0:T(8,128)(2,1)}, u32[]{:S(2)}, u32[]{:S(2)}) collective-permute-start(bf16[1,1024,512]{2,1,0:T(8,128)(2,1)S(1)} %copy-done), channel_id=1, source_target_pairs={{0,4},{4,0},{8,12},{12,8},{16,20},{20,16},{24,28},{28,24},{32,36},... | collective-permute-start | bytes 3145736 | tf_op jit(solution)/shard_map/ppermute | solution.py:747
  45.1 14.0 %collective-permute-start.12 = (bf16[1,1024,512]{2,1,0:T(8,128)(2,1)}, bf16[1,1024,512]{2,1,0:T(8,128)(2,1)}, u32[]{:S(2)}, u32[]{:S(2)}) collective-permute-start(bf16[1,1024,512]{2,1,0:T(8,128)(2,1)} %refs_6_.7), channel_id=1, source_target_pairs={{0,4},{4,0},{8,12},{12,8},{16,20},{20,16},{24,28},{28,24},{32,36},... | collective-permute-start | bytes 3145736 | tf_op jit(solution)/shard_map/ppermute | solution.py:747
  45.2 13.9 %collective-permute-start.13 = (bf16[1,512,1024]{2,1,0:T(8,128)(2,1)}, bf16[1,512,1024]{2,1,0:T(8,128)(2,1)}, u32[]{:S(2)}, u32[]{:S(2)}) collective-permute-start(bf16[1,512,1024]{2,1,0:T(8,128)(2,1)} %refs_7_.7), channel_id=1, source_target_pairs={{0,4},{4,0},{8,12},{12,8},{16,20},{20,16},{24,28},{28,24},{32,36},... | collective-permute-start | bytes 3145736 | tf_op jit(solution)/shard_map/ppermute | solution.py:747
  62.3 16.7 %collective-permute-start.14 = (bf16[256,1024]{1,0:T(8,128)(2,1)}, bf16[256,1024]{1,0:T(8,128)(2,1)}, u32[]{:S(2)}, u32[]{:S(2)}) collective-permute-start(bf16[256,1024]{1,0:T(8,128)(2,1)} %get-tuple-element.189), channel_id=1, source_target_pairs={{0,2},{1,3},{2,0},{3,1},{4,6},{5,7},{6,4},{7,5},{8,10},{9,11},{10,... | collective-permute-start | bytes 1572872 | tf_op jit(solution)/shard_map/ppermute | solution.py:762
  65.6 21.9 %collective-permute-start.16 = (bf16[256,1024]{1,0:T(8,128)(2,1)}, bf16[256,1024]{1,0:T(8,128)(2,1)}, u32[]{:S(2)}, u32[]{:S(2)}) collective-permute-start(bf16[256,1024]{1,0:T(8,128)(2,1)} %get-tuple-element.195), channel_id=1, source_target_pairs={{0,3},{1,0},{2,1},{3,2},{4,7},{5,4},{6,5},{7,6},{8,11},{9,8},{10,9... | collective-permute-start | bytes 1572872 | tf_op jit(solution)/shard_map/ppermute | solution.py:762
  71.0 18.4 %collective-permute-start.15 = (bf16[256,1024]{1,0:T(8,128)(2,1)}, bf16[256,1024]{1,0:T(8,128)(2,1)}, u32[]{:S(2)}, u32[]{:S(2)}) collective-permute-start(bf16[256,1024]{1,0:T(8,128)(2,1)} %get-tuple-element.193), channel_id=1, source_target_pairs={{0,1},{1,2},{2,3},{3,0},{4,5},{5,6},{6,7},{7,4},{8,9},{9,10},{10,1... | collective-permute-start | bytes 1572872 | tf_op jit(solution)/shard_map/ppermute | solution.py:762
  93.2 9.6 %collective-permute-start.17 = (bf16[272,1024]{1,0:T(8,128)(2,1)S(1)}, bf16[272,1024]{1,0:T(8,128)(2,1)S(1)}, u32[]{:S(2)}, u32[]{:S(2)}) collective-permute-start(bf16[272,1024]{1,0:T(8,128)(2,1)S(1)} %get-tuple-element.199.refs_0_.refs_4_), channel_id=1, source_target_pairs={{0,96},{4,28},{8,104},{12,4},{16,112},{20,12},{24,120},{28,20},{32... | collective-permute-start | bytes 1671176 | tf_op jit(solution)/shard_map/ppermute | solution.py:758
  95.3 10.8 %collective-permute-start.19 = (bf16[272,1024]{1,0:T(8,128)(2,1)S(1)}, bf16[272,1024]{1,0:T(8,128)(2,1)S(1)}, u32[]{:S(2)}, u32[]{:S(2)}) collective-permute-start(bf16[272,1024]{1,0:T(8,128)(2,1)S(1)} %get-tuple-element.199.refs_0_.refs_4_), channel_id=1, source_target_pairs={{0,32},{4,12},{8,40},{12,20},{16,48},{20,28},{24,56},{28,4},{32,64... | collective-permute-start | bytes 1671176 | tf_op jit(solution)/shard_map/ppermute | solution.py:758
  102.8 11.1 %collective-permute-start.20 = (bf16[144,1024]{1,0:T(8,128)(2,1)S(1)}, bf16[144,1024]{1,0:T(8,128)(2,1)S(1)}, u32[]{:S(2)}, u32[]{:S(2)}) collective-permute-start(bf16[144,1024]{1,0:T(8,128)(2,1)S(1)} %slice.98), channel_id=1, source_target_pairs={{0,96},{4,28},{8,104},{12,4},{16,112},{20,12},{24,120},{28,20},{32... | collective-permute-start | bytes 884744 | tf_op jit(solution)/shard_map/ppermute | solution.py:758
  107.4 25.4 %collective-permute-start.18 = (bf16[2,272,1024]{2,1,0:T(8,128)(2,1)}, bf16[2,272,1024]{2,1,0:T(8,128)(2,1)}, u32[]{:S(2)}, u32[]{:S(2)}) collective-permute-start(bf16[2,272,1024]{2,1,0:T(8,128)(2,1)} %pad_maximum_fusion.refs_1_), channel_id=1, source_target_pairs={{0,24},{4,100},{8,0},{12,108},{16,8},{20,116},{24,16},{28,124},{32... | collective-permute-start | bytes 3342344 | tf_op jit(solution)/shard_map/ppermute | solution.py:758
  115.0 17.8 %collective-permute-start.22 = (bf16[2,272,1024]{2,1,0:T(8,128)(2,1)}, bf16[2,272,1024]{2,1,0:T(8,128)(2,1)}, u32[]{:S(2)}, u32[]{:S(2)}) collective-permute-start(bf16[2,272,1024]{2,1,0:T(8,128)(2,1)} %pad_maximum_fusion.1.refs_2_), channel_id=1, source_target_pairs={{0,8},{4,36},{8,16},{12,44},{16,24},{20,52},{24,0},{28,60},{32,40}... | collective-permute-start | bytes 3342344 | tf_op jit(solution)/shard_map/ppermute | solution.py:758
  115.0 21.3 %collective-permute-start.25 = (bf16[2,272,1024]{2,1,0:T(8,128)(2,1)}, bf16[2,272,1024]{2,1,0:T(8,128)(2,1)}, u32[]{:S(2)}, u32[]{:S(2)}) collective-permute-start(bf16[2,272,1024]{2,1,0:T(8,128)(2,1)} %pad_maximum_fusion.1.refs_2_), channel_id=1, source_target_pairs={{0,24},{4,100},{8,0},{12,108},{16,8},{20,116},{24,16},{28,124},{32... | collective-permute-start | bytes 3342344 | tf_op jit(solution)/shard_map/ppermute | solution.py:758
  118.3 33.1 %collective-permute-start.27 = (bf16[2,272,1024]{2,1,0:T(8,128)(2,1)}, bf16[2,272,1024]{2,1,0:T(8,128)(2,1)}, u32[]{:S(2)}, u32[]{:S(2)}) collective-permute-start(bf16[2,272,1024]{2,1,0:T(8,128)(2,1)} %pad_maximum_fusion.refs_1_), channel_id=1, source_target_pairs={{0,8},{4,36},{8,16},{12,44},{16,24},{20,52},{24,0},{28,60},{32,40}... | collective-permute-start | bytes 3342344 | tf_op jit(solution)/shard_map/ppermute | solution.py:758
  132.8 18.7 %collective-permute-start.23 = (bf16[2,272,1024]{2,1,0:T(8,128)(2,1)}, bf16[2,272,1024]{2,1,0:T(8,128)(2,1)}, u32[]{:S(2)}, u32[]{:S(2)}) collective-permute-start(bf16[2,272,1024]{2,1,0:T(8,128)(2,1)} %collective-permute-done.18.refs_1_), channel_id=1, source_target_pairs={{0,24},{4,100},{8,0},{12,108},{16,8},{20,116},{24,16},{28,124},{32... | collective-permute-start | bytes 3342344 | tf_op jit(solution)/shard_map/ppermute | solution.py:758
  136.1 19.9 %collective-permute-start.24 = (bf16[2,272,1024]{2,1,0:T(8,128)(2,1)}, bf16[2,272,1024]{2,1,0:T(8,128)(2,1)}, u32[]{:S(2)}, u32[]{:S(2)}) collective-permute-start(bf16[2,272,1024]{2,1,0:T(8,128)(2,1)} %collective-permute-done.22.refs_2_), channel_id=1, source_target_pairs={{0,8},{4,36},{8,16},{12,44},{16,24},{20,52},{24,0},{28,60},{32,40}... | collective-permute-start | bytes 3342344 | tf_op jit(solution)/shard_map/ppermute | solution.py:758
  150.7 19.8 %collective-permute-start.26 = (bf16[2,272,1024]{2,1,0:T(8,128)(2,1)}, bf16[2,272,1024]{2,1,0:T(8,128)(2,1)}, u32[]{:S(2)}, u32[]{:S(2)}) collective-permute-start(bf16[2,272,1024]{2,1,0:T(8,128)(2,1)} %get-tuple-element.210), channel_id=1, source_target_pairs={{0,8},{4,36},{8,16},{12,44},{16,24},{20,52},{24,0},{28,60},{32,40}... | collective-permute-start | bytes 3342344 | tf_op jit(solution)/shard_map/ppermute | solution.py:758
  170.3 18.2 %collective-permute-start.30 = (bf16[2,272,1024]{2,1,0:T(8,128)(2,1)}, bf16[2,272,1024]{2,1,0:T(8,128)(2,1)S(1)}, u32[]{:S(2)}, u32[]{:S(2)}) collective-permute-start(bf16[2,272,1024]{2,1,0:T(8,128)(2,1)} %get-tuple-element.242), channel_id=1, source_target_pairs={{0,24},{4,100},{8,0},{12,108},{16,8},{20,116},{24,16},{28,124},{32... | collective-permute-start | bytes 3342344 | tf_op jit(solution)/shard_map/ppermute | solution.py:758
  185.0 17.0 %collective-permute-start.28 = (bf16[2,272,1024]{2,1,0:T(8,128)(2,1)}, bf16[2,272,1024]{2,1,0:T(8,128)(2,1)S(1)}, u32[]{:S(2)}, u32[]{:S(2)}) collective-permute-start(bf16[2,272,1024]{2,1,0:T(8,128)(2,1)} %get-tuple-element.234), channel_id=1, source_target_pairs={{0,8},{4,36},{8,16},{12,44},{16,24},{20,52},{24,0},{28,60},{32,40}... | collective-permute-start | bytes 3342344 | tf_op jit(solution)/shard_map/ppermute | solution.py:758
  187.0 15.9 %collective-permute-start.29 = (bf16[2,272,1024]{2,1,0:T(8,128)(2,1)}, bf16[2,272,1024]{2,1,0:T(8,128)(2,1)S(1)}, u32[]{:S(2)}, u32[]{:S(2)}) collective-permute-start(bf16[2,272,1024]{2,1,0:T(8,128)(2,1)} %get-tuple-element.236), channel_id=1, source_target_pairs={{0,24},{4,100},{8,0},{12,108},{16,8},{20,116},{24,16},{28,124},{32... | collective-permute-start | bytes 3342344 | tf_op jit(solution)/shard_map/ppermute | solution.py:758
  203.4 17.6 %collective-permute-start.33 = (bf16[2,272,1024]{2,1,0:T(8,128)(2,1)S(1)}, bf16[2,272,1024]{2,1,0:T(8,128)(2,1)S(1)}, u32[]{:S(2)}, u32[]{:S(2)}) collective-permute-start(bf16[2,272,1024]{2,1,0:T(8,128)(2,1)S(1)} %add_convert_fusion.2), channel_id=1, source_target_pairs={{0,24},{4,100},{8,0},{12,108},{16,8},{20,116},{24,16},{28,124},{32... | collective-permute-start | bytes 3342344 | tf_op jit(solution)/shard_map/ppermute | solution.py:758
  206.4 20.2 %collective-permute-start.32 = (bf16[2,272,1024]{2,1,0:T(8,128)(2,1)S(1)}, bf16[2,272,1024]{2,1,0:T(8,128)(2,1)S(1)}, u32[]{:S(2)}, u32[]{:S(2)}) collective-permute-start(bf16[2,272,1024]{2,1,0:T(8,128)(2,1)S(1)} %add_convert_fusion.3), channel_id=1, source_target_pairs={{0,8},{4,36},{8,16},{12,44},{16,24},{20,52},{24,0},{28,60},{32,40}... | collective-permute-start | bytes 3342344 | tf_op jit(solution)/shard_map/ppermute | solution.py:758
  217.3 17.4 %collective-permute-start.36 = (bf16[384,512]{1,0:T(8,128)(2,1)S(1)}, bf16[384,512]{1,0:T(8,128)(2,1)S(1)}, u32[]{:S(2)}, u32[]{:S(2)}) collective-permute-start(bf16[384,512]{1,0:T(8,128)(2,1)S(1)} %get-tuple-element.252), channel_id=1, source_target_pairs={{0,1},{1,2},{2,3},{3,0},{4,5},{5,6},{6,7},{7,4},{8,9},{9,10},{10,1... | collective-permute-start | bytes 1179656 | tf_op jit(solution)/shard_map/ppermute | solution.py:762
  217.4 17.3 %collective-permute-start.37 = (bf16[384,512]{1,0:T(8,128)(2,1)S(1)}, bf16[384,512]{1,0:T(8,128)(2,1)S(1)}, u32[]{:S(2)}, u32[]{:S(2)}) collective-permute-start(bf16[384,512]{1,0:T(8,128)(2,1)S(1)} %get-tuple-element.253), channel_id=1, source_target_pairs={{0,3},{1,0},{2,1},{3,2},{4,7},{5,4},{6,5},{7,6},{8,11},{9,8},{10,9... | collective-permute-start | bytes 1179656 | tf_op jit(solution)/shard_map/ppermute | solution.py:762
  236.7 10.7 %collective-permute-start.38 = (bf16[272,1024]{1,0:T(8,128)(2,1)S(1)}, bf16[272,1024]{1,0:T(8,128)(2,1)S(1)}, u32[]{:S(2)}, u32[]{:S(2)}) collective-permute-start(bf16[272,1024]{1,0:T(8,128)(2,1)S(1)} %pad_maximum_fusion.2), channel_id=1, source_target_pairs={{0,32},{4,12},{8,40},{12,20},{16,48},{20,28},{24,56},{28,4},{32,64... | collective-permute-start | bytes 1671176 | tf_op jit(solution)/shard_map/ppermute | solution.py:758
  236.7 10.7 %collective-permute-start.39 = (bf16[272,1024]{1,0:T(8,128)(2,1)S(1)}, bf16[272,1024]{1,0:T(8,128)(2,1)S(1)}, u32[]{:S(2)}, u32[]{:S(2)}) collective-permute-start(bf16[272,1024]{1,0:T(8,128)(2,1)S(1)} %pad_maximum_fusion.3), channel_id=1, source_target_pairs={{0,96},{4,28},{8,104},{12,4},{16,112},{20,12},{24,120},{28,20},{32... | collective-permute-start | bytes 1671176 | tf_op jit(solution)/shard_map/ppermute | solution.py:758
  252.8 10.8 %collective-permute-start.40 = (bf16[256,1024]{1,0:T(8,128)(2,1)S(1)}, bf16[256,1024]{1,0:T(8,128)(2,1)S(1)}, u32[]{:S(2)}, u32[]{:S(2)}) collective-permute-start(bf16[256,1024]{1,0:T(8,128)(2,1)S(1)} %copy-done.5), channel_id=1, source_target_pairs={{0,3},{1,0},{2,1},{3,2},{4,7},{5,4},{6,5},{7,6},{8,11},{9,8},{10,9... | collective-permute-start | bytes 1572872 | tf_op jit(solution)/shard_map/ppermute | solution.py:762
  252.8 12.1 %collective-permute-start.41 = (bf16[256,1024]{1,0:T(8,128)(2,1)S(1)}, bf16[256,1024]{1,0:T(8,128)(2,1)S(1)}, u32[]{:S(2)}, u32[]{:S(2)}) collective-permute-start(bf16[256,1024]{1,0:T(8,128)(2,1)S(1)} %copy-done.5), channel_id=1, source_target_pairs={{0,1},{1,2},{2,3},{3,0},{4,5},{5,6},{6,7},{7,4},{8,9},{9,10},{10,1... | collective-permute-start | bytes 1572872 | tf_op jit(solution)/shard_map/ppermute | solution.py:762
  264.9 29.0 %collective-permute-start.44 = (bf16[768,512]{1,0:T(8,128)(2,1)S(1)}, bf16[768,512]{1,0:T(8,128)(2,1)S(1)}, u32[]{:S(2)}, u32[]{:S(2)}) collective-permute-start(bf16[768,512]{1,0:T(8,128)(2,1)S(1)} %copy-done.9), channel_id=1, source_target_pairs={{0,1},{1,2},{2,3},{3,0},{4,5},{5,6},{6,7},{7,4},{8,9},{9,10},{10,1... | collective-permute-start | bytes 2359304 | tf_op jit(solution)/shard_map/ppermute | solution.py:762
  266.9 27.1 %collective-permute-start.45 = (bf16[768,512]{1,0:T(8,128)(2,1)S(1)}, bf16[768,512]{1,0:T(8,128)(2,1)S(1)}, u32[]{:S(2)}, u32[]{:S(2)}) collective-permute-start(bf16[768,512]{1,0:T(8,128)(2,1)S(1)} %copy-done.7), channel_id=1, source_target_pairs={{0,3},{1,0},{2,1},{3,2},{4,7},{5,4},{6,5},{7,6},{8,11},{9,8},{10,9... | collective-permute-start | bytes 2359304 | tf_op jit(solution)/shard_map/ppermute | solution.py:762
  275.1 10.8 %collective-permute-start.42 = (bf16[128,1024]{1,0:T(8,128)(2,1)S(1)}, bf16[128,1024]{1,0:T(8,128)(2,1)S(1)}, u32[]{:S(2)}, u32[]{:S(2)}) collective-permute-start(bf16[128,1024]{1,0:T(8,128)(2,1)S(1)} %slice.83), channel_id=1, source_target_pairs={{0,3},{1,0},{2,1},{3,2},{4,7},{5,4},{6,5},{7,6},{8,11},{9,8},{10,9... | collective-permute-start | bytes 786440 | tf_op jit(solution)/shard_map/ppermute | solution.py:762
  275.2 11.8 %collective-permute-start.43 = (bf16[128,1024]{1,0:T(8,128)(2,1)S(1)}, bf16[128,1024]{1,0:T(8,128)(2,1)S(1)}, u32[]{:S(2)}, u32[]{:S(2)}) collective-permute-start(bf16[128,1024]{1,0:T(8,128)(2,1)S(1)} %slice.84), channel_id=1, source_target_pairs={{0,1},{1,2},{2,3},{3,0},{4,5},{5,6},{6,7},{7,4},{8,9},{9,10},{10,1... | collective-permute-start | bytes 786440 | tf_op jit(solution)/shard_map/ppermute | solution.py:762
  298.9 16.6 %collective-permute-start.46 = (bf16[128,1024]{1,0:T(8,128)(2,1)S(1)}, bf16[128,1024]{1,0:T(8,128)(2,1)S(1)}, u32[]{:S(2)}, u32[]{:S(2)}) collective-permute-start(bf16[128,1024]{1,0:T(8,128)(2,1)S(1)} %get-tuple-element.298), channel_id=1, source_target_pairs={{0,1},{1,2},{2,3},{3,0},{4,5},{5,6},{6,7},{7,4},{8,9},{9,10},{10,1... | collective-permute-start | bytes 786440 | tf_op jit(solution)/shard_map/ppermute | solution.py:762
  299.6 16.0 %collective-permute-start.47 = (bf16[128,1024]{1,0:T(8,128)(2,1)S(1)}, bf16[128,1024]{1,0:T(8,128)(2,1)S(1)}, u32[]{:S(2)}, u32[]{:S(2)}) collective-permute-start(bf16[128,1024]{1,0:T(8,128)(2,1)S(1)} %get-tuple-element.299), channel_id=1, source_target_pairs={{0,3},{1,0},{2,1},{3,2},{4,7},{5,4},{6,5},{7,6},{8,11},{9,8},{10,9... | collective-permute-start | bytes 786440 | tf_op jit(solution)/shard_map/ppermute | solution.py:762
  315.5 13.4 %collective-permute-start.50 = (bf16[16,32,768]{2,1,0:T(8,128)(2,1)S(1)}, bf16[16,32,768]{2,1,0:T(8,128)(2,1)S(1)}, u32[]{:S(2)}, u32[]{:S(2)}) collective-permute-start(bf16[16,32,768]{2,1,0:T(8,128)(2,1)S(1)} %get-tuple-element.319), channel_id=1, source_target_pairs={{0,4},{4,0},{8,12},{12,8},{16,20},{20,16},{24,28},{28,24},{32,36},... | collective-permute-start | bytes 2359304 | tf_op jit(solution)/shard_map/ppermute | solution.py:747
  325.5 15.8 %collective-permute-start.48 = (bf16[256,1024]{1,0:T(8,128)(2,1)}, bf16[256,1024]{1,0:T(8,128)(2,1)S(1)}, u32[]{:S(2)}, u32[]{:S(2)}) collective-permute-start(bf16[256,1024]{1,0:T(8,128)(2,1)} %get-tuple-element.302), channel_id=1, source_target_pairs={{0,1},{1,2},{2,3},{3,0},{4,5},{5,6},{6,7},{7,4},{8,9},{9,10},{10,1... | collective-permute-start | bytes 1572872 | tf_op jit(solution)/shard_map/ppermute | solution.py:762
  325.8 15.6 %collective-permute-start.49 = (bf16[256,1024]{1,0:T(8,128)(2,1)S(1)}, bf16[256,1024]{1,0:T(8,128)(2,1)S(1)}, u32[]{:S(2)}, u32[]{:S(2)}) collective-permute-start(bf16[256,1024]{1,0:T(8,128)(2,1)S(1)} %get-tuple-element.303), channel_id=1, source_target_pairs={{0,3},{1,0},{2,1},{3,2},{4,7},{5,4},{6,5},{7,6},{8,11},{9,8},{10,9... | collective-permute-start | bytes 1572872 | tf_op jit(solution)/shard_map/ppermute | solution.py:762
  330.0 11.4 %collective-permute-start.55 = (bf16[208,768]{1,0:T(8,128)(2,1)}, bf16[208,768]{1,0:T(8,128)(2,1)S(1)}, u32[]{:S(2)}, u32[]{:S(2)}) collective-permute-start(bf16[208,768]{1,0:T(8,128)(2,1)} %get-tuple-element.322), channel_id=1, source_target_pairs={{0,32},{4,12},{8,40},{12,20},{16,48},{20,28},{24,56},{28,4},{32,64... | collective-permute-start | bytes 958472 | tf_op jit(solution)/shard_map/ppermute | solution.py:758
  330.1 13.4 %collective-permute-start.56 = (bf16[208,768]{1,0:T(8,128)(2,1)}, bf16[208,768]{1,0:T(8,128)(2,1)S(1)}, u32[]{:S(2)}, u32[]{:S(2)}) collective-permute-start(bf16[208,768]{1,0:T(8,128)(2,1)} %get-tuple-element.323), channel_id=1, source_target_pairs={{0,64},{4,20},{8,72},{12,28},{16,80},{20,4},{24,88},{28,12},{32,96... | collective-permute-start | bytes 958472 | tf_op jit(solution)/shard_map/ppermute | solution.py:758
  344.1 9.8 %collective-permute-start.59 = (bf16[112,768]{1,0:T(8,128)(2,1)S(1)}, bf16[112,768]{1,0:T(8,128)(2,1)S(1)}, u32[]{:S(2)}, u32[]{:S(2)}) collective-permute-start(bf16[112,768]{1,0:T(8,128)(2,1)S(1)} %get-tuple-element.331), channel_id=1, source_target_pairs={{0,16},{4,68},{8,24},{12,76},{16,0},{20,84},{24,8},{28,92},{32,48}... | collective-permute-start | bytes 516104 | tf_op jit(solution)/shard_map/ppermute | solution.py:758
  (37 other events, 269.2 us)
Sparse Core Ops, SparseCore 0:
  10.2 76.8 all-gather.2
  251.9 83.9 reduce-scatter.1

commit v4 on v3

--- a/solution.py
+++ b/solution.py
@@ -231,7 +231,8 @@
     return jnp.where(lane < HDIM, turn, 0.0), jnp.where(lane < HDIM, pltpu.roll(turn, HDIM, 1), 0.0)
 
 
-def attend_body(qa, ka, va, out_w, branch, mixed, qb):
+def attend_body(qa, ka, va, out_w, *refs):
+    branches, (mixed_out, qb_out, mixed, qb, sems) = refs[:-5], refs[-5:]
     lane = lanes((TOK, PITCH))
     for head in range(4):
         cols = slice(head * PITCH, (head + 1) * PITCH)
@@ -249,14 +250,30 @@
         qb[:, cols] = jnp.where(
             (lane > HDIM) & (lane < HDIM + 4), stats, query.astype(F32)
         ).astype(BF16)
-    branch[...] = nt(mixed[...], out_w[...]).astype(BF16)
-
-
-def middle_body(x, p0, p1, p2, p3, gain, coded, x_mid, h2):
-    total = (
-        x[...].astype(F32)
-        + ((p0[...].astype(F32) + p1[...].astype(F32)) + (p2[...].astype(F32) + p3[...].astype(F32)))
-    )
+    copies = [
+        pltpu.make_async_copy(mixed, mixed_out, sems.at[0]),
+        pltpu.make_async_copy(qb, qb_out, sems.at[1]),
+    ]
+    for one in copies:
+        one.start()
+    branch = nt(mixed[...], out_w[...]).astype(BF16)
+    rows = TOK // len(branches)
+    for n, target in enumerate(branches):
+        target[...] = branch[n * rows : (n + 1) * rows]
+    for one in copies:
+        one.wait()
+
+
+def near_body(up, down, far_up, far_down, out_up, out_down):
+    half = TOK // 2
+    out_up[:half, :] = (up[:half, :].astype(F32) + far_up[...].astype(F32)).astype(BF16)
+    out_up[half:, :] = up[half:, :]
+    out_down[:half, :] = down[:half, :]
+    out_down[half:, :] = (down[half:, :].astype(F32) + far_down[...].astype(F32)).astype(BF16)
+
+
+def middle_body(x, p0, p1, p2, gain, coded, x_mid, h2):
+    total = x[...].astype(F32) + (p0[...].astype(F32) + (p1[...].astype(F32) + p2[...].astype(F32)))
     x_mid[...] = total
     h2[0:TOK, :] = (total * row_scale(total) * gain[...]).astype(BF16)
     h2[TOK:ROWS, :] = coded[...]
@@ -708,14 +725,21 @@
         outs[second][64:112, :] = router
 
 
-def ride_last_body(own, g1, g2, g3, rows, gain, router, ffn):
-    rows[...] = add4(own, g1, g2, g3, 0, 32)
-    gain[...] = add_gains(own, g1, g2, g3, 32)
+def ride_last_body(own, g1, g2, g3, query, pair, out_w, attn, query_gain, key_gain, router, ffn):
+    rows = add4(own, g1, g2, g3, 0, 32)
+    query[...] = rows[:, 0:256]
+    pair[:, 0, :] = rows[:, 256:384]
+    pair[:, 1, :] = rows[:, 384:512]
+    out_w[...] = rows[:, 512:768]
+    gain = add_gains(own, g1, g2, g3, 32)
+    attn[:, 0:768] = gain[0:1, :]
+    attn[:, 768:1024] = gain[1:2, 0:256]
+    query_gain[...] = gain[1:2, 256:384]
+    key_gain[...] = gain[1:2, 384:512]
     total = add4(own, g1, g2, g3, 64, 112)
-    whole = jnp.concatenate(
-        [total[0:32], jnp.concatenate([total[32:48, 0:256], total[32:48, 256:512]], axis=0)], axis=1
-    )
-    router[...] = jnp.transpose(whole)
+    router[:, 0:768] = total[0:32]
+    router[0:16, 768:1024] = total[32:48, 0:256]
+    router[16:32, 768:1024] = total[32:48, 256:512]
     for quarter in range(4):
         ffn[:, quarter * 256 : (quarter + 1) * 256] = total[32 + quarter : 33 + quarter, 512:768]
 
@@ -865,25 +889,37 @@
     ka, va, out_w, turn_tab = out[15], out[16], out[17], out[18:22]
 
     qa = list(after(tuple(qa), weights_other))
-    branch, mixed, qb = [None] * 4, [None] * 4, [None] * 4
-    arrived = [None] * 4
-    for r in (2, 1, 3, 0):
-        if r == 0:
-            qa[0] = after(qa[0], arrived[2])
-        branch[r], mixed[r], qb[r] = call(
+    mixed, qb = [None] * 4, [None] * 4
+    def attend(r, parts=1):
+        *made, mixed[r], qb[r] = call(
             attend_body,
-            [((TOK, WIDTH), BF16), ((TOK, 512), BF16), ((TOK, 512), BF16)],
+            [((TOK // parts, WIDTH), BF16)] * parts + [((TOK, 512), BF16)] * 2,
             (qa[r], ka, va, out_w),
-            near=(0,),
+            any_out=(parts, parts + 1),
+            scratch=[pltpu.VMEM((TOK, 512), BF16), pltpu.VMEM((TOK, 512), BF16), pltpu.SemaphoreType.DMA((2,))],
+            near=range(parts),
             local=(0, 1, 2, 3),
         )
-        arrived[r] = shift_mp(branch[r], r) if r else branch[r]
+        return made
+
+    branch_up, branch_down = attend(2, 2)
+    branch_up, branch_down = shift_mp(branch_up, 1), shift_mp(branch_down, -1)
+    (part_up,), (part_down,) = attend(1), attend(3)
+    part_up, part_down = call(
+        near_body,
+        [((TOK, WIDTH), BF16)] * 2,
+        (part_up, part_down, branch_up, branch_down),
+        near=(0, 1),
+        local=range(4),
+    )
+    (branch,) = attend(0)
+    arrived = (branch, shift_mp(part_up, 1), shift_mp(part_down, -1))
     x_mid, h2 = call(
         middle_body,
         [((TOK, WIDTH), F32), ((ROWS, WIDTH), BF16)],
         (layer_input, *arrived, ffn_row, coded),
         near=(1,),
-        local=(1, 2, 3, 4),
+        local=(1, 2, 3),
     )
     (gates,) = call(gates_body, [((EXPERTS, TOK), F32)], (h2, router, ranks))
 
@@ -1092,13 +1128,21 @@
         near=range(4),
         local=range(4),
     )
-    weight_sum, gain_sum, router_grad, ffn_grad = call(
+    query_w_grad, pair_w_grad, out_w_grad, attn_grad, query_gain_grad, key_gain_grad, router_grad, ffn_grad = call(
         ride_last_body,
-        [((32, 768), F32), ((4, 768), F32), ((WIDTH, EXPERTS), F32), ((1, WIDTH), F32)],
+        [
+            ((32, 256), F32),
+            ((32, 2, 128), F32),
+            ((32, 256), F32),
+            ((1, WIDTH), F32),
+            ((1, PITCH), F32),
+            ((1, PITCH), F32),
+            ((EXPERTS, WIDTH), F32),
+            ((1, WIDTH), F32),
+        ],
         (second_msg[0], *(shift_axis(second_msg[s], 1, s) for s in (1, 2, 3))),
         local=range(4),
     )
-    attn_gain_grad = jnp.concatenate([gain_sum[0], gain_sum[1, 0:256]])
     (input_grad,) = call(
         input_body,
         [((TOK, WIDTH), F32)],
@@ -1109,14 +1153,14 @@
     return (
         layer_output,
         input_grad,
-        attn_gain_grad,
-        gain_sum[1, 256 : 256 + HDIM],
-        gain_sum[1, 384 : 384 + HDIM],
-        weight_sum[:, 0:256],
-        weight_sum[:, 256:512].reshape(32, 2, 128),
-        weight_sum[:, 512:768],
+        attn_grad.reshape(WIDTH),
+        query_gain_grad[0, :HDIM],
+        key_gain_grad[0, :HDIM],
+        query_w_grad,
+        pair_w_grad,
+        out_w_grad,
         ffn_grad.reshape(WIDTH),
-        router_grad,
+        router_grad.T,
         *expert_outs,
     )
 

time: 374 us -> 366 us (0.979)
  local copies, waits for them, and re-layouts: 16.3 us -> 10.9 us
    ppermute x22 -> x23, starting transfers between devices: 29.2 us -> 33.7 us  [shift_mp(): return lax.ppermute(tensor, 'mp', [(i, (i + step) % 4) for i in range(4)])]
    ppermute x22 -> x23, waiting for transfers between devices: 29.7 us -> 26.9 us  [shift_mp(): return lax.ppermute(tensor, 'mp', [(i, (i + step) % 4) for i in range(4)])]
    pallas_call x27 -> x28, Pallas kernels: 162 us -> 160 us  [call(): pl.pallas_call(kernel, out_shape=shapes, in_specs=in_specs, out_specs=out...]
    unnamed x52 -> x51, local copies, waits for them, and re-layouts: 7.71 us -> 5.83 us
  transfers between devices with their start and end apart: 63 -> 64, of which waited for: 32 -> 30; matrix products, arithmetic and copies ran while one was open for 4% -> 4% of each run, Pallas kernels for 42% -> 43%
where the time goes in v4:
time: 366 us; the launch traced here: 362 us
  Pallas kernels  160 us (44%)
  waiting for transfers between devices  84.8 us (23%)
  starting transfers between devices  80.8 us (22%)
  between operations  15.9 us (4%)
  local copies, waits for them, and re-layouts  10.9 us (3%)
  other arithmetic  9.6 us (3%)
    pallas_call x28, Pallas kernels, call(): pl.pallas_call(kernel, out_shape=shapes, in_specs=in_specs, out_specs=out...  160 us
    ppermute x32, waiting for transfers between devices, shift_axis(): return lax.ppermute(tensor, 'dp', pairs)  53.5 us
    ppermute x32, starting transfers between devices, shift_axis(): return lax.ppermute(tensor, 'dp', pairs)  45.8 us
    ppermute x23, starting transfers between devices, shift_mp(): return lax.ppermute(tensor, 'mp', [(i, (i + step) % 4) for i in range(4)])  33.7 us
    ppermute x23, waiting for transfers between devices, shift_mp(): return lax.ppermute(tensor, 'mp', [(i, (i + step) % 4) for i in range(4)])  26.9 us
  transfers between devices with their start and end apart: 64, of which 30 were waited for; matrix products, arithmetic and copies ran while one was open for 4% of the time, Pallas kernels for 43%

profile of v4, /device:TPU:0, one launch (start us, length us, event | category | flops | bytes accessed | tf_op | source)
XLA Modules:
  0.0 361.8 jit_solution(3665081571292576099)
XLA Ops:
  8.0 2.9 collective-permute-start.3
  13.0 3.0 collective-permute-start
  17.8 3.9 %collective-permute-done.1 = bf16[96,256]{1,0:T(8,128)(2,1)S(1)} collective-permute-done((bf16[96,256]{1,0:T(8,128)(2,1)S(1)}, bf16[96,256]{1,0:T(8,128)(2,1)S(1)}, u32[]{:S(2)}, u32[]{:S(2)}) %collective-permute-start.1) | collective-permute-done | bytes 49184 | tf_op jit(solution)/shard_map/ppermute | solution.py:782
  22.4 3.3 collective-permute-done.4.refs_6_
  25.7 4.0 %collective-permute-start.5 = (bf16[4,96,256]{2,1,0:T(8,128)(2,1)S(1)}, bf16[4,96,256]{2,1,0:T(8,128)(2,1)S(1)}, u32[]{:S(2)}, u32[]{:S(2)}) collective-permute-start(bf16[4,96,256]{2,1,0:T(8,128)(2,1)S(1)} %pad_maximum_fusion.4), channel_id=1, source_target_pairs={{0,24},{4,100},{8,0},{12,108},{16,8},{20,116},{24,16},{28,124},{32... | collective-permute-start | bytes 589832 | tf_op jit(solution)/shard_map/ppermute | solution.py:782
  35.1 4.4 %collective-permute-done.6 = bf16[4,96,256]{2,1,0:T(8,128)(2,1)S(1)} collective-permute-done((bf16[4,96,256]{2,1,0:T(8,128)(2,1)S(1)}, bf16[4,96,256]{2,1,0:T(8,128)(2,1)S(1)}, u32[]{:S(2)}, u32[]{:S(2)}) %collective-permute-start.6) | collective-permute-done | bytes 196640 | tf_op jit(solution)/shard_map/ppermute | solution.py:782
  47.5 11.6 %shard_map.282 = (bf16[1024,1024]{1,0:T(8,128)(2,1)}, bf16[1024,1024]{1,0:T(8,128)(2,1)}, bf16[1024,768]{1,0:T(8,128)(2,1)}, f32[256,512]{1,0:T(8,128)}, f32[256...) custom-call(s32[5]{0:T(128)S(1)} %stack.136.refs_0_, ...), custom_call_target="tpu_custom_call" | custom-call | flops 1 | bytes 1 | tf_op jit(solution)/shard_map/pallas_call | solution.py:126
  61.5 3.2 collective-permute-start.15
  72.4 3.2 collective-permute-start.17
  76.5 2.6 shard_map.288
  81.4 5.7 %collective-permute-done.16.refs_2_ = bf16[256,1024]{1,0:T(8,128)(2,1)} collective-permute-done((bf16[256,1024]{1,0:T(8,128)(2,1)}, bf16[256,1024]{1,0:T(8,128)(2,1)}, u32[]{:S(2)}, u32[]{:S(2)}) %collective-permute-start.16) | collective-permute-done | bytes 524320 | tf_op jit(solution)/shard_map/ppermute | solution.py:786
  87.1 3.6 shard_map.289
  92.8 7.5 %collective-permute-done.18 = bf16[272,1024]{1,0:T(8,128)(2,1)S(1)} collective-permute-done((bf16[272,1024]{1,0:T(8,128)(2,1)S(1)}, bf16[272,1024]{1,0:T(8,128)(2,1)S(1)}, u32[]{:S(2)}, u32[]{:S(2)}) %collective-permute-start.18) | collective-permute-done | bytes 557088 | tf_op jit(solution)/shard_map/ppermute | solution.py:782
  100.3 3.3 collective-permute-start.21
  105.5 5.9 %collective-permute-done.22 = bf16[128,1024]{1,0:T(8,128)(2,1)S(1)} collective-permute-done((bf16[128,1024]{1,0:T(8,128)(2,1)S(1)}, bf16[128,1024]{1,0:T(8,128)(2,1)S(1)}, u32[]{:S(2)}, u32[]{:S(2)}) %collective-permute-start.22) | collective-permute-done | bytes 262176 | tf_op jit(solution)/shard_map/ppermute | solution.py:782
  112.7 3.1 collective-permute-start.26
  116.2 14.4 %shard_map.290 = (bf16[16,256,1024]{2,1,0:T(8,128)(2,1)}, bf16[2,272,1024]{2,1,0:T(8,128)(2,1)}, bf16[2,272,1024]{2,1,0:T(8,128)(2,1)}, bf16[2,1536,1024]{2,1,0:...) custom-call(s32[6]{0:T(128)S(1)} %stack.160.refs_0_, ...), custom_call_target="tpu_custom_call" | custom-call | flops 1 | bytes 1 | tf_op jit(solution)/shard_map/pallas_call | solution.py:126
  130.6 3.3 collective-permute-start.24
  134.2 14.4 %shard_map.291 = (bf16[16,256,1024]{2,1,0:T(8,128)(2,1)}, bf16[2,272,1024]{2,1,0:T(8,128)(2,1)}, bf16[2,272,1024]{2,1,0:T(8,128)(2,1)}, bf16[2,1536,1024]{2,1,0:...) custom-call(s32[6]{0:T(128)S(1)} %stack.165.refs_0_, ...), custom_call_target="tpu_custom_call", output_to_operand_aliasing={{0}: (11, {}), {3}: (12, {}), {4}: (13, {}), {5}: (14, {}),... | custom-call | flops 1 | bytes 1 | tf_op jit(solution)/shard_map/pallas_call | solution.py:126
  149.4 4.1 %collective-permute-done.25.refs_2_ = bf16[2,272,1024]{2,1,0:T(8,128)(2,1)} collective-permute-done((bf16[2,272,1024]{2,1,0:T(8,128)(2,1)}, bf16[2,272,1024]{2,1,0:T(8,128)(2,1)}, u32[]{:S(2)}, u32[]{:S(2)}) %collective-permute-start.25) | collective-permute-done | bytes 1114144 | tf_op jit(solution)/shard_map/ppermute | solution.py:782
  153.5 14.4 %shard_map.292 = (bf16[16,256,1024]{2,1,0:T(8,128)(2,1)}, bf16[2,272,1024]{2,1,0:T(8,128)(2,1)}, bf16[2,272,1024]{2,1,0:T(8,128)(2,1)}, bf16[2,1536,1024]{2,1,0:...) custom-call(s32[6]{0:T(128)S(1)} %stack.170.refs_0_, ...), custom_call_target="tpu_custom_call", output_to_operand_aliasing={{0}: (11, {}), {3}: (12, {}), {4}: (13, {}), {5}: (14, {}),... | custom-call | flops 1 | bytes 1 | tf_op jit(solution)/shard_map/pallas_call | solution.py:126
  168.2 14.4 %shard_map.293 = (bf16[16,256,1024]{2,1,0:T(8,128)(2,1)}, bf16[2,272,1024]{2,1,0:T(8,128)(2,1)}, bf16[2,272,1024]{2,1,0:T(8,128)(2,1)}, bf16[2,1536,1024]{2,1,0:...) custom-call(s32[6]{0:T(128)S(1)} %stack.149.refs_0_, ...), custom_call_target="tpu_custom_call", output_to_operand_aliasing={{0}: (11, {}), {3}: (12, {}), {4}: (13, {}), {5}: (14, {}),... | custom-call | flops 1 | bytes 1 | tf_op jit(solution)/shard_map/pallas_call | solution.py:126
  186.1 8.1 %shard_map.294 = bf16[3072,512]{1,0:T(8,128)(2,1)S(1)} custom-call(s32[1]{0:T(128)} %bitcast.3.refs_0_, bf16[2,1536,1024]{2,1,0:T(8,128)(2,1)} %get-tuple-element.251.refs_1_, bf16[2,1536,512]{2,1,0:T(8,128)(2,1)} %get-tuple-element.252.refs_2_, bf16[2,1536,512]{2,1,0:T(8,128)(2,1)} %get-tuple-element.253.refs_3_, ...), custom_call_target="tpu_custom_call" | custom-call | flops 1 | bytes 1 | tf_op jit(solution)/shard_map/pallas_call | solution.py:126
  194.2 5.3 %collective-permute-done.29 = bf16[2,272,1024]{2,1,0:T(8,128)(2,1)S(1)} collective-permute-done((bf16[2,272,1024]{2,1,0:T(8,128)(2,1)}, bf16[2,272,1024]{2,1,0:T(8,128)(2,1)S(1)}, u32[]{:S(2)}, u32[]{:S(2)}) %collective-permute-start.29) | collective-permute-done | bytes 1114144 | tf_op jit(solution)/shard_map/ppermute | solution.py:782
  206.2 8.7 %shard_map.295 = (bf16[768,512]{1,0:T(8,128)(2,1)S(1)}, bf16[768,512]{1,0:T(8,128)(2,1)S(1)}, bf16[768,512]{1,0:T(8,128)(2,1)S(1)}, bf16[384,512]{1,0:T(8,128)(2,1)S(1)}, bf16[384,512]{1,0:T(8,128)(2,1)S(1)}) custom-call(s32[1]{0:T(128)} %bitcast.3.refs_0_, bf16[2,1536,1024]{2,1,0:T(8,128)(2,1)} %get-tuple-element.251.refs_1_, ...), custom_call_target="tpu_custom_call" | custom-call | flops 1 | bytes 1 | tf_op jit(solution)/shard_map/pallas_call | solution.py:126
  220.7 3.2 collective-permute-start.36
  224.8 3.0 collective-permute-done.36
  227.9 4.0 %collective-permute-done.35 = bf16[144,1024]{1,0:T(8,128)(2,1)S(1)} collective-permute-done((bf16[144,1024]{1,0:T(8,128)(2,1)S(1)}, bf16[144,1024]{1,0:T(8,128)(2,1)S(1)}, u32[]{:S(2)}, u32[]{:S(2)}) %collective-permute-start.35) | collective-permute-done | bytes 294944 | tf_op jit(solution)/shard_map/ppermute | solution.py:782
  234.2 3.2 collective-permute-start.40
  239.5 5.4 %collective-permute-done.39.refs_2_ = bf16[272,1024]{1,0:T(8,128)(2,1)S(1)} collective-permute-done((bf16[272,1024]{1,0:T(8,128)(2,1)S(1)}, bf16[272,1024]{1,0:T(8,128)(2,1)S(1)}, u32[]{:S(2)}, u32[]{:S(2)}) %collective-permute-start.39) | collective-permute-done | bytes 557088 | tf_op jit(solution)/shard_map/ppermute | solution.py:782
  244.9 4.3 %shard_map.298 = (f32[256,1024]{1,0:T(8,128)}, bf16[256,1024]{1,0:T(8,128)(2,1)}, f32[48,768]{1,0:T(8,128)}) custom-call(s32[2]{0:T(128)S(1)} %pad_add_fusion.refs_0_, bf16[272,1024]{1,0:T(8,128)(2,1)S(1)} %slice_bitcast_fusion.refs_1_, bf16[272,1024]{1,0:T(8,128)(2,1)S(1)} %collective-permute-done.39.refs_2_, ...), custom_call_target="tpu_custom_call" | custom-call | flops 1 | bytes 1 | tf_op jit(solution)/shard_map/pallas_call | solution.py:126
  252.3 6.6 %shard_map.299 = (bf16[256,512]{1,0:T(8,128)(2,1)}, f32[8,128]{1,0:T(8,128)}, bf16[256,256]{1,0:T(8,128)(2,1)}, f32[2,1024,256]{2,1,0:T(8,128)}) custom-call(bf16[256,1024]{1,0:T(8,128)(2,1)S(1)} %copy-done.5, bf16[1024,512]{1,0:T(8,128)(2,1)S(1)} %get-tuple-element.193.refs_3_.refs_1_, bf16[256,512]{1,0:T(8,128)(2,1)} %get-tuple-element.276.refs_2_, ...), custom_call_target="tpu_custom_call" | custom-call | flops 1 | bytes 1 | tf_op jit(solution)/shard_map/pallas_call | solution.py:126
  261.3 2.8 collective-permute-done.42.refs_0_.refs_11_
  264.1 3.2 collective-permute-start.46
  267.4 6.9 %shard_map.300 = (bf16[256,512]{1,0:T(8,128)(2,1)}, f32[8,128]{1,0:T(8,128)}, bf16[256,256]{1,0:T(8,128)(2,1)}, f32[2,1024,256]{2,1,0:T(8,128)}) custom-call(bf16[256,1024]{1,0:T(8,128)(2,1)S(1)} %collective-permute-done.41.refs_0_.refs_9_, bf16[1024,512]{1,0:T(8,128)(2,1)S(1)} %get-tuple-element.193.refs_3_.refs_1_, ...), custom_call_target="tpu_custom_call", output_to_operand_aliasing={{3}: (10, {})} | custom-call | flops 1 | bytes 1 | tf_op jit(solution)/shard_map/pallas_call | solution.py:126
  276.6 6.9 %shard_map.301 = (bf16[256,512]{1,0:T(8,128)(2,1)}, f32[8,128]{1,0:T(8,128)}, bf16[256,256]{1,0:T(8,128)(2,1)}, f32[2,1024,256]{2,1,0:T(8,128)}) custom-call(bf16[256,1024]{1,0:T(8,128)(2,1)S(1)} %collective-permute-done.42.refs_0_.refs_11_, bf16[1024,512]{1,0:T(8,128)(2,1)S(1)} %get-tuple-element.193.refs_3_.refs_1_, ...), custom_call_target="tpu_custom_call", output_to_operand_aliasing={{3}: (10, {})} | custom-call | flops 1 | bytes 1 | tf_op jit(solution)/shard_map/pallas_call | solution.py:126
  286.4 6.9 %shard_map.302 = (bf16[256,512]{1,0:T(8,128)(2,1)}, f32[8,128]{1,0:T(8,128)}, bf16[256,256]{1,0:T(8,128)(2,1)}, f32[2,1024,256]{2,1,0:T(8,128)}) custom-call(bf16[256,1024]{1,0:T(8,128)(2,1)S(1)} %constant_dynamic-update-slice_fusion.9.refs_0_.refs_10_, bf16[1024,512]{1,0:T(8,128)(2,1)S(1)} %get-tuple-element.193.refs_3_.refs_1_, ...), custom_call_target="tpu_custom_call", output_to_operand_aliasing={{3}: (10, {})} | custom-call | flops 1 | bytes 1 | tf_op jit(solution)/shard_map/pallas_call | solution.py:126
  293.3 5.0 %shard_map.303 = (bf16[128,1024]{1,0:T(8,128)(2,1)S(1)}, bf16[128,1024]{1,0:T(8,128)(2,1)S(1)}, bf16[1024,512]{1,0:T(8,128)(2,1)S(1)}, f32[8,128]{1,0:T(8,128)S(1)}) custom-call(f32[2,1024,256]{2,1,0:T(8,128)} %get-tuple-element.298.refs_0_, f32[256,256]{1,0:T(8,128)} %get-tuple-element.299.refs_1_, f32[256,256]{1,0:T(8,128)} %get-tuple-element.300.refs_2_, ...), custom_call_target="tpu_custom_call" | custom-call | flops 1 | bytes 1 | tf_op jit(solution)/shard_map/pallas_call | solution.py:126
  298.4 3.4 collective-permute-start.48
  301.9 9.5 %shard_map.306 = (bf16[16,32,768]{2,1,0:T(8,128)(2,1)S(1)}, bf16[16,32,768]{2,1,0:T(8,128)(2,1)S(1)}, f32[56,768]{1,0:T(8,128)S(1)}) custom-call(s32[3]{0:T(128)S(1)} %pad_add_fusion.1.refs_0_, bf16[1024,512]{1,0:T(8,128)(2,1)S(1)} %get-tuple-element.305.refs_0_.refs_1_, f32[8,128]{1,0:T(8,128)S(1)} %get-tuple-element.313.refs_2_, ...), custom_call_target="tpu_custom_call" | custom-call | flops 1 | bytes 1 | tf_op jit(solution)/shard_map/pallas_call | solution.py:126
  311.5 2.9 collective-permute-start.53
  316.4 3.5 collective-permute-done.52
  320.9 3.9 %shard_map.304 = (bf16[256,1024]{1,0:T(8,128)(2,1)}, bf16[256,1024]{1,0:T(8,128)(2,1)S(1)}, bf16[256,1024]{1,0:T(8,128)(2,1)S(1)}) custom-call(bf16[1024,512]{1,0:T(8,128)(2,1)S(1)} %get-tuple-element.305.refs_0_.refs_1_, bf16[128,1024]{1,0:T(8,128)(2,1)S(1)} %collective-permute-done.47.refs_1_, bf16[128,1024]{1,0:T(8,128)(2,1)S(1)} %collective-permute-done.48.refs_2_, ...), custom_call_target="tpu_custom_call" | custom-call | flops 1 | bytes 1 | tf_op jit(solution)/shard_map/pallas_call | solution.py:126
  325.2 3.0 collective-permute-start.50
  329.4 4.5 %collective-permute-start.57 = (bf16[208,768]{1,0:T(8,128)(2,1)}, bf16[208,768]{1,0:T(8,128)(2,1)S(1)}, u32[]{:S(2)}, u32[]{:S(2)}) collective-permute-start(bf16[208,768]{1,0:T(8,128)(2,1)} %get-tuple-element.331), channel_id=1, source_target_pairs={{0,64},{4,20},{8,72},{12,28},{16,80},{20,4},{24,88},{28,12},{32,96... | collective-permute-start | bytes 958472 | tf_op jit(solution)/shard_map/ppermute | solution.py:782
  337.0 3.7 %collective-permute-done.49.refs_1_ = bf16[256,1024]{1,0:T(8,128)(2,1)S(1)} collective-permute-done((bf16[256,1024]{1,0:T(8,128)(2,1)}, bf16[256,1024]{1,0:T(8,128)(2,1)S(1)}, u32[]{:S(2)}, u32[]{:S(2)}) %collective-permute-start.49) | collective-permute-done | bytes 524320 | tf_op jit(solution)/shard_map/ppermute | solution.py:786
  342.7 4.6 %collective-permute-start.60 = (bf16[112,768]{1,0:T(8,128)(2,1)S(1)}, bf16[112,768]{1,0:T(8,128)(2,1)S(1)}, u32[]{:S(2)}, u32[]{:S(2)}) collective-permute-start(bf16[112,768]{1,0:T(8,128)(2,1)S(1)} %get-tuple-element.339), channel_id=1, source_target_pairs={{0,16},{4,68},{8,24},{12,76},{16,0},{20,84},{24,8},{28,92},{32,48}... | collective-permute-start | bytes 516104 | tf_op jit(solution)/shard_map/ppermute | solution.py:782
  347.4 3.0 shard_map.305
  (205 shorter events, 83.9 us)
Async XLA Ops:
  7.2 109.0 %all-gather.3.cloned.1.call-start = ((), (), s32[]{:S(2)}) async-start(), calls=%async_computation.2 | async-start | bytes 8912896 | tf_op jit(solution)/shard_map/all_gather | solution.py:855
  7.9 326.8 %reduce-scatter.2.cloned.1.call-start = ((), (), s32[]{:S(2)}) async-start(), calls=%async_computation.1 | async-start | bytes 8912896 | tf_op jit(solution)/shard_map/reduce_scatter | solution.py:1033
  8.0 14.4 %collective-permute-start.3 = (bf16[256,1024]{1,0:T(8,128)(2,1)}, bf16[256,1024]{1,0:T(8,128)(2,1)S(1)}, u32[]{:S(2)}, u32[]{:S(2)}) collective-permute-start(bf16[256,1024]{1,0:T(8,128)(2,1)} %refs_3_.3), channel_id=1, source_target_pairs={{0,3},{1,0},{2,1},{3,2},{4,7},{5,4},{6,5},{7,6},{8,11},{9,8},{10,9... | collective-permute-start | bytes 1572872 | tf_op jit(solution)/shard_map/ppermute | solution.py:786
  10.9 14.8 %collective-permute-start.4 = (bf16[256,1024]{1,0:T(8,128)(2,1)}, bf16[256,1024]{1,0:T(8,128)(2,1)S(1)}, u32[]{:S(2)}, u32[]{:S(2)}) collective-permute-start(bf16[256,1024]{1,0:T(8,128)(2,1)} %refs_3_.3), channel_id=1, source_target_pairs={{0,1},{1,2},{2,3},{3,0},{4,5},{5,6},{6,7},{7,4},{8,9},{9,10},{10,1... | collective-permute-start | bytes 1572872 | tf_op jit(solution)/shard_map/ppermute | solution.py:786
  29.7 9.8 %collective-permute-start.6 = (bf16[4,96,256]{2,1,0:T(8,128)(2,1)S(1)}, bf16[4,96,256]{2,1,0:T(8,128)(2,1)S(1)}, u32[]{:S(2)}, u32[]{:S(2)}) collective-permute-start(bf16[4,96,256]{2,1,0:T(8,128)(2,1)S(1)} %pad_maximum_fusion.4), channel_id=1, source_target_pairs={{0,16},{4,68},{8,24},{12,76},{16,0},{20,84},{24,8},{28,92},{32,48}... | collective-permute-start | bytes 589832 | tf_op jit(solution)/shard_map/ppermute | solution.py:782
  29.7 12.0 %collective-permute-start.7 = (bf16[4,96,256]{2,1,0:T(8,128)(2,1)S(1)}, bf16[4,96,256]{2,1,0:T(8,128)(2,1)S(1)}, u32[]{:S(2)}, u32[]{:S(2)}) collective-permute-start(bf16[4,96,256]{2,1,0:T(8,128)(2,1)S(1)} %pad_maximum_fusion.4), channel_id=1, source_target_pairs={{0,8},{4,36},{8,16},{12,44},{16,24},{20,52},{24,0},{28,60},{32,40}... | collective-permute-start | bytes 589832 | tf_op jit(solution)/shard_map/ppermute | solution.py:782
  31.0 10.8 %collective-permute-start.8 = (bf16[128,1024]{1,0:T(8,128)(2,1)S(1)}, bf16[128,1024]{1,0:T(8,128)(2,1)S(1)}, u32[]{:S(2)}, u32[]{:S(2)}) collective-permute-start(bf16[128,1024]{1,0:T(8,128)(2,1)S(1)} %slice.76), channel_id=1, source_target_pairs={{0,3},{1,0},{2,1},{3,2},{4,7},{5,4},{6,5},{7,6},{8,11},{9,8},{10,9... | collective-permute-start | bytes 786440 | tf_op jit(solution)/shard_map/ppermute | solution.py:786
  31.5 10.3 %collective-permute-start.9 = (bf16[128,1024]{1,0:T(8,128)(2,1)S(1)}, bf16[128,1024]{1,0:T(8,128)(2,1)S(1)}, u32[]{:S(2)}, u32[]{:S(2)}) collective-permute-start(bf16[128,1024]{1,0:T(8,128)(2,1)S(1)} %slice.77), channel_id=1, source_target_pairs={{0,1},{1,2},{2,3},{3,0},{4,5},{5,6},{6,7},{7,4},{8,9},{9,10},{10,1... | collective-permute-start | bytes 786440 | tf_op jit(solution)/shard_map/ppermute | solution.py:786
  44.2 14.8 %collective-permute-start.11 = (bf16[1,1024,512]{2,1,0:T(8,128)(2,1)S(1)}, bf16[1,1024,512]{2,1,0:T(8,128)(2,1)}, u32[]{:S(2)}, u32[]{:S(2)}) collective-permute-start(bf16[1,1024,512]{2,1,0:T(8,128)(2,1)S(1)} %copy-done), channel_id=1, source_target_pairs={{0,4},{4,0},{8,12},{12,8},{16,20},{20,16},{24,28},{28,24},{32,36},... | collective-permute-start | bytes 3145736 | tf_op jit(solution)/shard_map/ppermute | solution.py:771
  45.1 14.0 %collective-permute-start.12 = (bf16[1,1024,512]{2,1,0:T(8,128)(2,1)}, bf16[1,1024,512]{2,1,0:T(8,128)(2,1)}, u32[]{:S(2)}, u32[]{:S(2)}) collective-permute-start(bf16[1,1024,512]{2,1,0:T(8,128)(2,1)} %refs_6_.7), channel_id=1, source_target_pairs={{0,4},{4,0},{8,12},{12,8},{16,20},{20,16},{24,28},{28,24},{32,36},... | collective-permute-start | bytes 3145736 | tf_op jit(solution)/shard_map/ppermute | solution.py:771
  45.2 13.8 %collective-permute-start.13 = (bf16[1,512,1024]{2,1,0:T(8,128)(2,1)}, bf16[1,512,1024]{2,1,0:T(8,128)(2,1)}, u32[]{:S(2)}, u32[]{:S(2)}) collective-permute-start(bf16[1,512,1024]{2,1,0:T(8,128)(2,1)} %refs_7_.7), channel_id=1, source_target_pairs={{0,4},{4,0},{8,12},{12,8},{16,20},{20,16},{24,28},{28,24},{32,36},... | collective-permute-start | bytes 3145736 | tf_op jit(solution)/shard_map/ppermute | solution.py:771
  61.4 9.6 %collective-permute-start.14 = (bf16[128,1024]{1,0:T(8,128)(2,1)S(1)}, bf16[128,1024]{1,0:T(8,128)(2,1)S(1)}, u32[]{:S(2)}, u32[]{:S(2)}) collective-permute-start(bf16[128,1024]{1,0:T(8,128)(2,1)S(1)} %get-tuple-element.200), channel_id=1, source_target_pairs={{0,1},{1,2},{2,3},{3,0},{4,5},{5,6},{6,7},{7,4},{8,9},{9,10},{10,1... | collective-permute-start | bytes 786440 | tf_op jit(solution)/shard_map/ppermute | solution.py:786
  61.5 9.5 %collective-permute-start.15 = (bf16[128,1024]{1,0:T(8,128)(2,1)S(1)}, bf16[128,1024]{1,0:T(8,128)(2,1)S(1)}, u32[]{:S(2)}, u32[]{:S(2)}) collective-permute-start(bf16[128,1024]{1,0:T(8,128)(2,1)S(1)} %get-tuple-element.201), channel_id=1, source_target_pairs={{0,3},{1,0},{2,1},{3,2},{4,7},{5,4},{6,5},{7,6},{8,11},{9,8},{10,9... | collective-permute-start | bytes 786440 | tf_op jit(solution)/shard_map/ppermute | solution.py:786
  72.1 15.0 %collective-permute-start.16 = (bf16[256,1024]{1,0:T(8,128)(2,1)}, bf16[256,1024]{1,0:T(8,128)(2,1)}, u32[]{:S(2)}, u32[]{:S(2)}) collective-permute-start(bf16[256,1024]{1,0:T(8,128)(2,1)} %get-tuple-element.202), channel_id=1, source_target_pairs={{0,1},{1,2},{2,3},{3,0},{4,5},{5,6},{6,7},{7,4},{8,9},{9,10},{10,1... | collective-permute-start | bytes 1572872 | tf_op jit(solution)/shard_map/ppermute | solution.py:786
  72.4 14.8 %collective-permute-start.17 = (bf16[256,1024]{1,0:T(8,128)(2,1)}, bf16[256,1024]{1,0:T(8,128)(2,1)}, u32[]{:S(2)}, u32[]{:S(2)}) collective-permute-start(bf16[256,1024]{1,0:T(8,128)(2,1)} %get-tuple-element.203), channel_id=1, source_target_pairs={{0,3},{1,0},{2,1},{3,2},{4,7},{5,4},{6,5},{7,6},{8,11},{9,8},{10,9... | collective-permute-start | bytes 1572872 | tf_op jit(solution)/shard_map/ppermute | solution.py:786
  90.7 9.6 %collective-permute-start.18 = (bf16[272,1024]{1,0:T(8,128)(2,1)S(1)}, bf16[272,1024]{1,0:T(8,128)(2,1)S(1)}, u32[]{:S(2)}, u32[]{:S(2)}) collective-permute-start(bf16[272,1024]{1,0:T(8,128)(2,1)S(1)} %get-tuple-element.207.refs_0_.refs_4_), channel_id=1, source_target_pairs={{0,96},{4,28},{8,104},{12,4},{16,112},{20,12},{24,120},{28,20},{32... | collective-permute-start | bytes 1671176 | tf_op jit(solution)/shard_map/ppermute | solution.py:782
  92.8 10.8 %collective-permute-start.20 = (bf16[272,1024]{1,0:T(8,128)(2,1)S(1)}, bf16[272,1024]{1,0:T(8,128)(2,1)S(1)}, u32[]{:S(2)}, u32[]{:S(2)}) collective-permute-start(bf16[272,1024]{1,0:T(8,128)(2,1)S(1)} %get-tuple-element.207.refs_0_.refs_4_), channel_id=1, source_target_pairs={{0,32},{4,12},{8,40},{12,20},{16,48},{20,28},{24,56},{28,4},{32,64... | collective-permute-start | bytes 1671176 | tf_op jit(solution)/shard_map/ppermute | solution.py:782
  100.3 11.2 %collective-permute-start.21 = (bf16[144,1024]{1,0:T(8,128)(2,1)S(1)}, bf16[144,1024]{1,0:T(8,128)(2,1)S(1)}, u32[]{:S(2)}, u32[]{:S(2)}) collective-permute-start(bf16[144,1024]{1,0:T(8,128)(2,1)S(1)} %slice.78), channel_id=1, source_target_pairs={{0,96},{4,28},{8,104},{12,4},{16,112},{20,12},{24,120},{28,20},{32... | collective-permute-start | bytes 884744 | tf_op jit(solution)/shard_map/ppermute | solution.py:782
  104.8 25.8 %collective-permute-start.19 = (bf16[2,272,1024]{2,1,0:T(8,128)(2,1)}, bf16[2,272,1024]{2,1,0:T(8,128)(2,1)}, u32[]{:S(2)}, u32[]{:S(2)}) collective-permute-start(bf16[2,272,1024]{2,1,0:T(8,128)(2,1)} %pad_maximum_fusion.refs_1_), channel_id=1, source_target_pairs={{0,24},{4,100},{8,0},{12,108},{16,8},{20,116},{24,16},{28,124},{32... | collective-permute-start | bytes 3342344 | tf_op jit(solution)/shard_map/ppermute | solution.py:782
  112.6 18.0 %collective-permute-start.23 = (bf16[2,272,1024]{2,1,0:T(8,128)(2,1)}, bf16[2,272,1024]{2,1,0:T(8,128)(2,1)}, u32[]{:S(2)}, u32[]{:S(2)}) collective-permute-start(bf16[2,272,1024]{2,1,0:T(8,128)(2,1)} %pad_maximum_fusion.1.refs_2_), channel_id=1, source_target_pairs={{0,8},{4,36},{8,16},{12,44},{16,24},{20,52},{24,0},{28,60},{32,40}... | collective-permute-start | bytes 3342344 | tf_op jit(solution)/shard_map/ppermute | solution.py:782
  112.7 21.5 %collective-permute-start.26 = (bf16[2,272,1024]{2,1,0:T(8,128)(2,1)}, bf16[2,272,1024]{2,1,0:T(8,128)(2,1)}, u32[]{:S(2)}, u32[]{:S(2)}) collective-permute-start(bf16[2,272,1024]{2,1,0:T(8,128)(2,1)} %pad_maximum_fusion.1.refs_2_), channel_id=1, source_target_pairs={{0,24},{4,100},{8,0},{12,108},{16,8},{20,116},{24,16},{28,124},{32... | collective-permute-start | bytes 3342344 | tf_op jit(solution)/shard_map/ppermute | solution.py:782
  115.9 33.5 %collective-permute-start.28 = (bf16[2,272,1024]{2,1,0:T(8,128)(2,1)}, bf16[2,272,1024]{2,1,0:T(8,128)(2,1)}, u32[]{:S(2)}, u32[]{:S(2)}) collective-permute-start(bf16[2,272,1024]{2,1,0:T(8,128)(2,1)} %pad_maximum_fusion.refs_1_), channel_id=1, source_target_pairs={{0,8},{4,36},{8,16},{12,44},{16,24},{20,52},{24,0},{28,60},{32,40}... | collective-permute-start | bytes 3342344 | tf_op jit(solution)/shard_map/ppermute | solution.py:782
  130.6 18.8 %collective-permute-start.24 = (bf16[2,272,1024]{2,1,0:T(8,128)(2,1)}, bf16[2,272,1024]{2,1,0:T(8,128)(2,1)}, u32[]{:S(2)}, u32[]{:S(2)}) collective-permute-start(bf16[2,272,1024]{2,1,0:T(8,128)(2,1)} %collective-permute-done.19.refs_1_), channel_id=1, source_target_pairs={{0,24},{4,100},{8,0},{12,108},{16,8},{20,116},{24,16},{28,124},{32... | collective-permute-start | bytes 3342344 | tf_op jit(solution)/shard_map/ppermute | solution.py:782
  133.9 19.6 %collective-permute-start.25 = (bf16[2,272,1024]{2,1,0:T(8,128)(2,1)}, bf16[2,272,1024]{2,1,0:T(8,128)(2,1)}, u32[]{:S(2)}, u32[]{:S(2)}) collective-permute-start(bf16[2,272,1024]{2,1,0:T(8,128)(2,1)} %collective-permute-done.23.refs_2_), channel_id=1, source_target_pairs={{0,8},{4,36},{8,16},{12,44},{16,24},{20,52},{24,0},{28,60},{32,40}... | collective-permute-start | bytes 3342344 | tf_op jit(solution)/shard_map/ppermute | solution.py:782
  148.6 19.5 %collective-permute-start.27 = (bf16[2,272,1024]{2,1,0:T(8,128)(2,1)}, bf16[2,272,1024]{2,1,0:T(8,128)(2,1)}, u32[]{:S(2)}, u32[]{:S(2)}) collective-permute-start(bf16[2,272,1024]{2,1,0:T(8,128)(2,1)} %get-tuple-element.218), channel_id=1, source_target_pairs={{0,8},{4,36},{8,16},{12,44},{16,24},{20,52},{24,0},{28,60},{32,40}... | collective-permute-start | bytes 3342344 | tf_op jit(solution)/shard_map/ppermute | solution.py:782
  167.9 18.2 %collective-permute-start.31 = (bf16[2,272,1024]{2,1,0:T(8,128)(2,1)}, bf16[2,272,1024]{2,1,0:T(8,128)(2,1)S(1)}, u32[]{:S(2)}, u32[]{:S(2)}) collective-permute-start(bf16[2,272,1024]{2,1,0:T(8,128)(2,1)} %get-tuple-element.250), channel_id=1, source_target_pairs={{0,24},{4,100},{8,0},{12,108},{16,8},{20,116},{24,16},{28,124},{32... | collective-permute-start | bytes 3342344 | tf_op jit(solution)/shard_map/ppermute | solution.py:782
  182.6 17.0 %collective-permute-start.29 = (bf16[2,272,1024]{2,1,0:T(8,128)(2,1)}, bf16[2,272,1024]{2,1,0:T(8,128)(2,1)S(1)}, u32[]{:S(2)}, u32[]{:S(2)}) collective-permute-start(bf16[2,272,1024]{2,1,0:T(8,128)(2,1)} %get-tuple-element.242), channel_id=1, source_target_pairs={{0,8},{4,36},{8,16},{12,44},{16,24},{20,52},{24,0},{28,60},{32,40}... | collective-permute-start | bytes 3342344 | tf_op jit(solution)/shard_map/ppermute | solution.py:782
  184.6 15.9 %collective-permute-start.30 = (bf16[2,272,1024]{2,1,0:T(8,128)(2,1)}, bf16[2,272,1024]{2,1,0:T(8,128)(2,1)S(1)}, u32[]{:S(2)}, u32[]{:S(2)}) collective-permute-start(bf16[2,272,1024]{2,1,0:T(8,128)(2,1)} %get-tuple-element.244), channel_id=1, source_target_pairs={{0,24},{4,100},{8,0},{12,108},{16,8},{20,116},{24,16},{28,124},{32... | collective-permute-start | bytes 3342344 | tf_op jit(solution)/shard_map/ppermute | solution.py:782
  201.0 17.7 %collective-permute-start.34 = (bf16[2,272,1024]{2,1,0:T(8,128)(2,1)S(1)}, bf16[2,272,1024]{2,1,0:T(8,128)(2,1)S(1)}, u32[]{:S(2)}, u32[]{:S(2)}) collective-permute-start(bf16[2,272,1024]{2,1,0:T(8,128)(2,1)S(1)} %add_convert_fusion.2), channel_id=1, source_target_pairs={{0,24},{4,100},{8,0},{12,108},{16,8},{20,116},{24,16},{28,124},{32... | collective-permute-start | bytes 3342344 | tf_op jit(solution)/shard_map/ppermute | solution.py:782
  204.0 20.1 %collective-permute-start.33 = (bf16[2,272,1024]{2,1,0:T(8,128)(2,1)S(1)}, bf16[2,272,1024]{2,1,0:T(8,128)(2,1)S(1)}, u32[]{:S(2)}, u32[]{:S(2)}) collective-permute-start(bf16[2,272,1024]{2,1,0:T(8,128)(2,1)S(1)} %add_convert_fusion.3), channel_id=1, source_target_pairs={{0,8},{4,36},{8,16},{12,44},{16,24},{20,52},{24,0},{28,60},{32,40}... | collective-permute-start | bytes 3342344 | tf_op jit(solution)/shard_map/ppermute | solution.py:782
  214.9 17.3 %collective-permute-start.37 = (bf16[384,512]{1,0:T(8,128)(2,1)S(1)}, bf16[384,512]{1,0:T(8,128)(2,1)S(1)}, u32[]{:S(2)}, u32[]{:S(2)}) collective-permute-start(bf16[384,512]{1,0:T(8,128)(2,1)S(1)} %get-tuple-element.260), channel_id=1, source_target_pairs={{0,1},{1,2},{2,3},{3,0},{4,5},{5,6},{6,7},{7,4},{8,9},{9,10},{10,1... | collective-permute-start | bytes 1179656 | tf_op jit(solution)/shard_map/ppermute | solution.py:786
  216.1 16.0 %collective-permute-start.38 = (bf16[384,512]{1,0:T(8,128)(2,1)S(1)}, bf16[384,512]{1,0:T(8,128)(2,1)S(1)}, u32[]{:S(2)}, u32[]{:S(2)}) collective-permute-start(bf16[384,512]{1,0:T(8,128)(2,1)S(1)} %get-tuple-element.261), channel_id=1, source_target_pairs={{0,3},{1,0},{2,1},{3,2},{4,7},{5,4},{6,5},{7,6},{8,11},{9,8},{10,9... | collective-permute-start | bytes 1179656 | tf_op jit(solution)/shard_map/ppermute | solution.py:786
  234.2 10.7 %collective-permute-start.39 = (bf16[272,1024]{1,0:T(8,128)(2,1)S(1)}, bf16[272,1024]{1,0:T(8,128)(2,1)S(1)}, u32[]{:S(2)}, u32[]{:S(2)}) collective-permute-start(bf16[272,1024]{1,0:T(8,128)(2,1)S(1)} %pad_maximum_fusion.2), channel_id=1, source_target_pairs={{0,32},{4,12},{8,40},{12,20},{16,48},{20,28},{24,56},{28,4},{32,64... | collective-permute-start | bytes 1671176 | tf_op jit(solution)/shard_map/ppermute | solution.py:782
  234.2 10.7 %collective-permute-start.40 = (bf16[272,1024]{1,0:T(8,128)(2,1)S(1)}, bf16[272,1024]{1,0:T(8,128)(2,1)S(1)}, u32[]{:S(2)}, u32[]{:S(2)}) collective-permute-start(bf16[272,1024]{1,0:T(8,128)(2,1)S(1)} %pad_maximum_fusion.3), channel_id=1, source_target_pairs={{0,96},{4,28},{8,104},{12,4},{16,112},{20,12},{24,120},{28,20},{32... | collective-permute-start | bytes 1671176 | tf_op jit(solution)/shard_map/ppermute | solution.py:782
  250.3 11.0 %collective-permute-start.41 = (bf16[256,1024]{1,0:T(8,128)(2,1)S(1)}, bf16[256,1024]{1,0:T(8,128)(2,1)S(1)}, u32[]{:S(2)}, u32[]{:S(2)}) collective-permute-start(bf16[256,1024]{1,0:T(8,128)(2,1)S(1)} %copy-done.5), channel_id=1, source_target_pairs={{0,3},{1,0},{2,1},{3,2},{4,7},{5,4},{6,5},{7,6},{8,11},{9,8},{10,9... | collective-permute-start | bytes 1572872 | tf_op jit(solution)/shard_map/ppermute | solution.py:786
  252.0 12.1 %collective-permute-start.42 = (bf16[256,1024]{1,0:T(8,128)(2,1)S(1)}, bf16[256,1024]{1,0:T(8,128)(2,1)S(1)}, u32[]{:S(2)}, u32[]{:S(2)}) collective-permute-start(bf16[256,1024]{1,0:T(8,128)(2,1)S(1)} %copy-done.5), channel_id=1, source_target_pairs={{0,1},{1,2},{2,3},{3,0},{4,5},{5,6},{6,7},{7,4},{8,9},{9,10},{10,1... | collective-permute-start | bytes 1572872 | tf_op jit(solution)/shard_map/ppermute | solution.py:786
  264.1 29.2 %collective-permute-start.45 = (bf16[768,512]{1,0:T(8,128)(2,1)S(1)}, bf16[768,512]{1,0:T(8,128)(2,1)S(1)}, u32[]{:S(2)}, u32[]{:S(2)}) collective-permute-start(bf16[768,512]{1,0:T(8,128)(2,1)S(1)} %copy-done.9), channel_id=1, source_target_pairs={{0,1},{1,2},{2,3},{3,0},{4,5},{5,6},{6,7},{7,4},{8,9},{9,10},{10,1... | collective-permute-start | bytes 2359304 | tf_op jit(solution)/shard_map/ppermute | solution.py:786
  264.1 29.2 %collective-permute-start.46 = (bf16[768,512]{1,0:T(8,128)(2,1)S(1)}, bf16[768,512]{1,0:T(8,128)(2,1)S(1)}, u32[]{:S(2)}, u32[]{:S(2)}) collective-permute-start(bf16[768,512]{1,0:T(8,128)(2,1)S(1)} %copy-done.7), channel_id=1, source_target_pairs={{0,3},{1,0},{2,1},{3,2},{4,7},{5,4},{6,5},{7,6},{8,11},{9,8},{10,9... | collective-permute-start | bytes 2359304 | tf_op jit(solution)/shard_map/ppermute | solution.py:786
  274.3 11.0 %collective-permute-start.43 = (bf16[128,1024]{1,0:T(8,128)(2,1)S(1)}, bf16[128,1024]{1,0:T(8,128)(2,1)S(1)}, u32[]{:S(2)}, u32[]{:S(2)}) collective-permute-start(bf16[128,1024]{1,0:T(8,128)(2,1)S(1)} %slice.68), channel_id=1, source_target_pairs={{0,3},{1,0},{2,1},{3,2},{4,7},{5,4},{6,5},{7,6},{8,11},{9,8},{10,9... | collective-permute-start | bytes 786440 | tf_op jit(solution)/shard_map/ppermute | solution.py:786
  274.4 12.0 %collective-permute-start.44 = (bf16[128,1024]{1,0:T(8,128)(2,1)S(1)}, bf16[128,1024]{1,0:T(8,128)(2,1)S(1)}, u32[]{:S(2)}, u32[]{:S(2)}) collective-permute-start(bf16[128,1024]{1,0:T(8,128)(2,1)S(1)} %slice.69), channel_id=1, source_target_pairs={{0,1},{1,2},{2,3},{3,0},{4,5},{5,6},{6,7},{7,4},{8,9},{9,10},{10,1... | collective-permute-start | bytes 786440 | tf_op jit(solution)/shard_map/ppermute | solution.py:786
  298.3 16.7 %collective-permute-start.47 = (bf16[128,1024]{1,0:T(8,128)(2,1)S(1)}, bf16[128,1024]{1,0:T(8,128)(2,1)S(1)}, u32[]{:S(2)}, u32[]{:S(2)}) collective-permute-start(bf16[128,1024]{1,0:T(8,128)(2,1)S(1)} %get-tuple-element.306), channel_id=1, source_target_pairs={{0,1},{1,2},{2,3},{3,0},{4,5},{5,6},{6,7},{7,4},{8,9},{9,10},{10,1... | collective-permute-start | bytes 786440 | tf_op jit(solution)/shard_map/ppermute | solution.py:786
  298.4 16.7 %collective-permute-start.48 = (bf16[128,1024]{1,0:T(8,128)(2,1)S(1)}, bf16[128,1024]{1,0:T(8,128)(2,1)S(1)}, u32[]{:S(2)}, u32[]{:S(2)}) collective-permute-start(bf16[128,1024]{1,0:T(8,128)(2,1)S(1)} %get-tuple-element.307), channel_id=1, source_target_pairs={{0,3},{1,0},{2,1},{3,2},{4,7},{5,4},{6,5},{7,6},{8,11},{9,8},{10,9... | collective-permute-start | bytes 786440 | tf_op jit(solution)/shard_map/ppermute | solution.py:786
  315.0 13.2 %collective-permute-start.51 = (bf16[16,32,768]{2,1,0:T(8,128)(2,1)S(1)}, bf16[16,32,768]{2,1,0:T(8,128)(2,1)S(1)}, u32[]{:S(2)}, u32[]{:S(2)}) collective-permute-start(bf16[16,32,768]{2,1,0:T(8,128)(2,1)S(1)} %get-tuple-element.327), channel_id=1, source_target_pairs={{0,4},{4,0},{8,12},{12,8},{16,20},{20,16},{24,28},{28,24},{32,36},... | collective-permute-start | bytes 2359304 | tf_op jit(solution)/shard_map/ppermute | solution.py:771
  324.9 15.8 %collective-permute-start.49 = (bf16[256,1024]{1,0:T(8,128)(2,1)}, bf16[256,1024]{1,0:T(8,128)(2,1)S(1)}, u32[]{:S(2)}, u32[]{:S(2)}) collective-permute-start(bf16[256,1024]{1,0:T(8,128)(2,1)} %get-tuple-element.310), channel_id=1, source_target_pairs={{0,1},{1,2},{2,3},{3,0},{4,5},{5,6},{6,7},{7,4},{8,9},{9,10},{10,1... | collective-permute-start | bytes 1572872 | tf_op jit(solution)/shard_map/ppermute | solution.py:786
  325.2 15.5 %collective-permute-start.50 = (bf16[256,1024]{1,0:T(8,128)(2,1)S(1)}, bf16[256,1024]{1,0:T(8,128)(2,1)S(1)}, u32[]{:S(2)}, u32[]{:S(2)}) collective-permute-start(bf16[256,1024]{1,0:T(8,128)(2,1)S(1)} %get-tuple-element.311), channel_id=1, source_target_pairs={{0,3},{1,0},{2,1},{3,2},{4,7},{5,4},{6,5},{7,6},{8,11},{9,8},{10,9... | collective-permute-start | bytes 1572872 | tf_op jit(solution)/shard_map/ppermute | solution.py:786
  329.3 11.3 %collective-permute-start.56 = (bf16[208,768]{1,0:T(8,128)(2,1)}, bf16[208,768]{1,0:T(8,128)(2,1)S(1)}, u32[]{:S(2)}, u32[]{:S(2)}) collective-permute-start(bf16[208,768]{1,0:T(8,128)(2,1)} %get-tuple-element.330), channel_id=1, source_target_pairs={{0,32},{4,12},{8,40},{12,20},{16,48},{20,28},{24,56},{28,4},{32,64... | collective-permute-start | bytes 958472 | tf_op jit(solution)/shard_map/ppermute | solution.py:782
  329.4 13.0 %collective-permute-start.57 = (bf16[208,768]{1,0:T(8,128)(2,1)}, bf16[208,768]{1,0:T(8,128)(2,1)S(1)}, u32[]{:S(2)}, u32[]{:S(2)}) collective-permute-start(bf16[208,768]{1,0:T(8,128)(2,1)} %get-tuple-element.331), channel_id=1, source_target_pairs={{0,64},{4,20},{8,72},{12,28},{16,80},{20,4},{24,88},{28,12},{32,96... | collective-permute-start | bytes 958472 | tf_op jit(solution)/shard_map/ppermute | solution.py:782
  342.7 9.9 %collective-permute-start.60 = (bf16[112,768]{1,0:T(8,128)(2,1)S(1)}, bf16[112,768]{1,0:T(8,128)(2,1)S(1)}, u32[]{:S(2)}, u32[]{:S(2)}) collective-permute-start(bf16[112,768]{1,0:T(8,128)(2,1)S(1)} %get-tuple-element.339), channel_id=1, source_target_pairs={{0,16},{4,68},{8,24},{12,76},{16,0},{20,84},{24,8},{28,92},{32,48}... | collective-permute-start | bytes 516104 | tf_op jit(solution)/shard_map/ppermute | solution.py:782
  (38 other events, 280.5 us)
Sparse Core Ops, SparseCore 0:
  10.2 76.8 all-gather.2
  249.4 84.7 reduce-scatter.1

commit v5 on v4

--- a/solution.py
+++ b/solution.py
@@ -325,7 +325,7 @@
     for i in range(4):
         ref, j = tok[i]
         rows = slice(i * CAP, (i + 1) * CAP)
-        ranks = unfold(ref[j, TOK : TOK + EXPERTS // 4, :].astype(F32))
+        ranks = unfold(ref[j, TOK:ROWS, :].astype(F32)[: EXPERTS // 4])
         all_ranks.append(ranks)
         for e in range(2):
             rank = jnp.sum(jnp.where(names == own_names[e], ranks, 0.0), axis=0, keepdims=True)
@@ -487,18 +487,22 @@
     )
 
 
-def token_back_body(sc, r0, r1, r2, h2, x_mid, ranks, gates, router, gain, cot, grad_mid, branch, small):
+def token_back_body(sc, r0, r1, r2, h2, x_mid, ranks, gates, router, gain, cot, grad_mid, branch, small, wait):
     total = r0[...].astype(F32) + (r1[...].astype(F32) + r2[...].astype(F32))
     marks = unfold(total[TOK : TOK + 8]) + unfold(total[TOK + 8 : TOK + 16])
+    wait(5, 6)
     gate = gates[...]
     centre = jnp.sum(gate * marks, axis=0, keepdims=True)
     grad_logits = jnp.where(ranks[...] >= 0.0, gate * (marks - centre), 0.0).astype(BF16)
+    wait(3)
     router_part = nn(grad_logits, h2[0:TOK, :])
     small[0:32, :] = router_part[:, 0:768]
     small[32:48, 0:256] = router_part[0:16, 768:1024]
     small[32:48, 256:512] = router_part[16:32, 768:1024]
     small[32:48, 512:768] = jnp.zeros((16, 256), F32)
+    wait(7)
     grad_h2 = total[0:TOK] + tn(grad_logits, router[...])
+    wait(4, 8, 9)
     x = x_mid[...]
     scale = row_scale(x)
     normed = x * scale
@@ -636,15 +640,17 @@
     wait(3, 4)
     slim_pair[:, 0:128] = nt(wide[:, 0:256], spread2[...]).astype(BF16)
     slim_pair[:, 128:256] = nt(wide[:, 256:512], spread2[...]).astype(BF16)
+    out_total = jnp.zeros((WIDTH, 256), F32)
+    for chunk in range(4):
+        wait(7 + chunk, 11 + chunk)
+        out_total = out_total + tn(rows[chunk][...], nt(mixed[chunk][...], spread4[...]).astype(BF16))
     wait(15)
     pair_total = tn(h1[...], slim_pair[...])
     query_total = jnp.zeros((WIDTH, 256), F32)
-    out_total = jnp.zeros((WIDTH, 256), F32)
     for chunk in range(4):
-        wait(7 + chunk, 11 + chunk, 16 + chunk)
+        wait(16 + chunk)
         at = slice(chunk * TOK, (chunk + 1) * TOK)
         query_total = query_total + tn(h1[at, :], slims[chunk][...])
-        out_total = out_total + tn(rows[chunk][...], nt(mixed[chunk][...], spread4[...]).astype(BF16))
     wait(2, 5, 6, 20, 21, 22, 23)
     shares = query_total * weights[:, 0:256].astype(F32) + pair_total * weights[:, 256:512].astype(F32)
     ones = jnp.ones((8, 256), BF16)
@@ -1027,7 +1033,9 @@
         [((TOK, WIDTH), F32), ((TOK, WIDTH), BF16), ((48, 768), F32)],
         (line_a[0], got_up, got_down, h2, x_mid, ranks, gates, router, ffn_row, cotangent),
         scalars=jnp.stack([mp_at, length]),
+        near=(1,),
         local=(0, 1, 2),
+        lazy=True,
     )
 
     returned = lax.psum_scatter(

time: 366 us -> 365 us (level)
  transfers between devices with their start and end apart: 64 -> 64, of which waited for: 30 -> 31; matrix products, arithmetic and copies ran while one was open for 4% -> 4% of each run, Pallas kernels for 43% -> 43%
where the time goes in v5:
time: 365 us; the launch traced here: 360 us
  Pallas kernels  159 us (44%)
  waiting for transfers between devices  84.8 us (23%)
  starting transfers between devices  80.8 us (22%)
  between operations  15.9 us (4%)
  local copies, waits for them, and re-layouts  9.89 us (3%)
  other arithmetic  9.6 us (3%)
    pallas_call x28, Pallas kernels, call(): pl.pallas_call(kernel, out_shape=shapes, in_specs=in_specs, out_specs=out...  159 us
    ppermute x32, waiting for transfers between devices, shift_axis(): return lax.ppermute(tensor, 'dp', pairs)  53.6 us
    ppermute x32, starting transfers between devices, shift_axis(): return lax.ppermute(tensor, 'dp', pairs)  45.7 us
    ppermute x23, starting transfers between devices, shift_mp(): return lax.ppermute(tensor, 'mp', [(i, (i + step) % 4) for i in range(4)])  33.8 us
    ppermute x23, waiting for transfers between devices, shift_mp(): return lax.ppermute(tensor, 'mp', [(i, (i + step) % 4) for i in range(4)])  23.5 us
  transfers between devices with their start and end apart: 64, of which 31 were waited for; matrix products, arithmetic and copies ran while one was open for 4% of the time, Pallas kernels for 43%

profile of v5, /device:TPU:0, one launch (start us, length us, event | category | flops | bytes accessed | tf_op | source)
XLA Modules:
  0.0 360.3 jit_solution(2282964409778007391)
XLA Ops:
  8.0 2.9 collective-permute-start.3
  13.0 3.0 collective-permute-start
  17.8 3.9 %collective-permute-done.1 = bf16[96,256]{1,0:T(8,128)(2,1)S(1)} collective-permute-done((bf16[96,256]{1,0:T(8,128)(2,1)S(1)}, bf16[96,256]{1,0:T(8,128)(2,1)S(1)}, u32[]{:S(2)}, u32[]{:S(2)}) %collective-permute-start.1) | collective-permute-done | bytes 49184 | tf_op jit(solution)/shard_map/ppermute | solution.py:788
  22.4 3.3 collective-permute-done.4.refs_6_
  25.7 4.0 %collective-permute-start.5 = (bf16[4,96,256]{2,1,0:T(8,128)(2,1)S(1)}, bf16[4,96,256]{2,1,0:T(8,128)(2,1)S(1)}, u32[]{:S(2)}, u32[]{:S(2)}) collective-permute-start(bf16[4,96,256]{2,1,0:T(8,128)(2,1)S(1)} %pad_maximum_fusion.4), channel_id=1, source_target_pairs={{0,24},{4,100},{8,0},{12,108},{16,8},{20,116},{24,16},{28,124},{32... | collective-permute-start | bytes 589832 | tf_op jit(solution)/shard_map/ppermute | solution.py:788
  35.1 4.4 %collective-permute-done.6 = bf16[4,96,256]{2,1,0:T(8,128)(2,1)S(1)} collective-permute-done((bf16[4,96,256]{2,1,0:T(8,128)(2,1)S(1)}, bf16[4,96,256]{2,1,0:T(8,128)(2,1)S(1)}, u32[]{:S(2)}, u32[]{:S(2)}) %collective-permute-start.6) | collective-permute-done | bytes 196640 | tf_op jit(solution)/shard_map/ppermute | solution.py:788
  47.5 11.6 %shard_map.282 = (bf16[1024,1024]{1,0:T(8,128)(2,1)}, bf16[1024,1024]{1,0:T(8,128)(2,1)}, bf16[1024,768]{1,0:T(8,128)(2,1)}, f32[256,512]{1,0:T(8,128)}, f32[256...) custom-call(s32[5]{0:T(128)S(1)} %stack.136.refs_0_, ...), custom_call_target="tpu_custom_call" | custom-call | flops 1 | bytes 1 | tf_op jit(solution)/shard_map/pallas_call | solution.py:126
  61.5 3.2 collective-permute-start.15
  72.4 3.2 collective-permute-start.17
  76.5 2.6 shard_map.288
  81.4 5.7 %collective-permute-done.16.refs_2_ = bf16[256,1024]{1,0:T(8,128)(2,1)} collective-permute-done((bf16[256,1024]{1,0:T(8,128)(2,1)}, bf16[256,1024]{1,0:T(8,128)(2,1)}, u32[]{:S(2)}, u32[]{:S(2)}) %collective-permute-start.16) | collective-permute-done | bytes 524320 | tf_op jit(solution)/shard_map/ppermute | solution.py:792
  87.1 3.6 shard_map.289
  92.8 7.5 %collective-permute-done.18 = bf16[272,1024]{1,0:T(8,128)(2,1)S(1)} collective-permute-done((bf16[272,1024]{1,0:T(8,128)(2,1)S(1)}, bf16[272,1024]{1,0:T(8,128)(2,1)S(1)}, u32[]{:S(2)}, u32[]{:S(2)}) %collective-permute-start.18) | collective-permute-done | bytes 557088 | tf_op jit(solution)/shard_map/ppermute | solution.py:788
  100.3 3.3 collective-permute-start.21
  105.5 5.9 %collective-permute-done.22 = bf16[128,1024]{1,0:T(8,128)(2,1)S(1)} collective-permute-done((bf16[128,1024]{1,0:T(8,128)(2,1)S(1)}, bf16[128,1024]{1,0:T(8,128)(2,1)S(1)}, u32[]{:S(2)}, u32[]{:S(2)}) %collective-permute-start.22) | collective-permute-done | bytes 262176 | tf_op jit(solution)/shard_map/ppermute | solution.py:788
  112.7 3.1 collective-permute-start.26
  116.2 14.4 %shard_map.290 = (bf16[16,256,1024]{2,1,0:T(8,128)(2,1)}, bf16[2,272,1024]{2,1,0:T(8,128)(2,1)}, bf16[2,272,1024]{2,1,0:T(8,128)(2,1)}, bf16[2,1536,1024]{2,1,0:...) custom-call(s32[6]{0:T(128)S(1)} %stack.160.refs_0_, ...), custom_call_target="tpu_custom_call" | custom-call | flops 1 | bytes 1 | tf_op jit(solution)/shard_map/pallas_call | solution.py:126
  130.6 3.3 collective-permute-start.24
  134.2 14.4 %shard_map.291 = (bf16[16,256,1024]{2,1,0:T(8,128)(2,1)}, bf16[2,272,1024]{2,1,0:T(8,128)(2,1)}, bf16[2,272,1024]{2,1,0:T(8,128)(2,1)}, bf16[2,1536,1024]{2,1,0:...) custom-call(s32[6]{0:T(128)S(1)} %stack.165.refs_0_, ...), custom_call_target="tpu_custom_call", output_to_operand_aliasing={{0}: (11, {}), {3}: (12, {}), {4}: (13, {}), {5}: (14, {}),... | custom-call | flops 1 | bytes 1 | tf_op jit(solution)/shard_map/pallas_call | solution.py:126
  149.4 4.1 %collective-permute-done.25.refs_2_ = bf16[2,272,1024]{2,1,0:T(8,128)(2,1)} collective-permute-done((bf16[2,272,1024]{2,1,0:T(8,128)(2,1)}, bf16[2,272,1024]{2,1,0:T(8,128)(2,1)}, u32[]{:S(2)}, u32[]{:S(2)}) %collective-permute-start.25) | collective-permute-done | bytes 1114144 | tf_op jit(solution)/shard_map/ppermute | solution.py:788
  153.5 14.4 %shard_map.292 = (bf16[16,256,1024]{2,1,0:T(8,128)(2,1)}, bf16[2,272,1024]{2,1,0:T(8,128)(2,1)}, bf16[2,272,1024]{2,1,0:T(8,128)(2,1)}, bf16[2,1536,1024]{2,1,0:...) custom-call(s32[6]{0:T(128)S(1)} %stack.170.refs_0_, ...), custom_call_target="tpu_custom_call", output_to_operand_aliasing={{0}: (11, {}), {3}: (12, {}), {4}: (13, {}), {5}: (14, {}),... | custom-call | flops 1 | bytes 1 | tf_op jit(solution)/shard_map/pallas_call | solution.py:126
  168.2 14.4 %shard_map.293 = (bf16[16,256,1024]{2,1,0:T(8,128)(2,1)}, bf16[2,272,1024]{2,1,0:T(8,128)(2,1)}, bf16[2,272,1024]{2,1,0:T(8,128)(2,1)}, bf16[2,1536,1024]{2,1,0:...) custom-call(s32[6]{0:T(128)S(1)} %stack.149.refs_0_, ...), custom_call_target="tpu_custom_call", output_to_operand_aliasing={{0}: (11, {}), {3}: (12, {}), {4}: (13, {}), {5}: (14, {}),... | custom-call | flops 1 | bytes 1 | tf_op jit(solution)/shard_map/pallas_call | solution.py:126
  186.1 8.1 %shard_map.294 = bf16[3072,512]{1,0:T(8,128)(2,1)S(1)} custom-call(s32[1]{0:T(128)} %bitcast.3.refs_0_, bf16[2,1536,1024]{2,1,0:T(8,128)(2,1)} %get-tuple-element.251.refs_1_, bf16[2,1536,512]{2,1,0:T(8,128)(2,1)} %get-tuple-element.252.refs_2_, bf16[2,1536,512]{2,1,0:T(8,128)(2,1)} %get-tuple-element.253.refs_3_, ...), custom_call_target="tpu_custom_call" | custom-call | flops 1 | bytes 1 | tf_op jit(solution)/shard_map/pallas_call | solution.py:126
  194.2 5.3 %collective-permute-done.29 = bf16[2,272,1024]{2,1,0:T(8,128)(2,1)S(1)} collective-permute-done((bf16[2,272,1024]{2,1,0:T(8,128)(2,1)}, bf16[2,272,1024]{2,1,0:T(8,128)(2,1)S(1)}, u32[]{:S(2)}, u32[]{:S(2)}) %collective-permute-start.29) | collective-permute-done | bytes 1114144 | tf_op jit(solution)/shard_map/ppermute | solution.py:788
  206.2 8.7 %shard_map.295 = (bf16[768,512]{1,0:T(8,128)(2,1)S(1)}, bf16[768,512]{1,0:T(8,128)(2,1)S(1)}, bf16[768,512]{1,0:T(8,128)(2,1)S(1)}, bf16[384,512]{1,0:T(8,128)(2,1)S(1)}, bf16[384,512]{1,0:T(8,128)(2,1)S(1)}) custom-call(s32[1]{0:T(128)} %bitcast.3.refs_0_, bf16[2,1536,1024]{2,1,0:T(8,128)(2,1)} %get-tuple-element.251.refs_1_, ...), custom_call_target="tpu_custom_call" | custom-call | flops 1 | bytes 1 | tf_op jit(solution)/shard_map/pallas_call | solution.py:126
  220.7 3.2 collective-permute-start.36
  224.8 3.0 collective-permute-done.36
  227.9 4.0 %collective-permute-done.35 = bf16[144,1024]{1,0:T(8,128)(2,1)S(1)} collective-permute-done((bf16[144,1024]{1,0:T(8,128)(2,1)S(1)}, bf16[144,1024]{1,0:T(8,128)(2,1)S(1)}, u32[]{:S(2)}, u32[]{:S(2)}) %collective-permute-start.35) | collective-permute-done | bytes 294944 | tf_op jit(solution)/shard_map/ppermute | solution.py:788
  234.2 3.2 collective-permute-start.40
  239.5 5.4 %collective-permute-done.39.refs_2_ = bf16[272,1024]{1,0:T(8,128)(2,1)S(1)} collective-permute-done((bf16[272,1024]{1,0:T(8,128)(2,1)S(1)}, bf16[272,1024]{1,0:T(8,128)(2,1)S(1)}, u32[]{:S(2)}, u32[]{:S(2)}) %collective-permute-start.39) | collective-permute-done | bytes 557088 | tf_op jit(solution)/shard_map/ppermute | solution.py:788
  244.9 4.0 %shard_map.298 = (f32[256,1024]{1,0:T(8,128)}, bf16[256,1024]{1,0:T(8,128)(2,1)S(1)}, f32[48,768]{1,0:T(8,128)}) custom-call(s32[2]{0:T(128)S(1)} %pad_add_fusion.refs_0_, bf16[272,1024]{1,0:T(8,128)(2,1)S(1)} %slice_bitcast_fusion.refs_1_, bf16[272,1024]{1,0:T(8,128)(2,1)S(1)} %collective-permute-done.39.refs_2_, ...), custom_call_target="tpu_custom_call" | custom-call | flops 1 | bytes 1 | tf_op jit(solution)/shard_map/pallas_call | solution.py:126
  251.1 6.6 %shard_map.299 = (bf16[256,512]{1,0:T(8,128)(2,1)}, f32[8,128]{1,0:T(8,128)}, bf16[256,256]{1,0:T(8,128)(2,1)}, f32[2,1024,256]{2,1,0:T(8,128)}) custom-call(bf16[256,1024]{1,0:T(8,128)(2,1)S(1)} %get-tuple-element.269.refs_0_.refs_8_, bf16[1024,512]{1,0:T(8,128)(2,1)S(1)} %get-tuple-element.193.refs_3_.refs_1_, ...), custom_call_target="tpu_custom_call" | custom-call | flops 1 | bytes 1 | tf_op jit(solution)/shard_map/pallas_call | solution.py:126
  260.1 2.8 collective-permute-done.42.refs_0_.refs_11_
  262.9 3.2 collective-permute-start.46
  266.1 6.9 %shard_map.300 = (bf16[256,512]{1,0:T(8,128)(2,1)}, f32[8,128]{1,0:T(8,128)}, bf16[256,256]{1,0:T(8,128)(2,1)}, f32[2,1024,256]{2,1,0:T(8,128)}) custom-call(bf16[256,1024]{1,0:T(8,128)(2,1)S(1)} %collective-permute-done.41.refs_0_.refs_9_, bf16[1024,512]{1,0:T(8,128)(2,1)S(1)} %get-tuple-element.193.refs_3_.refs_1_, ...), custom_call_target="tpu_custom_call", output_to_operand_aliasing={{3}: (10, {})} | custom-call | flops 1 | bytes 1 | tf_op jit(solution)/shard_map/pallas_call | solution.py:126
  275.4 6.9 %shard_map.301 = (bf16[256,512]{1,0:T(8,128)(2,1)}, f32[8,128]{1,0:T(8,128)}, bf16[256,256]{1,0:T(8,128)(2,1)}, f32[2,1024,256]{2,1,0:T(8,128)}) custom-call(bf16[256,1024]{1,0:T(8,128)(2,1)S(1)} %collective-permute-done.42.refs_0_.refs_11_, bf16[1024,512]{1,0:T(8,128)(2,1)S(1)} %get-tuple-element.193.refs_3_.refs_1_, ...), custom_call_target="tpu_custom_call", output_to_operand_aliasing={{3}: (10, {})} | custom-call | flops 1 | bytes 1 | tf_op jit(solution)/shard_map/pallas_call | solution.py:126
  285.1 6.9 %shard_map.302 = (bf16[256,512]{1,0:T(8,128)(2,1)}, f32[8,128]{1,0:T(8,128)}, bf16[256,256]{1,0:T(8,128)(2,1)}, f32[2,1024,256]{2,1,0:T(8,128)}) custom-call(bf16[256,1024]{1,0:T(8,128)(2,1)S(1)} %constant_dynamic-update-slice_fusion.9.refs_0_.refs_10_, bf16[1024,512]{1,0:T(8,128)(2,1)S(1)} %get-tuple-element.193.refs_3_.refs_1_, ...), custom_call_target="tpu_custom_call", output_to_operand_aliasing={{3}: (10, {})} | custom-call | flops 1 | bytes 1 | tf_op jit(solution)/shard_map/pallas_call | solution.py:126
  292.1 5.0 %shard_map.303 = (bf16[128,1024]{1,0:T(8,128)(2,1)S(1)}, bf16[128,1024]{1,0:T(8,128)(2,1)S(1)}, bf16[1024,512]{1,0:T(8,128)(2,1)S(1)}, f32[8,128]{1,0:T(8,128)S(1)}) custom-call(f32[2,1024,256]{2,1,0:T(8,128)} %get-tuple-element.298.refs_0_, f32[256,256]{1,0:T(8,128)} %get-tuple-element.299.refs_1_, f32[256,256]{1,0:T(8,128)} %get-tuple-element.300.refs_2_, ...), custom_call_target="tpu_custom_call" | custom-call | flops 1 | bytes 1 | tf_op jit(solution)/shard_map/pallas_call | solution.py:126
  297.2 3.4 collective-permute-start.48
  300.7 9.3 %shard_map.306 = (bf16[16,32,768]{2,1,0:T(8,128)(2,1)S(1)}, bf16[16,32,768]{2,1,0:T(8,128)(2,1)S(1)}, f32[56,768]{1,0:T(8,128)S(1)}) custom-call(s32[3]{0:T(128)S(1)} %pad_add_fusion.1.refs_0_, bf16[1024,512]{1,0:T(8,128)(2,1)S(1)} %get-tuple-element.305.refs_0_.refs_1_, f32[8,128]{1,0:T(8,128)S(1)} %get-tuple-element.313.refs_2_, ...), custom_call_target="tpu_custom_call" | custom-call | flops 1 | bytes 1 | tf_op jit(solution)/shard_map/pallas_call | solution.py:126
  310.0 2.9 collective-permute-start.53
  314.9 3.5 collective-permute-done.52
  319.5 3.9 %shard_map.304 = (bf16[256,1024]{1,0:T(8,128)(2,1)}, bf16[256,1024]{1,0:T(8,128)(2,1)S(1)}, bf16[256,1024]{1,0:T(8,128)(2,1)S(1)}) custom-call(bf16[1024,512]{1,0:T(8,128)(2,1)S(1)} %get-tuple-element.305.refs_0_.refs_1_, bf16[128,1024]{1,0:T(8,128)(2,1)S(1)} %collective-permute-done.47.refs_1_, bf16[128,1024]{1,0:T(8,128)(2,1)S(1)} %collective-permute-done.48.refs_2_, ...), custom_call_target="tpu_custom_call" | custom-call | flops 1 | bytes 1 | tf_op jit(solution)/shard_map/pallas_call | solution.py:126
  323.9 2.9 collective-permute-start.50
  328.0 4.6 %collective-permute-start.57 = (bf16[208,768]{1,0:T(8,128)(2,1)}, bf16[208,768]{1,0:T(8,128)(2,1)S(1)}, u32[]{:S(2)}, u32[]{:S(2)}) collective-permute-start(bf16[208,768]{1,0:T(8,128)(2,1)} %get-tuple-element.331), channel_id=1, source_target_pairs={{0,64},{4,20},{8,72},{12,28},{16,80},{20,4},{24,88},{28,12},{32,96... | collective-permute-start | bytes 958472 | tf_op jit(solution)/shard_map/ppermute | solution.py:788
  333.4 3.3 reduce-scatter.2.cloned.1.call-done
  341.4 4.4 %collective-permute-start.60 = (bf16[112,768]{1,0:T(8,128)(2,1)S(1)}, bf16[112,768]{1,0:T(8,128)(2,1)S(1)}, u32[]{:S(2)}, u32[]{:S(2)}) collective-permute-start(bf16[112,768]{1,0:T(8,128)(2,1)S(1)} %get-tuple-element.339), channel_id=1, source_target_pairs={{0,16},{4,68},{8,24},{12,76},{16,0},{20,84},{24,8},{28,92},{32,48}... | collective-permute-start | bytes 516104 | tf_op jit(solution)/shard_map/ppermute | solution.py:788
  345.8 3.0 shard_map.305
  (205 shorter events, 83.5 us)
Async XLA Ops:
  7.2 109.0 %all-gather.3.cloned.1.call-start = ((), (), s32[]{:S(2)}) async-start(), calls=%async_computation.2 | async-start | bytes 8912896 | tf_op jit(solution)/shard_map/all_gather | solution.py:861
  7.9 328.8 %reduce-scatter.2.cloned.1.call-start = ((), (), s32[]{:S(2)}) async-start(), calls=%async_computation.1 | async-start | bytes 8912896 | tf_op jit(solution)/shard_map/reduce_scatter | solution.py:1041
  8.0 14.4 %collective-permute-start.3 = (bf16[256,1024]{1,0:T(8,128)(2,1)}, bf16[256,1024]{1,0:T(8,128)(2,1)S(1)}, u32[]{:S(2)}, u32[]{:S(2)}) collective-permute-start(bf16[256,1024]{1,0:T(8,128)(2,1)} %refs_3_.3), channel_id=1, source_target_pairs={{0,3},{1,0},{2,1},{3,2},{4,7},{5,4},{6,5},{7,6},{8,11},{9,8},{10,9... | collective-permute-start | bytes 1572872 | tf_op jit(solution)/shard_map/ppermute | solution.py:792
  10.9 14.8 %collective-permute-start.4 = (bf16[256,1024]{1,0:T(8,128)(2,1)}, bf16[256,1024]{1,0:T(8,128)(2,1)S(1)}, u32[]{:S(2)}, u32[]{:S(2)}) collective-permute-start(bf16[256,1024]{1,0:T(8,128)(2,1)} %refs_3_.3), channel_id=1, source_target_pairs={{0,1},{1,2},{2,3},{3,0},{4,5},{5,6},{6,7},{7,4},{8,9},{9,10},{10,1... | collective-permute-start | bytes 1572872 | tf_op jit(solution)/shard_map/ppermute | solution.py:792
  29.7 9.8 %collective-permute-start.6 = (bf16[4,96,256]{2,1,0:T(8,128)(2,1)S(1)}, bf16[4,96,256]{2,1,0:T(8,128)(2,1)S(1)}, u32[]{:S(2)}, u32[]{:S(2)}) collective-permute-start(bf16[4,96,256]{2,1,0:T(8,128)(2,1)S(1)} %pad_maximum_fusion.4), channel_id=1, source_target_pairs={{0,16},{4,68},{8,24},{12,76},{16,0},{20,84},{24,8},{28,92},{32,48}... | collective-permute-start | bytes 589832 | tf_op jit(solution)/shard_map/ppermute | solution.py:788
  29.7 12.0 %collective-permute-start.7 = (bf16[4,96,256]{2,1,0:T(8,128)(2,1)S(1)}, bf16[4,96,256]{2,1,0:T(8,128)(2,1)S(1)}, u32[]{:S(2)}, u32[]{:S(2)}) collective-permute-start(bf16[4,96,256]{2,1,0:T(8,128)(2,1)S(1)} %pad_maximum_fusion.4), channel_id=1, source_target_pairs={{0,8},{4,36},{8,16},{12,44},{16,24},{20,52},{24,0},{28,60},{32,40}... | collective-permute-start | bytes 589832 | tf_op jit(solution)/shard_map/ppermute | solution.py:788
  31.0 10.8 %collective-permute-start.8 = (bf16[128,1024]{1,0:T(8,128)(2,1)S(1)}, bf16[128,1024]{1,0:T(8,128)(2,1)S(1)}, u32[]{:S(2)}, u32[]{:S(2)}) collective-permute-start(bf16[128,1024]{1,0:T(8,128)(2,1)S(1)} %slice.76), channel_id=1, source_target_pairs={{0,3},{1,0},{2,1},{3,2},{4,7},{5,4},{6,5},{7,6},{8,11},{9,8},{10,9... | collective-permute-start | bytes 786440 | tf_op jit(solution)/shard_map/ppermute | solution.py:792
  31.5 10.3 %collective-permute-start.9 = (bf16[128,1024]{1,0:T(8,128)(2,1)S(1)}, bf16[128,1024]{1,0:T(8,128)(2,1)S(1)}, u32[]{:S(2)}, u32[]{:S(2)}) collective-permute-start(bf16[128,1024]{1,0:T(8,128)(2,1)S(1)} %slice.77), channel_id=1, source_target_pairs={{0,1},{1,2},{2,3},{3,0},{4,5},{5,6},{6,7},{7,4},{8,9},{9,10},{10,1... | collective-permute-start | bytes 786440 | tf_op jit(solution)/shard_map/ppermute | solution.py:792
  44.2 14.8 %collective-permute-start.11 = (bf16[1,1024,512]{2,1,0:T(8,128)(2,1)S(1)}, bf16[1,1024,512]{2,1,0:T(8,128)(2,1)}, u32[]{:S(2)}, u32[]{:S(2)}) collective-permute-start(bf16[1,1024,512]{2,1,0:T(8,128)(2,1)S(1)} %copy-done), channel_id=1, source_target_pairs={{0,4},{4,0},{8,12},{12,8},{16,20},{20,16},{24,28},{28,24},{32,36},... | collective-permute-start | bytes 3145736 | tf_op jit(solution)/shard_map/ppermute | solution.py:777
  45.1 14.0 %collective-permute-start.12 = (bf16[1,1024,512]{2,1,0:T(8,128)(2,1)}, bf16[1,1024,512]{2,1,0:T(8,128)(2,1)}, u32[]{:S(2)}, u32[]{:S(2)}) collective-permute-start(bf16[1,1024,512]{2,1,0:T(8,128)(2,1)} %refs_6_.7), channel_id=1, source_target_pairs={{0,4},{4,0},{8,12},{12,8},{16,20},{20,16},{24,28},{28,24},{32,36},... | collective-permute-start | bytes 3145736 | tf_op jit(solution)/shard_map/ppermute | solution.py:777
  45.2 13.8 %collective-permute-start.13 = (bf16[1,512,1024]{2,1,0:T(8,128)(2,1)}, bf16[1,512,1024]{2,1,0:T(8,128)(2,1)}, u32[]{:S(2)}, u32[]{:S(2)}) collective-permute-start(bf16[1,512,1024]{2,1,0:T(8,128)(2,1)} %refs_7_.7), channel_id=1, source_target_pairs={{0,4},{4,0},{8,12},{12,8},{16,20},{20,16},{24,28},{28,24},{32,36},... | collective-permute-start | bytes 3145736 | tf_op jit(solution)/shard_map/ppermute | solution.py:777
  61.4 9.6 %collective-permute-start.14 = (bf16[128,1024]{1,0:T(8,128)(2,1)S(1)}, bf16[128,1024]{1,0:T(8,128)(2,1)S(1)}, u32[]{:S(2)}, u32[]{:S(2)}) collective-permute-start(bf16[128,1024]{1,0:T(8,128)(2,1)S(1)} %get-tuple-element.200), channel_id=1, source_target_pairs={{0,1},{1,2},{2,3},{3,0},{4,5},{5,6},{6,7},{7,4},{8,9},{9,10},{10,1... | collective-permute-start | bytes 786440 | tf_op jit(solution)/shard_map/ppermute | solution.py:792
  61.5 9.5 %collective-permute-start.15 = (bf16[128,1024]{1,0:T(8,128)(2,1)S(1)}, bf16[128,1024]{1,0:T(8,128)(2,1)S(1)}, u32[]{:S(2)}, u32[]{:S(2)}) collective-permute-start(bf16[128,1024]{1,0:T(8,128)(2,1)S(1)} %get-tuple-element.201), channel_id=1, source_target_pairs={{0,3},{1,0},{2,1},{3,2},{4,7},{5,4},{6,5},{7,6},{8,11},{9,8},{10,9... | collective-permute-start | bytes 786440 | tf_op jit(solution)/shard_map/ppermute | solution.py:792
  72.1 15.0 %collective-permute-start.16 = (bf16[256,1024]{1,0:T(8,128)(2,1)}, bf16[256,1024]{1,0:T(8,128)(2,1)}, u32[]{:S(2)}, u32[]{:S(2)}) collective-permute-start(bf16[256,1024]{1,0:T(8,128)(2,1)} %get-tuple-element.202), channel_id=1, source_target_pairs={{0,1},{1,2},{2,3},{3,0},{4,5},{5,6},{6,7},{7,4},{8,9},{9,10},{10,1... | collective-permute-start | bytes 1572872 | tf_op jit(solution)/shard_map/ppermute | solution.py:792
  72.4 14.8 %collective-permute-start.17 = (bf16[256,1024]{1,0:T(8,128)(2,1)}, bf16[256,1024]{1,0:T(8,128)(2,1)}, u32[]{:S(2)}, u32[]{:S(2)}) collective-permute-start(bf16[256,1024]{1,0:T(8,128)(2,1)} %get-tuple-element.203), channel_id=1, source_target_pairs={{0,3},{1,0},{2,1},{3,2},{4,7},{5,4},{6,5},{7,6},{8,11},{9,8},{10,9... | collective-permute-start | bytes 1572872 | tf_op jit(solution)/shard_map/ppermute | solution.py:792
  90.7 9.6 %collective-permute-start.18 = (bf16[272,1024]{1,0:T(8,128)(2,1)S(1)}, bf16[272,1024]{1,0:T(8,128)(2,1)S(1)}, u32[]{:S(2)}, u32[]{:S(2)}) collective-permute-start(bf16[272,1024]{1,0:T(8,128)(2,1)S(1)} %get-tuple-element.207.refs_0_.refs_4_), channel_id=1, source_target_pairs={{0,96},{4,28},{8,104},{12,4},{16,112},{20,12},{24,120},{28,20},{32... | collective-permute-start | bytes 1671176 | tf_op jit(solution)/shard_map/ppermute | solution.py:788
  92.8 10.8 %collective-permute-start.20 = (bf16[272,1024]{1,0:T(8,128)(2,1)S(1)}, bf16[272,1024]{1,0:T(8,128)(2,1)S(1)}, u32[]{:S(2)}, u32[]{:S(2)}) collective-permute-start(bf16[272,1024]{1,0:T(8,128)(2,1)S(1)} %get-tuple-element.207.refs_0_.refs_4_), channel_id=1, source_target_pairs={{0,32},{4,12},{8,40},{12,20},{16,48},{20,28},{24,56},{28,4},{32,64... | collective-permute-start | bytes 1671176 | tf_op jit(solution)/shard_map/ppermute | solution.py:788
  100.3 11.2 %collective-permute-start.21 = (bf16[144,1024]{1,0:T(8,128)(2,1)S(1)}, bf16[144,1024]{1,0:T(8,128)(2,1)S(1)}, u32[]{:S(2)}, u32[]{:S(2)}) collective-permute-start(bf16[144,1024]{1,0:T(8,128)(2,1)S(1)} %slice.78), channel_id=1, source_target_pairs={{0,96},{4,28},{8,104},{12,4},{16,112},{20,12},{24,120},{28,20},{32... | collective-permute-start | bytes 884744 | tf_op jit(solution)/shard_map/ppermute | solution.py:788
  104.8 25.8 %collective-permute-start.19 = (bf16[2,272,1024]{2,1,0:T(8,128)(2,1)}, bf16[2,272,1024]{2,1,0:T(8,128)(2,1)}, u32[]{:S(2)}, u32[]{:S(2)}) collective-permute-start(bf16[2,272,1024]{2,1,0:T(8,128)(2,1)} %pad_maximum_fusion.refs_1_), channel_id=1, source_target_pairs={{0,24},{4,100},{8,0},{12,108},{16,8},{20,116},{24,16},{28,124},{32... | collective-permute-start | bytes 3342344 | tf_op jit(solution)/shard_map/ppermute | solution.py:788
  112.6 18.0 %collective-permute-start.23 = (bf16[2,272,1024]{2,1,0:T(8,128)(2,1)}, bf16[2,272,1024]{2,1,0:T(8,128)(2,1)}, u32[]{:S(2)}, u32[]{:S(2)}) collective-permute-start(bf16[2,272,1024]{2,1,0:T(8,128)(2,1)} %pad_maximum_fusion.1.refs_2_), channel_id=1, source_target_pairs={{0,8},{4,36},{8,16},{12,44},{16,24},{20,52},{24,0},{28,60},{32,40}... | collective-permute-start | bytes 3342344 | tf_op jit(solution)/shard_map/ppermute | solution.py:788
  112.7 21.5 %collective-permute-start.26 = (bf16[2,272,1024]{2,1,0:T(8,128)(2,1)}, bf16[2,272,1024]{2,1,0:T(8,128)(2,1)}, u32[]{:S(2)}, u32[]{:S(2)}) collective-permute-start(bf16[2,272,1024]{2,1,0:T(8,128)(2,1)} %pad_maximum_fusion.1.refs_2_), channel_id=1, source_target_pairs={{0,24},{4,100},{8,0},{12,108},{16,8},{20,116},{24,16},{28,124},{32... | collective-permute-start | bytes 3342344 | tf_op jit(solution)/shard_map/ppermute | solution.py:788
  115.9 33.5 %collective-permute-start.28 = (bf16[2,272,1024]{2,1,0:T(8,128)(2,1)}, bf16[2,272,1024]{2,1,0:T(8,128)(2,1)}, u32[]{:S(2)}, u32[]{:S(2)}) collective-permute-start(bf16[2,272,1024]{2,1,0:T(8,128)(2,1)} %pad_maximum_fusion.refs_1_), channel_id=1, source_target_pairs={{0,8},{4,36},{8,16},{12,44},{16,24},{20,52},{24,0},{28,60},{32,40}... | collective-permute-start | bytes 3342344 | tf_op jit(solution)/shard_map/ppermute | solution.py:788
  130.6 18.8 %collective-permute-start.24 = (bf16[2,272,1024]{2,1,0:T(8,128)(2,1)}, bf16[2,272,1024]{2,1,0:T(8,128)(2,1)}, u32[]{:S(2)}, u32[]{:S(2)}) collective-permute-start(bf16[2,272,1024]{2,1,0:T(8,128)(2,1)} %collective-permute-done.19.refs_1_), channel_id=1, source_target_pairs={{0,24},{4,100},{8,0},{12,108},{16,8},{20,116},{24,16},{28,124},{32... | collective-permute-start | bytes 3342344 | tf_op jit(solution)/shard_map/ppermute | solution.py:788
  133.9 19.6 %collective-permute-start.25 = (bf16[2,272,1024]{2,1,0:T(8,128)(2,1)}, bf16[2,272,1024]{2,1,0:T(8,128)(2,1)}, u32[]{:S(2)}, u32[]{:S(2)}) collective-permute-start(bf16[2,272,1024]{2,1,0:T(8,128)(2,1)} %collective-permute-done.23.refs_2_), channel_id=1, source_target_pairs={{0,8},{4,36},{8,16},{12,44},{16,24},{20,52},{24,0},{28,60},{32,40}... | collective-permute-start | bytes 3342344 | tf_op jit(solution)/shard_map/ppermute | solution.py:788
  148.6 19.5 %collective-permute-start.27 = (bf16[2,272,1024]{2,1,0:T(8,128)(2,1)}, bf16[2,272,1024]{2,1,0:T(8,128)(2,1)}, u32[]{:S(2)}, u32[]{:S(2)}) collective-permute-start(bf16[2,272,1024]{2,1,0:T(8,128)(2,1)} %get-tuple-element.218), channel_id=1, source_target_pairs={{0,8},{4,36},{8,16},{12,44},{16,24},{20,52},{24,0},{28,60},{32,40}... | collective-permute-start | bytes 3342344 | tf_op jit(solution)/shard_map/ppermute | solution.py:788
  167.9 18.2 %collective-permute-start.31 = (bf16[2,272,1024]{2,1,0:T(8,128)(2,1)}, bf16[2,272,1024]{2,1,0:T(8,128)(2,1)S(1)}, u32[]{:S(2)}, u32[]{:S(2)}) collective-permute-start(bf16[2,272,1024]{2,1,0:T(8,128)(2,1)} %get-tuple-element.250), channel_id=1, source_target_pairs={{0,24},{4,100},{8,0},{12,108},{16,8},{20,116},{24,16},{28,124},{32... | collective-permute-start | bytes 3342344 | tf_op jit(solution)/shard_map/ppermute | solution.py:788
  182.6 17.0 %collective-permute-start.29 = (bf16[2,272,1024]{2,1,0:T(8,128)(2,1)}, bf16[2,272,1024]{2,1,0:T(8,128)(2,1)S(1)}, u32[]{:S(2)}, u32[]{:S(2)}) collective-permute-start(bf16[2,272,1024]{2,1,0:T(8,128)(2,1)} %get-tuple-element.242), channel_id=1, source_target_pairs={{0,8},{4,36},{8,16},{12,44},{16,24},{20,52},{24,0},{28,60},{32,40}... | collective-permute-start | bytes 3342344 | tf_op jit(solution)/shard_map/ppermute | solution.py:788
  184.6 15.9 %collective-permute-start.30 = (bf16[2,272,1024]{2,1,0:T(8,128)(2,1)}, bf16[2,272,1024]{2,1,0:T(8,128)(2,1)S(1)}, u32[]{:S(2)}, u32[]{:S(2)}) collective-permute-start(bf16[2,272,1024]{2,1,0:T(8,128)(2,1)} %get-tuple-element.244), channel_id=1, source_target_pairs={{0,24},{4,100},{8,0},{12,108},{16,8},{20,116},{24,16},{28,124},{32... | collective-permute-start | bytes 3342344 | tf_op jit(solution)/shard_map/ppermute | solution.py:788
  201.0 17.7 %collective-permute-start.34 = (bf16[2,272,1024]{2,1,0:T(8,128)(2,1)S(1)}, bf16[2,272,1024]{2,1,0:T(8,128)(2,1)S(1)}, u32[]{:S(2)}, u32[]{:S(2)}) collective-permute-start(bf16[2,272,1024]{2,1,0:T(8,128)(2,1)S(1)} %add_convert_fusion.2), channel_id=1, source_target_pairs={{0,24},{4,100},{8,0},{12,108},{16,8},{20,116},{24,16},{28,124},{32... | collective-permute-start | bytes 3342344 | tf_op jit(solution)/shard_map/ppermute | solution.py:788
  204.0 20.1 %collective-permute-start.33 = (bf16[2,272,1024]{2,1,0:T(8,128)(2,1)S(1)}, bf16[2,272,1024]{2,1,0:T(8,128)(2,1)S(1)}, u32[]{:S(2)}, u32[]{:S(2)}) collective-permute-start(bf16[2,272,1024]{2,1,0:T(8,128)(2,1)S(1)} %add_convert_fusion.3), channel_id=1, source_target_pairs={{0,8},{4,36},{8,16},{12,44},{16,24},{20,52},{24,0},{28,60},{32,40}... | collective-permute-start | bytes 3342344 | tf_op jit(solution)/shard_map/ppermute | solution.py:788
  214.9 17.3 %collective-permute-start.37 = (bf16[384,512]{1,0:T(8,128)(2,1)S(1)}, bf16[384,512]{1,0:T(8,128)(2,1)S(1)}, u32[]{:S(2)}, u32[]{:S(2)}) collective-permute-start(bf16[384,512]{1,0:T(8,128)(2,1)S(1)} %get-tuple-element.260), channel_id=1, source_target_pairs={{0,1},{1,2},{2,3},{3,0},{4,5},{5,6},{6,7},{7,4},{8,9},{9,10},{10,1... | collective-permute-start | bytes 1179656 | tf_op jit(solution)/shard_map/ppermute | solution.py:792
  216.1 16.0 %collective-permute-start.38 = (bf16[384,512]{1,0:T(8,128)(2,1)S(1)}, bf16[384,512]{1,0:T(8,128)(2,1)S(1)}, u32[]{:S(2)}, u32[]{:S(2)}) collective-permute-start(bf16[384,512]{1,0:T(8,128)(2,1)S(1)} %get-tuple-element.261), channel_id=1, source_target_pairs={{0,3},{1,0},{2,1},{3,2},{4,7},{5,4},{6,5},{7,6},{8,11},{9,8},{10,9... | collective-permute-start | bytes 1179656 | tf_op jit(solution)/shard_map/ppermute | solution.py:792
  234.2 10.7 %collective-permute-start.39 = (bf16[272,1024]{1,0:T(8,128)(2,1)S(1)}, bf16[272,1024]{1,0:T(8,128)(2,1)S(1)}, u32[]{:S(2)}, u32[]{:S(2)}) collective-permute-start(bf16[272,1024]{1,0:T(8,128)(2,1)S(1)} %pad_maximum_fusion.2), channel_id=1, source_target_pairs={{0,32},{4,12},{8,40},{12,20},{16,48},{20,28},{24,56},{28,4},{32,64... | collective-permute-start | bytes 1671176 | tf_op jit(solution)/shard_map/ppermute | solution.py:788
  234.2 10.7 %collective-permute-start.40 = (bf16[272,1024]{1,0:T(8,128)(2,1)S(1)}, bf16[272,1024]{1,0:T(8,128)(2,1)S(1)}, u32[]{:S(2)}, u32[]{:S(2)}) collective-permute-start(bf16[272,1024]{1,0:T(8,128)(2,1)S(1)} %pad_maximum_fusion.3), channel_id=1, source_target_pairs={{0,96},{4,28},{8,104},{12,4},{16,112},{20,12},{24,120},{28,20},{32... | collective-permute-start | bytes 1671176 | tf_op jit(solution)/shard_map/ppermute | solution.py:788
  249.0 11.1 %collective-permute-start.41 = (bf16[256,1024]{1,0:T(8,128)(2,1)S(1)}, bf16[256,1024]{1,0:T(8,128)(2,1)S(1)}, u32[]{:S(2)}, u32[]{:S(2)}) collective-permute-start(bf16[256,1024]{1,0:T(8,128)(2,1)S(1)} %get-tuple-element.269.refs_0_.refs_8_), channel_id=1, source_target_pairs={{0,3},{1,0},{2,1},{3,2},{4,7},{5,4},{6,5},{7,6},{8,11},{9,8},{10,9... | collective-permute-start | bytes 1572872 | tf_op jit(solution)/shard_map/ppermute | solution.py:792
  250.8 12.1 %collective-permute-start.42 = (bf16[256,1024]{1,0:T(8,128)(2,1)S(1)}, bf16[256,1024]{1,0:T(8,128)(2,1)S(1)}, u32[]{:S(2)}, u32[]{:S(2)}) collective-permute-start(bf16[256,1024]{1,0:T(8,128)(2,1)S(1)} %get-tuple-element.269.refs_0_.refs_8_), channel_id=1, source_target_pairs={{0,1},{1,2},{2,3},{3,0},{4,5},{5,6},{6,7},{7,4},{8,9},{9,10},{10,1... | collective-permute-start | bytes 1572872 | tf_op jit(solution)/shard_map/ppermute | solution.py:792
  262.9 29.2 %collective-permute-start.45 = (bf16[768,512]{1,0:T(8,128)(2,1)S(1)}, bf16[768,512]{1,0:T(8,128)(2,1)S(1)}, u32[]{:S(2)}, u32[]{:S(2)}) collective-permute-start(bf16[768,512]{1,0:T(8,128)(2,1)S(1)} %copy-done.9), channel_id=1, source_target_pairs={{0,1},{1,2},{2,3},{3,0},{4,5},{5,6},{6,7},{7,4},{8,9},{9,10},{10,1... | collective-permute-start | bytes 2359304 | tf_op jit(solution)/shard_map/ppermute | solution.py:792
  262.9 29.2 %collective-permute-start.46 = (bf16[768,512]{1,0:T(8,128)(2,1)S(1)}, bf16[768,512]{1,0:T(8,128)(2,1)S(1)}, u32[]{:S(2)}, u32[]{:S(2)}) collective-permute-start(bf16[768,512]{1,0:T(8,128)(2,1)S(1)} %copy-done.7), channel_id=1, source_target_pairs={{0,3},{1,0},{2,1},{3,2},{4,7},{5,4},{6,5},{7,6},{8,11},{9,8},{10,9... | collective-permute-start | bytes 2359304 | tf_op jit(solution)/shard_map/ppermute | solution.py:792
  273.0 11.0 %collective-permute-start.43 = (bf16[128,1024]{1,0:T(8,128)(2,1)S(1)}, bf16[128,1024]{1,0:T(8,128)(2,1)S(1)}, u32[]{:S(2)}, u32[]{:S(2)}) collective-permute-start(bf16[128,1024]{1,0:T(8,128)(2,1)S(1)} %slice.68), channel_id=1, source_target_pairs={{0,3},{1,0},{2,1},{3,2},{4,7},{5,4},{6,5},{7,6},{8,11},{9,8},{10,9... | collective-permute-start | bytes 786440 | tf_op jit(solution)/shard_map/ppermute | solution.py:792
  273.1 11.9 %collective-permute-start.44 = (bf16[128,1024]{1,0:T(8,128)(2,1)S(1)}, bf16[128,1024]{1,0:T(8,128)(2,1)S(1)}, u32[]{:S(2)}, u32[]{:S(2)}) collective-permute-start(bf16[128,1024]{1,0:T(8,128)(2,1)S(1)} %slice.69), channel_id=1, source_target_pairs={{0,1},{1,2},{2,3},{3,0},{4,5},{5,6},{6,7},{7,4},{8,9},{9,10},{10,1... | collective-permute-start | bytes 786440 | tf_op jit(solution)/shard_map/ppermute | solution.py:792
  297.1 16.5 %collective-permute-start.47 = (bf16[128,1024]{1,0:T(8,128)(2,1)S(1)}, bf16[128,1024]{1,0:T(8,128)(2,1)S(1)}, u32[]{:S(2)}, u32[]{:S(2)}) collective-permute-start(bf16[128,1024]{1,0:T(8,128)(2,1)S(1)} %get-tuple-element.306), channel_id=1, source_target_pairs={{0,1},{1,2},{2,3},{3,0},{4,5},{5,6},{6,7},{7,4},{8,9},{9,10},{10,1... | collective-permute-start | bytes 786440 | tf_op jit(solution)/shard_map/ppermute | solution.py:792
  297.2 16.4 %collective-permute-start.48 = (bf16[128,1024]{1,0:T(8,128)(2,1)S(1)}, bf16[128,1024]{1,0:T(8,128)(2,1)S(1)}, u32[]{:S(2)}, u32[]{:S(2)}) collective-permute-start(bf16[128,1024]{1,0:T(8,128)(2,1)S(1)} %get-tuple-element.307), channel_id=1, source_target_pairs={{0,3},{1,0},{2,1},{3,2},{4,7},{5,4},{6,5},{7,6},{8,11},{9,8},{10,9... | collective-permute-start | bytes 786440 | tf_op jit(solution)/shard_map/ppermute | solution.py:792
  313.6 13.2 %collective-permute-start.51 = (bf16[16,32,768]{2,1,0:T(8,128)(2,1)S(1)}, bf16[16,32,768]{2,1,0:T(8,128)(2,1)S(1)}, u32[]{:S(2)}, u32[]{:S(2)}) collective-permute-start(bf16[16,32,768]{2,1,0:T(8,128)(2,1)S(1)} %get-tuple-element.327), channel_id=1, source_target_pairs={{0,4},{4,0},{8,12},{12,8},{16,20},{20,16},{24,28},{28,24},{32,36},... | collective-permute-start | bytes 2359304 | tf_op jit(solution)/shard_map/ppermute | solution.py:777
  323.4 15.8 %collective-permute-start.49 = (bf16[256,1024]{1,0:T(8,128)(2,1)}, bf16[256,1024]{1,0:T(8,128)(2,1)S(1)}, u32[]{:S(2)}, u32[]{:S(2)}) collective-permute-start(bf16[256,1024]{1,0:T(8,128)(2,1)} %get-tuple-element.310), channel_id=1, source_target_pairs={{0,1},{1,2},{2,3},{3,0},{4,5},{5,6},{6,7},{7,4},{8,9},{9,10},{10,1... | collective-permute-start | bytes 1572872 | tf_op jit(solution)/shard_map/ppermute | solution.py:792
  323.9 15.4 %collective-permute-start.50 = (bf16[256,1024]{1,0:T(8,128)(2,1)S(1)}, bf16[256,1024]{1,0:T(8,128)(2,1)S(1)}, u32[]{:S(2)}, u32[]{:S(2)}) collective-permute-start(bf16[256,1024]{1,0:T(8,128)(2,1)S(1)} %get-tuple-element.311), channel_id=1, source_target_pairs={{0,3},{1,0},{2,1},{3,2},{4,7},{5,4},{6,5},{7,6},{8,11},{9,8},{10,9... | collective-permute-start | bytes 1572872 | tf_op jit(solution)/shard_map/ppermute | solution.py:792
  327.9 11.3 %collective-permute-start.56 = (bf16[208,768]{1,0:T(8,128)(2,1)}, bf16[208,768]{1,0:T(8,128)(2,1)S(1)}, u32[]{:S(2)}, u32[]{:S(2)}) collective-permute-start(bf16[208,768]{1,0:T(8,128)(2,1)} %get-tuple-element.330), channel_id=1, source_target_pairs={{0,32},{4,12},{8,40},{12,20},{16,48},{20,28},{24,56},{28,4},{32,64... | collective-permute-start | bytes 958472 | tf_op jit(solution)/shard_map/ppermute | solution.py:788
  328.0 13.2 %collective-permute-start.57 = (bf16[208,768]{1,0:T(8,128)(2,1)}, bf16[208,768]{1,0:T(8,128)(2,1)S(1)}, u32[]{:S(2)}, u32[]{:S(2)}) collective-permute-start(bf16[208,768]{1,0:T(8,128)(2,1)} %get-tuple-element.331), channel_id=1, source_target_pairs={{0,64},{4,20},{8,72},{12,28},{16,80},{20,4},{24,88},{28,12},{32,96... | collective-permute-start | bytes 958472 | tf_op jit(solution)/shard_map/ppermute | solution.py:788
  341.4 9.6 %collective-permute-start.60 = (bf16[112,768]{1,0:T(8,128)(2,1)S(1)}, bf16[112,768]{1,0:T(8,128)(2,1)S(1)}, u32[]{:S(2)}, u32[]{:S(2)}) collective-permute-start(bf16[112,768]{1,0:T(8,128)(2,1)S(1)} %get-tuple-element.339), channel_id=1, source_target_pairs={{0,16},{4,68},{8,24},{12,76},{16,0},{20,84},{24,8},{28,92},{32,48}... | collective-permute-start | bytes 516104 | tf_op jit(solution)/shard_map/ppermute | solution.py:788
  (38 other events, 281.4 us)
Sparse Core Ops, SparseCore 0:
  10.2 76.8 all-gather.2
  249.1 87.5 reduce-scatter.1
